TPU v7x, 256 devices: a whole 4x4x8 slice. The times are simulated.
256 devices in a mesh: section: 4 (over z_hi, core), dp: 64 (over y, z_lo, x).
Axes of the slice: x: 4, y: 4, z: 8 (z_hi: 2, z_lo: 4; z = z_hi * 4 + z_lo), core: 2. Of those that a mesh axis runs over, the one named last changes fastest.
Arguments:
- stash: bfloat16 [4, 8192, 3072], P('section', 'dp'), may hold values from -16 to 16
- cotangent: bfloat16 [8192, 3072], P('dp'), may hold values from -6 to 6
- domain_ids: int32 [64], P('dp'), may hold values from 0 to 3, never falling along the last dimension, each value on 1 to 32 neighbouring positions
- shared_weight: bfloat16 [4, 3072, 256], P('section', 'dp'), may hold values from 0.5 to 2
- domain_weight: bfloat16 [4, 4, 3072, 256], P('section', None, 'dp'), may hold values from -0.375 to 0.375
- shared_bias: bfloat16 [4, 3072], P('section', 'dp'), may hold values from -3 to 3
- domain_bias: bfloat16 [4, 4, 3072], P('section', None, 'dp'), may hold values from -3 to 3
Outputs:
- d_inputs: bfloat16 [4, 8192, 3072], P('section', 'dp')
- d_shared: float32 [4, 3072, 256], P('section', 'dp')
- d_domain: float32 [4, 4, 3072, 256], P('section', None, 'dp')
- d_bias_shared: float32 [4, 3072], P('section', 'dp')
- d_bias_domain: float32 [4, 4, 3072], P('section', None, 'dp')
Inputs may be any that keep to these rules, and one draw needn't show every extreme that they name: `domain_ids`: never falls from one micro-batch to the next; each of the 4 domains holds at least one micro-batch.
All inputs are finite; a program needn't handle non-finite values.
Results may differ from a plain program's by a relative error of at most 0.0077.
Values may be sent and summed in bfloat16 or wider, within the bound.
No kernel may reach another device: no remote copies, remote signals or barrier semaphores. Data moves between devices by JAX's collectives and lax.ppermute only.
A program may use at most 192 MiB of HBM per device.

v0:
```python
import jax
import jax.numpy as jnp
from jax import lax
from jax.sharding import PartitionSpec as P

D = 3072
GS = 256
DOMAINS = 4
ROWS = 128


def shifted(block, axis, distance):
    devices = range(lax.axis_size(axis))
    route = [(i - distance, i) for i in devices if i - distance in devices]
    return lax.ppermute(block, axis, route)


def block_grad(inputs, incoming, kernel, offset):
    count = inputs.shape[0]
    groups = kernel.shape[0]
    split_in = inputs.reshape(count, groups, -1)
    pre = (
        jnp.einsum("rgi,gio->rgo", split_in, kernel, preferred_element_type=jnp.float32).reshape(
            count, -1
        )
        + offset[None]
    )
    sigma = jax.nn.sigmoid(pre)
    slope = sigma * (1.0 + pre * (1.0 - sigma))
    signal = (incoming.astype(jnp.float32) * slope).astype(jnp.bfloat16)
    split_sig = signal.reshape(count, groups, -1)
    back = jnp.einsum(
        "rgo,gio->rgi", split_sig, kernel, preferred_element_type=jnp.float32
    ).reshape(count, -1)
    outgoing = (incoming.astype(jnp.float32) + back).astype(jnp.bfloat16)
    grad_kernel = jnp.einsum(
        "rgi,rgo->gio", split_in, split_sig, preferred_element_type=jnp.float32
    )
    grad_offset = jnp.sum(signal.astype(jnp.float32), axis=0)
    return (outgoing, grad_kernel, grad_offset)


def body(stash, cotangent, domain_ids, shared_weight, domain_weight, shared_bias, domain_bias):
    groups = D // GS
    bias_stack = jnp.concatenate([shared_bias, domain_bias[0]], axis=0)
    local_kernel = (
        shared_weight[0][None].astype(jnp.float32) * domain_weight[0].astype(jnp.float32)
    ).astype(jnp.bfloat16)
    kernels_full, biases_full = (
        lax.all_gather(local_kernel, "dp", axis=1, tiled=True),
        lax.all_gather(bias_stack, "dp", axis=1, tiled=True),
    )
    kernels = kernels_full.reshape(DOMAINS, groups, GS, GS)
    offsets = biases_full[0][None].astype(jnp.float32) + biases_full[1:].astype(jnp.float32)
    section_count = lax.axis_size("section")
    section_index = lax.axis_index("section")
    inputs_all = stash[0]
    blocks = inputs_all.shape[0] // ROWS
    start = (
        jnp.zeros((DOMAINS, groups, GS, GS), jnp.float32),
        jnp.zeros((DOMAINS, D), jnp.float32),
    )

    def apply(state, inputs, incoming, domain):
        grad_kernels, grad_offsets = state
        kernel = lax.dynamic_index_in_dim(kernels, domain, 0, keepdims=False)
        offset = lax.dynamic_index_in_dim(offsets, domain, 0, keepdims=False)
        outgoing, grad_kernel, grad_offset = block_grad(inputs, incoming, kernel, offset)
        grad_kernels = grad_kernels.at[domain].add(grad_kernel)
        grad_offsets = grad_offsets.at[domain].add(grad_offset)
        return (outgoing, (grad_kernels, grad_offsets))

    def section_pass(incoming_all):

        def advance(state, item):
            inputs, incoming, domain = item
            outgoing, state = apply(state, inputs, incoming, domain)
            return (state, outgoing)

        items = (
            inputs_all.reshape(blocks, ROWS, D),
            incoming_all.reshape(blocks, ROWS, D),
            domain_ids,
        )
        state, produced = lax.scan(advance, start, items)
        return (produced.reshape(-1, D), state[0], state[1])

    kept = (jnp.zeros_like(cotangent), start[0], start[1])
    incoming_all = cotangent
    for turn in range(section_count):
        active = section_count - 1 - turn
        kept = lax.cond(
            section_index == active,
            section_pass,
            lambda arriving, previous=kept: previous,
            incoming_all,
        )
        if turn + 1 < section_count:
            incoming_all = shifted(kept[0], "section", -1)
    outgoing_all, grad_kernels, grad_offsets = kept
    flat_kernels = grad_kernels.reshape(DOMAINS, D, GS)
    shares, offset_shares = (
        lax.psum_scatter(flat_kernels, "dp", scatter_dimension=1, tiled=True),
        lax.psum_scatter(grad_offsets, "dp", scatter_dimension=1, tiled=True),
    )
    grad_shared = jnp.sum(shares * domain_weight[0].astype(jnp.float32), axis=0)
    grad_domain = shares * shared_weight[0].astype(jnp.float32)[None]
    return (
        outgoing_all[None],
        grad_shared[None],
        grad_domain[None],
        jnp.sum(offset_shares, axis=0)[None],
        offset_shares[None],
    )


def solution(mesh):
    in_specs = (
        P("section", "dp", None),
        P("dp", None),
        P("dp"),
        P("section", "dp", None),
        P("section", None, "dp", None),
        P("section", "dp"),
        P("section", None, "dp"),
    )
    out_specs = (
        P("section", "dp", None),
        P("section", "dp", None),
        P("section", None, "dp", None),
        P("section", "dp"),
        P("section", None, "dp"),
    )
    return jax.shard_map(body, mesh=mesh, in_specs=in_specs, out_specs=out_specs, check_vma=False)
```

profile of v0, /device:TPU:0, one launch (start us, length us, event | category | flops | bytes accessed | tf_op | source)
XLA Modules:
  0.0 1289.5 jit_solution(14872477257716277792)
XLA Ops:
  7.2 0.0 all-gather.3.cloned.1.call-start
  7.2 0.7 bitcast_convert_fusion
  8.0 1.6 fusion.36
  9.5 0.0 all-gather.3.cloned.1.call-update
  9.5 0.0 reduce-scatter.7.cloned.1.call-start
  9.6 0.7 maximum_bitcast_fusion
  10.3 186.8 %all-gather = bf16[64,48,5]{1,2,0:T(8,128)(2,1)S(1)} all-gather(bf16[1,48,5]{1,2,0:T(8,128)(2,1)S(1)} %maximum_bitcast_fusion), channel_id=1, replica_groups=mesh['section'=4,'dp'=64] {'dp'}, dimensions={0}, use_global_device_ids=true | all-gather | bytes 31200 | tf_op jit(solution)/shard_map/all_gather | solution.py:51
  197.1 0.2 reshape.528
  197.3 172.2 %all-gather.3.cloned.1.call-done = bf16[4,3072,256]{2,1,0:T(8,128)(2,1)} async-done(((bf16[4,48,256]{2,1,0:T(8,128)(2,1)}), bf16[4,3072,256]{2,1,0:T(8,128)(2,1)}) %all-gather.3.cloned.1.call-update) | async-done | bytes 6291472 | tf_op jit(solution)/shard_map/all_gather | solution.py:50
  369.5 6.7 conditional.4
  369.5 0.6 broadcast_in_dim.63
  370.2 0.1 broadcast_in_dim.61
  370.3 6.0 broadcast_in_dim.62
  376.3 1.3 collective-permute-start
  377.6 2.9 collective-permute-done
  380.4 1.3 collective-permute-start.1
  381.7 12.1 collective-permute-done.1
  393.9 1.3 collective-permute-start.2
  395.1 78.1 %collective-permute-done.2 = bf16[128,3072]{0,1:T(8,128)(2,1)S(1)} collective-permute-done((bf16[128,3072]{0,1:T(8,128)(2,1)S(1)}, bf16[128,3072]{0,1:T(8,128)(2,1)S(1)}, u32[]{:S(2)}, u32[]{:S(2)}) %collective-permute-start.2) | collective-permute-done | bytes 786464 | tf_op jit(solution)/shard_map/ppermute | solution.py:15
  473.2 35.2 %conditional.7 = (f32[4,12,256,256]{2,3,1,0:T(8,128)}, f32[4,3072]{1,0:T(4,128)}, bf16[1,128,3072]{2,1,0:T(8,128)(2,1)}) conditional(s32[]{:T(128)} %convert_element_type.141, (f32[4,12,256,256]{2,3,1,0:T(8,128)}, f32[4,3072]{1,0:T(4,128)}, bf16[128,3072]{0,1:T(8,128)(2,1)S(1)}) %tuple.100, (s32[1]{0:T(128)}, bf16[128,3072]{0,1:T(8,128)(2,1)S(1)}, ...), branch_computations={%region_15.16_spmd, %region_16.20_spmd} | conditional | flops 614989824 | bytes 53676216 | solution.py:92
  475.2 0.5 broadcast.395
  475.7 0.7 fusion.41
  476.4 1.4 and_reduce_fusion.6
  477.7 1.4 and_reduce_fusion.7
  479.1 1.5 copy.89
  480.6 8.6 copy.88
  489.3 0.0 copy-done.1
  489.3 2.2 multiply_convert_fusion.7
  491.5 0.0 copy-start.2
  491.5 2.1 fusion.28
  493.6 0.0 copy-done.2
  493.6 2.0 fusion.27
  495.6 1.2 copy.111
  496.8 0.6 broadcast_select_fusion.3
  497.4 0.6 broadcast_in_dim.71
  498.1 1.5 scatter-add.29
  499.5 6.0 broadcast_in_dim.70
  505.5 2.9 bitcast_dynamic-update-slice_fusion.3
  508.4 2.5 copy.108
  511.0 0.0 reduce-scatter.7.cloned.1.call-update
  511.0 0.0 reduce-scatter.5.cloned.1.call-start
  511.0 12.6 copy.90
  523.6 0.0 reduce-scatter.5.cloned.1.call-update
  523.6 359.2 %reduce-scatter.7.cloned.1.call-done = f32[48,4]{1,0:T(8,128)} async-done(((f32[3072,4]{1,0:T(8,128)}), f32[48,4]{1,0:T(8,128)}) %reduce-scatter.7.cloned.1.call-update) | async-done | bytes 784
  882.9 1.4 copy.109
  884.3 1.4 bitcast_reduce_fusion
  885.6 395.1 %reduce-scatter.5.cloned.1.call-done = f32[4,48,256]{2,1,0:T(8,128)} async-done(((f32[4,3072,256]{2,1,0:T(8,128)}), f32[4,48,256]{2,1,0:T(8,128)}) %reduce-scatter.5.cloned.1.call-update) | async-done | bytes 196624 | tf_op jit(solution)/shard_map/reduce_scatter | solution.py:103
  1280.8 2.2 multiply_bitcast_fusion
  (9 shorter events, 0.1 us)
Async XLA Ops:
  7.2 362.4 %all-gather.3.cloned.1.call-start = ((), (), s32[]{:S(2)}) async-start(), calls=%async_computation.2 | async-start | bytes 6389760 | tf_op jit(solution)/shard_map/all_gather | solution.py:50
  9.5 873.3 %reduce-scatter.7.cloned.1.call-start = ((), (), s32[]{:S(2)}) async-start(), calls=%async_computation.4 | async-start | bytes 1597440
  376.3 4.2 collective-permute-start
  380.4 13.4 %collective-permute-start.1 = (bf16[128,3072]{0,1:T(8,128)(2,1)S(1)}, bf16[128,3072]{0,1:T(8,128)(2,1)S(1)}, u32[]{:S(2)}, u32[]{:S(2)}) collective-permute-start(bf16[128,3072]{0,1:T(8,128)(2,1)S(1)} %get-tuple-element.343), channel_id=1, source_target_pairs={{64,0},{128,64},{192,128},{65,1},{129,65},{193,129},{66,2},{130,66... | collective-permute-start | bytes 2359304 | tf_op jit(solution)/shard_map/ppermute | solution.py:15
  393.9 79.4 %collective-permute-start.2 = (bf16[128,3072]{0,1:T(8,128)(2,1)S(1)}, bf16[128,3072]{0,1:T(8,128)(2,1)S(1)}, u32[]{:S(2)}, u32[]{:S(2)}) collective-permute-start(bf16[128,3072]{0,1:T(8,128)(2,1)S(1)} %get-tuple-element.346), channel_id=1, source_target_pairs={{64,0},{128,64},{192,128},{65,1},{129,65},{193,129},{66,2},{130,66... | collective-permute-start | bytes 2359304 | tf_op jit(solution)/shard_map/ppermute | solution.py:15
  473.2 16.0 %copy-start.1 = (bf16[128,3072]{0,1:T(8,128)(2,1)}, bf16[128,3072]{0,1:T(8,128)(2,1)S(1)}, u32[]{:S(2)}) copy-start(bf16[128,3072]{0,1:T(8,128)(2,1)S(1)} %get-tuple-element.325) | copy-start | bytes 2359300 | tf_op jit(solution)/shard_map/cond
  491.5 2.1 copy-start.2
  511.0 769.8 %reduce-scatter.5.cloned.1.call-start = ((), (), s32[]{:S(2)}) async-start(), calls=%async_computation.3 | async-start | bytes 12779520 | tf_op jit(solution)/shard_map/reduce_scatter | solution.py:103
  523.6 757.1 %copy-start.3 = (bf16[1,4,48,256]{3,2,1,0:T(8,128)(2,1)S(1)}, bf16[1,4,48,256]{3,2,1,0:T(8,128)(2,1)}, u32[]{:S(2)}) copy-start(bf16[1,4,48,256]{3,2,1,0:T(8,128)(2,1)} %param.35) | copy-start | bytes 294916
Sparse Core Ops, SparseCore 0:
  10.4 359.1 all-gather.2
  511.1 371.7 reduce-scatter.6
  885.6 395.1 reduce-scatter.4
where the time goes:
time: 1290 us
  waiting for transfers between devices  1020 us (79%)
  blocking collectives  187 us (14%)
  local copies, waits for them, and re-layouts  44 us (3%)
  between operations  13.8 us (1%)
    reduce_scatter x1, waiting for transfers between devices, body(): lax.psum_scatter(flat_kernels, 'dp', scatter_dimension=1, tiled=True)  395 us
    unnamed x4, waiting for transfers between devices  359 us
    all_gather x1, blocking collectives, body(): lax.all_gather(bias_stack, 'dp', axis=1, tiled=True)  187 us
    all_gather x1, waiting for transfers between devices, body(): lax.all_gather(local_kernel, 'dp', axis=1, tiled=True)  172 us
    ppermute x3, waiting for transfers between devices, shifted(): return lax.ppermute(block, axis, route)  93.1 us
  transfers between devices with their start and end apart: 6, of which 6 were waited for; matrix products, arithmetic and copies ran while one was open for 1% of the time, Pallas kernels for 0%

commit v1 on v0

v1 whole, which is shorter than its diff:
```python
import jax
import jax.numpy as jnp
from jax import lax
from jax.experimental import pallas as pl
from jax.experimental.pallas import tpu as pltpu
from jax.sharding import Mesh, PartitionSpec as P

D = 3072
GS = 256
DOMAINS = 4
ROWS = 128
NY, NZ, NX = 4, 4, 4
SHARD = 48
SLAB = D // NY
SG = SLAB // GS
PIECE = NZ * SHARD
TILE = 16
BLOCK = PIECE + TILE
VMEM = pl.BlockSpec(memory_space=pltpu.VMEM)
SMEM = pl.BlockSpec(memory_space=pltpu.SMEM)
BF = jnp.bfloat16
F32 = jnp.float32


def params():
    return pltpu.CompilerParams(vmem_limit_bytes=48 * 1024 * 1024)


def cost(flops, bytes_accessed):
    return pl.CostEstimate(flops=flops, bytes_accessed=bytes_accessed, transcendentals=0)


def prep_kernel(sw, dw, tile, out):
    shared = sw[...].astype(F32)
    for k in range(DOMAINS):
        product = (shared * dw[k].astype(F32)).astype(BF)
        for z in range(NZ):
            out[z, k * SHARD : (k + 1) * SHARD, :] = product
    for z in range(NZ):
        out[z, PIECE:, :] = tile[...]


def prep(sw, dw, tile):
    return pl.pallas_call(
        prep_kernel,
        out_shape=jax.ShapeDtypeStruct((NZ, BLOCK, GS), BF),
        in_specs=[VMEM, VMEM, VMEM],
        out_specs=VMEM,
        cost_estimate=cost(10**5, 10**6),
        name="prep",
    )(sw, dw, tile)


def pick_kernel(ids, held, out):
    step = pl.program_id(0)
    tile = held[0, PIECE:, :].astype(F32)
    for z in range(1, NZ):
        tile = tile + held[z, PIECE:, :].astype(F32)
    tile = tile.astype(BF)
    for i in range(NX):
        start = pl.multiple_of(ids[step * NX + i, 0] * SHARD, TILE)
        for z in range(NZ):
            out[i, z * SHARD : (z + 1) * SHARD, :] = held[z, pl.ds(start, SHARD), :]
        out[i, PIECE:, :] = tile


def pick(ids, held):
    return pl.pallas_call(
        pick_kernel,
        grid=(NY,),
        out_shape=jax.ShapeDtypeStruct((NY * NX, BLOCK, GS), BF),
        in_specs=[SMEM, pl.BlockSpec((NZ, BLOCK, GS), lambda i: (0, 0, 0))],
        out_specs=pl.BlockSpec((NX, BLOCK, GS), lambda i: (i, 0, 0)),
        cost_estimate=cost(10**5, 2 * 10**6),
        name="pick",
    )(ids, held)


def slope_kernel(own, got, x, slope, kernel, offsets):
    domain = own[0]
    tile = got[0, PIECE:, :].astype(F32)
    for i in range(1, NX):
        tile = tile + got[i, PIECE:, :].astype(F32)
    offsets[...] = tile
    for z in range(NZ):
        for i in range(NX):
            at = (z * NX + i) * SHARD
            kernel[at : at + SHARD, :] = got[i, z * SHARD : (z + 1) * SHARD, :]
    for q in range(SG):
        lanes = slice(q * GS, (q + 1) * GS)
        offset = offsets[q : q + 1, :] + offsets[pl.ds((1 + domain) * SG + q, 1), :]
        pre = jnp.dot(x[:, lanes], kernel[lanes, :], preferred_element_type=F32) + offset
        sigma = jax.nn.sigmoid(pre)
        slope[:, lanes] = sigma * (1.0 + pre * (1.0 - sigma))


def slopes(own, got, x):
    return pl.pallas_call(
        slope_kernel,
        grid=(NY,),
        out_shape=(
            jax.ShapeDtypeStruct((ROWS, D), F32),
            jax.ShapeDtypeStruct((D, GS), BF),
        ),
        in_specs=[
            SMEM,
            pl.BlockSpec((NX, BLOCK, GS), lambda i: (i, 0, 0)),
            pl.BlockSpec((ROWS, SLAB), lambda i: (0, i)),
        ],
        out_specs=(
            pl.BlockSpec((ROWS, SLAB), lambda i: (0, i)),
            pl.BlockSpec((SLAB, GS), lambda i: (i, 0)),
        ),
        scratch_shapes=[pltpu.VMEM((TILE, GS), F32)],
        compiler_params=params(),
        cost_estimate=cost(2 * 10**8, 6 * 10**6),
        name="slopes",
    )(own, got, x)


def back_product(signal, kernel):
    return lax.dot_general(
        signal, kernel, (((1,), (1,)), ((), ())), preferred_element_type=F32
    )


def chain_kernel(up, slope, kernel, out):
    for q in range(SG):
        lanes = slice(q * GS, (q + 1) * GS)
        above = up[:, lanes].astype(F32)
        signal = (above * slope[:, lanes]).astype(BF)
        out[:, lanes] = (above + back_product(signal, kernel[lanes, :])).astype(BF)


def chain(up, slope, kernel):
    wide = pl.BlockSpec((ROWS, SLAB), lambda i: (0, i))
    return pl.pallas_call(
        chain_kernel,
        grid=(NY,),
        out_shape=jax.ShapeDtypeStruct((ROWS, D), BF),
        in_specs=[wide, wide, pl.BlockSpec((SLAB, GS), lambda i: (i, 0))],
        out_specs=wide,
        compiler_params=params(),
        cost_estimate=cost(2 * 10**8, 5 * 10**6),
        name="chain",
    )(up, slope, kernel)


def grads_kernel(section, up3, up2, up1, up0, slope, kernel, x, out, send, tile):
    s = section[0]
    tile[...] = jnp.zeros_like(tile)
    for q in range(SG):
        lanes = slice(q * GS, (q + 1) * GS)
        up = jnp.where(
            s == 3,
            up3[:, lanes],
            jnp.where(s == 2, up2[:, lanes], jnp.where(s == 1, up1[:, lanes], up0[:, lanes])),
        )
        above = up.astype(F32)
        signal = (above * slope[:, lanes]).astype(BF)
        out[:, lanes] = (above + back_product(signal, kernel[lanes, :])).astype(BF)
        grad = lax.dot_general(
            x[:, lanes], signal, (((0,), (0,)), ((), ())), preferred_element_type=F32
        ).astype(BF)
        for u in range(GS // TILE):
            row = q * GS + u * TILE
            shard, inner = row // SHARD, row % SHARD
            z, i = shard // NX, shard % NX
            at = z * SHARD + inner
            send[i, at : at + TILE, :] = grad[u * TILE : (u + 1) * TILE, :]
        total = jnp.sum(signal.astype(F32), axis=0, keepdims=True)
        high = total.astype(BF).astype(F32)
        tile[q : q + 1, :] = high
        tile[SG + q : SG + q + 1, :] = total - high
    for i in range(NX):
        send[i, PIECE:, :] = tile[...].astype(BF)


def grads(section, ups, slope, kernel, x):
    wide = pl.BlockSpec((ROWS, SLAB), lambda i: (0, i))
    return pl.pallas_call(
        grads_kernel,
        grid=(NY,),
        out_shape=(
            jax.ShapeDtypeStruct((ROWS, D), BF),
            jax.ShapeDtypeStruct((NY * NX, BLOCK, GS), BF),
        ),
        in_specs=[SMEM] + [wide] * 5 + [pl.BlockSpec((SLAB, GS), lambda i: (i, 0)), wide],
        out_specs=(wide, pl.BlockSpec((NX, BLOCK, GS), lambda i: (i, 0, 0))),
        scratch_shapes=[pltpu.VMEM((TILE, GS), F32)],
        compiler_params=params(),
        cost_estimate=cost(4 * 10**8, 8 * 10**6),
        name="grads",
    )(section, *ups, slope, kernel, x)


def merge_kernel(ids, got, out, total, tile):
    step = pl.program_id(0)

    @pl.when(step == 0)
    def _():
        total[...] = jnp.zeros_like(total)

    for i in range(NX):
        domain = ids[step * NX + i, 0]
        total[domain] += got[i].astype(F32)

    @pl.when(step == NY - 1)
    def _():
        tile[...] = jnp.zeros_like(tile)
        for k in range(DOMAINS):
            for z in range(NZ):
                out[z, k * SHARD : (k + 1) * SHARD, :] = total[
                    k, z * SHARD : (z + 1) * SHARD, :
                ].astype(BF)
            tile[k * SG : (k + 1) * SG, :] = (
                total[k, PIECE : PIECE + SG, :] + total[k, PIECE + SG : PIECE + 2 * SG, :]
            )
        for z in range(NZ):
            out[z, PIECE:, :] = tile[...].astype(BF)


def merge(ids, got):
    return pl.pallas_call(
        merge_kernel,
        grid=(NY,),
        out_shape=jax.ShapeDtypeStruct((NZ, BLOCK, GS), BF),
        in_specs=[SMEM, pl.BlockSpec((NX, BLOCK, GS), lambda i: (i, 0, 0))],
        out_specs=pl.BlockSpec((NZ, BLOCK, GS), lambda i: (0, 0, 0)),
        scratch_shapes=[pltpu.VMEM((DOMAINS, BLOCK, GS), F32), pltpu.VMEM((TILE, GS), F32)],
        compiler_params=params(),
        cost_estimate=cost(10**6, 2 * 10**6),
        name="merge",
    )(ids, got)


def finish_kernel(got, sw, dw, d_shared, d_domain, bias):
    shared = sw[...].astype(F32)
    summed = jnp.zeros((SHARD, GS), F32)
    for k in range(DOMAINS):
        rows = slice(k * SHARD, (k + 1) * SHARD)
        share = got[0, rows, :].astype(F32)
        for z in range(1, NZ):
            share = share + got[z, rows, :].astype(F32)
        summed = summed + share * dw[k].astype(F32)
        d_domain[k] = share * shared
    d_shared[...] = summed
    tile = got[0, PIECE:, :].astype(F32)
    for z in range(1, NZ):
        tile = tile + got[z, PIECE:, :].astype(F32)
    bias[...] = tile


def finish(got, sw, dw):
    return pl.pallas_call(
        finish_kernel,
        out_shape=(
            jax.ShapeDtypeStruct((SHARD, GS), F32),
            jax.ShapeDtypeStruct((DOMAINS, SHARD, GS), F32),
            jax.ShapeDtypeStruct((TILE, GS), F32),
        ),
        in_specs=[VMEM, VMEM, VMEM],
        out_specs=(VMEM, VMEM, VMEM),
        cost_estimate=cost(10**6, 10**6),
        name="finish",
    )(got, sw, dw)


def exchange(block, axes):
    return lax.all_to_all(block, axes, 0, 0, tiled=True)


def body(stash, cotangent, domain_ids, shared_weight, domain_weight, shared_bias, domain_bias):
    x = stash[0]
    sw, dw = shared_weight[0], domain_weight[0]
    section = 2 * lax.axis_index("zhi") + lax.axis_index("core")
    place = PIECE * lax.axis_index("zlo") + SHARD * lax.axis_index("x")

    biases = jnp.concatenate([shared_bias, domain_bias[0]], axis=0)
    spread = lax.dynamic_update_slice(jnp.zeros((5, SLAB), BF), biases, (0, place))
    tile = jnp.pad(spread.reshape(5 * SG, GS), ((0, 1), (0, 0)))

    plane_ids = exchange(
        jnp.broadcast_to(domain_ids[0], (NY * NX, 1, 128)), ("y", "x")
    ).reshape(NY * NX, 128)
    held = exchange(prep(sw, dw, tile), "zlo")
    got = exchange(pick(plane_ids, held), ("y", "x"))
    slope, kernel = slopes(domain_ids, got, x)

    ups = [cotangent]
    for turn in range(3):
        out = chain(ups[-1], slope, kernel)
        ups.append(lax.ppermute(out, ("zhi", "core"), [(3 - turn, 2 - turn)]))

    d_inputs, send = grads(jnp.reshape(section, (1,)), ups, slope, kernel, x)
    merged = merge(plane_ids, exchange(send, ("y", "x")))
    d_shared, d_domain, bias = finish(exchange(merged, "zlo"), sw, dw)
    d_bias = lax.dynamic_slice(
        bias[: DOMAINS * SG].reshape(DOMAINS, SLAB), (0, place), (DOMAINS, SHARD)
    )
    return (
        d_inputs[None],
        d_shared[None],
        d_domain[None],
        jnp.sum(d_bias, axis=0)[None],
        d_bias[None],
    )


def solution(mesh):
    fine = Mesh(mesh.devices.reshape(2, 2, NY, NZ, NX), ("zhi", "core", "y", "zlo", "x"))
    section, dp = ("zhi", "core"), ("y", "zlo", "x")
    in_specs = (
        P(section, dp, None),
        P(dp, None),
        P(dp),
        P(section, dp, None),
        P(section, None, dp, None),
        P(section, dp),
        P(section, None, dp),
    )
    out_specs = (
        P(section, dp, None),
        P(section, dp, None),
        P(section, None, dp, None),
        P(section, dp),
        P(section, None, dp),
    )
    return jax.shard_map(
        body, mesh=fine, in_specs=in_specs, out_specs=out_specs, check_vma=False
    )
```

time: 1290 us -> 160 us (0.12)
  the two profiles are of different devices: /device:TPU:0 before, /device:TPU:1 now
where the time goes in v1:
time: 160 us; the launch traced here: 159 us
  blocking collectives  92.4 us (58%)
  waiting for transfers between devices  26.9 us (17%)
  Pallas kernels  18.6 us (12%)
  starting transfers between devices  10.9 us (7%)
  local copies, waits for them, and re-layouts  6.67 us (4%)
  other arithmetic  1.86 us (1%)
    all_to_all x4, blocking collectives, exchange(): return lax.all_to_all(block, axes, 0, 0, tiled=True)  92.4 us
    ppermute x3, waiting for transfers between devices, body(): ups.append(lax.ppermute(out, ('zhi', 'core'), [(3 - turn, 2 - turn)]))  23.7 us
    all_to_all x1, starting transfers between devices, exchange(): return lax.all_to_all(block, axes, 0, 0, tiled=True)  7.58 us
    pallas_call x3, Pallas kernels, chain(): pl.pallas_call(chain_kernel, grid=(NY,), out_shape=jax.ShapeDtypeStruct((...  5.3 us
    pallas_call x1, Pallas kernels, grads(): pl.pallas_call(grads_kernel, grid=(NY,), out_shape=(jax.ShapeDtypeStruct(...  4.56 us
    unnamed x22, local copies, waits for them, and re-layouts  4.56 us
    ppermute x3, starting transfers between devices, body(): ups.append(lax.ppermute(out, ('zhi', 'core'), [(3 - turn, 2 - turn)]))  3.33 us
  transfers between devices with their start and end apart: 4, of which 3 were waited for; matrix products, arithmetic and copies ran while one was open for 1% of the time, Pallas kernels for 1%

profile of v1, /device:TPU:1, one launch (start us, length us, event | category | flops | bytes accessed | tf_op | source)
XLA Modules:
  0.0 158.7 jit_solution(6428841963758002768)
XLA Ops:
  1.3 0.6 broadcast_in_dim.21
  1.9 7.6 %all-to-all-start = ((s32[16,1,128]{2,1,0:T(1,128)}), s32[16,1,128]{2,1,0:T(1,128)S(1)}, u32[]{:S(2)}, u32[]{:S(2)}) async-start(s32[16,1,128]{2,1,0:T(1,128)} %broadcast_in_dim.21), calls=%async_computation | async-start | bytes 16384 | tf_op jit(solution)/shard_map/all_to_all | solution.py:270
  9.5 0.7 pad_maximum_fusion
  10.2 0.2 dynamic_update_slice.3
  10.4 0.6 pad.4.tile
  11.0 1.7 %prep.1 = bf16[4,208,256]{2,1,0:T(8,128)(2,1)} custom-call(bf16[48,256]{1,0:T(8,128)(2,1)} %bitcast.21, bf16[4,48,256]{2,1,0:T(8,128)(2,1)} %bitcast.19, bf16[16,256]{1,0:T(8,128)(2,1)} %pad.4.tile), custom_call_target="tpu_custom_call" | custom-call | flops 100000 | bytes 1000000 | tf_op jit(solution)/shard_map/prep/pallas_call | solution.py:44
  12.6 3.2 %all-to-all-done = s32[16,1,128]{2,1,0:T(1,128)S(1)} async-done(((s32[16,1,128]{2,1,0:T(1,128)}), s32[16,1,128]{2,1,0:T(1,128)S(1)}, u32[]{:S(2)}, u32[]{:S(2)}) %all-to-all-start) | async-done | bytes 8224 | tf_op jit(solution)/shard_map/all_to_all | solution.py:270
  15.8 0.0 copy-start.9
  15.8 16.5 %all_to_all.25.held = bf16[4,208,256]{2,1,0:T(8,128)(2,1)} all-to-all(bf16[4,208,256]{2,1,0:T(8,128)(2,1)} %prep.1), channel_id=1, replica_groups=mesh['zhi'=2,'core'=2,'y'=4,'zlo'=4,'x'=4] {'zlo'}, dimensions={0} | all-to-all | bytes 851968 | tf_op jit(solution)/shard_map/all_to_all | solution.py:270
  32.3 0.0 copy-done.9
  32.3 2.8 %pick.1 = bf16[16,208,256]{2,1,0:T(8,128)(2,1)} custom-call(s32[16,128]{1,0:T(8,128)} %bitcast.17, bf16[4,208,256]{2,1,0:T(8,128)(2,1)} %all_to_all.25.held), custom_call_target="tpu_custom_call" | custom-call | flops 100000 | bytes 2000000 | tf_op jit(solution)/shard_map/pick/pallas_call | solution.py:68
  35.1 0.0 copy-start.7
  35.1 27.1 %all_to_all.26.got = bf16[16,208,256]{2,1,0:T(8,128)(2,1)S(1)} all-to-all(bf16[16,208,256]{2,1,0:T(8,128)(2,1)} %pick.1), channel_id=1, replica_groups=mesh['zhi'=2,'core'=2,'y'=4,'zlo'=4,'x'=4] {'y','x'}, dimensions={0} | all-to-all | bytes 3407872 | tf_op jit(solution)/shard_map/all_to_all | solution.py:270
  62.1 0.0 copy-start.1
  62.1 0.0 copy-done.7
  62.1 1.3 slopes.1
  63.4 0.0 copy-start
  63.4 0.0 copy-done.1
  63.4 1.4 chain.3
  64.9 0.7 collective-permute-start
  65.6 0.0 collective-permute-done.up.up2
  65.6 0.0 copy-start.3
  65.6 1.4 chain.4
  67.1 0.0 copy-done.3
  67.1 1.3 collective-permute-start.1
  68.4 21.7 %collective-permute-done.1.up.up1 = bf16[128,3072]{1,0:T(8,128)(2,1)S(1)} collective-permute-done((bf16[128,3072]{1,0:T(8,128)(2,1)S(1)}, bf16[128,3072]{1,0:T(8,128)(2,1)S(1)}, u32[]{:S(2)}, u32[]{:S(2)}) %collective-permute-start.1) | collective-permute-done | bytes 786464 | tf_op jit(solution)/shard_map/ppermute | solution.py:293
  90.1 0.0 copy-done
  90.1 0.0 copy-start.5
  90.1 2.4 %chain.5 = bf16[128,3072]{1,0:T(8,128)(2,1)} custom-call(bf16[128,3072]{1,0:T(8,128)(2,1)S(1)} %collective-permute-done.1.up.up1, f32[128,3072]{1,0:T(8,128)S(1)} %get-tuple-element.12.slope, bf16[3072,256]{1,0:T(8,128)(2,1)S(1)} %get-tuple-element.13.kernel), custom_call_target="tpu_custom_call" | custom-call | flops 200000000 | bytes 5000000 | tf_op jit(solution)/shard_map/chain/pallas_call | solution.py:137
  92.5 0.0 copy-done.5
  92.5 1.3 collective-permute-start.2
  93.8 2.0 %collective-permute-done.2.up0 = bf16[128,3072]{1,0:T(8,128)(2,1)S(1)} collective-permute-done((bf16[128,3072]{1,0:T(8,128)(2,1)}, bf16[128,3072]{1,0:T(8,128)(2,1)S(1)}, u32[]{:S(2)}, u32[]{:S(2)}) %collective-permute-start.2) | collective-permute-done | bytes 786464 | tf_op jit(solution)/shard_map/ppermute | solution.py:293
  95.9 0.0 copy-start.2
  95.9 1.1 copy-done.2
  97.0 0.0 copy-start.4
  97.0 1.1 copy-done.4
  98.1 0.0 copy-start.6
  98.1 1.1 copy-done.6
  99.3 1.1 copy-done.8
  100.4 4.6 %grads.1 = (bf16[128,3072]{1,0:T(8,128)(2,1)}, bf16[16,208,256]{2,1,0:T(8,128)(2,1)}) custom-call(s32[1]{0:T(128)} %bitcast.section, bf16[128,3072]{1,0:T(8,128)(2,1)S(1)} %copy-done.2, bf16[128,3072]{1,0:T(8,128)(2,1)S(1)} %copy-done.4, bf16[128,3072]{1,0:T(8,128)(2,1)S(1)} %copy-done.6, bf16[128,3072]{1,0:T(8,128)(2,1)S(1)} %collective-permute-done.2.up0, ...), custom_call_target="tpu_custom_call" | custom-call | flops 400000000 | bytes 8000000 | tf_op jit(solution)/shard_map/grads/pallas_call | solution.py:181
  105.0 0.0 copy-start.10
  105.0 27.8 %all_to_all.27.got = bf16[16,208,256]{2,1,0:T(8,128)(2,1)S(1)} all-to-all(bf16[16,208,256]{2,1,0:T(8,128)(2,1)} %get-tuple-element.15), channel_id=1, replica_groups=mesh['zhi'=2,'core'=2,'y'=4,'zlo'=4,'x'=4] {'y','x'}, dimensions={0} | all-to-all | bytes 3407872 | tf_op jit(solution)/shard_map/all_to_all | solution.py:270
  132.8 0.0 copy-done.10
  132.8 1.2 merge.1
  134.0 21.1 %all_to_all.28.got = bf16[4,208,256]{2,1,0:T(8,128)(2,1)} all-to-all(bf16[4,208,256]{2,1,0:T(8,128)(2,1)S(1)} %merge.1), channel_id=1, replica_groups=mesh['zhi'=2,'core'=2,'y'=4,'zlo'=4,'x'=4] {'zlo'}, dimensions={0} | all-to-all | bytes 851968 | tf_op jit(solution)/shard_map/all_to_all | solution.py:270
  155.1 1.8 %finish.1 = (f32[48,256]{1,0:T(8,128)}, f32[4,48,256]{2,1,0:T(8,128)}, f32[16,256]{1,0:T(8,128)}) custom-call(bf16[4,208,256]{2,1,0:T(8,128)(2,1)} %all_to_all.28.got, bf16[48,256]{1,0:T(8,128)(2,1)} %bitcast.22, bf16[4,48,256]{2,1,0:T(8,128)(2,1)} %bitcast.20), custom_call_target="tpu_custom_call" | custom-call | flops 1000000 | bytes 1000000 | tf_op jit(solution)/shard_map/finish/pallas_call | solution.py:255
  156.8 0.7 reshape.25
  157.6 1.2 dynamic-slice_bitcast_fusion
  (3 shorter events, 0.0 us)
Async XLA Ops:
  1.9 13.9 %all-to-all-start = ((s32[16,1,128]{2,1,0:T(1,128)}), s32[16,1,128]{2,1,0:T(1,128)S(1)}, u32[]{:S(2)}, u32[]{:S(2)}) async-start(s32[16,1,128]{2,1,0:T(1,128)} %broadcast_in_dim.21), calls=%async_computation | async-start | bytes 16384 | tf_op jit(solution)/shard_map/all_to_all | solution.py:270
  15.8 16.5 %copy-start.9 = (s32[16,1,128]{2,1,0:T(1,128)}, s32[16,1,128]{2,1,0:T(1,128)S(1)}, u32[]{:S(2)}) copy-start(s32[16,1,128]{2,1,0:T(1,128)S(1)} %all-to-all-done) | copy-start | bytes 24580
  35.1 27.1 %copy-start.7 = (bf16[1,128,3072]{2,1,0:T(8,128)(2,1)S(1)}, bf16[1,128,3072]{2,1,0:T(8,128)(2,1)}, u32[]{:S(2)}) copy-start(bf16[1,128,3072]{2,1,0:T(8,128)(2,1)} %param.7) | copy-start | bytes 2359300
  62.1 1.3 copy-start.1
  63.4 26.6 %copy-start = (bf16[3072,256]{1,0:T(8,128)(2,1)}, bf16[3072,256]{1,0:T(8,128)(2,1)S(1)}, u32[]{:S(2)}) copy-start(bf16[3072,256]{1,0:T(8,128)(2,1)S(1)} %get-tuple-element.13.kernel) | copy-start | bytes 4718596
  64.9 0.7 collective-permute-start
  65.6 1.5 copy-start.3
  67.1 23.0 %collective-permute-start.1 = (bf16[128,3072]{1,0:T(8,128)(2,1)S(1)}, bf16[128,3072]{1,0:T(8,128)(2,1)S(1)}, u32[]{:S(2)}, u32[]{:S(2)}) collective-permute-start(bf16[128,3072]{1,0:T(8,128)(2,1)S(1)} %chain.4), channel_id=1, source_target_pairs={{128,64},{129,65},{130,66},{131,67},{132,68},{133,69},{134,70},{13... | collective-permute-start | bytes 2359304 | tf_op jit(solution)/shard_map/ppermute | solution.py:293
  90.1 2.4 %copy-start.5 = (bf16[128,3072]{1,0:T(8,128)(2,1)}, bf16[128,3072]{1,0:T(8,128)(2,1)S(1)}, u32[]{:S(2)}) copy-start(bf16[128,3072]{1,0:T(8,128)(2,1)S(1)} %collective-permute-done.1.up.up1) | copy-start | bytes 2359300
  92.5 3.4 %collective-permute-start.2 = (bf16[128,3072]{1,0:T(8,128)(2,1)}, bf16[128,3072]{1,0:T(8,128)(2,1)S(1)}, u32[]{:S(2)}, u32[]{:S(2)}) collective-permute-start(bf16[128,3072]{1,0:T(8,128)(2,1)} %chain.5), channel_id=1, source_target_pairs={{64,0},{65,1},{66,2},{67,3},{68,4},{69,5},{70,6},{71,7},{72,8},{73... | collective-permute-start | bytes 2359304 | tf_op jit(solution)/shard_map/ppermute | solution.py:293
  95.9 1.1 copy-start.2
  97.0 1.1 copy-start.4
  98.1 1.1 copy-start.6
  99.3 1.1 copy-start.8
  105.0 27.8 %copy-start.10 = (s32[16,1,128]{2,1,0:T(1,128)S(1)}, s32[16,1,128]{2,1,0:T(1,128)}, u32[]{:S(2)}) copy-start(s32[16,1,128]{2,1,0:T(1,128)} %copy-done.9) | copy-start | bytes 24580

commit v2 on v1

v2 whole, which is shorter than its diff:
```python
import jax
import jax.numpy as jnp
from jax import lax
from jax.experimental import pallas as pl
from jax.experimental.pallas import tpu as pltpu
from jax.sharding import Mesh, PartitionSpec as P

D = 3072
GS = 256
DOMAINS = 4
ROWS = 128
NY, NZ, NX = 4, 4, 4
SHARD = 48
SLAB = D // NY
SG = SLAB // GS
PIECE = NZ * SHARD
TILE = 16
BLOCK = PIECE + TILE
HALF = PIECE // 2
PART = HALF + TILE
FIRST = (0, 1)
LAST = (2,)
VMEM = pl.BlockSpec(memory_space=pltpu.VMEM)
SMEM = pl.BlockSpec(memory_space=pltpu.SMEM)
BF = jnp.bfloat16
F32 = jnp.float32


def call(kernel, name, flops, moved, limit=48, **rest):
    return pl.pallas_call(
        kernel,
        name=name,
        compiler_params=pltpu.CompilerParams(vmem_limit_bytes=limit * 1024 * 1024),
        cost_estimate=pl.CostEstimate(flops=flops, bytes_accessed=moved, transcendentals=0),
        **rest,
    )


def prep_kernel(at, sw, dw, sb, db, out, wide, tile):
    shared = sw[...].astype(F32)
    for k in range(DOMAINS):
        out[k * SHARD : (k + 1) * SHARD, :] = (shared * dw[k].astype(F32)).astype(BF)
    wide[...] = jnp.zeros_like(wide)
    wide[0:1, :SHARD] = sb[...].astype(F32)
    wide[1 : 1 + DOMAINS, :SHARD] = db[...].astype(F32)
    placed = pltpu.roll(wide[...], at[0], 1)
    tile[...] = jnp.zeros_like(tile)
    for k in range(1 + DOMAINS):
        for q in range(SG):
            row = k * SG + q
            tile[row : row + 1, :] = placed[k : k + 1, q * GS : (q + 1) * GS]
    out[PIECE:, :] = tile[...].astype(BF)


def prep(at, sw, dw, sb, db):
    return call(
        prep_kernel,
        "prep",
        10**5,
        3 * 10**5,
        out_shape=jax.ShapeDtypeStruct((BLOCK, GS), BF),
        in_specs=[SMEM, VMEM, VMEM, VMEM, VMEM],
        out_specs=VMEM,
        scratch_shapes=[pltpu.VMEM((8, SLAB), F32), pltpu.VMEM((TILE, GS), F32)],
    )(at, sw, dw, sb, db)


def pick_kernel(ids, z, *refs):
    held, out = refs[:NZ], refs[NZ]
    step = pl.program_id(0)
    tile = held[0][PIECE:, :].astype(F32)
    for k in range(1, NZ):
        tile = tile + held[k][PIECE:, :].astype(F32)
    tile = tile.astype(BF)
    for i in range(NX):
        start = pl.multiple_of(ids[step * NX + i, 0] * SHARD, TILE)
        for k in range(NZ):
            to = pl.multiple_of(((z[0] + NZ - k) % NZ) * SHARD, TILE)
            out[i, pl.ds(to, SHARD), :] = held[k][pl.ds(start, SHARD), :]
        out[i, PIECE:, :] = tile


def pick(ids, z, held):
    return call(
        pick_kernel,
        "pick",
        10**5,
        2 * 10**6,
        grid=(NY,),
        out_shape=jax.ShapeDtypeStruct((NY * NX, BLOCK, GS), BF),
        in_specs=[SMEM, SMEM] + [pl.BlockSpec((BLOCK, GS), lambda i: (0, 0))] * NZ,
        out_specs=pl.BlockSpec((NX, BLOCK, GS), lambda i: (i, 0, 0)),
    )(ids, z, *held)


def slope_kernel(own, got, x, slope0, slope1, kernel0, kernel1, kernel, offsets):
    domain = own[0]
    tile = got[0, PIECE:, :].astype(F32)
    for i in range(1, NX):
        tile = tile + got[i, PIECE:, :].astype(F32)
    offsets[...] = tile
    for z in range(NZ):
        for i in range(NX):
            at = (z * NX + i) * SHARD
            kernel[at : at + SHARD, :] = got[i, z * SHARD : (z + 1) * SHARD, :]
    cut = len(FIRST) * GS
    kernel0[...] = kernel[:cut, :]
    kernel1[...] = kernel[cut:, :]
    for q in range(SG):
        lanes = slice(q * GS, (q + 1) * GS)
        offset = offsets[q : q + 1, :] + offsets[pl.ds((1 + domain) * SG + q, 1), :]
        pre = jnp.dot(x[:, lanes], kernel[lanes, :], preferred_element_type=F32) + offset
        sigma = jax.nn.sigmoid(pre)
        slope = sigma * (1.0 + pre * (1.0 - sigma))
        if q in FIRST:
            slope0[:, lanes] = slope
        else:
            slope1[...] = slope


def columns(width):
    return pl.BlockSpec((ROWS, width), lambda i: (0, i))


def rows(height):
    return pl.BlockSpec((height, GS), lambda i: (i, 0))


def slopes(own, got, x):
    w0, w1 = len(FIRST) * GS, len(LAST) * GS
    return call(
        slope_kernel,
        "slopes",
        2 * 10**8,
        6 * 10**6,
        grid=(NY,),
        out_shape=(
            jax.ShapeDtypeStruct((ROWS, NY * w0), F32),
            jax.ShapeDtypeStruct((ROWS, NY * w1), F32),
            jax.ShapeDtypeStruct((NY * w0, GS), BF),
            jax.ShapeDtypeStruct((NY * w1, GS), BF),
        ),
        in_specs=[SMEM, pl.BlockSpec((NX, BLOCK, GS), lambda i: (i, 0, 0)), columns(SLAB)],
        out_specs=(columns(w0), columns(w1), rows(w0), rows(w1)),
        scratch_shapes=[pltpu.VMEM((SLAB, GS), BF), pltpu.VMEM((TILE, GS), F32)],
    )(own, got, x)


def back_product(signal, kernel):
    return lax.dot_general(
        signal, kernel, (((1,), (1,)), ((), ())), preferred_element_type=F32
    )


def first_kernel(section, up, slope, kernel, out, kept):
    for q in range(slope.shape[1] // GS):
        lanes = slice(q * GS, (q + 1) * GS)
        above = jnp.where(section[0] == 3, up[:, lanes].astype(F32), 0.0)
        kept[:, lanes] = above.astype(BF)
        signal = (above * slope[:, lanes]).astype(BF)
        out[:, lanes] = (above + back_product(signal, kernel[lanes, :])).astype(BF)


def next_kernel(before, up, slope, kernel, out, kept):
    for q in range(slope.shape[1] // GS):
        lanes = slice(q * GS, (q + 1) * GS)
        above = before[:, lanes].astype(F32) + up[:, lanes].astype(F32)
        kept[:, lanes] = above.astype(BF)
        signal = (above * slope[:, lanes]).astype(BF)
        out[:, lanes] = (above + back_product(signal, kernel[lanes, :])).astype(BF)


def of_slab(groups):
    if groups == FIRST:
        return columns(SLAB)
    return pl.BlockSpec((ROWS, GS), lambda i: (0, SG * i + LAST[0]))


def chain(groups, head, up, slope, kernel, first=False):
    width = len(groups) * GS
    shape = jax.ShapeDtypeStruct((ROWS, NY * width), BF)
    return call(
        first_kernel if first else next_kernel,
        "chain",
        10**8,
        2 * 10**6,
        grid=(NY,),
        out_shape=(shape, shape),
        in_specs=([SMEM, of_slab(groups)] if first else [columns(width)] * 2)
        + [columns(width), rows(width)],
        out_specs=(columns(width), columns(width)),
    )(head, up, slope, kernel)


def local_grads(before, up, slope, kernel, x, q, tile, row):
    lanes = slice(q * GS, (q + 1) * GS)
    above = before[:, lanes].astype(F32) + up[:, lanes].astype(F32)
    signal = (above * slope[:, lanes]).astype(BF)
    outgoing = (above + back_product(signal, kernel[lanes, :])).astype(BF)
    grad = lax.dot_general(
        x[:, lanes], signal, (((0,), (0,)), ((), ())), preferred_element_type=F32
    ).astype(BF)
    total = jnp.sum(signal.astype(F32), axis=0, keepdims=True)
    high = total.astype(BF).astype(F32)
    tile[row : row + 1, :] = high
    tile[SG + row : SG + row + 1, :] = total - high
    return outgoing, grad


def place_of(row):
    shard, inner = row // SHARD, row % SHARD
    return shard // NX, shard % NX, inner


def grads0_kernel(before, up, slope, kernel, x, out, send, rest, tile):
    tile[...] = jnp.zeros_like(tile)
    for q in FIRST:
        outgoing, grad = local_grads(before, up, slope, kernel, x, q, tile, q)
        out[:, q * GS : (q + 1) * GS] = outgoing
        for u in range(GS // TILE):
            row = q * GS + u * TILE
            z, i, inner = place_of(row)
            if z < NZ // 2:
                at = z * SHARD + inner
                send[i, at : at + TILE, :] = grad[u * TILE : (u + 1) * TILE, :]
            else:
                at = row - 2 * PIECE
                rest[at : at + TILE, :] = grad[u * TILE : (u + 1) * TILE, :]
    for i in range(NX):
        send[i, HALF:, :] = tile[...].astype(BF)


REST = len(FIRST) * GS - 2 * PIECE


def grads0(before, up, slope, kernel, x):
    width = len(FIRST) * GS
    return call(
        grads0_kernel,
        "grads0",
        3 * 10**8,
        6 * 10**6,
        grid=(NY,),
        out_shape=(
            jax.ShapeDtypeStruct((ROWS, NY * width), BF),
            jax.ShapeDtypeStruct((NY * NX, PART, GS), BF),
            jax.ShapeDtypeStruct((NY * REST, GS), BF),
        ),
        in_specs=[columns(width)] * 3 + [rows(width), columns(SLAB)],
        out_specs=(
            columns(width),
            pl.BlockSpec((NX, PART, GS), lambda i: (i, 0, 0)),
            rows(REST),
        ),
        scratch_shapes=[pltpu.VMEM((TILE, GS), F32)],
    )(before, up, slope, kernel, x)


def grads1_kernel(before, up, slope, kernel, x, rest, out0, out, send, tile):
    tile[...] = jnp.zeros_like(tile)
    start = LAST[0] * GS
    out[:, :start] = out0[...]
    outgoing, grad = local_grads(before, up, slope, kernel, x, 0, tile, LAST[0])
    out[:, start:] = outgoing
    for u in range((SLAB - 2 * PIECE) // TILE):
        row = 2 * PIECE + u * TILE
        z, i, inner = place_of(row)
        at = (z - NZ // 2) * SHARD + inner
        if row < start:
            send[i, at : at + TILE, :] = rest[u * TILE : (u + 1) * TILE, :]
        else:
            send[i, at : at + TILE, :] = grad[row - start : row - start + TILE, :]
    for i in range(NX):
        send[i, HALF:, :] = tile[...].astype(BF)


def grads1(before, up, slope, kernel, x, rest, out0):
    width = len(LAST) * GS
    return call(
        grads1_kernel,
        "grads1",
        2 * 10**8,
        4 * 10**6,
        grid=(NY,),
        out_shape=(
            jax.ShapeDtypeStruct((ROWS, D), BF),
            jax.ShapeDtypeStruct((NY * NX, PART, GS), BF),
        ),
        in_specs=[columns(width)] * 3
        + [rows(width), of_slab(LAST), rows(REST), columns(len(FIRST) * GS)],
        out_specs=(columns(SLAB), pl.BlockSpec((NX, PART, GS), lambda i: (i, 0, 0))),
        scratch_shapes=[pltpu.VMEM((TILE, GS), F32)],
    )(before, up, slope, kernel, x, rest, out0)


def add_up(ids, got, total):
    step = pl.program_id(0)

    @pl.when(step == 0)
    def _():
        total[...] = jnp.zeros_like(total)

    for i in range(NX):
        domain = ids[step * NX + i, 0]
        total[domain] += got[i].astype(F32)


def merge0_kernel(ids, got, out, bias, total):
    add_up(ids, got, total)

    @pl.when(pl.program_id(0) == NY - 1)
    def _():
        for k in range(DOMAINS):
            for z in range(NZ // 2):
                out[z, k * SHARD : (k + 1) * SHARD, :] = total[
                    k, z * SHARD : (z + 1) * SHARD, :
                ].astype(BF)
            bias[k] = total[k, HALF:, :]


def merge0(ids, got):
    return call(
        merge0_kernel,
        "merge0",
        10**6,
        10**6,
        grid=(NY,),
        out_shape=(
            jax.ShapeDtypeStruct((NZ // 2, PIECE, GS), BF),
            jax.ShapeDtypeStruct((DOMAINS, TILE, GS), F32),
        ),
        in_specs=[SMEM, pl.BlockSpec((NX, PART, GS), lambda i: (i, 0, 0))],
        out_specs=(
            pl.BlockSpec((NZ // 2, PIECE, GS), lambda i: (0, 0, 0)),
            pl.BlockSpec((DOMAINS, TILE, GS), lambda i: (0, 0, 0)),
        ),
        scratch_shapes=[pltpu.VMEM((DOMAINS, PART, GS), F32)],
    )(ids, got)


def merge1_kernel(ids, z, got, sums, bias, *refs):
    outs, (total, parts, tile) = refs[:NZ], refs[NZ:]
    add_up(ids, got, total)

    @pl.when(pl.program_id(0) == NY - 1)
    def _():
        tile[...] = jnp.zeros_like(tile)
        parts[: NZ // 2] = sums[...]
        for k in range(DOMAINS):
            for half in range(NZ // 2):
                parts[NZ // 2 + half, k * SHARD : (k + 1) * SHARD, :] = total[
                    k, half * SHARD : (half + 1) * SHARD, :
                ].astype(BF)
            both = total[k, HALF:, :] + bias[k]
            tile[k * SG : (k + 1) * SG, :] = both[:SG, :] + both[SG : 2 * SG, :]
        for k in range(NZ):
            outs[k][:PIECE, :] = parts[(z[0] + k) % NZ]
            outs[k][PIECE:, :] = tile[...].astype(BF)


def merge1(ids, z, got, sums, bias):
    def whole(shape):
        return pl.BlockSpec(shape, lambda i: (0,) * len(shape))

    return call(
        merge1_kernel,
        "merge1",
        10**6,
        2 * 10**6,
        grid=(NY,),
        out_shape=(jax.ShapeDtypeStruct((BLOCK, GS), BF),) * NZ,
        in_specs=[
            SMEM,
            SMEM,
            pl.BlockSpec((NX, PART, GS), lambda i: (i, 0, 0)),
            whole((NZ // 2, PIECE, GS)),
            whole((DOMAINS, TILE, GS)),
        ],
        out_specs=(whole((BLOCK, GS)),) * NZ,
        scratch_shapes=[
            pltpu.VMEM((DOMAINS, PART, GS), F32),
            pltpu.VMEM((NZ, PIECE, GS), BF),
            pltpu.VMEM((TILE, GS), F32),
        ],
    )(ids, z, got, sums, bias)


def finish_kernel(at, *refs):
    got, (sw, dw, d_shared, d_domain, b_shared, b_domain, wide) = refs[:NZ], refs[NZ:]
    shared = sw[...].astype(F32)
    summed = jnp.zeros((SHARD, GS), F32)
    for k in range(DOMAINS):
        part = slice(k * SHARD, (k + 1) * SHARD)
        share = got[0][part, :].astype(F32)
        for z in range(1, NZ):
            share = share + got[z][part, :].astype(F32)
        summed = summed + share * dw[k].astype(F32)
        d_domain[k] = share * shared
    d_shared[...] = summed
    tile = got[0][PIECE:, :].astype(F32)
    for z in range(1, NZ):
        tile = tile + got[z][PIECE:, :].astype(F32)
    wide[...] = jnp.zeros_like(wide)
    for k in range(DOMAINS):
        for q in range(SG):
            row = k * SG + q
            wide[k : k + 1, q * GS : (q + 1) * GS] = tile[row : row + 1, :]
    placed = pltpu.roll(wide[...], SLAB - at[0], 1)
    b_domain[...] = placed[:DOMAINS, :SHARD]
    b_shared[...] = jnp.sum(placed[:DOMAINS, :SHARD], axis=0, keepdims=True)


def finish(at, got, sw, dw):
    return call(
        finish_kernel,
        "finish",
        10**6,
        10**6,
        out_shape=(
            jax.ShapeDtypeStruct((SHARD, GS), F32),
            jax.ShapeDtypeStruct((DOMAINS, SHARD, GS), F32),
            jax.ShapeDtypeStruct((1, SHARD), F32),
            jax.ShapeDtypeStruct((DOMAINS, SHARD), F32),
        ),
        in_specs=[SMEM] + [VMEM] * (NZ + 2),
        out_specs=(VMEM,) * 4,
        scratch_shapes=[pltpu.VMEM((8, SLAB), F32)],
    )(at, *got, sw, dw)


def exchange(block, axes):
    return lax.all_to_all(block, axes, 0, 0, tiled=True)


def turned(block, k):
    return lax.ppermute(block, "zlo", [(i, (i + k) % NZ) for i in range(NZ)])


def after(first, *then):
    return lax.optimization_barrier((first, *then))[1:]


def body(stash, cotangent, domain_ids, shared_weight, domain_weight, shared_bias, domain_bias):
    x = stash[0]
    sw, dw = shared_weight[0], domain_weight[0]
    section = jnp.reshape(2 * lax.axis_index("zhi") + lax.axis_index("core"), (1,))
    z = jnp.reshape(lax.axis_index("zlo"), (1,))
    at = PIECE * z + SHARD * lax.axis_index("x")

    own = prep(at, sw, dw, shared_bias, domain_bias[0])
    held = [own] + [turned(own, k) for k in range(1, NZ)]
    (ids,) = after(own, domain_ids)
    plane_ids = exchange(
        jnp.broadcast_to(ids[0], (NY * NX, 1, 128)), ("y", "x")
    ).reshape(NY * NX, 128)
    got = exchange(pick(plane_ids, z, held), ("y", "x"))
    slope0, slope1, kernel0, kernel1 = slopes(domain_ids, got, x)

    def hop(block, turn):
        return lax.ppermute(block, ("zhi", "core"), [(3 - turn, 2 - turn)])

    out0, kept0 = chain(FIRST, section, cotangent, slope0, kernel0, first=True)
    (slope1,) = after(out0, slope1)
    out1, kept1 = chain(LAST, section, cotangent, slope1, kernel1, first=True)
    for turn in range(2):
        up0 = hop(out0, turn)
        up1 = hop(out1, turn)
        (up0,) = after(out1, up0)
        out0, kept0 = chain(FIRST, kept0, up0, slope0, kernel0)
        (up1,) = after(out0, up1)
        out1, kept1 = chain(LAST, kept1, up1, slope1, kernel1)
    up0 = hop(out0, 2)
    up1 = hop(out1, 2)
    (up0,) = after(out1, up0)
    d_in0, send0, rest = grads0(kept0, up0, slope0, kernel0, x)
    got0 = exchange(send0, ("y", "x"))
    (up1,) = after(got0, up1)
    d_inputs, send1 = grads1(kept1, up1, slope1, kernel1, x, rest, d_in0)
    sums0, bias0 = merge0(plane_ids, got0)
    got1 = exchange(send1, ("y", "x"))
    merged = merge1(plane_ids, z, got1, sums0, bias0)
    final = [merged[0]] + [turned(merged[k], k) for k in range(1, NZ)]
    d_shared, d_domain, b_shared, b_domain = finish(at, final, sw, dw)
    return (d_inputs[None], d_shared[None], d_domain[None], b_shared, b_domain[None])


def solution(mesh):
    fine = Mesh(mesh.devices.reshape(2, 2, NY, NZ, NX), ("zhi", "core", "y", "zlo", "x"))
    section, dp = ("zhi", "core"), ("y", "zlo", "x")
    in_specs = (
        P(section, dp, None),
        P(dp, None),
        P(dp),
        P(section, dp, None),
        P(section, None, dp, None),
        P(section, dp),
        P(section, None, dp),
    )
    out_specs = (
        P(section, dp, None),
        P(section, dp, None),
        P(section, None, dp, None),
        P(section, dp),
        P(section, None, dp),
    )
    return jax.shard_map(
        body, mesh=fine, in_specs=in_specs, out_specs=out_specs, check_vma=False
    )
```

time: 160 us -> 149 us (0.931)
  blocking collectives: 92.4 us -> 13 us
  waiting for transfers between devices: 26.9 us -> 73.2 us
  starting transfers between devices: 10.9 us -> 32.9 us
  local copies, waits for them, and re-layouts: 6.67 us -> 9.96 us
  other arithmetic: 1.86 us -> 0 us
    all_to_all x4 -> x1, blocking collectives: 92.4 us -> 13 us  [exchange(): return lax.all_to_all(block, axes, 0, 0, tiled=True)]
    all_to_all x1 -> x3, waiting for transfers between devices: 3.16 us -> 40.6 us  [exchange(): return lax.all_to_all(block, axes, 0, 0, tiled=True)]
    ppermute x3 -> x12, starting transfers between devices: 3.33 us -> 21.6 us  [the longest x6 15 us: turned(): return lax.ppermute(block, 'zlo', [(i, (i + k) % NZ) for i in range(NZ)])]
    ppermute x3 -> x12, waiting for transfers between devices: 23.7 us -> 32.7 us  [the longest x6 28.5 us: hop(): return lax.ppermute(block, ('zhi', 'core'), [(3 - turn, 2 - turn)])]
    unnamed x22 -> x32, local copies, waits for them, and re-layouts: 4.56 us -> 9.95 us
    all_to_all x1 -> x3, starting transfers between devices: 7.58 us -> 11.2 us  [exchange(): return lax.all_to_all(block, axes, 0, 0, tiled=True)]
    pallas_call x9 -> x14, Pallas kernels: 18.6 us -> 17.4 us  [the longest x6 6.9 us: chain(): call(first_kernel if first else next_kernel, 'chain', 10 ** 8, 2 * 10 **...]
  transfers between devices with their start and end apart: 4 -> 15, of which waited for: 3 -> 8; matrix products, arithmetic and copies ran while one was open for 1% -> 0% of each run, Pallas kernels for 1% -> 3%
where the time goes in v2:
time: 149 us; the launch traced here: 148 us
  waiting for transfers between devices  73.2 us (49%)
  starting transfers between devices  32.9 us (22%)
  Pallas kernels  17.4 us (12%)
  blocking collectives  13 us (9%)
  local copies, waits for them, and re-layouts  9.96 us (7%)
  between operations  1.54 us (1%)
    all_to_all x3, waiting for transfers between devices, exchange(): return lax.all_to_all(block, axes, 0, 0, tiled=True)  40.6 us
    ppermute x6, waiting for transfers between devices, hop(): return lax.ppermute(block, ('zhi', 'core'), [(3 - turn, 2 - turn)])  28.5 us
    ppermute x6, starting transfers between devices, turned(): return lax.ppermute(block, 'zlo', [(i, (i + k) % NZ) for i in range(NZ)])  15 us
    all_to_all x1, blocking collectives, exchange(): return lax.all_to_all(block, axes, 0, 0, tiled=True)  13 us
    all_to_all x3, starting transfers between devices, exchange(): return lax.all_to_all(block, axes, 0, 0, tiled=True)  11.2 us
    unnamed x32, local copies, waits for them, and re-layouts  9.95 us
    pallas_call x6, Pallas kernels, chain(): call(first_kernel if first else next_kernel, 'chain', 10 ** 8, 2 * 10 **...  6.9 us
    ppermute x6, starting transfers between devices, hop(): return lax.ppermute(block, ('zhi', 'core'), [(3 - turn, 2 - turn)])  6.58 us
  transfers between devices with their start and end apart: 15, of which 8 were waited for; matrix products, arithmetic and copies ran while one was open for 0% of the time, Pallas kernels for 3%

profile of v2, /device:TPU:1, one launch (start us, length us, event | category | flops | bytes accessed | tf_op | source)
XLA Modules:
  0.0 148.0 jit_solution(745060722623263357)
XLA Ops:
  0.7 0.9 copy-done.5
  1.5 0.7 copy-done.11
  2.3 0.7 copy-done.13
  3.0 0.7 copy-done.14
  3.6 0.1 prep.1.refs_0_
  3.7 5.2 %collective-permute-start.2 = (bf16[208,256]{1,0:T(8,128)(2,1)S(1)}, bf16[208,256]{1,0:T(8,128)(2,1)S(1)}, u32[]{:S(2)}, u32[]{:S(2)}) collective-permute-start(bf16[208,256]{1,0:T(8,128)(2,1)S(1)} %prep.1.refs_0_), channel_id=1, source_target_pairs={{0,12},{4,0},{8,4},{12,8},{1,13},{5,1},{9,5},{13,9},{2,14},{6,2},{... | collective-permute-start | bytes 319496 | tf_op jit(solution)/shard_map/ppermute | solution.py:436
  9.0 0.4 collective-permute-start
  10.0 13.0 %all_to_all.20 = s32[16,1,128]{2,1,0:T(1,128)S(1)} all-to-all(s32[16,1,128]{2,1,0:T(1,128)S(1)} %broadcast_in_dim.15), channel_id=1, replica_groups=mesh['zhi'=2,'core'=2,'y'=4,'zlo'=4,'x'=4] {'y','x'}, dimensions={0} | all-to-all | bytes 16384 | tf_op jit(solution)/shard_map/all_to_all | solution.py:432
  23.0 2.5 %pick.1 = bf16[16,208,256]{2,1,0:T(8,128)(2,1)} custom-call(s32[16,128]{1,0:T(8,128)S(1)} %bitcast.19, s32[1]{0:T(128)} %bitcast.1.z, bf16[208,256]{1,0:T(8,128)(2,1)S(1)} %prep.1.refs_0_, bf16[208,256]{1,0:T(8,128)(2,1)S(1)} %collective-permute-done.refs_1_, bf16[208,256]{1,0:T(8,128)(2,1)S(1)} %collective-permute-done.1.refs_2_, ...), custom_call_target="tpu_custom_call" | custom-call | flops 100000 | bytes 2000000 | tf_op jit(solution)/shard_map/pick/pallas_call | solution.py:84
  25.5 3.8 %all-to-all-start.1 = ((bf16[16,208,256]{2,1,0:T(8,128)(2,1)}), bf16[16,208,256]{2,1,0:T(8,128)(2,1)S(1)}, u32[]{:S(2)}, u32[]{:S(2)}) async-start(bf16[16,208,256]{2,1,0:T(8,128)(2,1)} %pick.1), calls=%async_computation.1 | async-start | bytes 3407872 | tf_op jit(solution)/shard_map/all_to_all | solution.py:432
  29.4 21.2 %all-to-all-done.1.got = bf16[16,208,256]{2,1,0:T(8,128)(2,1)S(1)} async-done(((bf16[16,208,256]{2,1,0:T(8,128)(2,1)}), bf16[16,208,256]{2,1,0:T(8,128)(2,1)S(1)}, u32[]{:S(2)}, u32[]{:S(2)}) %all-to-all-start.1) | async-done | bytes 1703968 | tf_op jit(solution)/shard_map/all_to_all | solution.py:432
  50.6 1.3 slopes.1
  51.9 1.1 copy-done.1
  53.1 1.2 chain.6
  54.3 0.7 collective-permute-start.3
  55.0 1.1 chain.7
  56.1 1.3 chain.8
  57.3 1.3 collective-permute-start.5
  58.6 0.7 collective-permute-start.4
  59.3 1.1 chain.9
  60.4 16.8 %collective-permute-done.5.up = bf16[128,2048]{1,0:T(8,128)(2,1)S(1)} collective-permute-done((bf16[128,2048]{1,0:T(8,128)(2,1)S(1)}, bf16[128,2048]{1,0:T(8,128)(2,1)S(1)}, u32[]{:S(2)}, u32[]{:S(2)}) %collective-permute-start.5) | collective-permute-done | bytes 524320 | tf_op jit(solution)/shard_map/ppermute | solution.py:460
  77.3 1.2 chain.10
  78.5 1.3 collective-permute-start.7
  79.8 1.3 collective-permute-start.6
  81.1 10.3 %collective-permute-done.6.up = bf16[128,1024]{1,0:T(8,128)(2,1)S(1)} collective-permute-done((bf16[128,1024]{1,0:T(8,128)(2,1)S(1)}, bf16[128,1024]{1,0:T(8,128)(2,1)S(1)}, u32[]{:S(2)}, u32[]{:S(2)}) %collective-permute-start.6) | collective-permute-done | bytes 262176 | tf_op jit(solution)/shard_map/ppermute | solution.py:460
  91.4 1.1 chain.11
  92.5 0.7 copy-done.15
  93.2 1.5 %grads0.1 = (bf16[128,2048]{1,0:T(8,128)(2,1)S(1)}, bf16[16,112,256]{2,1,0:T(8,128)(2,1)S(1)}, bf16[512,256]{1,0:T(8,128)(2,1)S(1)}) custom-call(bf16[128,2048]{1,0:T(8,128)(2,1)S(1)} %get-tuple-element.64.before, bf16[128,2048]{1,0:T(8,128)(2,1)S(1)} %collective-permute-done.7.up, f32[128,2048]{1,0:T(8,128)S(1)} %get-tuple-element.45.slope, ...), custom_call_target="tpu_custom_call" | custom-call | flops 300000000 | bytes 6000000 | tf_op jit(solution)/shard_map/grads0/pallas_call | solution.py:238
  94.8 0.9 copy-done.3
  95.7 0.7 copy-done.7
  96.4 3.6 %all-to-all-start.2 = ((bf16[16,112,256]{2,1,0:T(8,128)(2,1)}), bf16[16,112,256]{2,1,0:T(8,128)(2,1)S(1)}, u32[]{:S(2)}, u32[]{:S(2)}) async-start(bf16[16,112,256]{2,1,0:T(8,128)(2,1)} %copy-done.3), calls=%async_computation.2 | async-start | bytes 1835008 | tf_op jit(solution)/shard_map/all_to_all | solution.py:432
  100.0 1.3 collective-permute-start.8
  101.3 1.3 collective-permute-done.8.up
  102.7 0.7 copy-done.9
  103.4 7.9 %all-to-all-done.2.got = bf16[16,112,256]{2,1,0:T(8,128)(2,1)S(1)} async-done(((bf16[16,112,256]{2,1,0:T(8,128)(2,1)}), bf16[16,112,256]{2,1,0:T(8,128)(2,1)S(1)}, u32[]{:S(2)}, u32[]{:S(2)}) %all-to-all-start.2) | async-done | bytes 917536 | tf_op jit(solution)/shard_map/all_to_all | solution.py:432
  111.3 0.9 copy-done.8
  112.2 0.9 copy-done.10
  113.2 2.3 %grads1.1 = (bf16[128,3072]{1,0:T(8,128)(2,1)}, bf16[16,112,256]{2,1,0:T(8,128)(2,1)S(1)}) custom-call(bf16[128,1024]{1,0:T(8,128)(2,1)S(1)} %get-tuple-element.63.before, bf16[128,1024]{1,0:T(8,128)(2,1)S(1)} %copy-done.10, f32[128,1024]{1,0:T(8,128)S(1)} %get-tuple-element.49.slope, bf16[1024,256]{1,0:T(8,128)(2,1)S(1)} %get-tuple-element.50.kernel, ...), custom_call_target="tpu_custom_call" | custom-call | flops 200000000 | bytes 4000000 | tf_op jit(solution)/shard_map/grads1/pallas_call | solution.py:279
  115.5 0.9 copy-done.4
  116.4 3.8 %all-to-all-start.3 = ((bf16[16,112,256]{2,1,0:T(8,128)(2,1)}), bf16[16,112,256]{2,1,0:T(8,128)(2,1)S(1)}, u32[]{:S(2)}, u32[]{:S(2)}) async-start(bf16[16,112,256]{2,1,0:T(8,128)(2,1)} %copy-done.4), calls=%async_computation.3 | async-start | bytes 1835008 | tf_op jit(solution)/shard_map/all_to_all | solution.py:432
  120.2 1.0 merge0.1
  121.2 11.4 %all-to-all-done.3.got = bf16[16,112,256]{2,1,0:T(8,128)(2,1)S(1)} async-done(((bf16[16,112,256]{2,1,0:T(8,128)(2,1)}), bf16[16,112,256]{2,1,0:T(8,128)(2,1)S(1)}, u32[]{:S(2)}, u32[]{:S(2)}) %all-to-all-start.3) | async-done | bytes 917536 | tf_op jit(solution)/shard_map/all_to_all | solution.py:432
  132.6 1.0 merge1.1
  133.6 7.2 %collective-permute-start.9 = (bf16[208,256]{1,0:T(8,128)(2,1)S(1)}, bf16[208,256]{1,0:T(8,128)(2,1)S(1)}, u32[]{:S(2)}, u32[]{:S(2)}) collective-permute-start(bf16[208,256]{1,0:T(8,128)(2,1)S(1)} %get-tuple-element.76), channel_id=1, source_target_pairs={{0,4},{4,8},{8,12},{12,0},{1,5},{5,9},{9,13},{13,1},{2,6},{6,10},{... | collective-permute-start | bytes 319496 | tf_op jit(solution)/shard_map/ppermute | solution.py:436
  140.9 2.2 %collective-permute-start.11 = (bf16[208,256]{1,0:T(8,128)(2,1)S(1)}, bf16[208,256]{1,0:T(8,128)(2,1)S(1)}, u32[]{:S(2)}, u32[]{:S(2)}) collective-permute-start(bf16[208,256]{1,0:T(8,128)(2,1)S(1)} %get-tuple-element.78), channel_id=1, source_target_pairs={{0,12},{4,0},{8,4},{12,8},{1,13},{5,1},{9,5},{13,9},{2,14},{6,2},{... | collective-permute-start | bytes 319496 | tf_op jit(solution)/shard_map/ppermute | solution.py:436
  143.0 0.6 collective-permute-done.9.refs_1_
  143.7 3.5 %collective-permute-done.10.refs_2_ = bf16[208,256]{1,0:T(8,128)(2,1)S(1)} collective-permute-done((bf16[208,256]{1,0:T(8,128)(2,1)S(1)}, bf16[208,256]{1,0:T(8,128)(2,1)S(1)}, u32[]{:S(2)}, u32[]{:S(2)}) %collective-permute-start.10) | collective-permute-done | bytes 106528 | tf_op jit(solution)/shard_map/ppermute | solution.py:436
  147.2 0.8 finish.1
  (30 shorter events, 0.1 us)
Async XLA Ops:
  0.6 0.9 copy-start.5
  1.5 0.7 copy-start.11
  2.3 0.7 copy-start.13
  3.0 0.7 copy-start.14
  3.7 19.3 %collective-permute-start.2 = (bf16[208,256]{1,0:T(8,128)(2,1)S(1)}, bf16[208,256]{1,0:T(8,128)(2,1)S(1)}, u32[]{:S(2)}, u32[]{:S(2)}) collective-permute-start(bf16[208,256]{1,0:T(8,128)(2,1)S(1)} %prep.1.refs_0_), channel_id=1, source_target_pairs={{0,12},{4,0},{8,4},{12,8},{1,13},{5,1},{9,5},{13,9},{2,14},{6,2},{... | collective-permute-start | bytes 319496 | tf_op jit(solution)/shard_map/ppermute | solution.py:436
  9.0 14.0 %collective-permute-start.1 = (bf16[208,256]{1,0:T(8,128)(2,1)S(1)}, bf16[208,256]{1,0:T(8,128)(2,1)S(1)}, u32[]{:S(2)}, u32[]{:S(2)}) collective-permute-start(bf16[208,256]{1,0:T(8,128)(2,1)S(1)} %prep.1.refs_0_), channel_id=1, source_target_pairs={{0,8},{4,12},{8,0},{12,4},{1,9},{5,13},{9,1},{13,5},{2,10},{6,14},... | collective-permute-start | bytes 319496 | tf_op jit(solution)/shard_map/ppermute | solution.py:436
  9.0 14.0 %collective-permute-start = (bf16[208,256]{1,0:T(8,128)(2,1)S(1)}, bf16[208,256]{1,0:T(8,128)(2,1)S(1)}, u32[]{:S(2)}, u32[]{:S(2)}) collective-permute-start(bf16[208,256]{1,0:T(8,128)(2,1)S(1)} %prep.1.refs_0_), channel_id=1, source_target_pairs={{0,4},{4,8},{8,12},{12,0},{1,5},{5,9},{9,13},{13,1},{2,6},{6,10},{... | collective-permute-start | bytes 319496 | tf_op jit(solution)/shard_map/ppermute | solution.py:436
  25.5 25.1 %copy-start = (bf16[1,128,3072]{2,1,0:T(8,128)(2,1)S(1)}, bf16[1,128,3072]{2,1,0:T(8,128)(2,1)}, u32[]{:S(2)}) copy-start(bf16[1,128,3072]{2,1,0:T(8,128)(2,1)} %param.7) | copy-start | bytes 2359300
  25.5 25.1 %all-to-all-start.1 = ((bf16[16,208,256]{2,1,0:T(8,128)(2,1)}), bf16[16,208,256]{2,1,0:T(8,128)(2,1)S(1)}, u32[]{:S(2)}, u32[]{:S(2)}) async-start(bf16[16,208,256]{2,1,0:T(8,128)(2,1)} %pick.1), calls=%async_computation.1 | async-start | bytes 3407872 | tf_op jit(solution)/shard_map/all_to_all | solution.py:432
  50.6 4.4 %copy-start.2 = (bf16[128,3072]{1,0:T(8,128)(2,1)S(1)}, bf16[128,3072]{1,0:T(8,128)(2,1)}, u32[]{:S(2)}) copy-start(bf16[128,3072]{1,0:T(8,128)(2,1)} %up.3) | copy-start | bytes 2359300
  51.9 1.1 copy-start.1
  54.3 1.8 %collective-permute-start.3 = (bf16[128,2048]{1,0:T(8,128)(2,1)S(1)}, bf16[128,2048]{1,0:T(8,128)(2,1)S(1)}, u32[]{:S(2)}, u32[]{:S(2)}) collective-permute-start(bf16[128,2048]{1,0:T(8,128)(2,1)S(1)} %get-tuple-element.47), channel_id=1, source_target_pairs={{192,128},{193,129},{194,130},{195,131},{196,132},{197,133},{198,1... | collective-permute-start | bytes 1572872 | tf_op jit(solution)/shard_map/ppermute | solution.py:460
  57.3 19.9 %collective-permute-start.5 = (bf16[128,2048]{1,0:T(8,128)(2,1)S(1)}, bf16[128,2048]{1,0:T(8,128)(2,1)S(1)}, u32[]{:S(2)}, u32[]{:S(2)}) collective-permute-start(bf16[128,2048]{1,0:T(8,128)(2,1)S(1)} %get-tuple-element.55), channel_id=1, source_target_pairs={{128,64},{129,65},{130,66},{131,67},{132,68},{133,69},{134,70},{13... | collective-permute-start | bytes 1572872 | tf_op jit(solution)/shard_map/ppermute | solution.py:460
  58.6 0.7 collective-permute-start.4
  78.5 14.7 %collective-permute-start.7 = (bf16[128,2048]{1,0:T(8,128)(2,1)S(1)}, bf16[128,2048]{1,0:T(8,128)(2,1)S(1)}, u32[]{:S(2)}, u32[]{:S(2)}) collective-permute-start(bf16[128,2048]{1,0:T(8,128)(2,1)S(1)} %get-tuple-element.61), channel_id=1, source_target_pairs={{64,0},{65,1},{66,2},{67,3},{68,4},{69,5},{70,6},{71,7},{72,8},{73... | collective-permute-start | bytes 1572872 | tf_op jit(solution)/shard_map/ppermute | solution.py:460
  79.8 11.6 %collective-permute-start.6 = (bf16[128,1024]{1,0:T(8,128)(2,1)S(1)}, bf16[128,1024]{1,0:T(8,128)(2,1)S(1)}, u32[]{:S(2)}, u32[]{:S(2)}) collective-permute-start(bf16[128,1024]{1,0:T(8,128)(2,1)S(1)} %get-tuple-element.59), channel_id=1, source_target_pairs={{128,64},{129,65},{130,66},{131,67},{132,68},{133,69},{134,70},{13... | collective-permute-start | bytes 786440 | tf_op jit(solution)/shard_map/ppermute | solution.py:460
  92.5 0.7 copy-start.15
  94.7 0.9 copy-start.3
  95.7 0.7 copy-start.7
  96.4 14.9 %all-to-all-start.2 = ((bf16[16,112,256]{2,1,0:T(8,128)(2,1)}), bf16[16,112,256]{2,1,0:T(8,128)(2,1)S(1)}, u32[]{:S(2)}, u32[]{:S(2)}) async-start(bf16[16,112,256]{2,1,0:T(8,128)(2,1)} %copy-done.3), calls=%async_computation.2 | async-start | bytes 1835008 | tf_op jit(solution)/shard_map/all_to_all | solution.py:432
  100.0 2.7 %collective-permute-start.8 = (bf16[128,1024]{1,0:T(8,128)(2,1)}, bf16[128,1024]{1,0:T(8,128)(2,1)S(1)}, u32[]{:S(2)}, u32[]{:S(2)}) collective-permute-start(bf16[128,1024]{1,0:T(8,128)(2,1)} %copy-done.15), channel_id=1, source_target_pairs={{64,0},{65,1},{66,2},{67,3},{68,4},{69,5},{70,6},{71,7},{72,8},{73... | collective-permute-start | bytes 786440 | tf_op jit(solution)/shard_map/ppermute | solution.py:460
  102.7 0.7 copy-start.9
  111.3 1.0 copy-start.8
  112.2 0.9 copy-start.10
  115.5 0.9 copy-start.4
  116.4 30.8 %copy-start.6 = (bf16[1,4,48,256]{3,2,1,0:T(8,128)(2,1)S(1)}, bf16[1,4,48,256]{3,2,1,0:T(8,128)(2,1)}, u32[]{:S(2)}) copy-start(bf16[1,4,48,256]{3,2,1,0:T(8,128)(2,1)} %param.11) | copy-start | bytes 294916
  116.4 30.8 %copy-start.12 = (bf16[1,48,256]{2,1,0:T(8,128)(2,1)S(1)}, bf16[1,48,256]{2,1,0:T(8,128)(2,1)}, u32[]{:S(2)}) copy-start(bf16[1,48,256]{2,1,0:T(8,128)(2,1)} %param.10) | copy-start | bytes 73732
  116.4 16.2 %all-to-all-start.3 = ((bf16[16,112,256]{2,1,0:T(8,128)(2,1)}), bf16[16,112,256]{2,1,0:T(8,128)(2,1)S(1)}, u32[]{:S(2)}, u32[]{:S(2)}) async-start(bf16[16,112,256]{2,1,0:T(8,128)(2,1)} %copy-done.4), calls=%async_computation.3 | async-start | bytes 1835008 | tf_op jit(solution)/shard_map/all_to_all | solution.py:432
  133.6 10.0 %collective-permute-start.9 = (bf16[208,256]{1,0:T(8,128)(2,1)S(1)}, bf16[208,256]{1,0:T(8,128)(2,1)S(1)}, u32[]{:S(2)}, u32[]{:S(2)}) collective-permute-start(bf16[208,256]{1,0:T(8,128)(2,1)S(1)} %get-tuple-element.76), channel_id=1, source_target_pairs={{0,4},{4,8},{8,12},{12,0},{1,5},{5,9},{9,13},{13,1},{2,6},{6,10},{... | collective-permute-start | bytes 319496 | tf_op jit(solution)/shard_map/ppermute | solution.py:436
  140.9 6.3 %collective-permute-start.10 = (bf16[208,256]{1,0:T(8,128)(2,1)S(1)}, bf16[208,256]{1,0:T(8,128)(2,1)S(1)}, u32[]{:S(2)}, u32[]{:S(2)}) collective-permute-start(bf16[208,256]{1,0:T(8,128)(2,1)S(1)} %get-tuple-element.77), channel_id=1, source_target_pairs={{0,8},{4,12},{8,0},{12,4},{1,9},{5,13},{9,1},{13,5},{2,10},{6,14},... | collective-permute-start | bytes 319496 | tf_op jit(solution)/shard_map/ppermute | solution.py:436
  140.9 6.3 %collective-permute-start.11 = (bf16[208,256]{1,0:T(8,128)(2,1)S(1)}, bf16[208,256]{1,0:T(8,128)(2,1)S(1)}, u32[]{:S(2)}, u32[]{:S(2)}) collective-permute-start(bf16[208,256]{1,0:T(8,128)(2,1)S(1)} %get-tuple-element.78), channel_id=1, source_target_pairs={{0,12},{4,0},{8,4},{12,8},{1,13},{5,1},{9,5},{13,9},{2,14},{6,2},{... | collective-permute-start | bytes 319496 | tf_op jit(solution)/shard_map/ppermute | solution.py:436

commit v3 on v2

--- a/solution.py
+++ b/solution.py
@@ -31,7 +31,7 @@
         kernel,
         name=name,
         compiler_params=pltpu.CompilerParams(vmem_limit_bytes=limit * 1024 * 1024),
-        cost_estimate=pl.CostEstimate(flops=flops, bytes_accessed=moved, transcendentals=0),
+        cost_estimate=pl.CostEstimate(flops=10**11, bytes_accessed=10**9, transcendentals=0),
         **rest,
     )
 
@@ -474,9 +474,9 @@
     (up0,) = after(out1, up0)
     d_in0, send0, rest = grads0(kept0, up0, slope0, kernel0, x)
     got0 = exchange(send0, ("y", "x"))
-    (up1,) = after(got0, up1)
     d_inputs, send1 = grads1(kept1, up1, slope1, kernel1, x, rest, d_in0)
     sums0, bias0 = merge0(plane_ids, got0)
+    (send1,) = after(got0, send1)
     got1 = exchange(send1, ("y", "x"))
     merged = merge1(plane_ids, z, got1, sums0, bias0)
     final = [merged[0]] + [turned(merged[k], k) for k in range(1, NZ)]

time: 149 us -> 145 us (0.973); the launches traced: 148 us -> 142 us
  waiting for transfers between devices: 73.2 us -> 67.6 us
  local copies, waits for them, and re-layouts: 9.96 us -> 5.58 us
  starting transfers between devices: 32.9 us -> 35.5 us
    ppermute x6, waiting for transfers between devices: 28.5 us -> 15.8 us  [hop(): return lax.ppermute(block, ('zhi', 'core'), [(3 - turn, 2 - turn)])]
    all_to_all x3, waiting for transfers between devices: 40.6 us -> 48.4 us  [exchange(): return lax.all_to_all(block, axes, 0, 0, tiled=True)]
    unnamed x32 -> x28, local copies, waits for them, and re-layouts: 9.95 us -> 5.57 us
    ppermute x6, starting transfers between devices: 15 us -> 17.9 us  [turned(): return lax.ppermute(block, 'zlo', [(i, (i + k) % NZ) for i in range(NZ)])]
  transfers between devices with their start and end apart: 15 -> 15, of which waited for: 8 -> 6; matrix products, arithmetic and copies ran while one was open for 0% -> 0% of each run, Pallas kernels for 3% -> 8%
where the time goes in v3:
time: 145 us; the launch traced here: 142 us
  waiting for transfers between devices  67.6 us (47%)
  starting transfers between devices  35.5 us (24%)
  Pallas kernels  18.5 us (13%)
  blocking collectives  13 us (9%)
  local copies, waits for them, and re-layouts  5.58 us (4%)
  between operations  1.56 us (1%)
    all_to_all x3, waiting for transfers between devices, exchange(): return lax.all_to_all(block, axes, 0, 0, tiled=True)  48.4 us
    ppermute x6, starting transfers between devices, turned(): return lax.ppermute(block, 'zlo', [(i, (i + k) % NZ) for i in range(NZ)])  17.9 us
    ppermute x6, waiting for transfers between devices, hop(): return lax.ppermute(block, ('zhi', 'core'), [(3 - turn, 2 - turn)])  15.8 us
    all_to_all x1, blocking collectives, exchange(): return lax.all_to_all(block, axes, 0, 0, tiled=True)  13 us
    all_to_all x3, starting transfers between devices, exchange(): return lax.all_to_all(block, axes, 0, 0, tiled=True)  11.1 us
    pallas_call x6, Pallas kernels, chain(): call(first_kernel if first else next_kernel, 'chain', 10 ** 8, 2 * 10 **...  6.83 us
    ppermute x6, starting transfers between devices, hop(): return lax.ppermute(block, ('zhi', 'core'), [(3 - turn, 2 - turn)])  6.58 us
    unnamed x28, local copies, waits for them, and re-layouts  5.57 us
  transfers between devices with their start and end apart: 15, of which 6 were waited for; matrix products, arithmetic and copies ran while one was open for 0% of the time, Pallas kernels for 8%

profile of v3, /device:TPU:1, one launch (start us, length us, event | category | flops | bytes accessed | tf_op | source)
XLA Modules:
  0.0 141.8 jit_solution(13192355582836941945)
XLA Ops:
  0.6 0.0 copy-start.4
  0.7 0.9 copy-done.4
  1.5 0.7 copy-done.6
  2.3 0.7 copy-done.8
  3.0 0.7 copy-done.9
  3.6 0.1 prep.1.refs_0_
  3.7 5.2 %collective-permute-start.2 = (bf16[208,256]{1,0:T(8,128)(2,1)S(1)}, bf16[208,256]{1,0:T(8,128)(2,1)S(1)}, u32[]{:S(2)}, u32[]{:S(2)}) collective-permute-start(bf16[208,256]{1,0:T(8,128)(2,1)S(1)} %prep.1.refs_0_), channel_id=1, source_target_pairs={{0,12},{4,0},{8,4},{12,8},{1,13},{5,1},{9,5},{13,9},{2,14},{6,2},{... | collective-permute-start | bytes 319496 | tf_op jit(solution)/shard_map/ppermute | solution.py:436
  9.0 0.4 collective-permute-start
  10.0 13.0 %all_to_all.20 = s32[16,1,128]{2,1,0:T(1,128)S(1)} all-to-all(s32[16,1,128]{2,1,0:T(1,128)S(1)} %broadcast_in_dim.15), channel_id=1, replica_groups=mesh['zhi'=2,'core'=2,'y'=4,'zlo'=4,'x'=4] {'y','x'}, dimensions={0} | all-to-all | bytes 16384 | tf_op jit(solution)/shard_map/all_to_all | solution.py:432
  23.0 0.0 collective-permute-done.2.refs_3_
  23.0 0.0 collective-permute-done.1.refs_2_
  23.0 0.0 collective-permute-done.refs_1_
  23.0 2.5 %pick.1 = bf16[16,208,256]{2,1,0:T(8,128)(2,1)} custom-call(s32[16,128]{1,0:T(8,128)S(1)} %bitcast.14, s32[1]{0:T(128)} %bitcast.1.z, bf16[208,256]{1,0:T(8,128)(2,1)S(1)} %prep.1.refs_0_, bf16[208,256]{1,0:T(8,128)(2,1)S(1)} %collective-permute-done.refs_1_, bf16[208,256]{1,0:T(8,128)(2,1)S(1)} %collective-permute-done.1.refs_2_, ...), custom_call_target="tpu_custom_call" | custom-call | flops 99999997952 | bytes 1000000000 | tf_op jit(solution)/shard_map/pick/pallas_call | solution.py:84
  25.5 0.6 copy-done
  26.1 3.8 %all-to-all-start.1 = ((bf16[16,208,256]{2,1,0:T(8,128)(2,1)}), bf16[16,208,256]{2,1,0:T(8,128)(2,1)S(1)}, u32[]{:S(2)}, u32[]{:S(2)}) async-start(bf16[16,208,256]{2,1,0:T(8,128)(2,1)} %pick.1), calls=%async_computation.1 | async-start | bytes 3407872 | tf_op jit(solution)/shard_map/all_to_all | solution.py:432
  30.0 21.2 %all-to-all-done.1.got = bf16[16,208,256]{2,1,0:T(8,128)(2,1)S(1)} async-done(((bf16[16,208,256]{2,1,0:T(8,128)(2,1)}), bf16[16,208,256]{2,1,0:T(8,128)(2,1)S(1)}, u32[]{:S(2)}, u32[]{:S(2)}) %all-to-all-start.1) | async-done | bytes 1703968 | tf_op jit(solution)/shard_map/all_to_all | solution.py:432
  51.2 1.3 slopes.1
  52.5 0.0 copy-start.10
  52.6 1.2 chain.6
  53.8 0.7 collective-permute-start.3
  54.5 1.1 chain.7
  55.5 0.7 collective-permute-start.4
  56.2 0.0 collective-permute-done.3.up
  56.2 1.2 chain.8
  57.5 1.3 collective-permute-start.5
  58.8 1.1 chain.9
  59.9 1.3 collective-permute-start.6
  61.2 15.6 %collective-permute-done.5.up = bf16[128,2048]{1,0:T(8,128)(2,1)S(1)} collective-permute-done((bf16[128,2048]{1,0:T(8,128)(2,1)S(1)}, bf16[128,2048]{1,0:T(8,128)(2,1)S(1)}, u32[]{:S(2)}, u32[]{:S(2)}) %collective-permute-start.5) | collective-permute-done | bytes 524320 | tf_op jit(solution)/shard_map/ppermute | solution.py:460
  76.7 1.2 chain.10
  77.9 1.3 collective-permute-start.8
  79.3 0.3 collective-permute-done.6.up
  79.5 1.1 chain.11
  80.6 1.3 collective-permute-start.7
  81.9 2.5 %grads0.1 = (bf16[128,2048]{1,0:T(8,128)(2,1)S(1)}, bf16[16,112,256]{2,1,0:T(8,128)(2,1)}, bf16[512,256]{1,0:T(8,128)(2,1)S(1)}) custom-call(bf16[128,2048]{1,0:T(8,128)(2,1)S(1)} %get-tuple-element.65.before, bf16[128,2048]{1,0:T(8,128)(2,1)S(1)} %collective-permute-done.8.up, f32[128,2048]{1,0:T(8,128)S(1)} %get-tuple-element.45.slope, ...), custom_call_target="tpu_custom_call" | custom-call | flops 99999997952 | bytes 1000000000 | tf_op jit(solution)/shard_map/grads0/pallas_call | solution.py:238
  84.4 3.6 %all-to-all-start.2 = ((bf16[16,112,256]{2,1,0:T(8,128)(2,1)}), bf16[16,112,256]{2,1,0:T(8,128)(2,1)S(1)}, u32[]{:S(2)}, u32[]{:S(2)}) async-start(bf16[16,112,256]{2,1,0:T(8,128)(2,1)} %get-tuple-element.70), calls=%async_computation.2 | async-start | bytes 1835008 | tf_op jit(solution)/shard_map/all_to_all | solution.py:432
  88.1 0.0 copy-start.11
  88.1 1.0 copy-done.11
  89.1 0.9 copy-done.13
  90.1 2.4 %grads1.1 = (bf16[128,3072]{1,0:T(8,128)(2,1)}, bf16[16,112,256]{2,1,0:T(8,128)(2,1)}) custom-call(bf16[128,1024]{1,0:T(8,128)(2,1)S(1)} %copy-done.13, bf16[128,1024]{1,0:T(8,128)(2,1)S(1)} %collective-permute-done.7.up, f32[128,1024]{1,0:T(8,128)S(1)} %get-tuple-element.49.slope, bf16[1024,256]{1,0:T(8,128)(2,1)S(1)} %copy-done.11, ...), custom_call_target="tpu_custom_call" | custom-call | flops 99999997952 | bytes 1000000000 | tf_op jit(solution)/shard_map/grads1/pallas_call | solution.py:279
  92.5 13.1 %all-to-all-done.2.got = bf16[16,112,256]{2,1,0:T(8,128)(2,1)S(1)} async-done(((bf16[16,112,256]{2,1,0:T(8,128)(2,1)}), bf16[16,112,256]{2,1,0:T(8,128)(2,1)S(1)}, u32[]{:S(2)}, u32[]{:S(2)}) %all-to-all-start.2) | async-done | bytes 917536 | tf_op jit(solution)/shard_map/all_to_all | solution.py:432
  105.6 3.6 %all-to-all-start.3 = ((bf16[16,112,256]{2,1,0:T(8,128)(2,1)}), bf16[16,112,256]{2,1,0:T(8,128)(2,1)S(1)}, u32[]{:S(2)}, u32[]{:S(2)}) async-start(bf16[16,112,256]{2,1,0:T(8,128)(2,1)} %get-tuple-element.72), calls=%async_computation.3 | async-start | bytes 1835008 | tf_op jit(solution)/shard_map/all_to_all | solution.py:432
  109.2 1.0 merge0.1
  110.2 14.1 %all-to-all-done.3.got = bf16[16,112,256]{2,1,0:T(8,128)(2,1)S(1)} async-done(((bf16[16,112,256]{2,1,0:T(8,128)(2,1)}), bf16[16,112,256]{2,1,0:T(8,128)(2,1)S(1)}, u32[]{:S(2)}, u32[]{:S(2)}) %all-to-all-start.3) | async-done | bytes 917536 | tf_op jit(solution)/shard_map/all_to_all | solution.py:432
  124.3 1.0 merge1.1
  125.4 10.0 %collective-permute-start.9 = (bf16[208,256]{1,0:T(8,128)(2,1)S(1)}, bf16[208,256]{1,0:T(8,128)(2,1)S(1)}, u32[]{:S(2)}, u32[]{:S(2)}) collective-permute-start(bf16[208,256]{1,0:T(8,128)(2,1)S(1)} %get-tuple-element.76), channel_id=1, source_target_pairs={{0,4},{4,8},{8,12},{12,0},{1,5},{5,9},{9,13},{13,1},{2,6},{6,10},{... | collective-permute-start | bytes 319496 | tf_op jit(solution)/shard_map/ppermute | solution.py:436
  135.4 2.2 %collective-permute-start.11 = (bf16[208,256]{1,0:T(8,128)(2,1)S(1)}, bf16[208,256]{1,0:T(8,128)(2,1)S(1)}, u32[]{:S(2)}, u32[]{:S(2)}) collective-permute-start(bf16[208,256]{1,0:T(8,128)(2,1)S(1)} %get-tuple-element.78), channel_id=1, source_target_pairs={{0,12},{4,0},{8,4},{12,8},{1,13},{5,1},{9,5},{13,9},{2,14},{6,2},{... | collective-permute-start | bytes 319496 | tf_op jit(solution)/shard_map/ppermute | solution.py:436
  137.6 3.4 %collective-permute-done.10.refs_2_ = bf16[208,256]{1,0:T(8,128)(2,1)S(1)} collective-permute-done((bf16[208,256]{1,0:T(8,128)(2,1)S(1)}, bf16[208,256]{1,0:T(8,128)(2,1)S(1)}, u32[]{:S(2)}, u32[]{:S(2)}) %collective-permute-start.10) | collective-permute-done | bytes 106528 | tf_op jit(solution)/shard_map/ppermute | solution.py:436
  141.0 0.8 finish.1
  (26 shorter events, 0.1 us)
Async XLA Ops:
  0.6 0.9 copy-start.4
  1.5 0.7 copy-start.6
  2.3 0.7 copy-start.8
  3.0 0.7 copy-start.9
  3.7 19.3 %collective-permute-start.2 = (bf16[208,256]{1,0:T(8,128)(2,1)S(1)}, bf16[208,256]{1,0:T(8,128)(2,1)S(1)}, u32[]{:S(2)}, u32[]{:S(2)}) collective-permute-start(bf16[208,256]{1,0:T(8,128)(2,1)S(1)} %prep.1.refs_0_), channel_id=1, source_target_pairs={{0,12},{4,0},{8,4},{12,8},{1,13},{5,1},{9,5},{13,9},{2,14},{6,2},{... | collective-permute-start | bytes 319496 | tf_op jit(solution)/shard_map/ppermute | solution.py:436
  9.0 14.0 %collective-permute-start.1 = (bf16[208,256]{1,0:T(8,128)(2,1)S(1)}, bf16[208,256]{1,0:T(8,128)(2,1)S(1)}, u32[]{:S(2)}, u32[]{:S(2)}) collective-permute-start(bf16[208,256]{1,0:T(8,128)(2,1)S(1)} %prep.1.refs_0_), channel_id=1, source_target_pairs={{0,8},{4,12},{8,0},{12,4},{1,9},{5,13},{9,1},{13,5},{2,10},{6,14},... | collective-permute-start | bytes 319496 | tf_op jit(solution)/shard_map/ppermute | solution.py:436
  9.0 14.0 %collective-permute-start = (bf16[208,256]{1,0:T(8,128)(2,1)S(1)}, bf16[208,256]{1,0:T(8,128)(2,1)S(1)}, u32[]{:S(2)}, u32[]{:S(2)}) collective-permute-start(bf16[208,256]{1,0:T(8,128)(2,1)S(1)} %prep.1.refs_0_), channel_id=1, source_target_pairs={{0,4},{4,8},{8,12},{12,0},{1,5},{5,9},{9,13},{13,1},{2,6},{6,10},{... | collective-permute-start | bytes 319496 | tf_op jit(solution)/shard_map/ppermute | solution.py:436
  25.5 0.6 copy-start
  26.1 25.1 %copy-start.3 = (bf16[1,128,3072]{2,1,0:T(8,128)(2,1)S(1)}, bf16[1,128,3072]{2,1,0:T(8,128)(2,1)}, u32[]{:S(2)}) copy-start(bf16[1,128,3072]{2,1,0:T(8,128)(2,1)} %param.7) | copy-start | bytes 2359300
  26.1 25.1 %all-to-all-start.1 = ((bf16[16,208,256]{2,1,0:T(8,128)(2,1)}), bf16[16,208,256]{2,1,0:T(8,128)(2,1)S(1)}, u32[]{:S(2)}, u32[]{:S(2)}) async-start(bf16[16,208,256]{2,1,0:T(8,128)(2,1)} %pick.1), calls=%async_computation.1 | async-start | bytes 3407872 | tf_op jit(solution)/shard_map/all_to_all | solution.py:432
  51.2 1.3 copy-start.2
  52.5 27.0 %copy-start.10 = (bf16[1024,256]{1,0:T(8,128)(2,1)}, bf16[1024,256]{1,0:T(8,128)(2,1)S(1)}, u32[]{:S(2)}) copy-start(bf16[1024,256]{1,0:T(8,128)(2,1)S(1)} %get-tuple-element.50.kernel) | copy-start | bytes 1572868
  53.8 2.4 %collective-permute-start.3 = (bf16[128,2048]{1,0:T(8,128)(2,1)S(1)}, bf16[128,2048]{1,0:T(8,128)(2,1)S(1)}, u32[]{:S(2)}, u32[]{:S(2)}) collective-permute-start(bf16[128,2048]{1,0:T(8,128)(2,1)S(1)} %get-tuple-element.47), channel_id=1, source_target_pairs={{192,128},{193,129},{194,130},{195,131},{196,132},{197,133},{198,1... | collective-permute-start | bytes 1572872 | tf_op jit(solution)/shard_map/ppermute | solution.py:460
  55.5 3.2 %collective-permute-start.4 = (bf16[128,1024]{1,0:T(8,128)(2,1)S(1)}, bf16[128,1024]{1,0:T(8,128)(2,1)S(1)}, u32[]{:S(2)}, u32[]{:S(2)}) collective-permute-start(bf16[128,1024]{1,0:T(8,128)(2,1)S(1)} %get-tuple-element.53), channel_id=1, source_target_pairs={{192,128},{193,129},{194,130},{195,131},{196,132},{197,133},{198,1... | collective-permute-start | bytes 786440 | tf_op jit(solution)/shard_map/ppermute | solution.py:460
  57.5 19.2 %collective-permute-start.5 = (bf16[128,2048]{1,0:T(8,128)(2,1)S(1)}, bf16[128,2048]{1,0:T(8,128)(2,1)S(1)}, u32[]{:S(2)}, u32[]{:S(2)}) collective-permute-start(bf16[128,2048]{1,0:T(8,128)(2,1)S(1)} %get-tuple-element.55), channel_id=1, source_target_pairs={{128,64},{129,65},{130,66},{131,67},{132,68},{133,69},{134,70},{13... | collective-permute-start | bytes 1572872 | tf_op jit(solution)/shard_map/ppermute | solution.py:460
  59.9 19.7 %collective-permute-start.6 = (bf16[128,1024]{1,0:T(8,128)(2,1)S(1)}, bf16[128,1024]{1,0:T(8,128)(2,1)S(1)}, u32[]{:S(2)}, u32[]{:S(2)}) collective-permute-start(bf16[128,1024]{1,0:T(8,128)(2,1)S(1)} %get-tuple-element.59), channel_id=1, source_target_pairs={{128,64},{129,65},{130,66},{131,67},{132,68},{133,69},{134,70},{13... | collective-permute-start | bytes 786440 | tf_op jit(solution)/shard_map/ppermute | solution.py:460
  77.9 4.0 %collective-permute-start.8 = (bf16[128,2048]{1,0:T(8,128)(2,1)S(1)}, bf16[128,2048]{1,0:T(8,128)(2,1)S(1)}, u32[]{:S(2)}, u32[]{:S(2)}) collective-permute-start(bf16[128,2048]{1,0:T(8,128)(2,1)S(1)} %get-tuple-element.61), channel_id=1, source_target_pairs={{64,0},{65,1},{66,2},{67,3},{68,4},{69,5},{70,6},{71,7},{72,8},{73... | collective-permute-start | bytes 1572872 | tf_op jit(solution)/shard_map/ppermute | solution.py:460
  80.6 3.8 %copy-start.12 = (bf16[128,1024]{1,0:T(8,128)(2,1)}, bf16[128,1024]{1,0:T(8,128)(2,1)S(1)}, u32[]{:S(2)}) copy-start(bf16[128,1024]{1,0:T(8,128)(2,1)S(1)} %get-tuple-element.63.before) | copy-start | bytes 786436
  80.6 7.5 %collective-permute-start.7 = (bf16[128,1024]{1,0:T(8,128)(2,1)S(1)}, bf16[128,1024]{1,0:T(8,128)(2,1)S(1)}, u32[]{:S(2)}, u32[]{:S(2)}) collective-permute-start(bf16[128,1024]{1,0:T(8,128)(2,1)S(1)} %get-tuple-element.64), channel_id=1, source_target_pairs={{64,0},{65,1},{66,2},{67,3},{68,4},{69,5},{70,6},{71,7},{72,8},{73... | collective-permute-start | bytes 786440 | tf_op jit(solution)/shard_map/ppermute | solution.py:460
  84.4 21.1 %all-to-all-start.2 = ((bf16[16,112,256]{2,1,0:T(8,128)(2,1)}), bf16[16,112,256]{2,1,0:T(8,128)(2,1)S(1)}, u32[]{:S(2)}, u32[]{:S(2)}) async-start(bf16[16,112,256]{2,1,0:T(8,128)(2,1)} %get-tuple-element.70), calls=%async_computation.2 | async-start | bytes 1835008 | tf_op jit(solution)/shard_map/all_to_all | solution.py:432
  88.1 1.0 copy-start.11
  89.1 0.9 copy-start.13
  92.5 16.7 %copy-start.1 = (s32[16,1,128]{2,1,0:T(1,128)S(1)}, s32[16,1,128]{2,1,0:T(1,128)}, u32[]{:S(2)}) copy-start(s32[16,1,128]{2,1,0:T(1,128)} %copy-done) | copy-start | bytes 24580
  105.6 18.8 %all-to-all-start.3 = ((bf16[16,112,256]{2,1,0:T(8,128)(2,1)}), bf16[16,112,256]{2,1,0:T(8,128)(2,1)S(1)}, u32[]{:S(2)}, u32[]{:S(2)}) async-start(bf16[16,112,256]{2,1,0:T(8,128)(2,1)} %get-tuple-element.72), calls=%async_computation.3 | async-start | bytes 1835008 | tf_op jit(solution)/shard_map/all_to_all | solution.py:432
  124.3 16.7 %copy-start.5 = (bf16[1,4,48,256]{3,2,1,0:T(8,128)(2,1)S(1)}, bf16[1,4,48,256]{3,2,1,0:T(8,128)(2,1)}, u32[]{:S(2)}) copy-start(bf16[1,4,48,256]{3,2,1,0:T(8,128)(2,1)} %param.11) | copy-start | bytes 294916
  124.3 16.7 %copy-start.7 = (bf16[1,48,256]{2,1,0:T(8,128)(2,1)S(1)}, bf16[1,48,256]{2,1,0:T(8,128)(2,1)}, u32[]{:S(2)}) copy-start(bf16[1,48,256]{2,1,0:T(8,128)(2,1)} %param.10) | copy-start | bytes 73732
  125.4 12.2 %collective-permute-start.9 = (bf16[208,256]{1,0:T(8,128)(2,1)S(1)}, bf16[208,256]{1,0:T(8,128)(2,1)S(1)}, u32[]{:S(2)}, u32[]{:S(2)}) collective-permute-start(bf16[208,256]{1,0:T(8,128)(2,1)S(1)} %get-tuple-element.76), channel_id=1, source_target_pairs={{0,4},{4,8},{8,12},{12,0},{1,5},{5,9},{9,13},{13,1},{2,6},{6,10},{... | collective-permute-start | bytes 319496 | tf_op jit(solution)/shard_map/ppermute | solution.py:436
  135.4 5.6 %collective-permute-start.10 = (bf16[208,256]{1,0:T(8,128)(2,1)S(1)}, bf16[208,256]{1,0:T(8,128)(2,1)S(1)}, u32[]{:S(2)}, u32[]{:S(2)}) collective-permute-start(bf16[208,256]{1,0:T(8,128)(2,1)S(1)} %get-tuple-element.77), channel_id=1, source_target_pairs={{0,8},{4,12},{8,0},{12,4},{1,9},{5,13},{9,1},{13,5},{2,10},{6,14},... | collective-permute-start | bytes 319496 | tf_op jit(solution)/shard_map/ppermute | solution.py:436
  135.4 5.6 %collective-permute-start.11 = (bf16[208,256]{1,0:T(8,128)(2,1)S(1)}, bf16[208,256]{1,0:T(8,128)(2,1)S(1)}, u32[]{:S(2)}, u32[]{:S(2)}) collective-permute-start(bf16[208,256]{1,0:T(8,128)(2,1)S(1)} %get-tuple-element.78), channel_id=1, source_target_pairs={{0,12},{4,0},{8,4},{12,8},{1,13},{5,1},{9,5},{13,9},{2,14},{6,2},{... | collective-permute-start | bytes 319496 | tf_op jit(solution)/shard_map/ppermute | solution.py:436

commit v4 on v3

--- a/solution.py
+++ b/solution.py
@@ -1,3 +1,5 @@
+import functools
+
 import jax
 import jax.numpy as jnp
 from jax import lax
@@ -16,10 +18,12 @@
 PIECE = NZ * SHARD
 TILE = 16
 BLOCK = PIECE + TILE
-HALF = PIECE // 2
-PART = HALF + TILE
-FIRST = (0, 1)
-LAST = (2,)
+FIRST = (0,)
+LAST = (1, 2)
+EARLY = 1
+ROWS0 = EARLY * SHARD
+ROWS1 = PIECE - ROWS0
+REST = len(FIRST) * GS - EARLY * PIECE
 VMEM = pl.BlockSpec(memory_space=pltpu.VMEM)
 SMEM = pl.BlockSpec(memory_space=pltpu.SMEM)
 BF = jnp.bfloat16
@@ -115,7 +119,7 @@
         if q in FIRST:
             slope0[:, lanes] = slope
         else:
-            slope1[...] = slope
+            slope1[:, q * GS - cut : (q + 1) * GS - cut] = slope
 
 
 def columns(width):
@@ -152,10 +156,11 @@
     )
 
 
-def first_kernel(section, up, slope, kernel, out, kept):
+def first_kernel(base, section, up, slope, kernel, out, kept):
     for q in range(slope.shape[1] // GS):
         lanes = slice(q * GS, (q + 1) * GS)
-        above = jnp.where(section[0] == 3, up[:, lanes].astype(F32), 0.0)
+        above = up[:, base + q * GS : base + (q + 1) * GS].astype(F32)
+        above = jnp.where(section[0] == 3, above, 0.0)
         kept[:, lanes] = above.astype(BF)
         signal = (above * slope[:, lanes]).astype(BF)
         out[:, lanes] = (above + back_product(signal, kernel[lanes, :])).astype(BF)
@@ -170,41 +175,41 @@
         out[:, lanes] = (above + back_product(signal, kernel[lanes, :])).astype(BF)
 
 
-def of_slab(groups):
-    if groups == FIRST:
-        return columns(SLAB)
-    return pl.BlockSpec((ROWS, GS), lambda i: (0, SG * i + LAST[0]))
-
-
 def chain(groups, head, up, slope, kernel, first=False):
     width = len(groups) * GS
     shape = jax.ShapeDtypeStruct((ROWS, NY * width), BF)
     return call(
-        first_kernel if first else next_kernel,
+        functools.partial(first_kernel, groups[0] * GS) if first else next_kernel,
         "chain",
         10**8,
         2 * 10**6,
         grid=(NY,),
         out_shape=(shape, shape),
-        in_specs=([SMEM, of_slab(groups)] if first else [columns(width)] * 2)
+        in_specs=([SMEM, columns(SLAB)] if first else [columns(width)] * 2)
         + [columns(width), rows(width)],
         out_specs=(columns(width), columns(width)),
     )(head, up, slope, kernel)
 
 
-def local_grads(before, up, slope, kernel, x, q, tile, row):
-    lanes = slice(q * GS, (q + 1) * GS)
-    above = before[:, lanes].astype(F32) + up[:, lanes].astype(F32)
-    signal = (above * slope[:, lanes]).astype(BF)
-    outgoing = (above + back_product(signal, kernel[lanes, :])).astype(BF)
-    grad = lax.dot_general(
-        x[:, lanes], signal, (((0,), (0,)), ((), ())), preferred_element_type=F32
-    ).astype(BF)
-    total = jnp.sum(signal.astype(F32), axis=0, keepdims=True)
-    high = total.astype(BF).astype(F32)
-    tile[row : row + 1, :] = high
-    tile[SG + row : SG + row + 1, :] = total - high
-    return outgoing, grad
+def local_grads(groups, before, up, slope, kernel, x, out, tile):
+    found = []
+    tile[...] = jnp.zeros_like(tile)
+    for j, q in enumerate(groups):
+        lanes = slice(j * GS, (j + 1) * GS)
+        above = before[:, lanes].astype(F32) + up[:, lanes].astype(F32)
+        signal = (above * slope[:, lanes]).astype(BF)
+        outgoing = (above + back_product(signal, kernel[lanes, :])).astype(BF)
+        here = slice(q * GS, (q + 1) * GS)
+        out[:, here] = outgoing
+        grad = lax.dot_general(
+            x[:, here], signal, (((0,), (0,)), ((), ())), preferred_element_type=F32
+        )
+        found.append(grad.astype(BF))
+        total = jnp.sum(signal.astype(F32), axis=0, keepdims=True)
+        high = total.astype(BF).astype(F32)
+        tile[q : q + 1, :] = high
+        tile[SG + q : SG + q + 1, :] = total - high
+    return found
 
 
 def place_of(row):
@@ -213,24 +218,17 @@
 
 
 def grads0_kernel(before, up, slope, kernel, x, out, send, rest, tile):
-    tile[...] = jnp.zeros_like(tile)
-    for q in FIRST:
-        outgoing, grad = local_grads(before, up, slope, kernel, x, q, tile, q)
-        out[:, q * GS : (q + 1) * GS] = outgoing
-        for u in range(GS // TILE):
-            row = q * GS + u * TILE
-            z, i, inner = place_of(row)
-            if z < NZ // 2:
-                at = z * SHARD + inner
-                send[i, at : at + TILE, :] = grad[u * TILE : (u + 1) * TILE, :]
-            else:
-                at = row - 2 * PIECE
-                rest[at : at + TILE, :] = grad[u * TILE : (u + 1) * TILE, :]
+    found = local_grads(FIRST, before, up, slope, kernel, x, out, tile)
+    for row in range(0, len(FIRST) * GS, TILE):
+        z, i, inner = place_of(row)
+        part = found[row // GS][row % GS : row % GS + TILE, :]
+        if z < EARLY:
+            at = z * SHARD + inner
+            send[i, at : at + TILE, :] = part
+        else:
+            rest[row - EARLY * PIECE : row - EARLY * PIECE + TILE, :] = part
     for i in range(NX):
-        send[i, HALF:, :] = tile[...].astype(BF)
-
-
-REST = len(FIRST) * GS - 2 * PIECE
+        send[i, ROWS0:, :] = tile[...].astype(BF)
 
 
 def grads0(before, up, slope, kernel, x):
@@ -243,13 +241,13 @@
         grid=(NY,),
         out_shape=(
             jax.ShapeDtypeStruct((ROWS, NY * width), BF),
-            jax.ShapeDtypeStruct((NY * NX, PART, GS), BF),
+            jax.ShapeDtypeStruct((NY * NX, ROWS0 + TILE, GS), BF),
             jax.ShapeDtypeStruct((NY * REST, GS), BF),
         ),
         in_specs=[columns(width)] * 3 + [rows(width), columns(SLAB)],
         out_specs=(
             columns(width),
-            pl.BlockSpec((NX, PART, GS), lambda i: (i, 0, 0)),
+            pl.BlockSpec((NX, ROWS0 + TILE, GS), lambda i: (i, 0, 0)),
             rows(REST),
         ),
         scratch_shapes=[pltpu.VMEM((TILE, GS), F32)],
@@ -257,21 +255,19 @@
 
 
 def grads1_kernel(before, up, slope, kernel, x, rest, out0, out, send, tile):
-    tile[...] = jnp.zeros_like(tile)
     start = LAST[0] * GS
     out[:, :start] = out0[...]
-    outgoing, grad = local_grads(before, up, slope, kernel, x, 0, tile, LAST[0])
-    out[:, start:] = outgoing
-    for u in range((SLAB - 2 * PIECE) // TILE):
-        row = 2 * PIECE + u * TILE
+    found = local_grads(LAST, before, up, slope, kernel, x, out, tile)
+    for row in range(EARLY * PIECE, SLAB, TILE):
         z, i, inner = place_of(row)
-        at = (z - NZ // 2) * SHARD + inner
+        at = (z - EARLY) * SHARD + inner
         if row < start:
-            send[i, at : at + TILE, :] = rest[u * TILE : (u + 1) * TILE, :]
+            part = rest[row - EARLY * PIECE : row - EARLY * PIECE + TILE, :]
         else:
-            send[i, at : at + TILE, :] = grad[row - start : row - start + TILE, :]
+            part = found[(row - start) // GS][row % GS : row % GS + TILE, :]
+        send[i, at : at + TILE, :] = part
     for i in range(NX):
-        send[i, HALF:, :] = tile[...].astype(BF)
+        send[i, ROWS1:, :] = tile[...].astype(BF)
 
 
 def grads1(before, up, slope, kernel, x, rest, out0):
@@ -284,11 +280,11 @@
         grid=(NY,),
         out_shape=(
             jax.ShapeDtypeStruct((ROWS, D), BF),
-            jax.ShapeDtypeStruct((NY * NX, PART, GS), BF),
+            jax.ShapeDtypeStruct((NY * NX, ROWS1 + TILE, GS), BF),
         ),
         in_specs=[columns(width)] * 3
-        + [rows(width), of_slab(LAST), rows(REST), columns(len(FIRST) * GS)],
-        out_specs=(columns(SLAB), pl.BlockSpec((NX, PART, GS), lambda i: (i, 0, 0))),
+        + [rows(width), columns(SLAB), rows(REST), columns(len(FIRST) * GS)],
+        out_specs=(columns(SLAB), pl.BlockSpec((NX, ROWS1 + TILE, GS), lambda i: (i, 0, 0))),
         scratch_shapes=[pltpu.VMEM((TILE, GS), F32)],
     )(before, up, slope, kernel, x, rest, out0)
 
@@ -311,11 +307,15 @@
     @pl.when(pl.program_id(0) == NY - 1)
     def _():
         for k in range(DOMAINS):
-            for z in range(NZ // 2):
+            for z in range(EARLY):
                 out[z, k * SHARD : (k + 1) * SHARD, :] = total[
                     k, z * SHARD : (z + 1) * SHARD, :
                 ].astype(BF)
-            bias[k] = total[k, HALF:, :]
+            bias[k] = total[k, ROWS0:, :]
+
+
+def whole(shape):
+    return pl.BlockSpec(shape, lambda i: (0,) * len(shape))
 
 
 def merge0(ids, got):
@@ -326,15 +326,12 @@
         10**6,
         grid=(NY,),
         out_shape=(
-            jax.ShapeDtypeStruct((NZ // 2, PIECE, GS), BF),
+            jax.ShapeDtypeStruct((EARLY, PIECE, GS), BF),
             jax.ShapeDtypeStruct((DOMAINS, TILE, GS), F32),
         ),
-        in_specs=[SMEM, pl.BlockSpec((NX, PART, GS), lambda i: (i, 0, 0))],
-        out_specs=(
-            pl.BlockSpec((NZ // 2, PIECE, GS), lambda i: (0, 0, 0)),
-            pl.BlockSpec((DOMAINS, TILE, GS), lambda i: (0, 0, 0)),
-        ),
-        scratch_shapes=[pltpu.VMEM((DOMAINS, PART, GS), F32)],
+        in_specs=[SMEM, pl.BlockSpec((NX, ROWS0 + TILE, GS), lambda i: (i, 0, 0))],
+        out_specs=(whole((EARLY, PIECE, GS)), whole((DOMAINS, TILE, GS))),
+        scratch_shapes=[pltpu.VMEM((DOMAINS, ROWS0 + TILE, GS), F32)],
     )(ids, got)
 
 
@@ -345,13 +342,13 @@
     @pl.when(pl.program_id(0) == NY - 1)
     def _():
         tile[...] = jnp.zeros_like(tile)
-        parts[: NZ // 2] = sums[...]
+        parts[:EARLY] = sums[...]
         for k in range(DOMAINS):
-            for half in range(NZ // 2):
-                parts[NZ // 2 + half, k * SHARD : (k + 1) * SHARD, :] = total[
-                    k, half * SHARD : (half + 1) * SHARD, :
+            for late in range(NZ - EARLY):
+                parts[EARLY + late, k * SHARD : (k + 1) * SHARD, :] = total[
+                    k, late * SHARD : (late + 1) * SHARD, :
                 ].astype(BF)
-            both = total[k, HALF:, :] + bias[k]
+            both = total[k, ROWS1:, :] + bias[k]
             tile[k * SG : (k + 1) * SG, :] = both[:SG, :] + both[SG : 2 * SG, :]
         for k in range(NZ):
             outs[k][:PIECE, :] = parts[(z[0] + k) % NZ]
@@ -359,9 +356,6 @@
 
 
 def merge1(ids, z, got, sums, bias):
-    def whole(shape):
-        return pl.BlockSpec(shape, lambda i: (0,) * len(shape))
-
     return call(
         merge1_kernel,
         "merge1",
@@ -372,13 +366,13 @@
         in_specs=[
             SMEM,
             SMEM,
-            pl.BlockSpec((NX, PART, GS), lambda i: (i, 0, 0)),
-            whole((NZ // 2, PIECE, GS)),
+            pl.BlockSpec((NX, ROWS1 + TILE, GS), lambda i: (i, 0, 0)),
+            whole((EARLY, PIECE, GS)),
             whole((DOMAINS, TILE, GS)),
         ],
         out_specs=(whole((BLOCK, GS)),) * NZ,
         scratch_shapes=[
-            pltpu.VMEM((DOMAINS, PART, GS), F32),
+            pltpu.VMEM((DOMAINS, ROWS1 + TILE, GS), F32),
             pltpu.VMEM((NZ, PIECE, GS), BF),
             pltpu.VMEM((TILE, GS), F32),
         ],
@@ -462,16 +456,14 @@
     out0, kept0 = chain(FIRST, section, cotangent, slope0, kernel0, first=True)
     (slope1,) = after(out0, slope1)
     out1, kept1 = chain(LAST, section, cotangent, slope1, kernel1, first=True)
-    for turn in range(2):
+    for turn in range(3):
         up0 = hop(out0, turn)
+        if turn == 1:
+            (out1,) = after(up0, out1)
         up1 = hop(out1, turn)
-        (up0,) = after(out1, up0)
-        out0, kept0 = chain(FIRST, kept0, up0, slope0, kernel0)
-        (up1,) = after(out0, up1)
-        out1, kept1 = chain(LAST, kept1, up1, slope1, kernel1)
-    up0 = hop(out0, 2)
-    up1 = hop(out1, 2)
-    (up0,) = after(out1, up0)
+        if turn < 2:
+            out0, kept0 = chain(FIRST, kept0, up0, slope0, kernel0)
+            out1, kept1 = chain(LAST, kept1, up1, slope1, kernel1)
     d_in0, send0, rest = grads0(kept0, up0, slope0, kernel0, x)
     got0 = exchange(send0, ("y", "x"))
     d_inputs, send1 = grads1(kept1, up1, slope1, kernel1, x, rest, d_in0)

time: 145 us -> 143 us (0.986); the launches traced: 142 us -> 142 us
  local copies, waits for them, and re-layouts: 5.58 us -> 9.25 us
  waiting for transfers between devices: 67.6 us -> 65.9 us
    all_to_all x3, waiting for transfers between devices: 48.4 us -> 36.2 us  [exchange(): return lax.all_to_all(block, axes, 0, 0, tiled=True)]
    ppermute x6, waiting for transfers between devices: 15.8 us -> 25 us  [hop(): return lax.ppermute(block, ('zhi', 'core'), [(3 - turn, 2 - turn)])]
    unnamed x28 -> x38, local copies, waits for them, and re-layouts: 5.57 us -> 9.24 us
    ppermute x6, starting transfers between devices: 17.9 us -> 15.4 us  [turned(): return lax.ppermute(block, 'zlo', [(i, (i + k) % NZ) for i in range(NZ)])]
  transfers between devices with their start and end apart: 15 -> 15, of which waited for: 6 -> 8; matrix products, arithmetic and copies ran while one was open for 0% -> 0% of each run, Pallas kernels for 8% -> 8%
where the time goes in v4:
time: 143 us; the launch traced here: 142 us
  waiting for transfers between devices  65.9 us (46%)
  starting transfers between devices  34.2 us (24%)
  Pallas kernels  18.5 us (13%)
  blocking collectives  13 us (9%)
  local copies, waits for them, and re-layouts  9.25 us (6%)
  between operations  1.57 us (1%)
    all_to_all x3, waiting for transfers between devices, exchange(): return lax.all_to_all(block, axes, 0, 0, tiled=True)  36.2 us
    ppermute x6, waiting for transfers between devices, hop(): return lax.ppermute(block, ('zhi', 'core'), [(3 - turn, 2 - turn)])  25 us
    ppermute x6, starting transfers between devices, turned(): return lax.ppermute(block, 'zlo', [(i, (i + k) % NZ) for i in range(NZ)])  15.4 us
    all_to_all x1, blocking collectives, exchange(): return lax.all_to_all(block, axes, 0, 0, tiled=True)  13 us
    all_to_all x3, starting transfers between devices, exchange(): return lax.all_to_all(block, axes, 0, 0, tiled=True)  12.2 us
    unnamed x38, local copies, waits for them, and re-layouts  9.24 us
    pallas_call x6, Pallas kernels, chain(): call(functools.partial(first_kernel, groups[0] * GS) if first else next_k...  6.84 us
    ppermute x6, starting transfers between devices, hop(): return lax.ppermute(block, ('zhi', 'core'), [(3 - turn, 2 - turn)])  6.57 us
  transfers between devices with their start and end apart: 15, of which 8 were waited for; matrix products, arithmetic and copies ran while one was open for 0% of the time, Pallas kernels for 8%

profile of v4, /device:TPU:1, one launch (start us, length us, event | category | flops | bytes accessed | tf_op | source)
XLA Modules:
  0.0 142.4 jit_solution(7753295559096135687)
XLA Ops:
  0.7 0.9 copy-done.5
  1.5 0.7 copy-done.7
  2.3 0.7 copy-done.9
  3.0 0.7 copy-done.10
  3.7 2.5 %collective-permute-start = (bf16[208,256]{1,0:T(8,128)(2,1)S(1)}, bf16[208,256]{1,0:T(8,128)(2,1)S(1)}, u32[]{:S(2)}, u32[]{:S(2)}) collective-permute-start(bf16[208,256]{1,0:T(8,128)(2,1)S(1)} %prep.1.refs_0_), channel_id=1, source_target_pairs={{0,4},{4,8},{8,12},{12,0},{1,5},{5,9},{9,13},{13,1},{2,6},{6,10},{... | collective-permute-start | bytes 319496 | tf_op jit(solution)/shard_map/ppermute | solution.py:430
  6.3 3.0 %collective-permute-start.1 = (bf16[208,256]{1,0:T(8,128)(2,1)S(1)}, bf16[208,256]{1,0:T(8,128)(2,1)S(1)}, u32[]{:S(2)}, u32[]{:S(2)}) collective-permute-start(bf16[208,256]{1,0:T(8,128)(2,1)S(1)} %prep.1.refs_0_), channel_id=1, source_target_pairs={{0,8},{4,12},{8,0},{12,4},{1,9},{5,13},{9,1},{13,5},{2,10},{6,14},... | collective-permute-start | bytes 319496 | tf_op jit(solution)/shard_map/ppermute | solution.py:430
  9.2 0.7 collective-permute-start.2
  10.6 13.0 %all_to_all.20 = s32[16,1,128]{2,1,0:T(1,128)S(1)} all-to-all(s32[16,1,128]{2,1,0:T(1,128)S(1)} %broadcast_in_dim.15), channel_id=1, replica_groups=mesh['zhi'=2,'core'=2,'y'=4,'zlo'=4,'x'=4] {'y','x'}, dimensions={0} | all-to-all | bytes 16384 | tf_op jit(solution)/shard_map/all_to_all | solution.py:426
  23.6 2.5 %pick.1 = bf16[16,208,256]{2,1,0:T(8,128)(2,1)} custom-call(s32[16,128]{1,0:T(8,128)S(1)} %bitcast.14, s32[1]{0:T(128)} %bitcast.1.z, bf16[208,256]{1,0:T(8,128)(2,1)S(1)} %prep.1.refs_0_, bf16[208,256]{1,0:T(8,128)(2,1)S(1)} %collective-permute-done.refs_1_, bf16[208,256]{1,0:T(8,128)(2,1)S(1)} %collective-permute-done.1.refs_2_, ...), custom_call_target="tpu_custom_call" | custom-call | flops 99999997952 | bytes 1000000000 | tf_op jit(solution)/shard_map/pick/pallas_call | solution.py:88
  26.1 0.6 copy-done
  26.7 3.8 %all-to-all-start.1 = ((bf16[16,208,256]{2,1,0:T(8,128)(2,1)}), bf16[16,208,256]{2,1,0:T(8,128)(2,1)S(1)}, u32[]{:S(2)}, u32[]{:S(2)}) async-start(bf16[16,208,256]{2,1,0:T(8,128)(2,1)} %pick.1), calls=%async_computation.1 | async-start | bytes 3407872 | tf_op jit(solution)/shard_map/all_to_all | solution.py:426
  30.6 21.1 %all-to-all-done.1.got = bf16[16,208,256]{2,1,0:T(8,128)(2,1)S(1)} async-done(((bf16[16,208,256]{2,1,0:T(8,128)(2,1)}), bf16[16,208,256]{2,1,0:T(8,128)(2,1)S(1)}, u32[]{:S(2)}, u32[]{:S(2)}) %all-to-all-start.1) | async-done | bytes 1703968 | tf_op jit(solution)/shard_map/all_to_all | solution.py:426
  51.6 1.3 slopes.1
  53.0 1.0 chain.6
  54.0 0.7 collective-permute-start.4
  54.7 1.2 chain.7
  55.9 0.7 collective-permute-start.3
  56.7 1.1 chain.9
  57.7 1.3 collective-permute-start.5
  59.0 1.2 chain.8
  60.3 14.2 %collective-permute-done.5.up = bf16[128,1024]{1,0:T(8,128)(2,1)S(1)} collective-permute-done((bf16[128,1024]{1,0:T(8,128)(2,1)S(1)}, bf16[128,1024]{1,0:T(8,128)(2,1)S(1)}, u32[]{:S(2)}, u32[]{:S(2)}) %collective-permute-start.5) | collective-permute-done | bytes 262176 | tf_op jit(solution)/shard_map/ppermute | solution.py:454
  74.5 1.3 collective-permute-start.6
  75.8 1.1 chain.11
  76.9 1.3 collective-permute-start.8
  78.2 10.8 %collective-permute-done.6.up = bf16[128,2048]{1,0:T(8,128)(2,1)S(1)} collective-permute-done((bf16[128,2048]{1,0:T(8,128)(2,1)S(1)}, bf16[128,2048]{1,0:T(8,128)(2,1)S(1)}, u32[]{:S(2)}, u32[]{:S(2)}) %collective-permute-start.6) | collective-permute-done | bytes 524320 | tf_op jit(solution)/shard_map/ppermute | solution.py:454
  89.0 1.2 chain.10
  90.2 1.3 collective-permute-start.7
  91.6 2.3 %grads0.1 = (bf16[128,1024]{1,0:T(8,128)(2,1)S(1)}, bf16[16,64,256]{2,1,0:T(8,128)(2,1)}, bf16[256,256]{1,0:T(8,128)(2,1)S(1)}) custom-call(bf16[128,1024]{1,0:T(8,128)(2,1)S(1)} %get-tuple-element.57.before, bf16[128,1024]{1,0:T(8,128)(2,1)S(1)} %collective-permute-done.8.up, f32[128,1024]{1,0:T(8,128)S(1)} %get-tuple-element.41.slope, ...), custom_call_target="tpu_custom_call" | custom-call | flops 99999997952 | bytes 1000000000 | tf_op jit(solution)/shard_map/grads0/pallas_call | solution.py:236
  93.8 0.7 copy-done.15
  94.5 0.7 copy-done.17
  95.2 3.6 %all-to-all-start.2 = ((bf16[16,64,256]{2,1,0:T(8,128)(2,1)}), bf16[16,64,256]{2,1,0:T(8,128)(2,1)S(1)}, u32[]{:S(2)}, u32[]{:S(2)}) async-start(bf16[16,64,256]{2,1,0:T(8,128)(2,1)} %get-tuple-element.62), calls=%async_computation.2 | async-start | bytes 1048576 | tf_op jit(solution)/shard_map/all_to_all | solution.py:426
  98.8 1.2 copy-done.12
  100.0 1.2 copy-done.14
  101.3 0.9 copy-done.16
  102.2 0.9 copy-done.18
  103.1 2.7 %grads1.1 = (bf16[128,3072]{1,0:T(8,128)(2,1)}, bf16[16,160,256]{2,1,0:T(8,128)(2,1)}) custom-call(bf16[128,2048]{1,0:T(8,128)(2,1)S(1)} %get-tuple-element.54.before, bf16[128,2048]{1,0:T(8,128)(2,1)S(1)} %collective-permute-done.7.up, f32[128,2048]{1,0:T(8,128)S(1)} %copy-done.12, bf16[2048,256]{1,0:T(8,128)(2,1)S(1)} %copy-done.14, ...), custom_call_target="tpu_custom_call" | custom-call | flops 99999997952 | bytes 1000000000 | tf_op jit(solution)/shard_map/grads1/pallas_call | solution.py:275
  105.8 1.9 %all-to-all-done.2.got = bf16[16,64,256]{2,1,0:T(8,128)(2,1)S(1)} async-done(((bf16[16,64,256]{2,1,0:T(8,128)(2,1)}), bf16[16,64,256]{2,1,0:T(8,128)(2,1)S(1)}, u32[]{:S(2)}, u32[]{:S(2)}) %all-to-all-start.2) | async-done | bytes 524320 | tf_op jit(solution)/shard_map/all_to_all | solution.py:426
  107.7 4.8 %all-to-all-start.3 = ((bf16[16,160,256]{2,1,0:T(8,128)(2,1)}), bf16[16,160,256]{2,1,0:T(8,128)(2,1)S(1)}, u32[]{:S(2)}, u32[]{:S(2)}) async-start(bf16[16,160,256]{2,1,0:T(8,128)(2,1)} %get-tuple-element.64), calls=%async_computation.3 | async-start | bytes 2621440 | tf_op jit(solution)/shard_map/all_to_all | solution.py:426
  112.5 0.9 merge0.1
  113.5 13.2 %all-to-all-done.3.got = bf16[16,160,256]{2,1,0:T(8,128)(2,1)S(1)} async-done(((bf16[16,160,256]{2,1,0:T(8,128)(2,1)}), bf16[16,160,256]{2,1,0:T(8,128)(2,1)S(1)}, u32[]{:S(2)}, u32[]{:S(2)}) %all-to-all-start.3) | async-done | bytes 1310752 | tf_op jit(solution)/shard_map/all_to_all | solution.py:426
  126.7 1.1 merge1.1
  127.8 7.7 %collective-permute-start.10 = (bf16[208,256]{1,0:T(8,128)(2,1)S(1)}, bf16[208,256]{1,0:T(8,128)(2,1)S(1)}, u32[]{:S(2)}, u32[]{:S(2)}) collective-permute-start(bf16[208,256]{1,0:T(8,128)(2,1)S(1)} %get-tuple-element.69), channel_id=1, source_target_pairs={{0,8},{4,12},{8,0},{12,4},{1,9},{5,13},{9,1},{13,5},{2,10},{6,14},... | collective-permute-start | bytes 319496 | tf_op jit(solution)/shard_map/ppermute | solution.py:430
  135.5 0.7 collective-permute-start.11
  136.3 0.7 collective-permute-start.9
  137.0 1.9 %collective-permute-done.10.refs_2_ = bf16[208,256]{1,0:T(8,128)(2,1)S(1)} collective-permute-done((bf16[208,256]{1,0:T(8,128)(2,1)S(1)}, bf16[208,256]{1,0:T(8,128)(2,1)S(1)}, u32[]{:S(2)}, u32[]{:S(2)}) %collective-permute-start.10) | collective-permute-done | bytes 106528 | tf_op jit(solution)/shard_map/ppermute | solution.py:430
  138.9 0.5 collective-permute-done.11.refs_3_
  139.4 2.2 %collective-permute-done.9.refs_1_ = bf16[208,256]{1,0:T(8,128)(2,1)S(1)} collective-permute-done((bf16[208,256]{1,0:T(8,128)(2,1)S(1)}, bf16[208,256]{1,0:T(8,128)(2,1)S(1)}, u32[]{:S(2)}, u32[]{:S(2)}) %collective-permute-start.9) | collective-permute-done | bytes 106528 | tf_op jit(solution)/shard_map/ppermute | solution.py:430
  141.6 0.8 finish.1
  (36 shorter events, 0.2 us)
Async XLA Ops:
  0.6 0.9 copy-start.5
  1.5 0.7 copy-start.7
  2.3 0.7 copy-start.9
  3.0 0.7 copy-start.10
  3.7 19.9 %collective-permute-start = (bf16[208,256]{1,0:T(8,128)(2,1)S(1)}, bf16[208,256]{1,0:T(8,128)(2,1)S(1)}, u32[]{:S(2)}, u32[]{:S(2)}) collective-permute-start(bf16[208,256]{1,0:T(8,128)(2,1)S(1)} %prep.1.refs_0_), channel_id=1, source_target_pairs={{0,4},{4,8},{8,12},{12,0},{1,5},{5,9},{9,13},{13,1},{2,6},{6,10},{... | collective-permute-start | bytes 319496 | tf_op jit(solution)/shard_map/ppermute | solution.py:430
  6.3 17.4 %collective-permute-start.1 = (bf16[208,256]{1,0:T(8,128)(2,1)S(1)}, bf16[208,256]{1,0:T(8,128)(2,1)S(1)}, u32[]{:S(2)}, u32[]{:S(2)}) collective-permute-start(bf16[208,256]{1,0:T(8,128)(2,1)S(1)} %prep.1.refs_0_), channel_id=1, source_target_pairs={{0,8},{4,12},{8,0},{12,4},{1,9},{5,13},{9,1},{13,5},{2,10},{6,14},... | collective-permute-start | bytes 319496 | tf_op jit(solution)/shard_map/ppermute | solution.py:430
  9.2 14.4 %collective-permute-start.2 = (bf16[208,256]{1,0:T(8,128)(2,1)S(1)}, bf16[208,256]{1,0:T(8,128)(2,1)S(1)}, u32[]{:S(2)}, u32[]{:S(2)}) collective-permute-start(bf16[208,256]{1,0:T(8,128)(2,1)S(1)} %prep.1.refs_0_), channel_id=1, source_target_pairs={{0,12},{4,0},{8,4},{12,8},{1,13},{5,1},{9,5},{13,9},{2,14},{6,2},{... | collective-permute-start | bytes 319496 | tf_op jit(solution)/shard_map/ppermute | solution.py:430
  26.1 0.6 copy-start
  26.7 24.9 %copy-start.3 = (bf16[1,128,3072]{2,1,0:T(8,128)(2,1)S(1)}, bf16[1,128,3072]{2,1,0:T(8,128)(2,1)}, u32[]{:S(2)}) copy-start(bf16[1,128,3072]{2,1,0:T(8,128)(2,1)} %param.7) | copy-start | bytes 2359300
  26.7 24.9 %all-to-all-start.1 = ((bf16[16,208,256]{2,1,0:T(8,128)(2,1)}), bf16[16,208,256]{2,1,0:T(8,128)(2,1)S(1)}, u32[]{:S(2)}, u32[]{:S(2)}) async-start(bf16[16,208,256]{2,1,0:T(8,128)(2,1)} %pick.1), calls=%async_computation.1 | async-start | bytes 3407872 | tf_op jit(solution)/shard_map/all_to_all | solution.py:426
  51.6 1.3 copy-start.2
  53.0 36.0 %copy-start.11 = (f32[128,2048]{1,0:T(8,128)}, f32[128,2048]{1,0:T(8,128)S(1)}, u32[]{:S(2)}) copy-start(f32[128,2048]{1,0:T(8,128)S(1)} %get-tuple-element.45.slope) | copy-start | bytes 3145732
  53.0 36.0 %copy-start.13 = (bf16[2048,256]{1,0:T(8,128)(2,1)}, bf16[2048,256]{1,0:T(8,128)(2,1)S(1)}, u32[]{:S(2)}) copy-start(bf16[2048,256]{1,0:T(8,128)(2,1)S(1)} %get-tuple-element.46.kernel) | copy-start | bytes 3145732
  54.0 2.6 %collective-permute-start.4 = (bf16[128,1024]{1,0:T(8,128)(2,1)S(1)}, bf16[128,1024]{1,0:T(8,128)(2,1)S(1)}, u32[]{:S(2)}, u32[]{:S(2)}) collective-permute-start(bf16[128,1024]{1,0:T(8,128)(2,1)S(1)} %get-tuple-element.43), channel_id=1, source_target_pairs={{192,128},{193,129},{194,130},{195,131},{196,132},{197,133},{198,1... | collective-permute-start | bytes 786440 | tf_op jit(solution)/shard_map/ppermute | solution.py:454
  55.9 3.1 %collective-permute-start.3 = (bf16[128,2048]{1,0:T(8,128)(2,1)S(1)}, bf16[128,2048]{1,0:T(8,128)(2,1)S(1)}, u32[]{:S(2)}, u32[]{:S(2)}) collective-permute-start(bf16[128,2048]{1,0:T(8,128)(2,1)S(1)} %get-tuple-element.48), channel_id=1, source_target_pairs={{192,128},{193,129},{194,130},{195,131},{196,132},{197,133},{198,1... | collective-permute-start | bytes 1572872 | tf_op jit(solution)/shard_map/ppermute | solution.py:454
  57.7 16.8 %collective-permute-start.5 = (bf16[128,1024]{1,0:T(8,128)(2,1)S(1)}, bf16[128,1024]{1,0:T(8,128)(2,1)S(1)}, u32[]{:S(2)}, u32[]{:S(2)}) collective-permute-start(bf16[128,1024]{1,0:T(8,128)(2,1)S(1)} %get-tuple-element.51), channel_id=1, source_target_pairs={{128,64},{129,65},{130,66},{131,67},{132,68},{133,69},{134,70},{13... | collective-permute-start | bytes 786440 | tf_op jit(solution)/shard_map/ppermute | solution.py:454
  74.5 14.5 %collective-permute-start.6 = (bf16[128,2048]{1,0:T(8,128)(2,1)S(1)}, bf16[128,2048]{1,0:T(8,128)(2,1)S(1)}, u32[]{:S(2)}, u32[]{:S(2)}) collective-permute-start(bf16[128,2048]{1,0:T(8,128)(2,1)S(1)} %get-tuple-element.53), channel_id=1, source_target_pairs={{128,64},{129,65},{130,66},{131,67},{132,68},{133,69},{134,70},{13... | collective-permute-start | bytes 1572872 | tf_op jit(solution)/shard_map/ppermute | solution.py:454
  76.9 14.7 %collective-permute-start.8 = (bf16[128,1024]{1,0:T(8,128)(2,1)S(1)}, bf16[128,1024]{1,0:T(8,128)(2,1)S(1)}, u32[]{:S(2)}, u32[]{:S(2)}) collective-permute-start(bf16[128,1024]{1,0:T(8,128)(2,1)S(1)} %get-tuple-element.58), channel_id=1, source_target_pairs={{64,0},{65,1},{66,2},{67,3},{68,4},{69,5},{70,6},{71,7},{72,8},{73... | collective-permute-start | bytes 786440 | tf_op jit(solution)/shard_map/ppermute | solution.py:454
  90.2 8.5 %collective-permute-start.7 = (bf16[128,2048]{1,0:T(8,128)(2,1)S(1)}, bf16[128,2048]{1,0:T(8,128)(2,1)S(1)}, u32[]{:S(2)}, u32[]{:S(2)}) collective-permute-start(bf16[128,2048]{1,0:T(8,128)(2,1)S(1)} %get-tuple-element.55), channel_id=1, source_target_pairs={{64,0},{65,1},{66,2},{67,3},{68,4},{69,5},{70,6},{71,7},{72,8},{73... | collective-permute-start | bytes 1572872 | tf_op jit(solution)/shard_map/ppermute | solution.py:454
  91.6 7.2 %copy-start.4 = (bf16[1,128,3072]{2,1,0:T(8,128)(2,1)S(1)}, bf16[1,128,3072]{2,1,0:T(8,128)(2,1)}, u32[]{:S(2)}) copy-start(bf16[1,128,3072]{2,1,0:T(8,128)(2,1)} %param.7) | copy-start | bytes 2359300
  93.8 0.7 copy-start.15
  94.5 0.7 copy-start.17
  95.2 12.5 %all-to-all-start.2 = ((bf16[16,64,256]{2,1,0:T(8,128)(2,1)}), bf16[16,64,256]{2,1,0:T(8,128)(2,1)S(1)}, u32[]{:S(2)}, u32[]{:S(2)}) async-start(bf16[16,64,256]{2,1,0:T(8,128)(2,1)} %get-tuple-element.62), calls=%async_computation.2 | async-start | bytes 1048576 | tf_op jit(solution)/shard_map/all_to_all | solution.py:426
  98.8 1.2 copy-start.12
  100.0 1.2 copy-start.14
  101.2 0.9 copy-start.16
  102.2 0.9 copy-start.18
  105.8 6.7 %copy-start.1 = (s32[16,1,128]{2,1,0:T(1,128)S(1)}, s32[16,1,128]{2,1,0:T(1,128)}, u32[]{:S(2)}) copy-start(s32[16,1,128]{2,1,0:T(1,128)} %copy-done) | copy-start | bytes 24580
  107.7 19.0 %all-to-all-start.3 = ((bf16[16,160,256]{2,1,0:T(8,128)(2,1)}), bf16[16,160,256]{2,1,0:T(8,128)(2,1)S(1)}, u32[]{:S(2)}, u32[]{:S(2)}) async-start(bf16[16,160,256]{2,1,0:T(8,128)(2,1)} %get-tuple-element.64), calls=%async_computation.3 | async-start | bytes 2621440 | tf_op jit(solution)/shard_map/all_to_all | solution.py:426
  126.7 14.9 %copy-start.6 = (bf16[1,4,48,256]{3,2,1,0:T(8,128)(2,1)S(1)}, bf16[1,4,48,256]{3,2,1,0:T(8,128)(2,1)}, u32[]{:S(2)}) copy-start(bf16[1,4,48,256]{3,2,1,0:T(8,128)(2,1)} %param.11) | copy-start | bytes 294916
  126.7 14.9 %copy-start.8 = (bf16[1,48,256]{2,1,0:T(8,128)(2,1)S(1)}, bf16[1,48,256]{2,1,0:T(8,128)(2,1)}, u32[]{:S(2)}) copy-start(bf16[1,48,256]{2,1,0:T(8,128)(2,1)} %param.10) | copy-start | bytes 73732
  127.8 11.0 %collective-permute-start.10 = (bf16[208,256]{1,0:T(8,128)(2,1)S(1)}, bf16[208,256]{1,0:T(8,128)(2,1)S(1)}, u32[]{:S(2)}, u32[]{:S(2)}) collective-permute-start(bf16[208,256]{1,0:T(8,128)(2,1)S(1)} %get-tuple-element.69), channel_id=1, source_target_pairs={{0,8},{4,12},{8,0},{12,4},{1,9},{5,13},{9,1},{13,5},{2,10},{6,14},... | collective-permute-start | bytes 319496 | tf_op jit(solution)/shard_map/ppermute | solution.py:430
  135.5 3.9 %collective-permute-start.11 = (bf16[208,256]{1,0:T(8,128)(2,1)S(1)}, bf16[208,256]{1,0:T(8,128)(2,1)S(1)}, u32[]{:S(2)}, u32[]{:S(2)}) collective-permute-start(bf16[208,256]{1,0:T(8,128)(2,1)S(1)} %get-tuple-element.70), channel_id=1, source_target_pairs={{0,12},{4,0},{8,4},{12,8},{1,13},{5,1},{9,5},{13,9},{2,14},{6,2},{... | collective-permute-start | bytes 319496 | tf_op jit(solution)/shard_map/ppermute | solution.py:430
  136.3 5.4 %collective-permute-start.9 = (bf16[208,256]{1,0:T(8,128)(2,1)S(1)}, bf16[208,256]{1,0:T(8,128)(2,1)S(1)}, u32[]{:S(2)}, u32[]{:S(2)}) collective-permute-start(bf16[208,256]{1,0:T(8,128)(2,1)S(1)} %get-tuple-element.68), channel_id=1, source_target_pairs={{0,4},{4,8},{8,12},{12,0},{1,5},{5,9},{9,13},{13,1},{2,6},{6,10},{... | collective-permute-start | bytes 319496 | tf_op jit(solution)/shard_map/ppermute | solution.py:430

commit v5 on v1

v5 whole, which is shorter than its diff:
```python
import jax
import jax.numpy as jnp
from jax import lax
from jax.experimental import pallas as pl
from jax.experimental.pallas import tpu as pltpu
from jax.sharding import Mesh, PartitionSpec as P

D = 3072
GS = 256
DOMAINS = 4
ROWS = 128
NY, NZ, NX = 4, 4, 4
SHARD = 48
SLAB = D // NY
SG = SLAB // GS
WIDE = D // 2
SLABS = NY // 2
PIECE = NZ * SHARD
TILE = 16
BLOCK = PIECE + TILE
VMEM = pl.BlockSpec(memory_space=pltpu.VMEM)
SMEM = pl.BlockSpec(memory_space=pltpu.SMEM)
BF = jnp.bfloat16
F32 = jnp.float32
HEAVY = 10**11


def call(kernel, name, limit=48, weight=HEAVY, **rest):
    return pl.pallas_call(
        kernel,
        name=name,
        compiler_params=pltpu.CompilerParams(vmem_limit_bytes=limit * 1024 * 1024),
        cost_estimate=pl.CostEstimate(
            flops=weight, bytes_accessed=weight // 100, transcendentals=0
        ),
        **rest,
    )


def prep_kernel(at, sw, dw, sb, db, out, wide, tile):
    shared = sw[...].astype(F32)
    for k in range(DOMAINS):
        out[k * SHARD : (k + 1) * SHARD, :] = (shared * dw[k].astype(F32)).astype(BF)
    wide[...] = jnp.zeros_like(wide)
    wide[0:1, :SHARD] = sb[...].astype(F32)
    wide[1 : 1 + DOMAINS, :SHARD] = db[...].astype(F32)
    placed = pltpu.roll(wide[...], at[0], 1)
    tile[...] = jnp.zeros_like(tile)
    for k in range(1 + DOMAINS):
        for q in range(SG):
            row = k * SG + q
            tile[row : row + 1, :] = placed[k : k + 1, q * GS : (q + 1) * GS]
    out[PIECE:, :] = tile[...].astype(BF)


def prep(at, sw, dw, sb, db):
    return call(
        prep_kernel,
        "prep",
        limit=58,
        out_shape=jax.ShapeDtypeStruct((BLOCK, GS), BF),
        in_specs=[SMEM, VMEM, VMEM, VMEM, VMEM],
        out_specs=VMEM,
        scratch_shapes=[pltpu.VMEM((8, SLAB), F32), pltpu.VMEM((TILE, GS), F32)],
    )(at, sw, dw, sb, db)


def pick_kernel(ids, z, *refs):
    held, out = refs[:NZ], refs[NZ]
    step = pl.program_id(0)
    tile = held[0][PIECE:, :].astype(F32)
    for k in range(1, NZ):
        tile = tile + held[k][PIECE:, :].astype(F32)
    tile = tile.astype(BF)
    for i in range(NX):
        start = pl.multiple_of(ids[step * NX + i, 0] * SHARD, TILE)
        for k in range(NZ):
            to = pl.multiple_of(((z[0] + NZ - k) % NZ) * SHARD, TILE)
            out[i, pl.ds(to, SHARD), :] = held[k][pl.ds(start, SHARD), :]
        out[i, PIECE:, :] = tile


def pick(ids, z, held):
    return call(
        pick_kernel,
        "pick",
        grid=(NY,),
        out_shape=jax.ShapeDtypeStruct((NY * NX, BLOCK, GS), BF),
        in_specs=[SMEM, SMEM] + [pl.BlockSpec((BLOCK, GS), lambda i: (0, 0))] * NZ,
        out_specs=pl.BlockSpec((NX, BLOCK, GS), lambda i: (i, 0, 0)),
    )(ids, z, *held)


def gather_kernel(core, own, other, cotangent, x, up):
    even = core[0] == 0
    x[0] = jnp.where(even, own[:, :WIDE], other[...])
    x[1] = jnp.where(even, other[...], own[:, WIDE:])
    up[...] = jnp.where(even, cotangent[:, :WIDE], cotangent[:, WIDE:])


def gather(core, own, other, cotangent):
    return call(
        gather_kernel,
        "gather",
        out_shape=(
            jax.ShapeDtypeStruct((2, ROWS, WIDE), BF),
            jax.ShapeDtypeStruct((ROWS, WIDE), BF),
        ),
        in_specs=[SMEM, VMEM, VMEM, VMEM],
        out_specs=(VMEM, VMEM),
    )(core, own, other, cotangent)


def slope_kernel(own, got, x, slope, kernel, offsets):
    domain = own[0]
    tile = got[0, PIECE:, :].astype(F32)
    for i in range(1, NX):
        tile = tile + got[i, PIECE:, :].astype(F32)
    offsets[...] = tile
    for z in range(NZ):
        for i in range(NX):
            at = (z * NX + i) * SHARD
            kernel[0, at : at + SHARD, :] = got[i, z * SHARD : (z + 1) * SHARD, :]
    for q in range(SG):
        lanes = slice(q * GS, (q + 1) * GS)
        offset = offsets[q : q + 1, :] + offsets[pl.ds((1 + domain) * SG + q, 1), :]
        pre = jnp.dot(x[0, :, lanes], kernel[0, lanes, :], preferred_element_type=F32) + offset
        sigma = jax.nn.sigmoid(pre)
        slope[0, :, lanes] = sigma * (1.0 + pre * (1.0 - sigma))


def slopes(own, got, x):
    return call(
        slope_kernel,
        "slopes",
        grid=(2, SLABS),
        out_shape=(
            jax.ShapeDtypeStruct((2, ROWS, WIDE), F32),
            jax.ShapeDtypeStruct((2, WIDE, GS), BF),
        ),
        in_specs=[
            SMEM,
            pl.BlockSpec((NX, BLOCK, GS), lambda p, h: (SLABS * p + h, 0, 0)),
            pl.BlockSpec((1, ROWS, SLAB), lambda p, h: (p, 0, h)),
        ],
        out_specs=(
            pl.BlockSpec((1, ROWS, SLAB), lambda p, h: (p, 0, h)),
            pl.BlockSpec((1, SLAB, GS), lambda p, h: (p, h, 0)),
        ),
        scratch_shapes=[pltpu.VMEM((TILE, GS), F32)],
    )(own, got, x)


def layer(above, slope, kernel):
    signal = (above * slope).astype(BF)
    back = lax.dot_general(signal, kernel, (((1,), (1,)), ((), ())), preferred_element_type=F32)
    return signal, (above + back).astype(BF)


COLUMNS = pl.BlockSpec((ROWS, SLAB), lambda h: (0, h))
BOTH_COLUMNS = pl.BlockSpec((2, ROWS, SLAB), lambda h: (0, 0, h))
BOTH_ROWS = pl.BlockSpec((2, SLAB, GS), lambda h: (0, h, 0))


def pair_kernel(up, slope, kernel, out):
    for q in range(SG):
        lanes = slice(q * GS, (q + 1) * GS)
        above = up[:, lanes].astype(F32)
        _, middle = layer(above, slope[1, :, lanes], kernel[1, lanes, :])
        _, out[:, lanes] = layer(middle.astype(F32), slope[0, :, lanes], kernel[0, lanes, :])


def pair(up, slope, kernel):
    return call(
        pair_kernel,
        "pair",
        grid=(SLABS,),
        out_shape=jax.ShapeDtypeStruct((ROWS, WIDE), BF),
        in_specs=[COLUMNS, BOTH_COLUMNS, BOTH_ROWS],
        out_specs=COLUMNS,
    )(up, slope, kernel)


def grads_kernel(place, top, hop, slope, kernel, x, keep, give, send, tile):
    even = place[0] == 0
    last = place[1] == 1
    for q in range(SG):
        lanes = slice(q * GS, (q + 1) * GS)
        above = jnp.where(last, top[:, lanes], hop[:, lanes]).astype(F32)
        outs = [None, None]
        for p in (1, 0):
            signal, outs[p] = layer(above, slope[p, :, lanes], kernel[p, lanes, :])
            above = outs[p].astype(F32)
            grad = lax.dot_general(
                x[p, :, lanes], signal, (((0,), (0,)), ((), ())), preferred_element_type=F32
            ).astype(BF)
            for row in range(q * GS, (q + 1) * GS, TILE):
                shard, inner = row // SHARD, row % SHARD
                at = shard // NX * SHARD + inner
                send[p, 0, shard % NX, at : at + TILE, :] = grad[row - q * GS : row - q * GS + TILE]
            total = jnp.sum(signal.astype(F32), axis=0, keepdims=True)
            high = total.astype(BF).astype(F32)
            tile[p, q : q + 1, :] = high
            tile[p, SG + q : SG + q + 1, :] = total - high
        keep[:, lanes] = jnp.where(even, outs[0], outs[1])
        give[:, lanes] = jnp.where(even, outs[1], outs[0])
    tile[:, 2 * SG :, :] = jnp.zeros((2, TILE - 2 * SG, GS), F32)
    for p in range(2):
        for i in range(NX):
            send[p, 0, i, PIECE:, :] = tile[p].astype(BF)


def grads(place, top, hop, slope, kernel, x):
    half = jax.ShapeDtypeStruct((ROWS, WIDE), BF)
    return call(
        grads_kernel,
        "grads",
        grid=(SLABS,),
        out_shape=(half, half, jax.ShapeDtypeStruct((2, SLABS, NX, BLOCK, GS), BF)),
        in_specs=[SMEM, COLUMNS, COLUMNS, BOTH_COLUMNS, BOTH_ROWS, BOTH_COLUMNS],
        out_specs=(
            COLUMNS,
            COLUMNS,
            pl.BlockSpec((2, 1, NX, BLOCK, GS), lambda h: (0, h, 0, 0, 0)),
        ),
        scratch_shapes=[pltpu.VMEM((2, TILE, GS), F32)],
    )(place, top, hop, slope, kernel, x)


def join_kernel(core, keep, other, out):
    even = core[0] == 0
    out[:, :WIDE] = jnp.where(even, keep[...], other[...])
    out[:, WIDE:] = jnp.where(even, other[...], keep[...])


def join(core, keep, other):
    return call(
        join_kernel,
        "join",
        out_shape=jax.ShapeDtypeStruct((ROWS, D), BF),
        in_specs=[SMEM, VMEM, VMEM],
        out_specs=VMEM,
    )(core, keep, other)


def merge_kernel(ids, z, got, *refs):
    outs, (total, parts, tile) = refs[:NZ], refs[NZ:]
    step = pl.program_id(0)

    @pl.when(step == 0)
    def _():
        total[...] = jnp.zeros_like(total)

    for i in range(NX):
        domain = ids[step * NX + i, 0]
        total[domain] += got[i].astype(F32)

    @pl.when(step == NY - 1)
    def _():
        tile[...] = jnp.zeros_like(tile)
        for k in range(DOMAINS):
            for to in range(NZ):
                parts[to, k * SHARD : (k + 1) * SHARD, :] = total[
                    k, to * SHARD : (to + 1) * SHARD, :
                ].astype(BF)
            tile[k * SG : (k + 1) * SG, :] = (
                total[k, PIECE : PIECE + SG, :] + total[k, PIECE + SG : PIECE + 2 * SG, :]
            )
        for k in range(NZ):
            outs[k][:PIECE, :] = parts[(z[0] + k) % NZ]
            outs[k][PIECE:, :] = tile[...].astype(BF)


def merge(ids, z, got):
    return call(
        merge_kernel,
        "merge",
        grid=(NY,),
        out_shape=(jax.ShapeDtypeStruct((BLOCK, GS), BF),) * NZ,
        in_specs=[SMEM, SMEM, pl.BlockSpec((NX, BLOCK, GS), lambda i: (i, 0, 0))],
        out_specs=(pl.BlockSpec((BLOCK, GS), lambda i: (0, 0)),) * NZ,
        scratch_shapes=[
            pltpu.VMEM((DOMAINS, BLOCK, GS), F32),
            pltpu.VMEM((NZ, PIECE, GS), BF),
            pltpu.VMEM((TILE, GS), F32),
        ],
    )(ids, z, got)


def finish_kernel(at, *refs):
    got, (sw, dw, d_shared, d_domain, b_shared, b_domain, wide) = refs[:NZ], refs[NZ:]
    shared = sw[...].astype(F32)
    summed = jnp.zeros((SHARD, GS), F32)
    for k in range(DOMAINS):
        part = slice(k * SHARD, (k + 1) * SHARD)
        share = got[0][part, :].astype(F32)
        for z in range(1, NZ):
            share = share + got[z][part, :].astype(F32)
        summed = summed + share * dw[k].astype(F32)
        d_domain[k] = share * shared
    d_shared[...] = summed
    tile = got[0][PIECE:, :].astype(F32)
    for z in range(1, NZ):
        tile = tile + got[z][PIECE:, :].astype(F32)
    wide[...] = jnp.zeros_like(wide)
    for k in range(DOMAINS):
        for q in range(SG):
            row = k * SG + q
            wide[k : k + 1, q * GS : (q + 1) * GS] = tile[row : row + 1, :]
    placed = pltpu.roll(wide[...], SLAB - at[0], 1)
    b_domain[...] = placed[:DOMAINS, :SHARD]
    b_shared[...] = jnp.sum(placed[:DOMAINS, :SHARD], axis=0, keepdims=True)


def finish(at, got, sw, dw):
    return call(
        finish_kernel,
        "finish",
        out_shape=(
            jax.ShapeDtypeStruct((SHARD, GS), F32),
            jax.ShapeDtypeStruct((DOMAINS, SHARD, GS), F32),
            jax.ShapeDtypeStruct((1, SHARD), F32),
            jax.ShapeDtypeStruct((DOMAINS, SHARD), F32),
        ),
        in_specs=[SMEM] + [VMEM] * (NZ + 2),
        out_specs=(VMEM,) * 4,
        scratch_shapes=[pltpu.VMEM((8, SLAB), F32)],
    )(at, *got, sw, dw)


def exchange(block, axes):
    return lax.all_to_all(block, axes, 0, 0, tiled=True)


def turned(block, k):
    pairs = []
    for core in range(2):
        for y in range(NY):
            for z in range(NZ):
                to = (y // SLABS * NY + core * SLABS + y % SLABS) * NZ + (z + k) % NZ
                pairs.append(((core * NY + y) * NZ + z, to))
    return lax.ppermute(block, ("core", "y", "zlo"), pairs)


def swapped(block):
    return lax.ppermute(block, "core", [(0, 1), (1, 0)])


def after(first, *then):
    return lax.optimization_barrier((first, *then))[1:]


def body(stash, cotangent, domain_ids, shared_weight, domain_weight, shared_bias, domain_bias):
    own = stash[0]
    sw, dw = shared_weight[0], domain_weight[0]
    core = lax.axis_index("core")
    place = jnp.stack([core, lax.axis_index("zhi")])
    z = jnp.reshape(lax.axis_index("zlo"), (1,))
    at = PIECE * z + SHARD * lax.axis_index("x")

    mine = prep(at, sw, dw, shared_bias, domain_bias[0])
    held = [turned(mine, k) for k in range(NZ)]
    (ids,) = after(mine, domain_ids)
    plane_ids = exchange(
        jnp.broadcast_to(ids[0], (NY * NX, 1, 128)), ("y", "x")
    ).reshape(NY * NX, 128)
    (own,) = after(plane_ids, own)
    other = swapped(lax.dynamic_slice(own, (0, (1 - core) * WIDE), (ROWS, WIDE)))
    got = exchange(pick(plane_ids, z, held), ("y", "x"))
    x, top = gather(place, own, other, cotangent)

    slope, kernel = slopes(domain_ids, got, x)
    out = pair(top, slope, kernel)
    hop = lax.ppermute(out, "zhi", [(1, 0)])
    keep, give, send = grads(place, top, hop, slope, kernel, x)
    got = exchange(send.reshape(NY * NX, BLOCK, GS), ("y", "x"))
    d_inputs = join(place, keep, swapped(give))
    merged = merge(plane_ids, z, got)
    final = [turned(merged[k], k) for k in range(NZ)]
    d_shared, d_domain, b_shared, b_domain = finish(at, final, sw, dw)
    return (d_inputs[None], d_shared[None], d_domain[None], b_shared, b_domain[None])


def solution(mesh):
    fine = Mesh(mesh.devices.reshape(2, 2, NY, NZ, NX), ("zhi", "core", "y", "zlo", "x"))
    section, dp = ("zhi", "core"), ("y", "zlo", "x")
    in_specs = (
        P(section, dp, None),
        P(dp, None),
        P(dp),
        P(section, dp, None),
        P(section, None, dp, None),
        P(section, dp),
        P(section, None, dp),
    )
    out_specs = (
        P(section, dp, None),
        P(section, dp, None),
        P(section, None, dp, None),
        P(section, dp),
        P(section, None, dp),
    )
    return jax.shard_map(
        body, mesh=fine, in_specs=in_specs, out_specs=out_specs, check_vma=False
    )
```

time: 160 us -> 147 us (0.919)
  blocking collectives: 92.4 us -> 0 us
  starting transfers between devices: 10.9 us -> 56.8 us
  waiting for transfers between devices: 26.9 us -> 69.1 us
  Pallas kernels: 18.6 us -> 14.7 us
  local copies, waits for them, and re-layouts: 6.67 us -> 4.17 us
  other arithmetic: 1.86 us -> 0.08 us
    all_to_all x4 -> x0, blocking collectives: 92.4 us -> none  [exchange(): return lax.all_to_all(block, axes, 0, 0, tiled=True)]
    all_to_all x1 -> x3, waiting for transfers between devices: 3.16 us -> 52.2 us  [exchange(): return lax.all_to_all(block, axes, 0, 0, tiled=True)]
    ppermute x3 -> x11, starting transfers between devices: 3.33 us -> 44.7 us  [the longest x8 37.8 us: turned(): return lax.ppermute(block, ('core', 'y', 'zlo'), pairs)]
    ppermute x3 -> x11, waiting for transfers between devices: 23.7 us -> 16.9 us  [the longest x1 14.4 us: body(): hop = lax.ppermute(out, 'zhi', [(1, 0)])]
    all_to_all x1 -> x3, starting transfers between devices: 7.58 us -> 12.1 us  [exchange(): return lax.all_to_all(block, axes, 0, 0, tiled=True)]
    pallas_call x9, Pallas kernels: 18.6 us -> 14.7 us  [the longest x1 3.26 us: grads(): call(grads_kernel, 'grads', grid=(SLABS,), out_shape=(half, half, jax.Sha...]
    unnamed x22, local copies, waits for them, and re-layouts: 4.56 us -> 2.8 us
  transfers between devices with their start and end apart: 4 -> 14, of which waited for: 3 -> 6; matrix products, arithmetic and copies ran while one was open for 1% -> 1% of each run, Pallas kernels for 1% -> 4%
where the time goes in v5:
time: 147 us; the launch traced here: 146 us
  waiting for transfers between devices  69.1 us (47%)
  starting transfers between devices  56.8 us (39%)
  Pallas kernels  14.7 us (10%)
  local copies, waits for them, and re-layouts  4.17 us (3%)
    all_to_all x3, waiting for transfers between devices, exchange(): return lax.all_to_all(block, axes, 0, 0, tiled=True)  52.2 us
    ppermute x8, starting transfers between devices, turned(): return lax.ppermute(block, ('core', 'y', 'zlo'), pairs)  37.8 us
    ppermute x1, waiting for transfers between devices, body(): hop = lax.ppermute(out, 'zhi', [(1, 0)])  14.4 us
    all_to_all x3, starting transfers between devices, exchange(): return lax.all_to_all(block, axes, 0, 0, tiled=True)  12.1 us
    ppermute x2, starting transfers between devices, swapped(): return lax.ppermute(block, 'core', [(0, 1), (1, 0)])  5.59 us
    pallas_call x1, Pallas kernels, grads(): call(grads_kernel, 'grads', grid=(SLABS,), out_shape=(half, half, jax.Sha...  3.26 us
  transfers between devices with their start and end apart: 14, of which 6 were waited for; matrix products, arithmetic and copies ran while one was open for 1% of the time, Pallas kernels for 4%

profile of v5, /device:TPU:1, one launch (start us, length us, event | category | flops | bytes accessed | tf_op | source)
XLA Modules:
  0.0 146.3 jit_solution(5973261608817312809)
XLA Ops:
  0.7 1.7 %prep.1 = bf16[208,256]{1,0:T(8,128)(2,1)} custom-call(s32[1]{0:T(128)S(6)} %add.10.at, bf16[48,256]{1,0:T(8,128)(2,1)} %bitcast.22, bf16[4,48,256]{2,1,0:T(8,128)(2,1)} %bitcast.20, bf16[1,48]{1,0:T(2,128)(2,1)} %sb.1, bf16[4,48]{1,0:T(4,128)(2,1)} %bitcast.25), custom_call_target="tpu_custom_call" | custom-call | flops 99999997952 | bytes 1000000000 | tf_op jit(solution)/shard_map/prep/pallas_call | solution.py:57
  2.4 8.4 %collective-permute-start.4 = (bf16[208,256]{1,0:T(8,128)(2,1)}, bf16[208,256]{1,0:T(8,128)(2,1)S(1)}, u32[]{:S(2)}, u32[]{:S(2)}) collective-permute-start(bf16[208,256]{1,0:T(8,128)(2,1)} %prep.1), channel_id=1, source_target_pairs={{0,12},{4,0},{8,4},{12,8},{16,28},{20,16},{24,20},{28,24},{32,76},... | collective-permute-start | bytes 319496 | tf_op jit(solution)/shard_map/ppermute | solution.py:342
  10.7 0.0 collective-permute-start.3
  10.7 2.8 %collective-permute-start.2 = (bf16[208,256]{1,0:T(8,128)(2,1)}, bf16[208,256]{1,0:T(8,128)(2,1)S(1)}, u32[]{:S(2)}, u32[]{:S(2)}) collective-permute-start(bf16[208,256]{1,0:T(8,128)(2,1)} %prep.1), channel_id=1, source_target_pairs={{0,4},{4,8},{8,12},{12,0},{16,20},{20,24},{24,28},{28,16},{32,68},... | collective-permute-start | bytes 319496 | tf_op jit(solution)/shard_map/ppermute | solution.py:342
  13.5 2.4 %collective-permute-start.1 = (bf16[208,256]{1,0:T(8,128)(2,1)}, bf16[208,256]{1,0:T(8,128)(2,1)S(1)}, u32[]{:S(2)}, u32[]{:S(2)}) collective-permute-start(bf16[208,256]{1,0:T(8,128)(2,1)} %prep.1), channel_id=1, source_target_pairs={{0,0},{4,4},{8,8},{12,12},{16,16},{20,20},{24,24},{28,28},{32,64},... | collective-permute-start | bytes 319496 | tf_op jit(solution)/shard_map/ppermute | solution.py:342
  16.5 0.6 broadcast_in_dim.15
  17.1 4.5 %all-to-all-start = ((s32[16,1,128]{2,1,0:T(1,128)}), s32[16,1,128]{2,1,0:T(1,128)S(1)}, u32[]{:S(2)}, u32[]{:S(2)}) async-start(s32[16,1,128]{2,1,0:T(1,128)} %broadcast_in_dim.15), calls=%async_computation | async-start | bytes 16384 | tf_op jit(solution)/shard_map/all_to_all | solution.py:332
  21.6 0.1 pad_add_fusion.core.place
  21.7 6.2 %all-to-all-done = s32[16,1,128]{2,1,0:T(1,128)S(1)} async-done(((s32[16,1,128]{2,1,0:T(1,128)}), s32[16,1,128]{2,1,0:T(1,128)S(1)}, u32[]{:S(2)}, u32[]{:S(2)}) %all-to-all-start) | async-done | bytes 8224 | tf_op jit(solution)/shard_map/all_to_all | solution.py:332
  27.9 0.8 constant_dynamic-slice_fusion
  28.7 3.7 %collective-permute-start = (bf16[128,1536]{1,0:T(8,128)(2,1)}, bf16[128,1536]{1,0:T(8,128)(2,1)}, u32[]{:S(2)}, u32[]{:S(2)}) collective-permute-start(bf16[128,1536]{1,0:T(8,128)(2,1)} %constant_dynamic-slice_fusion), channel_id=1, source_target_pairs={{0,64},{64,0},{1,65},{65,1},{2,66},{66,2},{3,67},{67,3},{4,68},{68... | collective-permute-start | bytes 1179656 | tf_op jit(solution)/shard_map/ppermute | solution.py:346
  32.4 0.0 collective-permute-done.4.refs_3_
  32.4 0.0 collective-permute-done.3.refs_2_
  32.4 0.0 collective-permute-done.2.refs_1_
  32.4 0.0 collective-permute-done.1.refs_0_
  32.5 2.5 %pick.1 = bf16[16,208,256]{2,1,0:T(8,128)(2,1)} custom-call(s32[16,128]{1,0:T(8,128)S(1)} %bitcast.18, s32[1]{0:T(128)} %bitcast.2.z, bf16[208,256]{1,0:T(8,128)(2,1)S(1)} %collective-permute-done.1.refs_0_, bf16[208,256]{1,0:T(8,128)(2,1)S(1)} %collective-permute-done.2.refs_1_, bf16[208,256]{1,0:T(8,128)(2,1)S(1)} %collective-permute-done.3.refs_2_, ...), custom_call_target="tpu_custom_call" | custom-call | flops 99999997952 | bytes 1000000000 | tf_op jit(solution)/shard_map/pick/pallas_call | solution.py:84
  35.0 3.8 %all-to-all-start.1 = ((bf16[16,208,256]{2,1,0:T(8,128)(2,1)}), bf16[16,208,256]{2,1,0:T(8,128)(2,1)S(1)}, u32[]{:S(2)}, u32[]{:S(2)}) async-start(bf16[16,208,256]{2,1,0:T(8,128)(2,1)} %pick.1), calls=%async_computation.1 | async-start | bytes 3407872 | tf_op jit(solution)/shard_map/all_to_all | solution.py:332
  38.8 0.0 collective-permute-done.other
  38.8 0.0 copy-done.3
  38.8 1.1 gather.1
  40.0 0.0 copy-start.6
  40.0 0.9 copy-done.6
  40.9 0.8 copy-done.9
  41.6 25.7 %all-to-all-done.1.got = bf16[16,208,256]{2,1,0:T(8,128)(2,1)S(1)} async-done(((bf16[16,208,256]{2,1,0:T(8,128)(2,1)}), bf16[16,208,256]{2,1,0:T(8,128)(2,1)S(1)}, u32[]{:S(2)}, u32[]{:S(2)}) %all-to-all-start.1) | async-done | bytes 1703968 | tf_op jit(solution)/shard_map/all_to_all | solution.py:332
  67.3 1.1 copy-done.7
  68.4 1.3 slopes.1
  69.8 0.0 copy-done.10
  69.8 0.0 copy-start.8
  69.8 1.3 pair.1
  71.1 1.3 collective-permute-start.5
  72.4 14.4 %collective-permute-done.5.hop = bf16[128,1536]{1,0:T(8,128)(2,1)S(1)} collective-permute-done((bf16[128,1536]{1,0:T(8,128)(2,1)S(1)}, bf16[128,1536]{1,0:T(8,128)(2,1)S(1)}, u32[]{:S(2)}, u32[]{:S(2)}) %collective-permute-start.5) | collective-permute-done | bytes 393248 | tf_op jit(solution)/shard_map/ppermute | solution.py:374
  86.7 3.3 %grads.1 = (bf16[128,1536]{1,0:T(8,128)(2,1)S(1)}, bf16[128,1536]{1,0:T(8,128)(2,1)S(1)}, bf16[2,2,4,208,256]{4,3,2,1,0:T(8,128)(2,1)}) custom-call(s32[2]{0:T(128)S(1)} %pad_add_fusion.core.place, bf16[128,1536]{1,0:T(8,128)(2,1)S(1)} %copy-done.10, bf16[128,1536]{1,0:T(8,128)(2,1)S(1)} %collective-permute-done.5.hop, ...), custom_call_target="tpu_custom_call" | custom-call | flops 99999997952 | bytes 1000000000 | tf_op jit(solution)/shard_map/grads/pallas_call | solution.py:215
  90.0 3.8 %all-to-all-start.2 = ((bf16[16,208,256]{2,1,0:T(8,128)(2,1)}), bf16[16,208,256]{2,1,0:T(8,128)(2,1)S(1)}, u32[]{:S(2)}, u32[]{:S(2)}) async-start(bf16[16,208,256]{2,1,0:T(8,128)(2,1)} %bitcast.24), calls=%async_computation.2 | async-start | bytes 3407872 | tf_op jit(solution)/shard_map/all_to_all | solution.py:332
  93.8 1.9 %collective-permute-start.6 = (bf16[128,1536]{1,0:T(8,128)(2,1)S(1)}, bf16[128,1536]{1,0:T(8,128)(2,1)S(1)}, u32[]{:S(2)}, u32[]{:S(2)}) collective-permute-start(bf16[128,1536]{1,0:T(8,128)(2,1)S(1)} %get-tuple-element.29), channel_id=1, source_target_pairs={{0,64},{64,0},{1,65},{65,1},{2,66},{66,2},{3,67},{67,3},{4,68},{68... | collective-permute-start | bytes 1179656 | tf_op jit(solution)/shard_map/ppermute | solution.py:346
  95.7 20.3 %all-to-all-done.2.got = bf16[16,208,256]{2,1,0:T(8,128)(2,1)S(1)} async-done(((bf16[16,208,256]{2,1,0:T(8,128)(2,1)}), bf16[16,208,256]{2,1,0:T(8,128)(2,1)S(1)}, u32[]{:S(2)}, u32[]{:S(2)}) %all-to-all-start.2) | async-done | bytes 1703968 | tf_op jit(solution)/shard_map/all_to_all | solution.py:332
  116.0 1.2 merge.1
  117.2 6.8 %collective-permute-start.7 = (bf16[208,256]{1,0:T(8,128)(2,1)S(1)}, bf16[208,256]{1,0:T(8,128)(2,1)S(1)}, u32[]{:S(2)}, u32[]{:S(2)}) collective-permute-start(bf16[208,256]{1,0:T(8,128)(2,1)S(1)} %get-tuple-element.31), channel_id=1, source_target_pairs={{0,0},{4,4},{8,8},{12,12},{16,16},{20,20},{24,24},{28,28},{32,64},... | collective-permute-start | bytes 319496 | tf_op jit(solution)/shard_map/ppermute | solution.py:342
  124.0 13.8 %collective-permute-start.8 = (bf16[208,256]{1,0:T(8,128)(2,1)S(1)}, bf16[208,256]{1,0:T(8,128)(2,1)S(1)}, u32[]{:S(2)}, u32[]{:S(2)}) collective-permute-start(bf16[208,256]{1,0:T(8,128)(2,1)S(1)} %get-tuple-element.32), channel_id=1, source_target_pairs={{0,4},{4,8},{8,12},{12,0},{16,20},{20,24},{24,28},{28,16},{32,68},... | collective-permute-start | bytes 319496 | tf_op jit(solution)/shard_map/ppermute | solution.py:342
  137.8 0.0 collective-permute-start.9
  137.8 3.6 %collective-permute-start.10 = (bf16[208,256]{1,0:T(8,128)(2,1)S(1)}, bf16[208,256]{1,0:T(8,128)(2,1)S(1)}, u32[]{:S(2)}, u32[]{:S(2)}) collective-permute-start(bf16[208,256]{1,0:T(8,128)(2,1)S(1)} %get-tuple-element.34), channel_id=1, source_target_pairs={{0,12},{4,0},{8,4},{12,8},{16,28},{20,16},{24,20},{28,24},{32,76},... | collective-permute-start | bytes 319496 | tf_op jit(solution)/shard_map/ppermute | solution.py:342
  141.5 0.0 collective-permute-done.6.other
  141.5 1.5 %join.1 = bf16[128,3072]{1,0:T(8,128)(2,1)} custom-call(s32[2]{0:T(128)S(1)} %pad_add_fusion.core.place, bf16[128,1536]{1,0:T(8,128)(2,1)S(1)} %get-tuple-element.28.keep, bf16[128,1536]{1,0:T(8,128)(2,1)S(1)} %collective-permute-done.6.other), custom_call_target="tpu_custom_call" | custom-call | flops 99999997952 | bytes 1000000000 | tf_op jit(solution)/shard_map/join/pallas_call | solution.py:237
  143.0 0.0 collective-permute-done.7.refs_0_
  143.0 0.0 collective-permute-done.8.refs_1_
  143.0 2.4 %collective-permute-done.9.refs_2_ = bf16[208,256]{1,0:T(8,128)(2,1)S(1)} collective-permute-done((bf16[208,256]{1,0:T(8,128)(2,1)S(1)}, bf16[208,256]{1,0:T(8,128)(2,1)S(1)}, u32[]{:S(2)}, u32[]{:S(2)}) %collective-permute-start.9) | collective-permute-done | bytes 106528 | tf_op jit(solution)/shard_map/ppermute | solution.py:342
  145.4 0.1 collective-permute-done.10.refs_3_
  145.5 0.0 copy-done.5
  145.5 0.8 finish.1
  (14 shorter events, 0.0 us)
Async XLA Ops:
  0.6 27.3 %copy-start = (bf16[1,128,3072]{2,1,0:T(8,128)(2,1)S(1)}, bf16[1,128,3072]{2,1,0:T(8,128)(2,1)}, u32[]{:S(2)}) copy-start(bf16[1,128,3072]{2,1,0:T(8,128)(2,1)} %param.7) | copy-start | bytes 2359300
  2.4 30.1 %collective-permute-start.4 = (bf16[208,256]{1,0:T(8,128)(2,1)}, bf16[208,256]{1,0:T(8,128)(2,1)S(1)}, u32[]{:S(2)}, u32[]{:S(2)}) collective-permute-start(bf16[208,256]{1,0:T(8,128)(2,1)} %prep.1), channel_id=1, source_target_pairs={{0,12},{4,0},{8,4},{12,8},{16,28},{20,16},{24,20},{28,24},{32,76},... | collective-permute-start | bytes 319496 | tf_op jit(solution)/shard_map/ppermute | solution.py:342
  10.7 21.7 %collective-permute-start.3 = (bf16[208,256]{1,0:T(8,128)(2,1)}, bf16[208,256]{1,0:T(8,128)(2,1)S(1)}, u32[]{:S(2)}, u32[]{:S(2)}) collective-permute-start(bf16[208,256]{1,0:T(8,128)(2,1)} %prep.1), channel_id=1, source_target_pairs={{0,8},{4,12},{8,0},{12,4},{16,24},{20,28},{24,16},{28,20},{32,72},... | collective-permute-start | bytes 319496 | tf_op jit(solution)/shard_map/ppermute | solution.py:342
  10.7 21.7 %collective-permute-start.2 = (bf16[208,256]{1,0:T(8,128)(2,1)}, bf16[208,256]{1,0:T(8,128)(2,1)S(1)}, u32[]{:S(2)}, u32[]{:S(2)}) collective-permute-start(bf16[208,256]{1,0:T(8,128)(2,1)} %prep.1), channel_id=1, source_target_pairs={{0,4},{4,8},{8,12},{12,0},{16,20},{20,24},{24,28},{28,16},{32,68},... | collective-permute-start | bytes 319496 | tf_op jit(solution)/shard_map/ppermute | solution.py:342
  13.5 18.9 %collective-permute-start.1 = (bf16[208,256]{1,0:T(8,128)(2,1)}, bf16[208,256]{1,0:T(8,128)(2,1)S(1)}, u32[]{:S(2)}, u32[]{:S(2)}) collective-permute-start(bf16[208,256]{1,0:T(8,128)(2,1)} %prep.1), channel_id=1, source_target_pairs={{0,0},{4,4},{8,8},{12,12},{16,16},{20,20},{24,24},{28,28},{32,64},... | collective-permute-start | bytes 319496 | tf_op jit(solution)/shard_map/ppermute | solution.py:342
  17.1 10.8 %all-to-all-start = ((s32[16,1,128]{2,1,0:T(1,128)}), s32[16,1,128]{2,1,0:T(1,128)S(1)}, u32[]{:S(2)}, u32[]{:S(2)}) async-start(s32[16,1,128]{2,1,0:T(1,128)} %broadcast_in_dim.15), calls=%async_computation | async-start | bytes 16384 | tf_op jit(solution)/shard_map/all_to_all | solution.py:332
  27.9 7.0 %copy-start.1 = (s32[16,1,128]{2,1,0:T(1,128)}, s32[16,1,128]{2,1,0:T(1,128)S(1)}, u32[]{:S(2)}) copy-start(s32[16,1,128]{2,1,0:T(1,128)S(1)} %all-to-all-done) | copy-start | bytes 24580
  28.7 10.1 %collective-permute-start = (bf16[128,1536]{1,0:T(8,128)(2,1)}, bf16[128,1536]{1,0:T(8,128)(2,1)}, u32[]{:S(2)}, u32[]{:S(2)}) collective-permute-start(bf16[128,1536]{1,0:T(8,128)(2,1)} %constant_dynamic-slice_fusion), channel_id=1, source_target_pairs={{0,64},{64,0},{1,65},{65,1},{2,66},{66,2},{3,67},{67,3},{4,68},{68... | collective-permute-start | bytes 1179656 | tf_op jit(solution)/shard_map/ppermute | solution.py:346
  35.0 3.9 %copy-start.3 = (bf16[128,3072]{1,0:T(8,128)(2,1)S(1)}, bf16[128,3072]{1,0:T(8,128)(2,1)}, u32[]{:S(2)}) copy-start(bf16[128,3072]{1,0:T(8,128)(2,1)} %cotangent.1) | copy-start | bytes 2359300
  35.0 32.3 %all-to-all-start.1 = ((bf16[16,208,256]{2,1,0:T(8,128)(2,1)}), bf16[16,208,256]{2,1,0:T(8,128)(2,1)S(1)}, u32[]{:S(2)}, u32[]{:S(2)}) async-start(bf16[16,208,256]{2,1,0:T(8,128)(2,1)} %pick.1), calls=%async_computation.1 | async-start | bytes 3407872 | tf_op jit(solution)/shard_map/all_to_all | solution.py:332
  40.0 0.9 copy-start.6
  40.9 0.8 copy-start.9
  67.3 1.1 copy-start.7
  68.4 1.4 copy-start.10
  69.8 17.0 %copy-start.8 = (bf16[2,128,1536]{2,1,0:T(8,128)(2,1)S(1)}, bf16[2,128,1536]{2,1,0:T(8,128)(2,1)}, u32[]{:S(2)}) copy-start(bf16[2,128,1536]{2,1,0:T(8,128)(2,1)} %copy-done.6) | copy-start | bytes 2359300
  71.1 15.7 %collective-permute-start.5 = (bf16[128,1536]{1,0:T(8,128)(2,1)S(1)}, bf16[128,1536]{1,0:T(8,128)(2,1)S(1)}, u32[]{:S(2)}, u32[]{:S(2)}) collective-permute-start(bf16[128,1536]{1,0:T(8,128)(2,1)S(1)} %pair.1), channel_id=1, source_target_pairs={{128,0},{129,1},{130,2},{131,3},{132,4},{133,5},{134,6},{135,7},{1... | collective-permute-start | bytes 1179656 | tf_op jit(solution)/shard_map/ppermute | solution.py:374
  90.0 26.0 %copy-start.2 = (s32[16,1,128]{2,1,0:T(1,128)S(1)}, s32[16,1,128]{2,1,0:T(1,128)}, u32[]{:S(2)}) copy-start(s32[16,1,128]{2,1,0:T(1,128)} %copy-done.1) | copy-start | bytes 24580
  90.0 26.0 %all-to-all-start.2 = ((bf16[16,208,256]{2,1,0:T(8,128)(2,1)}), bf16[16,208,256]{2,1,0:T(8,128)(2,1)S(1)}, u32[]{:S(2)}, u32[]{:S(2)}) async-start(bf16[16,208,256]{2,1,0:T(8,128)(2,1)} %bitcast.24), calls=%async_computation.2 | async-start | bytes 3407872 | tf_op jit(solution)/shard_map/all_to_all | solution.py:332
  93.8 47.6 %collective-permute-start.6 = (bf16[128,1536]{1,0:T(8,128)(2,1)S(1)}, bf16[128,1536]{1,0:T(8,128)(2,1)S(1)}, u32[]{:S(2)}, u32[]{:S(2)}) collective-permute-start(bf16[128,1536]{1,0:T(8,128)(2,1)S(1)} %get-tuple-element.29), channel_id=1, source_target_pairs={{0,64},{64,0},{1,65},{65,1},{2,66},{66,2},{3,67},{67,3},{4,68},{68... | collective-permute-start | bytes 1179656 | tf_op jit(solution)/shard_map/ppermute | solution.py:346
  117.2 25.8 %collective-permute-start.7 = (bf16[208,256]{1,0:T(8,128)(2,1)S(1)}, bf16[208,256]{1,0:T(8,128)(2,1)S(1)}, u32[]{:S(2)}, u32[]{:S(2)}) collective-permute-start(bf16[208,256]{1,0:T(8,128)(2,1)S(1)} %get-tuple-element.31), channel_id=1, source_target_pairs={{0,0},{4,4},{8,8},{12,12},{16,16},{20,20},{24,24},{28,28},{32,64},... | collective-permute-start | bytes 319496 | tf_op jit(solution)/shard_map/ppermute | solution.py:342
  124.0 18.9 %collective-permute-start.8 = (bf16[208,256]{1,0:T(8,128)(2,1)S(1)}, bf16[208,256]{1,0:T(8,128)(2,1)S(1)}, u32[]{:S(2)}, u32[]{:S(2)}) collective-permute-start(bf16[208,256]{1,0:T(8,128)(2,1)S(1)} %get-tuple-element.32), channel_id=1, source_target_pairs={{0,4},{4,8},{8,12},{12,0},{16,20},{20,24},{24,28},{28,16},{32,68},... | collective-permute-start | bytes 319496 | tf_op jit(solution)/shard_map/ppermute | solution.py:342
  137.8 7.5 %collective-permute-start.9 = (bf16[208,256]{1,0:T(8,128)(2,1)S(1)}, bf16[208,256]{1,0:T(8,128)(2,1)S(1)}, u32[]{:S(2)}, u32[]{:S(2)}) collective-permute-start(bf16[208,256]{1,0:T(8,128)(2,1)S(1)} %get-tuple-element.33), channel_id=1, source_target_pairs={{0,8},{4,12},{8,0},{12,4},{16,24},{20,28},{24,16},{28,20},{32,72},... | collective-permute-start | bytes 319496 | tf_op jit(solution)/shard_map/ppermute | solution.py:342
  137.8 7.7 %collective-permute-start.10 = (bf16[208,256]{1,0:T(8,128)(2,1)S(1)}, bf16[208,256]{1,0:T(8,128)(2,1)S(1)}, u32[]{:S(2)}, u32[]{:S(2)}) collective-permute-start(bf16[208,256]{1,0:T(8,128)(2,1)S(1)} %get-tuple-element.34), channel_id=1, source_target_pairs={{0,12},{4,0},{8,4},{12,8},{16,28},{20,16},{24,20},{28,24},{32,76},... | collective-permute-start | bytes 319496 | tf_op jit(solution)/shard_map/ppermute | solution.py:342
  141.5 4.0 %copy-start.4 = (bf16[1,4,48,256]{3,2,1,0:T(8,128)(2,1)S(1)}, bf16[1,4,48,256]{3,2,1,0:T(8,128)(2,1)}, u32[]{:S(2)}) copy-start(bf16[1,4,48,256]{3,2,1,0:T(8,128)(2,1)} %param.11) | copy-start | bytes 294916
  141.5 4.0 %copy-start.5 = (bf16[1,48,256]{2,1,0:T(8,128)(2,1)S(1)}, bf16[1,48,256]{2,1,0:T(8,128)(2,1)}, u32[]{:S(2)}) copy-start(bf16[1,48,256]{2,1,0:T(8,128)(2,1)} %param.10) | copy-start | bytes 73732

commit v6 on v5

--- a/solution.py
+++ b/solution.py
@@ -13,8 +13,7 @@
 SHARD = 48
 SLAB = D // NY
 SG = SLAB // GS
-WIDE = D // 2
-SLABS = NY // 2
+SECTIONS = 4
 PIECE = NZ * SHARD
 TILE = 16
 BLOCK = PIECE + TILE
@@ -91,24 +90,55 @@
     )(ids, z, *held)
 
 
-def gather_kernel(core, own, other, cotangent, x, up):
-    even = core[0] == 0
-    x[0] = jnp.where(even, own[:, :WIDE], other[...])
-    x[1] = jnp.where(even, other[...], own[:, WIDE:])
-    up[...] = jnp.where(even, cotangent[:, :WIDE], cotangent[:, WIDE:])
-
-
-def gather(core, own, other, cotangent):
+def fixed(shape):
+    return pl.BlockSpec(shape, lambda i, s: (0,) * len(shape))
+
+
+def slab_of(k):
+    return pl.BlockSpec((ROWS, SLAB), lambda i, s: (0, s[0] ^ k))
+
+
+def cut_kernel(s, *refs):
+    for k in range(1, SECTIONS):
+        refs[SECTIONS - 2 + k][...] = refs[k - 1][...]
+
+
+def cut(section, stash):
+    quarter = jax.ShapeDtypeStruct((ROWS, SLAB), BF)
+    return call(
+        cut_kernel,
+        "cut",
+        out_shape=(quarter,) * (SECTIONS - 1),
+        grid_spec=pltpu.PrefetchScalarGridSpec(
+            num_scalar_prefetch=1,
+            grid=(1,),
+            in_specs=[slab_of(k) for k in range(1, SECTIONS)],
+            out_specs=[fixed((ROWS, SLAB))] * (SECTIONS - 1),
+        ),
+    )(section, stash, stash, stash)
+
+
+def gather_kernel(s, own, other1, other2, other3, cotangent, x, top):
+    for k, part in enumerate((own, other1, other2, other3)):
+        x[s[0] ^ k] = part[...]
+    top[...] = cotangent[...]
+
+
+def gather(section, stash, others, cotangent):
     return call(
         gather_kernel,
         "gather",
         out_shape=(
-            jax.ShapeDtypeStruct((2, ROWS, WIDE), BF),
-            jax.ShapeDtypeStruct((ROWS, WIDE), BF),
-        ),
-        in_specs=[SMEM, VMEM, VMEM, VMEM],
-        out_specs=(VMEM, VMEM),
-    )(core, own, other, cotangent)
+            jax.ShapeDtypeStruct((SECTIONS, ROWS, SLAB), BF),
+            jax.ShapeDtypeStruct((ROWS, SLAB), BF),
+        ),
+        grid_spec=pltpu.PrefetchScalarGridSpec(
+            num_scalar_prefetch=1,
+            grid=(1,),
+            in_specs=[slab_of(0)] + [fixed((ROWS, SLAB))] * (SECTIONS - 1) + [slab_of(0)],
+            out_specs=[fixed((SECTIONS, ROWS, SLAB)), fixed((ROWS, SLAB))],
+        ),
+    )(section, stash, *others, cotangent)
 
 
 def slope_kernel(own, got, x, slope, kernel, offsets):
@@ -130,117 +160,100 @@
 
 
 def slopes(own, got, x):
+    tokens = pl.BlockSpec((1, ROWS, SLAB), lambda i: (i, 0, 0))
     return call(
         slope_kernel,
         "slopes",
-        grid=(2, SLABS),
+        grid=(SECTIONS,),
         out_shape=(
-            jax.ShapeDtypeStruct((2, ROWS, WIDE), F32),
-            jax.ShapeDtypeStruct((2, WIDE, GS), BF),
-        ),
-        in_specs=[
-            SMEM,
-            pl.BlockSpec((NX, BLOCK, GS), lambda p, h: (SLABS * p + h, 0, 0)),
-            pl.BlockSpec((1, ROWS, SLAB), lambda p, h: (p, 0, h)),
-        ],
-        out_specs=(
-            pl.BlockSpec((1, ROWS, SLAB), lambda p, h: (p, 0, h)),
-            pl.BlockSpec((1, SLAB, GS), lambda p, h: (p, h, 0)),
-        ),
+            jax.ShapeDtypeStruct((SECTIONS, ROWS, SLAB), F32),
+            jax.ShapeDtypeStruct((SECTIONS, SLAB, GS), BF),
+        ),
+        in_specs=[SMEM, pl.BlockSpec((NX, BLOCK, GS), lambda i: (i, 0, 0)), tokens],
+        out_specs=(tokens, pl.BlockSpec((1, SLAB, GS), lambda i: (i, 0, 0))),
         scratch_shapes=[pltpu.VMEM((TILE, GS), F32)],
     )(own, got, x)
 
 
-def layer(above, slope, kernel):
-    signal = (above * slope).astype(BF)
-    back = lax.dot_general(signal, kernel, (((1,), (1,)), ((), ())), preferred_element_type=F32)
-    return signal, (above + back).astype(BF)
-
-
-COLUMNS = pl.BlockSpec((ROWS, SLAB), lambda h: (0, h))
-BOTH_COLUMNS = pl.BlockSpec((2, ROWS, SLAB), lambda h: (0, 0, h))
-BOTH_ROWS = pl.BlockSpec((2, SLAB, GS), lambda h: (0, h, 0))
-
-
-def pair_kernel(up, slope, kernel, out):
+def grads_kernel(s, top, slope, kernel, x, out, send, above, tile):
+    @pl.when(pl.program_id(0) == 0)
+    def _():
+        above[...] = top[...]
+
+    tile[...] = jnp.zeros_like(tile)
     for q in range(SG):
         lanes = slice(q * GS, (q + 1) * GS)
-        above = up[:, lanes].astype(F32)
-        _, middle = layer(above, slope[1, :, lanes], kernel[1, lanes, :])
-        _, out[:, lanes] = layer(middle.astype(F32), slope[0, :, lanes], kernel[0, lanes, :])
-
-
-def pair(up, slope, kernel):
-    return call(
-        pair_kernel,
-        "pair",
-        grid=(SLABS,),
-        out_shape=jax.ShapeDtypeStruct((ROWS, WIDE), BF),
-        in_specs=[COLUMNS, BOTH_COLUMNS, BOTH_ROWS],
-        out_specs=COLUMNS,
-    )(up, slope, kernel)
-
-
-def grads_kernel(place, top, hop, slope, kernel, x, keep, give, send, tile):
-    even = place[0] == 0
-    last = place[1] == 1
-    for q in range(SG):
-        lanes = slice(q * GS, (q + 1) * GS)
-        above = jnp.where(last, top[:, lanes], hop[:, lanes]).astype(F32)
-        outs = [None, None]
-        for p in (1, 0):
-            signal, outs[p] = layer(above, slope[p, :, lanes], kernel[p, lanes, :])
-            above = outs[p].astype(F32)
-            grad = lax.dot_general(
-                x[p, :, lanes], signal, (((0,), (0,)), ((), ())), preferred_element_type=F32
-            ).astype(BF)
-            for row in range(q * GS, (q + 1) * GS, TILE):
-                shard, inner = row // SHARD, row % SHARD
-                at = shard // NX * SHARD + inner
-                send[p, 0, shard % NX, at : at + TILE, :] = grad[row - q * GS : row - q * GS + TILE]
-            total = jnp.sum(signal.astype(F32), axis=0, keepdims=True)
-            high = total.astype(BF).astype(F32)
-            tile[p, q : q + 1, :] = high
-            tile[p, SG + q : SG + q + 1, :] = total - high
-        keep[:, lanes] = jnp.where(even, outs[0], outs[1])
-        give[:, lanes] = jnp.where(even, outs[1], outs[0])
-    tile[:, 2 * SG :, :] = jnp.zeros((2, TILE - 2 * SG, GS), F32)
-    for p in range(2):
-        for i in range(NX):
-            send[p, 0, i, PIECE:, :] = tile[p].astype(BF)
-
-
-def grads(place, top, hop, slope, kernel, x):
-    half = jax.ShapeDtypeStruct((ROWS, WIDE), BF)
+        incoming = above[:, lanes].astype(F32)
+        signal = (incoming * slope[0, :, lanes]).astype(BF)
+        back = lax.dot_general(
+            signal, kernel[0, lanes, :], (((1,), (1,)), ((), ())), preferred_element_type=F32
+        )
+        outgoing = (incoming + back).astype(BF)
+        out[0, :, lanes] = outgoing
+        above[:, lanes] = outgoing
+        grad = lax.dot_general(
+            x[0, :, lanes], signal, (((0,), (0,)), ((), ())), preferred_element_type=F32
+        ).astype(BF)
+        for row in range(q * GS, (q + 1) * GS, TILE):
+            shard, inner = row // SHARD, row % SHARD
+            at = shard // NX * SHARD + inner
+            send[shard % NX, at : at + TILE, :] = grad[row - q * GS : row - q * GS + TILE]
+        total = jnp.sum(signal.astype(F32), axis=0, keepdims=True)
+        high = total.astype(BF).astype(F32)
+        tile[q : q + 1, :] = high
+        tile[SG + q : SG + q + 1, :] = total - high
+    for i in range(NX):
+        send[i, PIECE:, :] = tile[...].astype(BF)
+
+
+def grads(section, top, slope, kernel, x):
+    last = SECTIONS - 1
+    tokens = pl.BlockSpec((1, ROWS, SLAB), lambda i, s: (last - i, 0, 0))
     return call(
         grads_kernel,
         "grads",
-        grid=(SLABS,),
-        out_shape=(half, half, jax.ShapeDtypeStruct((2, SLABS, NX, BLOCK, GS), BF)),
-        in_specs=[SMEM, COLUMNS, COLUMNS, BOTH_COLUMNS, BOTH_ROWS, BOTH_COLUMNS],
-        out_specs=(
-            COLUMNS,
-            COLUMNS,
-            pl.BlockSpec((2, 1, NX, BLOCK, GS), lambda h: (0, h, 0, 0, 0)),
-        ),
-        scratch_shapes=[pltpu.VMEM((2, TILE, GS), F32)],
-    )(place, top, hop, slope, kernel, x)
-
-
-def join_kernel(core, keep, other, out):
-    even = core[0] == 0
-    out[:, :WIDE] = jnp.where(even, keep[...], other[...])
-    out[:, WIDE:] = jnp.where(even, other[...], keep[...])
-
-
-def join(core, keep, other):
+        out_shape=(
+            jax.ShapeDtypeStruct((SECTIONS, ROWS, SLAB), BF),
+            jax.ShapeDtypeStruct((SECTIONS * NX, BLOCK, GS), BF),
+        ),
+        grid_spec=pltpu.PrefetchScalarGridSpec(
+            num_scalar_prefetch=1,
+            grid=(SECTIONS,),
+            in_specs=[
+                fixed((ROWS, SLAB)),
+                tokens,
+                pl.BlockSpec((1, SLAB, GS), lambda i, s: (last - i, 0, 0)),
+                tokens,
+            ],
+            out_specs=[
+                pl.BlockSpec((1, ROWS, SLAB), lambda i, s: ((last - i) ^ s[0], 0, 0)),
+                pl.BlockSpec((NX, BLOCK, GS), lambda i, s: (last - i, 0, 0)),
+            ],
+            scratch_shapes=[pltpu.VMEM((ROWS, SLAB), BF), pltpu.VMEM((TILE, GS), F32)],
+        ),
+    )(section, top, slope, kernel, x)
+
+
+def join_kernel(s, own, other1, other2, other3, out):
+    for k, part in enumerate((own, other1, other2, other3)):
+
+        @pl.when(pl.program_id(0) == k)
+        def _(part=part):
+            out[...] = part[...]
+
+
+def join(section, own, others):
     return call(
         join_kernel,
         "join",
         out_shape=jax.ShapeDtypeStruct((ROWS, D), BF),
-        in_specs=[SMEM, VMEM, VMEM],
-        out_specs=VMEM,
-    )(core, keep, other)
+        grid_spec=pltpu.PrefetchScalarGridSpec(
+            num_scalar_prefetch=1,
+            grid=(SECTIONS,),
+            in_specs=[fixed((ROWS, SLAB))] * SECTIONS,
+            out_specs=pl.BlockSpec((ROWS, SLAB), lambda i, s: (0, i ^ s[0])),
+        ),
+    )(section, own, *others)
 
 
 def merge_kernel(ids, z, got, *refs):
@@ -334,16 +347,17 @@
 
 def turned(block, k):
     pairs = []
-    for core in range(2):
+    for section in range(SECTIONS):
         for y in range(NY):
             for z in range(NZ):
-                to = (y // SLABS * NY + core * SLABS + y % SLABS) * NZ + (z + k) % NZ
-                pairs.append(((core * NY + y) * NZ + z, to))
-    return lax.ppermute(block, ("core", "y", "zlo"), pairs)
-
-
-def swapped(block):
-    return lax.ppermute(block, "core", [(0, 1), (1, 0)])
+                to = (y * NY + section) * NZ + (z + k) % NZ
+                pairs.append(((section * NY + y) * NZ + z, to))
+    return lax.ppermute(block, ("zhi", "core", "y", "zlo"), pairs)
+
+
+def swapped(block, k):
+    pairs = [(section, section ^ k) for section in range(SECTIONS)]
+    return lax.ppermute(block, ("zhi", "core"), pairs)
 
 
 def after(first, *then):
@@ -351,30 +365,28 @@
 
 
 def body(stash, cotangent, domain_ids, shared_weight, domain_weight, shared_bias, domain_bias):
-    own = stash[0]
+    stash = stash[0]
     sw, dw = shared_weight[0], domain_weight[0]
-    core = lax.axis_index("core")
-    place = jnp.stack([core, lax.axis_index("zhi")])
+    section = jnp.reshape(2 * lax.axis_index("zhi") + lax.axis_index("core"), (1,))
     z = jnp.reshape(lax.axis_index("zlo"), (1,))
     at = PIECE * z + SHARD * lax.axis_index("x")
 
+    plane_ids = exchange(
+        jnp.broadcast_to(domain_ids[0], (NY * NX, 1, 128)), ("y", "x")
+    ).reshape(NY * NX, 128)
     mine = prep(at, sw, dw, shared_bias, domain_bias[0])
     held = [turned(mine, k) for k in range(NZ)]
-    (ids,) = after(mine, domain_ids)
-    plane_ids = exchange(
-        jnp.broadcast_to(ids[0], (NY * NX, 1, 128)), ("y", "x")
-    ).reshape(NY * NX, 128)
-    (own,) = after(plane_ids, own)
-    other = swapped(lax.dynamic_slice(own, (0, (1 - core) * WIDE), (ROWS, WIDE)))
-    got = exchange(pick(plane_ids, z, held), ("y", "x"))
-    x, top = gather(place, own, other, cotangent)
+    picked = pick(plane_ids, z, held)
+    got = exchange(picked, ("y", "x"))
+    (late,) = after(picked, stash)
+    parts = cut(section, late)
+    others = [swapped(parts[k - 1], k) for k in range(1, SECTIONS)]
+    x, top = gather(section, late, others, cotangent)
 
     slope, kernel = slopes(domain_ids, got, x)
-    out = pair(top, slope, kernel)
-    hop = lax.ppermute(out, "zhi", [(1, 0)])
-    keep, give, send = grads(place, top, hop, slope, kernel, x)
-    got = exchange(send.reshape(NY * NX, BLOCK, GS), ("y", "x"))
-    d_inputs = join(place, keep, swapped(give))
+    out, send = grads(section, top, slope, kernel, x)
+    got = exchange(send, ("y", "x"))
+    d_inputs = join(section, out[0], [swapped(out[k], k) for k in range(1, SECTIONS)])
     merged = merge(plane_ids, z, got)
     final = [turned(merged[k], k) for k in range(NZ)]
     d_shared, d_domain, b_shared, b_domain = finish(at, final, sw, dw)

time: 147 us -> 140 us (0.952)
  the two profiles are of different devices: /device:TPU:1 before, /device:TPU:80 now
where the time goes in v6:
time: 140 us; the launch traced here: 139 us
  starting transfers between devices  64 us (46%)
  waiting for transfers between devices  56.9 us (41%)
  Pallas kernels  13.4 us (10%)
  local copies, waits for them, and re-layouts  3.38 us (2%)
    all_to_all x3, waiting for transfers between devices, exchange(): return lax.all_to_all(block, axes, 0, 0, tiled=True)  39.5 us
    ppermute x8, starting transfers between devices, turned(): return lax.ppermute(block, ('zhi', 'core', 'y', 'zlo'), pairs)  32.7 us
    all_to_all x3, starting transfers between devices, exchange(): return lax.all_to_all(block, axes, 0, 0, tiled=True)  19.7 us
    ppermute x6, starting transfers between devices, swapped(): return lax.ppermute(block, ('zhi', 'core'), pairs)  11.6 us
    ppermute x8, waiting for transfers between devices, turned(): return lax.ppermute(block, ('zhi', 'core', 'y', 'zlo'), pairs)  10.7 us
    ppermute x6, waiting for transfers between devices, swapped(): return lax.ppermute(block, ('zhi', 'core'), pairs)  6.7 us
  transfers between devices with their start and end apart: 17, of which 8 were waited for; matrix products, arithmetic and copies ran while one was open for 0% of the time, Pallas kernels for 3%

profile of v6, /device:TPU:80, one launch (start us, length us, event | category | flops | bytes accessed | tf_op | source)
XLA Modules:
  0.0 139.1 jit_solution(2527081441881621413)
XLA Ops:
  0.6 1.6 %prep.1 = bf16[208,256]{1,0:T(8,128)(2,1)} custom-call(s32[1]{0:T(128)S(6)} %add.11.at, bf16[48,256]{1,0:T(8,128)(2,1)} %bitcast.30, bf16[4,48,256]{2,1,0:T(8,128)(2,1)} %bitcast.28, bf16[1,48]{1,0:T(2,128)(2,1)} %sb.1, bf16[4,48]{1,0:T(4,128)(2,1)} %bitcast.32), custom_call_target="tpu_custom_call" | custom-call | flops 99999997952 | bytes 1000000000 | tf_op jit(solution)/shard_map/prep/pallas_call | solution.py:56
  2.3 4.7 %collective-permute-start.3 = (bf16[208,256]{1,0:T(8,128)(2,1)}, bf16[208,256]{1,0:T(8,128)(2,1)S(1)}, u32[]{:S(2)}, u32[]{:S(2)}) collective-permute-start(bf16[208,256]{1,0:T(8,128)(2,1)} %prep.1), channel_id=1, source_target_pairs={{0,12},{4,0},{8,4},{12,8},{16,76},{20,64},{24,68},{28,72},{32,140}... | collective-permute-start | bytes 319496 | tf_op jit(solution)/shard_map/ppermute | solution.py:355
  7.0 2.3 %collective-permute-start.2 = (bf16[208,256]{1,0:T(8,128)(2,1)}, bf16[208,256]{1,0:T(8,128)(2,1)S(1)}, u32[]{:S(2)}, u32[]{:S(2)}) collective-permute-start(bf16[208,256]{1,0:T(8,128)(2,1)} %prep.1), channel_id=1, source_target_pairs={{0,8},{4,12},{8,0},{12,4},{16,72},{20,76},{24,64},{28,68},{32,136}... | collective-permute-start | bytes 319496 | tf_op jit(solution)/shard_map/ppermute | solution.py:355
  9.3 4.7 %collective-permute-start.1 = (bf16[208,256]{1,0:T(8,128)(2,1)}, bf16[208,256]{1,0:T(8,128)(2,1)S(1)}, u32[]{:S(2)}, u32[]{:S(2)}) collective-permute-start(bf16[208,256]{1,0:T(8,128)(2,1)} %prep.1), channel_id=1, source_target_pairs={{0,4},{4,8},{8,12},{12,0},{16,68},{20,72},{24,76},{28,64},{32,132}... | collective-permute-start | bytes 319496 | tf_op jit(solution)/shard_map/ppermute | solution.py:355
  14.0 3.3 %collective-permute-start = (bf16[208,256]{1,0:T(8,128)(2,1)}, bf16[208,256]{1,0:T(8,128)(2,1)S(1)}, u32[]{:S(2)}, u32[]{:S(2)}) collective-permute-start(bf16[208,256]{1,0:T(8,128)(2,1)} %prep.1), channel_id=1, source_target_pairs={{0,0},{4,4},{8,8},{12,12},{16,64},{20,68},{24,72},{28,76},{32,128}... | collective-permute-start | bytes 319496 | tf_op jit(solution)/shard_map/ppermute | solution.py:355
  17.9 0.6 broadcast_in_dim.15
  18.5 7.3 %all-to-all-start = ((s32[16,1,128]{2,1,0:T(1,128)}), s32[16,1,128]{2,1,0:T(1,128)S(1)}, u32[]{:S(2)}, u32[]{:S(2)}) async-start(s32[16,1,128]{2,1,0:T(1,128)} %broadcast_in_dim.15), calls=%async_computation | async-start | bytes 16384 | tf_op jit(solution)/shard_map/all_to_all | solution.py:345
  25.8 5.2 %all-to-all-done = s32[16,1,128]{2,1,0:T(1,128)S(1)} async-done(((s32[16,1,128]{2,1,0:T(1,128)}), s32[16,1,128]{2,1,0:T(1,128)S(1)}, u32[]{:S(2)}, u32[]{:S(2)}) %all-to-all-start) | async-done | bytes 8224 | tf_op jit(solution)/shard_map/all_to_all | solution.py:345
  31.0 0.0 collective-permute-done.3.refs_3_
  31.0 0.0 collective-permute-done.2.refs_2_
  31.0 0.0 collective-permute-done.1.refs_1_
  31.0 0.0 collective-permute-done.refs_0_
  31.0 0.0 copy-start.2
  31.1 2.5 %pick.1 = bf16[16,208,256]{2,1,0:T(8,128)(2,1)} custom-call(s32[16,128]{1,0:T(8,128)S(1)} %bitcast.22, s32[1]{0:T(128)} %bitcast.3.z, bf16[208,256]{1,0:T(8,128)(2,1)S(1)} %collective-permute-done.refs_0_, bf16[208,256]{1,0:T(8,128)(2,1)S(1)} %collective-permute-done.1.refs_1_, bf16[208,256]{1,0:T(8,128)(2,1)S(1)} %collective-permute-done.2.refs_2_, ...), custom_call_target="tpu_custom_call" | custom-call | flops 99999997952 | bytes 1000000000 | tf_op jit(solution)/shard_map/pick/pallas_call | solution.py:83
  33.6 0.8 cut.1
  34.4 0.0 collective-permute-start.4
  34.4 4.6 %collective-permute-start.5 = (bf16[128,768]{1,0:T(8,128)(2,1)}, bf16[128,768]{1,0:T(8,128)(2,1)}, u32[]{:S(2)}, u32[]{:S(2)}) collective-permute-start(bf16[128,768]{1,0:T(8,128)(2,1)} %get-tuple-element.25), channel_id=1, source_target_pairs={{0,128},{64,192},{128,0},{192,64},{1,129},{65,193},{129,1},{193,65... | collective-permute-start | bytes 589832 | tf_op jit(solution)/shard_map/ppermute | solution.py:360
  39.0 1.2 collective-permute-start.6
  40.2 5.9 %all-to-all-start.1 = ((bf16[16,208,256]{2,1,0:T(8,128)(2,1)}), bf16[16,208,256]{2,1,0:T(8,128)(2,1)S(1)}, u32[]{:S(2)}, u32[]{:S(2)}) async-start(bf16[16,208,256]{2,1,0:T(8,128)(2,1)} %pick.1), calls=%async_computation.1 | async-start | bytes 3407872 | tf_op jit(solution)/shard_map/all_to_all | solution.py:345
  46.1 1.8 %collective-permute-done.5.other2 = bf16[128,768]{1,0:T(8,128)(2,1)} collective-permute-done((bf16[128,768]{1,0:T(8,128)(2,1)}, bf16[128,768]{1,0:T(8,128)(2,1)}, u32[]{:S(2)}, u32[]{:S(2)}) %collective-permute-start.5) | collective-permute-done | bytes 196640 | tf_op jit(solution)/shard_map/ppermute | solution.py:360
  47.8 4.9 %collective-permute-done.6.other3 = bf16[128,768]{1,0:T(8,128)(2,1)} collective-permute-done((bf16[128,768]{1,0:T(8,128)(2,1)}, bf16[128,768]{1,0:T(8,128)(2,1)}, u32[]{:S(2)}, u32[]{:S(2)}) %collective-permute-start.6) | collective-permute-done | bytes 196640 | tf_op jit(solution)/shard_map/ppermute | solution.py:360
  52.8 1.1 gather.1
  53.9 0.0 copy-start.6
  53.9 0.9 copy-done.6
  54.8 0.7 copy-done.9
  55.4 16.8 %all-to-all-done.1.got = bf16[16,208,256]{2,1,0:T(8,128)(2,1)S(1)} async-done(((bf16[16,208,256]{2,1,0:T(8,128)(2,1)}), bf16[16,208,256]{2,1,0:T(8,128)(2,1)S(1)}, u32[]{:S(2)}, u32[]{:S(2)}) %all-to-all-start.1) | async-done | bytes 1703968 | tf_op jit(solution)/shard_map/all_to_all | solution.py:345
  72.2 1.1 copy-done.7
  73.4 1.1 slopes.1
  74.5 0.0 copy-done.10
  74.5 2.8 %grads.1 = (bf16[4,128,768]{2,1,0:T(8,128)(2,1)S(1)}, bf16[16,208,256]{2,1,0:T(8,128)(2,1)}) custom-call(s32[1]{0:T(128)} %bitcast.s, bf16[128,768]{1,0:T(8,128)(2,1)S(1)} %copy-done.10, f32[4,128,768]{2,1,0:T(8,128)S(1)} %get-tuple-element.29.slope, bf16[4,768,256]{2,1,0:T(8,128)(2,1)S(1)} %get-tuple-element.30.kernel, bf16[4,128,768]{2,1,0:T(8,128)(2,1)S(1)} %copy-done.8), custom_call_target="tpu_custom_call" | custom-call | flops 99999997952 | bytes 1000000000 | tf_op jit(solution)/shard_map/grads/pallas_call | solution.py:212
  77.3 6.5 %all-to-all-start.2 = ((bf16[16,208,256]{2,1,0:T(8,128)(2,1)}), bf16[16,208,256]{2,1,0:T(8,128)(2,1)S(1)}, u32[]{:S(2)}, u32[]{:S(2)}) async-start(bf16[16,208,256]{2,1,0:T(8,128)(2,1)} %get-tuple-element.32), calls=%async_computation.2 | async-start | bytes 3407872 | tf_op jit(solution)/shard_map/all_to_all | solution.py:345
  83.8 0.1 slice_bitcast_fusion
  83.8 3.4 %collective-permute-start.9 = (bf16[128,768]{1,0:T(8,128)(2,1)S(1)}, bf16[128,768]{1,0:T(8,128)(2,1)S(1)}, u32[]{:S(2)}, u32[]{:S(2)}) collective-permute-start(bf16[128,768]{1,0:T(8,128)(2,1)S(1)} %get-tuple-element.41), channel_id=1, source_target_pairs={{0,192},{64,128},{128,64},{192,0},{1,193},{65,129},{129,65},{193,1... | collective-permute-start | bytes 589832 | tf_op jit(solution)/shard_map/ppermute | solution.py:360
  87.3 1.4 collective-permute-start.8
  88.7 1.0 collective-permute-start.7
  89.7 17.5 %all-to-all-done.2.got = bf16[16,208,256]{2,1,0:T(8,128)(2,1)S(1)} async-done(((bf16[16,208,256]{2,1,0:T(8,128)(2,1)}), bf16[16,208,256]{2,1,0:T(8,128)(2,1)S(1)}, u32[]{:S(2)}, u32[]{:S(2)}) %all-to-all-start.2) | async-done | bytes 1703968 | tf_op jit(solution)/shard_map/all_to_all | solution.py:345
  107.2 1.2 merge.1
  108.4 8.6 %collective-permute-start.10 = (bf16[208,256]{1,0:T(8,128)(2,1)S(1)}, bf16[208,256]{1,0:T(8,128)(2,1)S(1)}, u32[]{:S(2)}, u32[]{:S(2)}) collective-permute-start(bf16[208,256]{1,0:T(8,128)(2,1)S(1)} %get-tuple-element.33), channel_id=1, source_target_pairs={{0,0},{4,4},{8,8},{12,12},{16,64},{20,68},{24,72},{28,76},{32,128}... | collective-permute-start | bytes 319496 | tf_op jit(solution)/shard_map/ppermute | solution.py:355
  117.0 1.2 collective-permute-start.11
  118.3 4.9 %collective-permute-start.12 = (bf16[208,256]{1,0:T(8,128)(2,1)S(1)}, bf16[208,256]{1,0:T(8,128)(2,1)S(1)}, u32[]{:S(2)}, u32[]{:S(2)}) collective-permute-start(bf16[208,256]{1,0:T(8,128)(2,1)S(1)} %get-tuple-element.35), channel_id=1, source_target_pairs={{0,8},{4,12},{8,0},{12,4},{16,72},{20,76},{24,64},{28,68},{32,136}... | collective-permute-start | bytes 319496 | tf_op jit(solution)/shard_map/ppermute | solution.py:355
  123.2 0.0 collective-permute-done.8.other2
  123.2 3.0 %collective-permute-start.13 = (bf16[208,256]{1,0:T(8,128)(2,1)S(1)}, bf16[208,256]{1,0:T(8,128)(2,1)S(1)}, u32[]{:S(2)}, u32[]{:S(2)}) collective-permute-start(bf16[208,256]{1,0:T(8,128)(2,1)S(1)} %get-tuple-element.36), channel_id=1, source_target_pairs={{0,12},{4,0},{8,4},{12,8},{16,76},{20,64},{24,68},{28,72},{32,140}... | collective-permute-start | bytes 319496 | tf_op jit(solution)/shard_map/ppermute | solution.py:355
  126.2 0.0 collective-permute-done.7.other1
  126.2 1.5 %join.1 = bf16[128,3072]{1,0:T(8,128)(2,1)} custom-call(s32[1]{0:T(128)} %bitcast.s, bf16[128,768]{1,0:T(8,128)(2,1)S(1)} %get-tuple-element.44.own, bf16[128,768]{1,0:T(8,128)(2,1)S(1)} %collective-permute-done.7.other1, bf16[128,768]{1,0:T(8,128)(2,1)S(1)} %collective-permute-done.8.other2, bf16[128,768]{1,0:T(8,128)(2,1)S(1)} %collective-permute-done.9.other3), custom_call_target="tpu_custom_call" | custom-call | flops 99999997952 | bytes 1000000000 | tf_op jit(solution)/shard_map/join/pallas_call | solution.py:246
  127.7 2.1 %collective-permute-done.11.refs_1_ = bf16[208,256]{1,0:T(8,128)(2,1)S(1)} collective-permute-done((bf16[208,256]{1,0:T(8,128)(2,1)S(1)}, bf16[208,256]{1,0:T(8,128)(2,1)S(1)}, u32[]{:S(2)}, u32[]{:S(2)}) %collective-permute-start.11) | collective-permute-done | bytes 106528 | tf_op jit(solution)/shard_map/ppermute | solution.py:355
  129.8 6.8 %collective-permute-done.12.refs_2_ = bf16[208,256]{1,0:T(8,128)(2,1)S(1)} collective-permute-done((bf16[208,256]{1,0:T(8,128)(2,1)S(1)}, bf16[208,256]{1,0:T(8,128)(2,1)S(1)}, u32[]{:S(2)}, u32[]{:S(2)}) %collective-permute-start.12) | collective-permute-done | bytes 106528 | tf_op jit(solution)/shard_map/ppermute | solution.py:355
  136.6 1.7 %collective-permute-done.13.refs_3_ = bf16[208,256]{1,0:T(8,128)(2,1)S(1)} collective-permute-done((bf16[208,256]{1,0:T(8,128)(2,1)S(1)}, bf16[208,256]{1,0:T(8,128)(2,1)S(1)}, u32[]{:S(2)}, u32[]{:S(2)}) %collective-permute-start.13) | collective-permute-done | bytes 106528 | tf_op jit(solution)/shard_map/ppermute | solution.py:355
  138.3 0.8 finish.1
  (19 shorter events, 0.0 us)
Async XLA Ops:
  2.3 28.7 %collective-permute-start.3 = (bf16[208,256]{1,0:T(8,128)(2,1)}, bf16[208,256]{1,0:T(8,128)(2,1)S(1)}, u32[]{:S(2)}, u32[]{:S(2)}) collective-permute-start(bf16[208,256]{1,0:T(8,128)(2,1)} %prep.1), channel_id=1, source_target_pairs={{0,12},{4,0},{8,4},{12,8},{16,76},{20,64},{24,68},{28,72},{32,140}... | collective-permute-start | bytes 319496 | tf_op jit(solution)/shard_map/ppermute | solution.py:355
  7.0 24.0 %collective-permute-start.2 = (bf16[208,256]{1,0:T(8,128)(2,1)}, bf16[208,256]{1,0:T(8,128)(2,1)S(1)}, u32[]{:S(2)}, u32[]{:S(2)}) collective-permute-start(bf16[208,256]{1,0:T(8,128)(2,1)} %prep.1), channel_id=1, source_target_pairs={{0,8},{4,12},{8,0},{12,4},{16,72},{20,76},{24,64},{28,68},{32,136}... | collective-permute-start | bytes 319496 | tf_op jit(solution)/shard_map/ppermute | solution.py:355
  9.3 21.7 %collective-permute-start.1 = (bf16[208,256]{1,0:T(8,128)(2,1)}, bf16[208,256]{1,0:T(8,128)(2,1)S(1)}, u32[]{:S(2)}, u32[]{:S(2)}) collective-permute-start(bf16[208,256]{1,0:T(8,128)(2,1)} %prep.1), channel_id=1, source_target_pairs={{0,4},{4,8},{8,12},{12,0},{16,68},{20,72},{24,76},{28,64},{32,132}... | collective-permute-start | bytes 319496 | tf_op jit(solution)/shard_map/ppermute | solution.py:355
  14.0 17.1 %collective-permute-start = (bf16[208,256]{1,0:T(8,128)(2,1)}, bf16[208,256]{1,0:T(8,128)(2,1)S(1)}, u32[]{:S(2)}, u32[]{:S(2)}) collective-permute-start(bf16[208,256]{1,0:T(8,128)(2,1)} %prep.1), channel_id=1, source_target_pairs={{0,0},{4,4},{8,8},{12,12},{16,64},{20,68},{24,72},{28,76},{32,128}... | collective-permute-start | bytes 319496 | tf_op jit(solution)/shard_map/ppermute | solution.py:355
  18.5 12.5 %all-to-all-start = ((s32[16,1,128]{2,1,0:T(1,128)}), s32[16,1,128]{2,1,0:T(1,128)S(1)}, u32[]{:S(2)}, u32[]{:S(2)}) async-start(s32[16,1,128]{2,1,0:T(1,128)} %broadcast_in_dim.15), calls=%async_computation | async-start | bytes 16384 | tf_op jit(solution)/shard_map/all_to_all | solution.py:345
  31.0 2.5 %copy-start = (s32[16,1,128]{2,1,0:T(1,128)}, s32[16,1,128]{2,1,0:T(1,128)S(1)}, u32[]{:S(2)}) copy-start(s32[16,1,128]{2,1,0:T(1,128)S(1)} %all-to-all-done) | copy-start | bytes 24580
  31.0 2.5 %copy-start.2 = (bf16[1,128,3072]{2,1,0:T(8,128)(2,1)S(1)}, bf16[1,128,3072]{2,1,0:T(8,128)(2,1)}, u32[]{:S(2)}) copy-start(bf16[1,128,3072]{2,1,0:T(8,128)(2,1)} %param.7) | copy-start | bytes 2359300
  34.4 11.7 %collective-permute-start.4 = (bf16[128,768]{1,0:T(8,128)(2,1)}, bf16[128,768]{1,0:T(8,128)(2,1)S(1)}, u32[]{:S(2)}, u32[]{:S(2)}) collective-permute-start(bf16[128,768]{1,0:T(8,128)(2,1)} %get-tuple-element.24), channel_id=1, source_target_pairs={{0,64},{64,0},{128,192},{192,128},{1,65},{65,1},{129,193},{193,129... | collective-permute-start | bytes 589832 | tf_op jit(solution)/shard_map/ppermute | solution.py:360
  34.4 13.5 %collective-permute-start.5 = (bf16[128,768]{1,0:T(8,128)(2,1)}, bf16[128,768]{1,0:T(8,128)(2,1)}, u32[]{:S(2)}, u32[]{:S(2)}) collective-permute-start(bf16[128,768]{1,0:T(8,128)(2,1)} %get-tuple-element.25), channel_id=1, source_target_pairs={{0,128},{64,192},{128,0},{192,64},{1,129},{65,193},{129,1},{193,65... | collective-permute-start | bytes 589832 | tf_op jit(solution)/shard_map/ppermute | solution.py:360
  39.0 13.8 %copy-start.3 = (bf16[128,3072]{1,0:T(8,128)(2,1)S(1)}, bf16[128,3072]{1,0:T(8,128)(2,1)}, u32[]{:S(2)}) copy-start(bf16[128,3072]{1,0:T(8,128)(2,1)} %cotangent.1) | copy-start | bytes 2359300
  39.0 13.8 %collective-permute-start.6 = (bf16[128,768]{1,0:T(8,128)(2,1)}, bf16[128,768]{1,0:T(8,128)(2,1)}, u32[]{:S(2)}, u32[]{:S(2)}) collective-permute-start(bf16[128,768]{1,0:T(8,128)(2,1)} %get-tuple-element.26), channel_id=1, source_target_pairs={{0,192},{64,128},{128,64},{192,0},{1,193},{65,129},{129,65},{193,1... | collective-permute-start | bytes 589832 | tf_op jit(solution)/shard_map/ppermute | solution.py:360
  40.2 32.1 %all-to-all-start.1 = ((bf16[16,208,256]{2,1,0:T(8,128)(2,1)}), bf16[16,208,256]{2,1,0:T(8,128)(2,1)S(1)}, u32[]{:S(2)}, u32[]{:S(2)}) async-start(bf16[16,208,256]{2,1,0:T(8,128)(2,1)} %pick.1), calls=%async_computation.1 | async-start | bytes 3407872 | tf_op jit(solution)/shard_map/all_to_all | solution.py:345
  53.9 0.9 copy-start.6
  54.7 0.7 copy-start.9
  72.2 1.1 copy-start.7
  73.4 1.1 copy-start.8
  73.4 1.2 copy-start.10
  77.3 29.9 %copy-start.1 = (s32[16,1,128]{2,1,0:T(1,128)S(1)}, s32[16,1,128]{2,1,0:T(1,128)}, u32[]{:S(2)}) copy-start(s32[16,1,128]{2,1,0:T(1,128)} %copy-done) | copy-start | bytes 24580
  77.3 29.9 %all-to-all-start.2 = ((bf16[16,208,256]{2,1,0:T(8,128)(2,1)}), bf16[16,208,256]{2,1,0:T(8,128)(2,1)S(1)}, u32[]{:S(2)}, u32[]{:S(2)}) async-start(bf16[16,208,256]{2,1,0:T(8,128)(2,1)} %get-tuple-element.32), calls=%async_computation.2 | async-start | bytes 3407872 | tf_op jit(solution)/shard_map/all_to_all | solution.py:345
  83.8 34.4 %collective-permute-start.9 = (bf16[128,768]{1,0:T(8,128)(2,1)S(1)}, bf16[128,768]{1,0:T(8,128)(2,1)S(1)}, u32[]{:S(2)}, u32[]{:S(2)}) collective-permute-start(bf16[128,768]{1,0:T(8,128)(2,1)S(1)} %get-tuple-element.41), channel_id=1, source_target_pairs={{0,192},{64,128},{128,64},{192,0},{1,193},{65,129},{129,65},{193,1... | collective-permute-start | bytes 589832 | tf_op jit(solution)/shard_map/ppermute | solution.py:360
  87.3 35.9 %collective-permute-start.8 = (bf16[128,768]{1,0:T(8,128)(2,1)S(1)}, bf16[128,768]{1,0:T(8,128)(2,1)S(1)}, u32[]{:S(2)}, u32[]{:S(2)}) collective-permute-start(bf16[128,768]{1,0:T(8,128)(2,1)S(1)} %get-tuple-element.42), channel_id=1, source_target_pairs={{0,128},{64,192},{128,0},{192,64},{1,129},{65,193},{129,1},{193,65... | collective-permute-start | bytes 589832 | tf_op jit(solution)/shard_map/ppermute | solution.py:360
  88.7 37.5 %collective-permute-start.7 = (bf16[128,768]{1,0:T(8,128)(2,1)S(1)}, bf16[128,768]{1,0:T(8,128)(2,1)S(1)}, u32[]{:S(2)}, u32[]{:S(2)}) collective-permute-start(bf16[128,768]{1,0:T(8,128)(2,1)S(1)} %get-tuple-element.43), channel_id=1, source_target_pairs={{0,64},{64,0},{128,192},{192,128},{1,65},{65,1},{129,193},{193,129... | collective-permute-start | bytes 589832 | tf_op jit(solution)/shard_map/ppermute | solution.py:360
  108.4 19.3 %collective-permute-start.10 = (bf16[208,256]{1,0:T(8,128)(2,1)S(1)}, bf16[208,256]{1,0:T(8,128)(2,1)S(1)}, u32[]{:S(2)}, u32[]{:S(2)}) collective-permute-start(bf16[208,256]{1,0:T(8,128)(2,1)S(1)} %get-tuple-element.33), channel_id=1, source_target_pairs={{0,0},{4,4},{8,8},{12,12},{16,64},{20,68},{24,72},{28,76},{32,128}... | collective-permute-start | bytes 319496 | tf_op jit(solution)/shard_map/ppermute | solution.py:355
  117.0 12.7 %collective-permute-start.11 = (bf16[208,256]{1,0:T(8,128)(2,1)S(1)}, bf16[208,256]{1,0:T(8,128)(2,1)S(1)}, u32[]{:S(2)}, u32[]{:S(2)}) collective-permute-start(bf16[208,256]{1,0:T(8,128)(2,1)S(1)} %get-tuple-element.34), channel_id=1, source_target_pairs={{0,4},{4,8},{8,12},{12,0},{16,68},{20,72},{24,76},{28,64},{32,132}... | collective-permute-start | bytes 319496 | tf_op jit(solution)/shard_map/ppermute | solution.py:355
  118.3 18.3 %collective-permute-start.12 = (bf16[208,256]{1,0:T(8,128)(2,1)S(1)}, bf16[208,256]{1,0:T(8,128)(2,1)S(1)}, u32[]{:S(2)}, u32[]{:S(2)}) collective-permute-start(bf16[208,256]{1,0:T(8,128)(2,1)S(1)} %get-tuple-element.35), channel_id=1, source_target_pairs={{0,8},{4,12},{8,0},{12,4},{16,72},{20,76},{24,64},{28,68},{32,136}... | collective-permute-start | bytes 319496 | tf_op jit(solution)/shard_map/ppermute | solution.py:355
  123.2 15.1 %collective-permute-start.13 = (bf16[208,256]{1,0:T(8,128)(2,1)S(1)}, bf16[208,256]{1,0:T(8,128)(2,1)S(1)}, u32[]{:S(2)}, u32[]{:S(2)}) collective-permute-start(bf16[208,256]{1,0:T(8,128)(2,1)S(1)} %get-tuple-element.36), channel_id=1, source_target_pairs={{0,12},{4,0},{8,4},{12,8},{16,76},{20,64},{24,68},{28,72},{32,140}... | collective-permute-start | bytes 319496 | tf_op jit(solution)/shard_map/ppermute | solution.py:355
  126.2 12.2 %copy-start.4 = (bf16[1,4,48,256]{3,2,1,0:T(8,128)(2,1)S(1)}, bf16[1,4,48,256]{3,2,1,0:T(8,128)(2,1)}, u32[]{:S(2)}) copy-start(bf16[1,4,48,256]{3,2,1,0:T(8,128)(2,1)} %param.11) | copy-start | bytes 294916
  126.2 12.2 %copy-start.5 = (bf16[1,48,256]{2,1,0:T(8,128)(2,1)S(1)}, bf16[1,48,256]{2,1,0:T(8,128)(2,1)}, u32[]{:S(2)}) copy-start(bf16[1,48,256]{2,1,0:T(8,128)(2,1)} %param.10) | copy-start | bytes 73732

commit v7 on v6

--- a/solution.py
+++ b/solution.py
@@ -71,8 +71,8 @@
     for k in range(1, NZ):
         tile = tile + held[k][PIECE:, :].astype(F32)
     tile = tile.astype(BF)
-    for i in range(NX):
-        start = pl.multiple_of(ids[step * NX + i, 0] * SHARD, TILE)
+    for i in range(out.shape[0]):
+        start = pl.multiple_of(ids[step * out.shape[0] + i, 0] * SHARD, TILE)
         for k in range(NZ):
             to = pl.multiple_of(((z[0] + NZ - k) % NZ) * SHARD, TILE)
             out[i, pl.ds(to, SHARD), :] = held[k][pl.ds(start, SHARD), :]
@@ -83,10 +83,10 @@
     return call(
         pick_kernel,
         "pick",
-        grid=(NY,),
+        grid=(2,),
         out_shape=jax.ShapeDtypeStruct((NY * NX, BLOCK, GS), BF),
         in_specs=[SMEM, SMEM] + [pl.BlockSpec((BLOCK, GS), lambda i: (0, 0))] * NZ,
-        out_specs=pl.BlockSpec((NX, BLOCK, GS), lambda i: (i, 0, 0)),
+        out_specs=pl.BlockSpec((NY * NX // 2, BLOCK, GS), lambda i: (i, 0, 0)),
     )(ids, z, *held)
 
 
@@ -128,6 +128,7 @@
     return call(
         gather_kernel,
         "gather",
+        weight=0,
         out_shape=(
             jax.ShapeDtypeStruct((SECTIONS, ROWS, SLAB), BF),
             jax.ShapeDtypeStruct((ROWS, SLAB), BF),
@@ -375,6 +376,7 @@
         jnp.broadcast_to(domain_ids[0], (NY * NX, 1, 128)), ("y", "x")
     ).reshape(NY * NX, 128)
     mine = prep(at, sw, dw, shared_bias, domain_bias[0])
+    (mine,) = after(plane_ids, mine)
     held = [turned(mine, k) for k in range(NZ)]
     picked = pick(plane_ids, z, held)
     got = exchange(picked, ("y", "x"))

time: 140 us -> 140 us (level)
  starting transfers between devices: 64 us -> 66.7 us
  local copies, waits for them, and re-layouts: 3.38 us -> 0.68 us
  waiting for transfers between devices: 56.9 us -> 59.5 us
  Pallas kernels: 13.4 us -> 11.1 us
    all_to_all x3, waiting for transfers between devices: 39.5 us -> 21.4 us  [exchange(): return lax.all_to_all(block, axes, 0, 0, tiled=True)]
    ppermute x8, waiting for transfers between devices: 10.7 us -> 22.6 us  [turned(): return lax.ppermute(block, ('zhi', 'core', 'y', 'zlo'), pairs)]
    ppermute x6, waiting for transfers between devices: 6.7 us -> 15.5 us  [swapped(): return lax.ppermute(block, ('zhi', 'core'), pairs)]
    unnamed x22 -> x12, local copies, waits for them, and re-layouts: 2.73 us -> 0.02 us
    ppermute x8, starting transfers between devices: 32.7 us -> 34.8 us  [turned(): return lax.ppermute(block, ('zhi', 'core', 'y', 'zlo'), pairs)]
    pallas_call x2, Pallas kernels: 3.59 us -> 2.05 us  [the longest x1 1.98 us: pick(): call(pick_kernel, 'pick', grid=(2,), out_shape=jax.ShapeDtypeStruct((NY *...]
  transfers between devices with their start and end apart: 17 -> 17, of which waited for: 8 -> 9; matrix products, arithmetic and copies ran while one was open for 0% -> 0% of each run, Pallas kernels for 3% -> 3%
where the time goes in v7:
time: 140 us; the launch traced here: 139 us
  starting transfers between devices  66.7 us (48%)
  waiting for transfers between devices  59.5 us (42%)
  Pallas kernels  11.1 us (8%)
    ppermute x8, starting transfers between devices, turned(): return lax.ppermute(block, ('zhi', 'core', 'y', 'zlo'), pairs)  34.8 us
    ppermute x8, waiting for transfers between devices, turned(): return lax.ppermute(block, ('zhi', 'core', 'y', 'zlo'), pairs)  22.6 us
    all_to_all x3, waiting for transfers between devices, exchange(): return lax.all_to_all(block, axes, 0, 0, tiled=True)  21.4 us
    all_to_all x3, starting transfers between devices, exchange(): return lax.all_to_all(block, axes, 0, 0, tiled=True)  20.2 us
    ppermute x6, waiting for transfers between devices, swapped(): return lax.ppermute(block, ('zhi', 'core'), pairs)  15.5 us
    ppermute x6, starting transfers between devices, swapped(): return lax.ppermute(block, ('zhi', 'core'), pairs)  11.7 us
  transfers between devices with their start and end apart: 17, of which 9 were waited for; matrix products, arithmetic and copies ran while one was open for 0% of the time, Pallas kernels for 3%

profile of v7, /device:TPU:80, one launch (start us, length us, event | category | flops | bytes accessed | tf_op | source)
XLA Modules:
  0.0 139.4 jit_solution(16507744758978474289)
XLA Ops:
  1.3 0.6 broadcast_in_dim.15
  1.9 7.3 %all-to-all-start = ((s32[16,1,128]{2,1,0:T(1,128)}), s32[16,1,128]{2,1,0:T(1,128)S(1)}, u32[]{:S(2)}, u32[]{:S(2)}) async-start(s32[16,1,128]{2,1,0:T(1,128)} %broadcast_in_dim.15), calls=%async_computation | async-start | bytes 16384 | tf_op jit(solution)/shard_map/all_to_all | solution.py:346
  9.2 1.6 %prep.1 = bf16[208,256]{1,0:T(8,128)(2,1)} custom-call(s32[1]{0:T(128)S(6)} %add.11.at, bf16[48,256]{1,0:T(8,128)(2,1)} %bitcast.30, bf16[4,48,256]{2,1,0:T(8,128)(2,1)} %bitcast.28, bf16[1,48]{1,0:T(2,128)(2,1)} %sb.1, bf16[4,48]{1,0:T(4,128)(2,1)} %bitcast.32), custom_call_target="tpu_custom_call" | custom-call | flops 99999997952 | bytes 1000000000 | tf_op jit(solution)/shard_map/prep/pallas_call | solution.py:56
  10.8 3.6 %all-to-all-done = s32[16,1,128]{2,1,0:T(1,128)S(1)} async-done(((s32[16,1,128]{2,1,0:T(1,128)}), s32[16,1,128]{2,1,0:T(1,128)S(1)}, u32[]{:S(2)}, u32[]{:S(2)}) %all-to-all-start) | async-done | bytes 8224 | tf_op jit(solution)/shard_map/all_to_all | solution.py:346
  14.4 6.7 %collective-permute-start.3 = (bf16[208,256]{1,0:T(8,128)(2,1)}, bf16[208,256]{1,0:T(8,128)(2,1)S(1)}, u32[]{:S(2)}, u32[]{:S(2)}) collective-permute-start(bf16[208,256]{1,0:T(8,128)(2,1)} %prep.1), channel_id=1, source_target_pairs={{0,12},{4,0},{8,4},{12,8},{16,76},{20,64},{24,68},{28,72},{32,140}... | collective-permute-start | bytes 319496 | tf_op jit(solution)/shard_map/ppermute | solution.py:356
  21.1 0.3 collective-permute-start.2
  21.4 6.7 %collective-permute-start.1 = (bf16[208,256]{1,0:T(8,128)(2,1)}, bf16[208,256]{1,0:T(8,128)(2,1)S(1)}, u32[]{:S(2)}, u32[]{:S(2)}) collective-permute-start(bf16[208,256]{1,0:T(8,128)(2,1)} %prep.1), channel_id=1, source_target_pairs={{0,4},{4,8},{8,12},{12,0},{16,68},{20,72},{24,76},{28,64},{32,132}... | collective-permute-start | bytes 319496 | tf_op jit(solution)/shard_map/ppermute | solution.py:356
  28.1 2.8 %collective-permute-start = (bf16[208,256]{1,0:T(8,128)(2,1)}, bf16[208,256]{1,0:T(8,128)(2,1)S(1)}, u32[]{:S(2)}, u32[]{:S(2)}) collective-permute-start(bf16[208,256]{1,0:T(8,128)(2,1)} %prep.1), channel_id=1, source_target_pairs={{0,0},{4,4},{8,8},{12,12},{16,64},{20,68},{24,72},{28,76},{32,128}... | collective-permute-start | bytes 319496 | tf_op jit(solution)/shard_map/ppermute | solution.py:356
  30.9 0.4 collective-permute-done.3.refs_3_
  31.4 7.2 %collective-permute-done.2.refs_2_ = bf16[208,256]{1,0:T(8,128)(2,1)S(1)} collective-permute-done((bf16[208,256]{1,0:T(8,128)(2,1)}, bf16[208,256]{1,0:T(8,128)(2,1)S(1)}, u32[]{:S(2)}, u32[]{:S(2)}) %collective-permute-start.2) | collective-permute-done | bytes 106528 | tf_op jit(solution)/shard_map/ppermute | solution.py:356
  38.6 0.0 collective-permute-done.1.refs_1_
  38.6 3.7 %collective-permute-done.refs_0_ = bf16[208,256]{1,0:T(8,128)(2,1)S(1)} collective-permute-done((bf16[208,256]{1,0:T(8,128)(2,1)}, bf16[208,256]{1,0:T(8,128)(2,1)S(1)}, u32[]{:S(2)}, u32[]{:S(2)}) %collective-permute-start) | collective-permute-done | bytes 106528 | tf_op jit(solution)/shard_map/ppermute | solution.py:356
  42.3 2.0 %pick.1 = bf16[16,208,256]{2,1,0:T(8,128)(2,1)} custom-call(s32[16,128]{1,0:T(8,128)S(1)} %bitcast.26, s32[1]{0:T(128)} %bitcast.3.z, bf16[208,256]{1,0:T(8,128)(2,1)S(1)} %collective-permute-done.refs_0_, bf16[208,256]{1,0:T(8,128)(2,1)S(1)} %collective-permute-done.1.refs_1_, bf16[208,256]{1,0:T(8,128)(2,1)S(1)} %collective-permute-done.2.refs_2_, ...), custom_call_target="tpu_custom_call" | custom-call | flops 99999997952 | bytes 1000000000 | tf_op jit(solution)/shard_map/pick/pallas_call | solution.py:83
  44.3 0.0 copy-done.2
  44.3 5.6 %all-to-all-start.1 = ((bf16[16,208,256]{2,1,0:T(8,128)(2,1)}), bf16[16,208,256]{2,1,0:T(8,128)(2,1)S(1)}, u32[]{:S(2)}, u32[]{:S(2)}) async-start(bf16[16,208,256]{2,1,0:T(8,128)(2,1)} %pick.1), calls=%async_computation.1 | async-start | bytes 3407872 | tf_op jit(solution)/shard_map/all_to_all | solution.py:346
  49.9 0.0 copy-done
  49.9 0.0 copy-start.1
  50.0 0.1 collective-permute-start.4
  50.1 1.4 collective-permute-start.5
  51.5 4.4 %collective-permute-start.6 = (bf16[128,768]{1,0:T(8,128)(2,1)S(1)}, bf16[128,768]{1,0:T(8,128)(2,1)S(1)}, u32[]{:S(2)}, u32[]{:S(2)}) collective-permute-start(bf16[128,768]{1,0:T(8,128)(2,1)S(1)} %get-tuple-element.28), channel_id=1, source_target_pairs={{0,192},{64,128},{128,64},{192,0},{1,193},{65,129},{129,65},{193,1... | collective-permute-start | bytes 589832 | tf_op jit(solution)/shard_map/ppermute | solution.py:361
  55.9 0.0 collective-permute-done.4.other1
  55.9 8.9 %collective-permute-done.5.other2 = bf16[128,768]{1,0:T(8,128)(2,1)S(1)} collective-permute-done((bf16[128,768]{1,0:T(8,128)(2,1)S(1)}, bf16[128,768]{1,0:T(8,128)(2,1)S(1)}, u32[]{:S(2)}, u32[]{:S(2)}) %collective-permute-start.5) | collective-permute-done | bytes 196640 | tf_op jit(solution)/shard_map/ppermute | solution.py:361
  64.8 6.6 %collective-permute-done.6.other3 = bf16[128,768]{1,0:T(8,128)(2,1)S(1)} collective-permute-done((bf16[128,768]{1,0:T(8,128)(2,1)S(1)}, bf16[128,768]{1,0:T(8,128)(2,1)S(1)}, u32[]{:S(2)}, u32[]{:S(2)}) %collective-permute-start.6) | collective-permute-done | bytes 196640 | tf_op jit(solution)/shard_map/ppermute | solution.py:361
  71.4 0.0 copy-done.1
  71.4 0.1 gather.1
  71.5 0.0 all-to-all-done.1.got
  71.5 1.2 slopes.1
  72.6 2.8 %grads.1 = (bf16[4,128,768]{2,1,0:T(8,128)(2,1)S(1)}, bf16[16,208,256]{2,1,0:T(8,128)(2,1)}) custom-call(s32[1]{0:T(128)} %bitcast.s, bf16[128,768]{1,0:T(8,128)(2,1)S(1)} %get-tuple-element.29.top, f32[4,128,768]{2,1,0:T(8,128)S(1)} %get-tuple-element.31.slope, bf16[4,768,256]{2,1,0:T(8,128)(2,1)S(1)} %get-tuple-element.32.kernel, ...), custom_call_target="tpu_custom_call" | custom-call | flops 99999997952 | bytes 1000000000 | tf_op jit(solution)/shard_map/grads/pallas_call | solution.py:213
  75.4 7.4 %all-to-all-start.2 = ((bf16[16,208,256]{2,1,0:T(8,128)(2,1)}), bf16[16,208,256]{2,1,0:T(8,128)(2,1)S(1)}, u32[]{:S(2)}, u32[]{:S(2)}) async-start(bf16[16,208,256]{2,1,0:T(8,128)(2,1)} %get-tuple-element.34), calls=%async_computation.2 | async-start | bytes 3407872 | tf_op jit(solution)/shard_map/all_to_all | solution.py:346
  82.8 0.1 slice_bitcast_fusion
  82.8 1.8 %collective-permute-start.9 = (bf16[128,768]{1,0:T(8,128)(2,1)S(1)}, bf16[128,768]{1,0:T(8,128)(2,1)S(1)}, u32[]{:S(2)}, u32[]{:S(2)}) collective-permute-start(bf16[128,768]{1,0:T(8,128)(2,1)S(1)} %get-tuple-element.43), channel_id=1, source_target_pairs={{0,192},{64,128},{128,64},{192,0},{1,193},{65,129},{129,65},{193,1... | collective-permute-start | bytes 589832 | tf_op jit(solution)/shard_map/ppermute | solution.py:361
  84.7 3.1 %collective-permute-start.8 = (bf16[128,768]{1,0:T(8,128)(2,1)S(1)}, bf16[128,768]{1,0:T(8,128)(2,1)S(1)}, u32[]{:S(2)}, u32[]{:S(2)}) collective-permute-start(bf16[128,768]{1,0:T(8,128)(2,1)S(1)} %get-tuple-element.44), channel_id=1, source_target_pairs={{0,128},{64,192},{128,0},{192,64},{1,129},{65,193},{129,1},{193,65... | collective-permute-start | bytes 589832 | tf_op jit(solution)/shard_map/ppermute | solution.py:361
  87.8 0.9 collective-permute-start.7
  88.7 17.8 %all-to-all-done.2.got = bf16[16,208,256]{2,1,0:T(8,128)(2,1)S(1)} async-done(((bf16[16,208,256]{2,1,0:T(8,128)(2,1)}), bf16[16,208,256]{2,1,0:T(8,128)(2,1)S(1)}, u32[]{:S(2)}, u32[]{:S(2)}) %all-to-all-start.2) | async-done | bytes 1703968 | tf_op jit(solution)/shard_map/all_to_all | solution.py:346
  106.5 1.2 merge.1
  107.7 3.5 %collective-permute-start.10 = (bf16[208,256]{1,0:T(8,128)(2,1)S(1)}, bf16[208,256]{1,0:T(8,128)(2,1)S(1)}, u32[]{:S(2)}, u32[]{:S(2)}) collective-permute-start(bf16[208,256]{1,0:T(8,128)(2,1)S(1)} %get-tuple-element.35), channel_id=1, source_target_pairs={{0,0},{4,4},{8,8},{12,12},{16,64},{20,68},{24,72},{28,76},{32,128}... | collective-permute-start | bytes 319496 | tf_op jit(solution)/shard_map/ppermute | solution.py:356
  111.2 0.3 collective-permute-start.11
  111.5 0.0 collective-permute-done.9.other3
  111.5 9.9 %collective-permute-start.12 = (bf16[208,256]{1,0:T(8,128)(2,1)S(1)}, bf16[208,256]{1,0:T(8,128)(2,1)S(1)}, u32[]{:S(2)}, u32[]{:S(2)}) collective-permute-start(bf16[208,256]{1,0:T(8,128)(2,1)S(1)} %get-tuple-element.37), channel_id=1, source_target_pairs={{0,8},{4,12},{8,0},{12,4},{16,72},{20,76},{24,64},{28,68},{32,136}... | collective-permute-start | bytes 319496 | tf_op jit(solution)/shard_map/ppermute | solution.py:356
  121.4 0.0 collective-permute-done.8.other2
  121.4 4.6 %collective-permute-start.13 = (bf16[208,256]{1,0:T(8,128)(2,1)S(1)}, bf16[208,256]{1,0:T(8,128)(2,1)S(1)}, u32[]{:S(2)}, u32[]{:S(2)}) collective-permute-start(bf16[208,256]{1,0:T(8,128)(2,1)S(1)} %get-tuple-element.38), channel_id=1, source_target_pairs={{0,12},{4,0},{8,4},{12,8},{16,76},{20,64},{24,68},{28,72},{32,140}... | collective-permute-start | bytes 319496 | tf_op jit(solution)/shard_map/ppermute | solution.py:356
  126.0 0.0 collective-permute-done.7.other1
  126.0 1.5 %join.1 = bf16[128,3072]{1,0:T(8,128)(2,1)} custom-call(s32[1]{0:T(128)} %bitcast.s, bf16[128,768]{1,0:T(8,128)(2,1)S(1)} %get-tuple-element.46.own, bf16[128,768]{1,0:T(8,128)(2,1)S(1)} %collective-permute-done.7.other1, bf16[128,768]{1,0:T(8,128)(2,1)S(1)} %collective-permute-done.8.other2, bf16[128,768]{1,0:T(8,128)(2,1)S(1)} %collective-permute-done.9.other3), custom_call_target="tpu_custom_call" | custom-call | flops 99999997952 | bytes 1000000000 | tf_op jit(solution)/shard_map/join/pallas_call | solution.py:247
  127.5 0.0 collective-permute-done.10.refs_0_
  127.5 0.0 collective-permute-done.11.refs_1_
  127.5 5.7 %collective-permute-done.12.refs_2_ = bf16[208,256]{1,0:T(8,128)(2,1)S(1)} collective-permute-done((bf16[208,256]{1,0:T(8,128)(2,1)S(1)}, bf16[208,256]{1,0:T(8,128)(2,1)S(1)}, u32[]{:S(2)}, u32[]{:S(2)}) %collective-permute-start.12) | collective-permute-done | bytes 106528 | tf_op jit(solution)/shard_map/ppermute | solution.py:356
  133.2 5.5 %collective-permute-done.13.refs_3_ = bf16[208,256]{1,0:T(8,128)(2,1)S(1)} collective-permute-done((bf16[208,256]{1,0:T(8,128)(2,1)S(1)}, bf16[208,256]{1,0:T(8,128)(2,1)S(1)}, u32[]{:S(2)}, u32[]{:S(2)}) %collective-permute-start.13) | collective-permute-done | bytes 106528 | tf_op jit(solution)/shard_map/ppermute | solution.py:356
  138.7 0.8 finish.1
  (9 shorter events, 0.1 us)
Async XLA Ops:
  1.9 12.5 %all-to-all-start = ((s32[16,1,128]{2,1,0:T(1,128)}), s32[16,1,128]{2,1,0:T(1,128)S(1)}, u32[]{:S(2)}, u32[]{:S(2)}) async-start(s32[16,1,128]{2,1,0:T(1,128)} %broadcast_in_dim.15), calls=%async_computation | async-start | bytes 16384 | tf_op jit(solution)/shard_map/all_to_all | solution.py:346
  14.4 29.9 %copy-start.2 = (s32[16,1,128]{2,1,0:T(1,128)}, s32[16,1,128]{2,1,0:T(1,128)S(1)}, u32[]{:S(2)}) copy-start(s32[16,1,128]{2,1,0:T(1,128)S(1)} %all-to-all-done) | copy-start | bytes 24580
  14.4 17.0 %collective-permute-start.3 = (bf16[208,256]{1,0:T(8,128)(2,1)}, bf16[208,256]{1,0:T(8,128)(2,1)S(1)}, u32[]{:S(2)}, u32[]{:S(2)}) collective-permute-start(bf16[208,256]{1,0:T(8,128)(2,1)} %prep.1), channel_id=1, source_target_pairs={{0,12},{4,0},{8,4},{12,8},{16,76},{20,64},{24,68},{28,72},{32,140}... | collective-permute-start | bytes 319496 | tf_op jit(solution)/shard_map/ppermute | solution.py:356
  21.1 17.5 %collective-permute-start.2 = (bf16[208,256]{1,0:T(8,128)(2,1)}, bf16[208,256]{1,0:T(8,128)(2,1)S(1)}, u32[]{:S(2)}, u32[]{:S(2)}) collective-permute-start(bf16[208,256]{1,0:T(8,128)(2,1)} %prep.1), channel_id=1, source_target_pairs={{0,8},{4,12},{8,0},{12,4},{16,72},{20,76},{24,64},{28,68},{32,136}... | collective-permute-start | bytes 319496 | tf_op jit(solution)/shard_map/ppermute | solution.py:356
  21.4 17.2 %collective-permute-start.1 = (bf16[208,256]{1,0:T(8,128)(2,1)}, bf16[208,256]{1,0:T(8,128)(2,1)S(1)}, u32[]{:S(2)}, u32[]{:S(2)}) collective-permute-start(bf16[208,256]{1,0:T(8,128)(2,1)} %prep.1), channel_id=1, source_target_pairs={{0,4},{4,8},{8,12},{12,0},{16,68},{20,72},{24,76},{28,64},{32,132}... | collective-permute-start | bytes 319496 | tf_op jit(solution)/shard_map/ppermute | solution.py:356
  28.1 14.2 %collective-permute-start = (bf16[208,256]{1,0:T(8,128)(2,1)}, bf16[208,256]{1,0:T(8,128)(2,1)S(1)}, u32[]{:S(2)}, u32[]{:S(2)}) collective-permute-start(bf16[208,256]{1,0:T(8,128)(2,1)} %prep.1), channel_id=1, source_target_pairs={{0,0},{4,4},{8,8},{12,12},{16,64},{20,68},{24,72},{28,76},{32,128}... | collective-permute-start | bytes 319496 | tf_op jit(solution)/shard_map/ppermute | solution.py:356
  44.3 5.6 %copy-start = (bf16[1,128,3072]{2,1,0:T(8,128)(2,1)S(1)}, bf16[1,128,3072]{2,1,0:T(8,128)(2,1)}, u32[]{:S(2)}) copy-start(bf16[1,128,3072]{2,1,0:T(8,128)(2,1)} %param.7) | copy-start | bytes 2359300
  44.3 27.1 %all-to-all-start.1 = ((bf16[16,208,256]{2,1,0:T(8,128)(2,1)}), bf16[16,208,256]{2,1,0:T(8,128)(2,1)S(1)}, u32[]{:S(2)}, u32[]{:S(2)}) async-start(bf16[16,208,256]{2,1,0:T(8,128)(2,1)} %pick.1), calls=%async_computation.1 | async-start | bytes 3407872 | tf_op jit(solution)/shard_map/all_to_all | solution.py:346
  49.9 21.5 %copy-start.1 = (bf16[128,3072]{1,0:T(8,128)(2,1)S(1)}, bf16[128,3072]{1,0:T(8,128)(2,1)}, u32[]{:S(2)}) copy-start(bf16[128,3072]{1,0:T(8,128)(2,1)} %cotangent.1) | copy-start | bytes 2359300
  50.0 5.9 %collective-permute-start.4 = (bf16[128,768]{1,0:T(8,128)(2,1)S(1)}, bf16[128,768]{1,0:T(8,128)(2,1)S(1)}, u32[]{:S(2)}, u32[]{:S(2)}) collective-permute-start(bf16[128,768]{1,0:T(8,128)(2,1)S(1)} %get-tuple-element.26), channel_id=1, source_target_pairs={{0,64},{64,0},{128,192},{192,128},{1,65},{65,1},{129,193},{193,129... | collective-permute-start | bytes 589832 | tf_op jit(solution)/shard_map/ppermute | solution.py:361
  50.1 14.7 %collective-permute-start.5 = (bf16[128,768]{1,0:T(8,128)(2,1)S(1)}, bf16[128,768]{1,0:T(8,128)(2,1)S(1)}, u32[]{:S(2)}, u32[]{:S(2)}) collective-permute-start(bf16[128,768]{1,0:T(8,128)(2,1)S(1)} %get-tuple-element.27), channel_id=1, source_target_pairs={{0,128},{64,192},{128,0},{192,64},{1,129},{65,193},{129,1},{193,65... | collective-permute-start | bytes 589832 | tf_op jit(solution)/shard_map/ppermute | solution.py:361
  51.5 19.9 %collective-permute-start.6 = (bf16[128,768]{1,0:T(8,128)(2,1)S(1)}, bf16[128,768]{1,0:T(8,128)(2,1)S(1)}, u32[]{:S(2)}, u32[]{:S(2)}) collective-permute-start(bf16[128,768]{1,0:T(8,128)(2,1)S(1)} %get-tuple-element.28), channel_id=1, source_target_pairs={{0,192},{64,128},{128,64},{192,0},{1,193},{65,129},{129,65},{193,1... | collective-permute-start | bytes 589832 | tf_op jit(solution)/shard_map/ppermute | solution.py:361
  75.4 31.1 %copy-start.3 = (s32[16,1,128]{2,1,0:T(1,128)S(1)}, s32[16,1,128]{2,1,0:T(1,128)}, u32[]{:S(2)}) copy-start(s32[16,1,128]{2,1,0:T(1,128)} %copy-done.2) | copy-start | bytes 24580
  75.4 31.1 %all-to-all-start.2 = ((bf16[16,208,256]{2,1,0:T(8,128)(2,1)}), bf16[16,208,256]{2,1,0:T(8,128)(2,1)S(1)}, u32[]{:S(2)}, u32[]{:S(2)}) async-start(bf16[16,208,256]{2,1,0:T(8,128)(2,1)} %get-tuple-element.34), calls=%async_computation.2 | async-start | bytes 3407872 | tf_op jit(solution)/shard_map/all_to_all | solution.py:346
  82.8 28.6 %collective-permute-start.9 = (bf16[128,768]{1,0:T(8,128)(2,1)S(1)}, bf16[128,768]{1,0:T(8,128)(2,1)S(1)}, u32[]{:S(2)}, u32[]{:S(2)}) collective-permute-start(bf16[128,768]{1,0:T(8,128)(2,1)S(1)} %get-tuple-element.43), channel_id=1, source_target_pairs={{0,192},{64,128},{128,64},{192,0},{1,193},{65,129},{129,65},{193,1... | collective-permute-start | bytes 589832 | tf_op jit(solution)/shard_map/ppermute | solution.py:361
  84.7 36.7 %collective-permute-start.8 = (bf16[128,768]{1,0:T(8,128)(2,1)S(1)}, bf16[128,768]{1,0:T(8,128)(2,1)S(1)}, u32[]{:S(2)}, u32[]{:S(2)}) collective-permute-start(bf16[128,768]{1,0:T(8,128)(2,1)S(1)} %get-tuple-element.44), channel_id=1, source_target_pairs={{0,128},{64,192},{128,0},{192,64},{1,129},{65,193},{129,1},{193,65... | collective-permute-start | bytes 589832 | tf_op jit(solution)/shard_map/ppermute | solution.py:361
  87.8 38.2 %collective-permute-start.7 = (bf16[128,768]{1,0:T(8,128)(2,1)S(1)}, bf16[128,768]{1,0:T(8,128)(2,1)S(1)}, u32[]{:S(2)}, u32[]{:S(2)}) collective-permute-start(bf16[128,768]{1,0:T(8,128)(2,1)S(1)} %get-tuple-element.45), channel_id=1, source_target_pairs={{0,64},{64,0},{128,192},{192,128},{1,65},{65,1},{129,193},{193,129... | collective-permute-start | bytes 589832 | tf_op jit(solution)/shard_map/ppermute | solution.py:361
  107.7 19.8 %collective-permute-start.10 = (bf16[208,256]{1,0:T(8,128)(2,1)S(1)}, bf16[208,256]{1,0:T(8,128)(2,1)S(1)}, u32[]{:S(2)}, u32[]{:S(2)}) collective-permute-start(bf16[208,256]{1,0:T(8,128)(2,1)S(1)} %get-tuple-element.35), channel_id=1, source_target_pairs={{0,0},{4,4},{8,8},{12,12},{16,64},{20,68},{24,72},{28,76},{32,128}... | collective-permute-start | bytes 319496 | tf_op jit(solution)/shard_map/ppermute | solution.py:356
  111.2 16.3 %collective-permute-start.11 = (bf16[208,256]{1,0:T(8,128)(2,1)S(1)}, bf16[208,256]{1,0:T(8,128)(2,1)S(1)}, u32[]{:S(2)}, u32[]{:S(2)}) collective-permute-start(bf16[208,256]{1,0:T(8,128)(2,1)S(1)} %get-tuple-element.36), channel_id=1, source_target_pairs={{0,4},{4,8},{8,12},{12,0},{16,68},{20,72},{24,76},{28,64},{32,132}... | collective-permute-start | bytes 319496 | tf_op jit(solution)/shard_map/ppermute | solution.py:356
  111.5 21.7 %collective-permute-start.12 = (bf16[208,256]{1,0:T(8,128)(2,1)S(1)}, bf16[208,256]{1,0:T(8,128)(2,1)S(1)}, u32[]{:S(2)}, u32[]{:S(2)}) collective-permute-start(bf16[208,256]{1,0:T(8,128)(2,1)S(1)} %get-tuple-element.37), channel_id=1, source_target_pairs={{0,8},{4,12},{8,0},{12,4},{16,72},{20,76},{24,64},{28,68},{32,136}... | collective-permute-start | bytes 319496 | tf_op jit(solution)/shard_map/ppermute | solution.py:356
  121.4 17.3 %collective-permute-start.13 = (bf16[208,256]{1,0:T(8,128)(2,1)S(1)}, bf16[208,256]{1,0:T(8,128)(2,1)S(1)}, u32[]{:S(2)}, u32[]{:S(2)}) collective-permute-start(bf16[208,256]{1,0:T(8,128)(2,1)S(1)} %get-tuple-element.38), channel_id=1, source_target_pairs={{0,12},{4,0},{8,4},{12,8},{16,76},{20,64},{24,68},{28,72},{32,140}... | collective-permute-start | bytes 319496 | tf_op jit(solution)/shard_map/ppermute | solution.py:356
  126.0 12.7 %copy-start.4 = (bf16[1,4,48,256]{3,2,1,0:T(8,128)(2,1)S(1)}, bf16[1,4,48,256]{3,2,1,0:T(8,128)(2,1)}, u32[]{:S(2)}) copy-start(bf16[1,4,48,256]{3,2,1,0:T(8,128)(2,1)} %param.11) | copy-start | bytes 294916
  126.0 12.7 %copy-start.5 = (bf16[1,48,256]{2,1,0:T(8,128)(2,1)S(1)}, bf16[1,48,256]{2,1,0:T(8,128)(2,1)}, u32[]{:S(2)}) copy-start(bf16[1,48,256]{2,1,0:T(8,128)(2,1)} %param.10) | copy-start | bytes 73732

commit v8 on v7

--- a/solution.py
+++ b/solution.py
@@ -214,7 +214,7 @@
         grads_kernel,
         "grads",
         out_shape=(
-            jax.ShapeDtypeStruct((SECTIONS, ROWS, SLAB), BF),
+            pltpu.HBM((SECTIONS, ROWS, SLAB), BF),
             jax.ShapeDtypeStruct((SECTIONS * NX, BLOCK, GS), BF),
         ),
         grid_spec=pltpu.PrefetchScalarGridSpec(
@@ -235,6 +235,21 @@
     )(section, top, slope, kernel, x)
 
 
+def split_kernel(out, *parts):
+    for k in range(SECTIONS):
+        parts[k][...] = out[k]
+
+
+def split(out):
+    return call(
+        split_kernel,
+        "split",
+        out_shape=(jax.ShapeDtypeStruct((ROWS, SLAB), BF),) * SECTIONS,
+        in_specs=[VMEM],
+        out_specs=(VMEM,) * SECTIONS,
+    )(out)
+
+
 def join_kernel(s, own, other1, other2, other3, out):
     for k, part in enumerate((own, other1, other2, other3)):
 
@@ -247,6 +262,7 @@
     return call(
         join_kernel,
         "join",
+        weight=0,
         out_shape=jax.ShapeDtypeStruct((ROWS, D), BF),
         grid_spec=pltpu.PrefetchScalarGridSpec(
             num_scalar_prefetch=1,
@@ -301,21 +317,30 @@
     )(ids, z, got)
 
 
-def finish_kernel(at, *refs):
-    got, (sw, dw, d_shared, d_domain, b_shared, b_domain, wide) = refs[:NZ], refs[NZ:]
+def total_kernel(a, b, c, d, out):
+    both = a[...].astype(F32) + b[...].astype(F32)
+    out[...] = (both + c[...].astype(F32) + d[...].astype(F32)).astype(BF)
+
+
+def total(got):
+    return call(
+        total_kernel,
+        "total",
+        out_shape=jax.ShapeDtypeStruct((BLOCK, GS), BF),
+        in_specs=[VMEM] * NZ,
+        out_specs=VMEM,
+    )(*got)
+
+
+def finish_kernel(at, got, sw, dw, d_shared, d_domain, b_shared, b_domain, wide):
     shared = sw[...].astype(F32)
     summed = jnp.zeros((SHARD, GS), F32)
     for k in range(DOMAINS):
-        part = slice(k * SHARD, (k + 1) * SHARD)
-        share = got[0][part, :].astype(F32)
-        for z in range(1, NZ):
-            share = share + got[z][part, :].astype(F32)
+        share = got[k * SHARD : (k + 1) * SHARD, :].astype(F32)
         summed = summed + share * dw[k].astype(F32)
         d_domain[k] = share * shared
     d_shared[...] = summed
-    tile = got[0][PIECE:, :].astype(F32)
-    for z in range(1, NZ):
-        tile = tile + got[z][PIECE:, :].astype(F32)
+    tile = got[PIECE:, :].astype(F32)
     wide[...] = jnp.zeros_like(wide)
     for k in range(DOMAINS):
         for q in range(SG):
@@ -336,10 +361,10 @@
             jax.ShapeDtypeStruct((1, SHARD), F32),
             jax.ShapeDtypeStruct((DOMAINS, SHARD), F32),
         ),
-        in_specs=[SMEM] + [VMEM] * (NZ + 2),
+        in_specs=[SMEM, VMEM, VMEM, VMEM],
         out_specs=(VMEM,) * 4,
         scratch_shapes=[pltpu.VMEM((8, SLAB), F32)],
-    )(at, *got, sw, dw)
+    )(at, got, sw, dw)
 
 
 def exchange(block, axes):
@@ -347,13 +372,12 @@
 
 
 def turned(block, k):
-    pairs = []
-    for section in range(SECTIONS):
-        for y in range(NY):
-            for z in range(NZ):
-                to = (y * NY + section) * NZ + (z + k) % NZ
-                pairs.append(((section * NY + y) * NZ + z, to))
-    return lax.ppermute(block, ("zhi", "core", "y", "zlo"), pairs)
+    return lax.ppermute(block, "zlo", [(z, (z + k) % NZ) for z in range(NZ)])
+
+
+def crossed(block):
+    pairs = [(a * NY + b, b * NY + a) for a in range(SECTIONS) for b in range(NY)]
+    return lax.ppermute(block, ("zhi", "core", "y"), pairs)
 
 
 def swapped(block, k):
@@ -372,12 +396,13 @@
     z = jnp.reshape(lax.axis_index("zlo"), (1,))
     at = PIECE * z + SHARD * lax.axis_index("x")
 
+    mine = prep(at, sw, dw, shared_bias, domain_bias[0])
+    (ids,) = after(mine, domain_ids)
     plane_ids = exchange(
-        jnp.broadcast_to(domain_ids[0], (NY * NX, 1, 128)), ("y", "x")
+        jnp.broadcast_to(ids[0], (NY * NX, 1, 128)), ("y", "x")
     ).reshape(NY * NX, 128)
-    mine = prep(at, sw, dw, shared_bias, domain_bias[0])
-    (mine,) = after(plane_ids, mine)
-    held = [turned(mine, k) for k in range(NZ)]
+    (mine,) = after(plane_ids, crossed(mine))
+    held = [mine] + [turned(mine, k) for k in range(1, NZ)]
     picked = pick(plane_ids, z, held)
     got = exchange(picked, ("y", "x"))
     (late,) = after(picked, stash)
@@ -388,9 +413,11 @@
     slope, kernel = slopes(domain_ids, got, x)
     out, send = grads(section, top, slope, kernel, x)
     got = exchange(send, ("y", "x"))
-    d_inputs = join(section, out[0], [swapped(out[k], k) for k in range(1, SECTIONS)])
+    parts = split(out)
+    d_inputs = join(section, parts[0], [swapped(parts[k], k) for k in range(1, SECTIONS)])
+    (got,) = after(d_inputs, got)
     merged = merge(plane_ids, z, got)
-    final = [turned(merged[k], k) for k in range(NZ)]
+    final = crossed(total([merged[0]] + [turned(merged[k], k) for k in range(1, NZ)]))
     d_shared, d_domain, b_shared, b_domain = finish(at, final, sw, dw)
     return (d_inputs[None], d_shared[None], d_domain[None], b_shared, b_domain[None])
 

time: 140 us -> 130 us (0.929)
  the two profiles are of different devices: /device:TPU:80 before, /device:TPU:59 now
where the time goes in v8:
time: 130 us
  waiting for transfers between devices  62.9 us (48%)
  starting transfers between devices  44.1 us (34%)
  Pallas kernels  11.2 us (9%)
  blocking collectives  10 us (8%)
  between operations  1.4 us (1%)
    ppermute x6, waiting for transfers between devices, swapped(): return lax.ppermute(block, ('zhi', 'core'), pairs)  35.1 us
    ppermute x6, waiting for transfers between devices, turned(): return lax.ppermute(block, 'zlo', [(z, (z + k) % NZ) for z in range(NZ)])  16.4 us
    all_to_all x2, starting transfers between devices, exchange(): return lax.all_to_all(block, axes, 0, 0, tiled=True)  13.2 us
    ppermute x6, starting transfers between devices, swapped(): return lax.ppermute(block, ('zhi', 'core'), pairs)  13.2 us
    ppermute x2, starting transfers between devices, crossed(): return lax.ppermute(block, ('zhi', 'core', 'y'), pairs)  12.3 us
    ppermute x2, waiting for transfers between devices, crossed(): return lax.ppermute(block, ('zhi', 'core', 'y'), pairs)  11.4 us
    all_to_all x1, blocking collectives, exchange(): return lax.all_to_all(block, axes, 0, 0, tiled=True)  10 us
    ppermute x6, starting transfers between devices, turned(): return lax.ppermute(block, 'zlo', [(z, (z + k) % NZ) for z in range(NZ)])  5.41 us
  transfers between devices with their start and end apart: 16, of which 10 were waited for; matrix products, arithmetic and copies ran while one was open for 0% of the time, Pallas kernels for 1%

profile of v8, /device:TPU:59, one launch (start us, length us, event | category | flops | bytes accessed | tf_op | source)
XLA Modules:
  0.0 129.6 jit_solution(15162798254967921349)
XLA Ops:
  0.6 1.6 %prep.1 = bf16[208,256]{1,0:T(8,128)(2,1)} custom-call(s32[1]{0:T(128)S(6)} %add.11.at, bf16[48,256]{1,0:T(8,128)(2,1)} %bitcast.22, bf16[4,48,256]{2,1,0:T(8,128)(2,1)} %bitcast.20, bf16[1,48]{1,0:T(2,128)(2,1)} %sb.1, bf16[4,48]{1,0:T(4,128)(2,1)} %bitcast.25), custom_call_target="tpu_custom_call" | custom-call | flops 99999997952 | bytes 1000000000 | tf_op jit(solution)/shard_map/prep/pallas_call | solution.py:56
  2.3 8.6 %collective-permute-start = (bf16[208,256]{1,0:T(8,128)(2,1)}, bf16[208,256]{1,0:T(8,128)(2,1)S(1)}, u32[]{:S(2)}, u32[]{:S(2)}) collective-permute-start(bf16[208,256]{1,0:T(8,128)(2,1)} %prep.1), channel_id=1, source_target_pairs={{0,0},{16,64},{32,128},{48,192},{64,16},{80,80},{96,144},{112,208}... | collective-permute-start | bytes 319496 | tf_op jit(solution)/shard_map/ppermute | solution.py:380
  11.5 10.0 %all_to_all.15 = s32[16,1,128]{2,1,0:T(1,128)S(1)} all-to-all(s32[16,1,128]{2,1,0:T(1,128)S(1)} %broadcast_in_dim.15), channel_id=1, replica_groups=mesh['zhi'=2,'core'=2,'y'=4,'zlo'=4,'x'=4] {'y','x'}, dimensions={0} | all-to-all | bytes 16384 | tf_op jit(solution)/shard_map/all_to_all | solution.py:371
  21.5 0.0 collective-permute-done.refs_0_
  21.5 0.7 collective-permute-start.3
  22.3 1.2 collective-permute-start.2
  23.5 1.6 %collective-permute-start.1 = (bf16[208,256]{1,0:T(8,128)(2,1)S(1)}, bf16[208,256]{1,0:T(8,128)(2,1)S(1)}, u32[]{:S(2)}, u32[]{:S(2)}) collective-permute-start(bf16[208,256]{1,0:T(8,128)(2,1)S(1)} %collective-permute-done.refs_0_), channel_id=1, source_target_pairs={{0,4},{4,8},{8,12},{12,0},{1,5},{5,9},{9,13},{13,1},{2,6},{6,10},{... | collective-permute-start | bytes 319496 | tf_op jit(solution)/shard_map/ppermute | solution.py:375
  25.1 0.0 collective-permute-done.3.refs_3_
  25.1 5.3 %collective-permute-done.2.refs_2_ = bf16[208,256]{1,0:T(8,128)(2,1)S(1)} collective-permute-done((bf16[208,256]{1,0:T(8,128)(2,1)S(1)}, bf16[208,256]{1,0:T(8,128)(2,1)S(1)}, u32[]{:S(2)}, u32[]{:S(2)}) %collective-permute-start.2) | collective-permute-done | bytes 106528 | tf_op jit(solution)/shard_map/ppermute | solution.py:375
  30.4 2.4 %collective-permute-done.1.refs_1_ = bf16[208,256]{1,0:T(8,128)(2,1)S(1)} collective-permute-done((bf16[208,256]{1,0:T(8,128)(2,1)S(1)}, bf16[208,256]{1,0:T(8,128)(2,1)S(1)}, u32[]{:S(2)}, u32[]{:S(2)}) %collective-permute-start.1) | collective-permute-done | bytes 106528 | tf_op jit(solution)/shard_map/ppermute | solution.py:375
  32.8 2.0 %pick.1 = bf16[16,208,256]{2,1,0:T(8,128)(2,1)} custom-call(s32[16,128]{1,0:T(8,128)S(1)} %bitcast.18, s32[1]{0:T(128)} %bitcast.1.z, bf16[208,256]{1,0:T(8,128)(2,1)S(1)} %collective-permute-done.refs_0_, bf16[208,256]{1,0:T(8,128)(2,1)S(1)} %collective-permute-done.1.refs_1_, bf16[208,256]{1,0:T(8,128)(2,1)S(1)} %collective-permute-done.2.refs_2_, ...), custom_call_target="tpu_custom_call" | custom-call | flops 99999997952 | bytes 1000000000 | tf_op jit(solution)/shard_map/pick/pallas_call | solution.py:83
  34.8 0.0 copy-done.2
  34.8 6.4 %all-to-all-start.1 = ((bf16[16,208,256]{2,1,0:T(8,128)(2,1)}), bf16[16,208,256]{2,1,0:T(8,128)(2,1)S(1)}, u32[]{:S(2)}, u32[]{:S(2)}) async-start(bf16[16,208,256]{2,1,0:T(8,128)(2,1)} %pick.1), calls=%async_computation.1 | async-start | bytes 3407872 | tf_op jit(solution)/shard_map/all_to_all | solution.py:371
  41.2 0.0 copy-done
  41.2 0.0 copy-start.1
  41.3 1.0 collective-permute-start.4
  42.3 1.1 collective-permute-start.5
  43.4 4.6 %collective-permute-start.6 = (bf16[128,768]{1,0:T(8,128)(2,1)S(1)}, bf16[128,768]{1,0:T(8,128)(2,1)S(1)}, u32[]{:S(2)}, u32[]{:S(2)}) collective-permute-start(bf16[128,768]{1,0:T(8,128)(2,1)S(1)} %get-tuple-element.35), channel_id=1, source_target_pairs={{0,192},{64,128},{128,64},{192,0},{1,193},{65,129},{129,65},{193,1... | collective-permute-start | bytes 589832 | tf_op jit(solution)/shard_map/ppermute | solution.py:385
  48.0 0.0 collective-permute-done.4.other1
  48.0 11.5 %collective-permute-done.5.other2 = bf16[128,768]{1,0:T(8,128)(2,1)S(1)} collective-permute-done((bf16[128,768]{1,0:T(8,128)(2,1)S(1)}, bf16[128,768]{1,0:T(8,128)(2,1)S(1)}, u32[]{:S(2)}, u32[]{:S(2)}) %collective-permute-start.5) | collective-permute-done | bytes 196640 | tf_op jit(solution)/shard_map/ppermute | solution.py:385
  59.5 6.0 %collective-permute-done.6.other3 = bf16[128,768]{1,0:T(8,128)(2,1)S(1)} collective-permute-done((bf16[128,768]{1,0:T(8,128)(2,1)S(1)}, bf16[128,768]{1,0:T(8,128)(2,1)S(1)}, u32[]{:S(2)}, u32[]{:S(2)}) %collective-permute-start.6) | collective-permute-done | bytes 196640 | tf_op jit(solution)/shard_map/ppermute | solution.py:385
  65.5 0.1 gather.1
  65.6 0.0 all-to-all-done.1.got
  65.6 1.2 slopes.1
  66.8 2.9 %grads.1 = (bf16[4,128,768]{2,1,0:T(8,128)(2,1)}, bf16[16,208,256]{2,1,0:T(8,128)(2,1)}) custom-call(s32[1]{0:T(128)} %bitcast.s, bf16[128,768]{1,0:T(8,128)(2,1)S(1)} %get-tuple-element.36.top, f32[4,128,768]{2,1,0:T(8,128)S(1)} %get-tuple-element.38.slope, bf16[4,768,256]{2,1,0:T(8,128)(2,1)S(1)} %get-tuple-element.39.kernel, ...), custom_call_target="tpu_custom_call" | custom-call | flops 99999997952 | bytes 1000000000 | tf_op jit(solution)/shard_map/grads/pallas_call | solution.py:213
  69.6 6.8 %all-to-all-start.2 = ((bf16[16,208,256]{2,1,0:T(8,128)(2,1)}), bf16[16,208,256]{2,1,0:T(8,128)(2,1)S(1)}, u32[]{:S(2)}, u32[]{:S(2)}) async-start(bf16[16,208,256]{2,1,0:T(8,128)(2,1)} %get-tuple-element.45), calls=%async_computation.2 | async-start | bytes 3407872 | tf_op jit(solution)/shard_map/all_to_all | solution.py:371
  76.4 0.0 copy-start.3
  76.4 0.1 split.1
  76.5 0.9 collective-permute-start.7
  77.4 1.2 collective-permute-start.8
  78.6 4.4 %collective-permute-start.9 = (bf16[128,768]{1,0:T(8,128)(2,1)S(1)}, bf16[128,768]{1,0:T(8,128)(2,1)S(1)}, u32[]{:S(2)}, u32[]{:S(2)}) collective-permute-start(bf16[128,768]{1,0:T(8,128)(2,1)S(1)} %get-tuple-element.44), channel_id=1, source_target_pairs={{0,192},{64,128},{128,64},{192,0},{1,193},{65,129},{129,65},{193,1... | collective-permute-start | bytes 589832 | tf_op jit(solution)/shard_map/ppermute | solution.py:385
  83.0 0.0 collective-permute-done.7.other1
  83.0 13.3 %collective-permute-done.8.other2 = bf16[128,768]{1,0:T(8,128)(2,1)S(1)} collective-permute-done((bf16[128,768]{1,0:T(8,128)(2,1)S(1)}, bf16[128,768]{1,0:T(8,128)(2,1)S(1)}, u32[]{:S(2)}, u32[]{:S(2)}) %collective-permute-start.8) | collective-permute-done | bytes 196640 | tf_op jit(solution)/shard_map/ppermute | solution.py:385
  96.3 4.2 %collective-permute-done.9.other3 = bf16[128,768]{1,0:T(8,128)(2,1)S(1)} collective-permute-done((bf16[128,768]{1,0:T(8,128)(2,1)S(1)}, bf16[128,768]{1,0:T(8,128)(2,1)S(1)}, u32[]{:S(2)}, u32[]{:S(2)}) %collective-permute-start.9) | collective-permute-done | bytes 196640 | tf_op jit(solution)/shard_map/ppermute | solution.py:385
  100.6 1.5 %join.1 = bf16[128,3072]{1,0:T(8,128)(2,1)} custom-call(s32[1]{0:T(128)} %bitcast.s, bf16[128,768]{1,0:T(8,128)(2,1)S(1)} %get-tuple-element.41.own, bf16[128,768]{1,0:T(8,128)(2,1)S(1)} %collective-permute-done.7.other1, bf16[128,768]{1,0:T(8,128)(2,1)S(1)} %collective-permute-done.8.other2, bf16[128,768]{1,0:T(8,128)(2,1)S(1)} %collective-permute-done.9.other3), custom_call_target="tpu_custom_call" | custom-call | tf_op jit(solution)/shard_map/join/pallas_call | solution.py:262
  102.0 0.0 all-to-all-done.2.got
  102.0 1.2 merge.1
  103.2 0.6 collective-permute-start.10
  103.8 0.0 collective-permute-start.11
  103.8 1.3 collective-permute-start.12
  105.1 2.3 %collective-permute-done.10.b = bf16[208,256]{1,0:T(8,128)(2,1)S(1)} collective-permute-done((bf16[208,256]{1,0:T(8,128)(2,1)S(1)}, bf16[208,256]{1,0:T(8,128)(2,1)S(1)}, u32[]{:S(2)}, u32[]{:S(2)}) %collective-permute-start.10) | collective-permute-done | bytes 106528 | tf_op jit(solution)/shard_map/ppermute | solution.py:375
  107.4 5.0 %collective-permute-done.11.c = bf16[208,256]{1,0:T(8,128)(2,1)S(1)} collective-permute-done((bf16[208,256]{1,0:T(8,128)(2,1)S(1)}, bf16[208,256]{1,0:T(8,128)(2,1)S(1)}, u32[]{:S(2)}, u32[]{:S(2)}) %collective-permute-start.11) | collective-permute-done | bytes 106528 | tf_op jit(solution)/shard_map/ppermute | solution.py:375
  112.5 1.3 collective-permute-done.12.d
  113.7 0.1 total.1
  113.8 3.7 %collective-permute-start.13 = (bf16[208,256]{1,0:T(8,128)(2,1)S(1)}, bf16[208,256]{1,0:T(8,128)(2,1)S(1)}, u32[]{:S(2)}, u32[]{:S(2)}) collective-permute-start(bf16[208,256]{1,0:T(8,128)(2,1)S(1)} %total.1), channel_id=1, source_target_pairs={{0,0},{16,64},{32,128},{48,192},{64,16},{80,80},{96,144},{112,208}... | collective-permute-start | bytes 319496 | tf_op jit(solution)/shard_map/ppermute | solution.py:380
  117.5 11.4 %collective-permute-done.13.got = bf16[208,256]{1,0:T(8,128)(2,1)S(1)} collective-permute-done((bf16[208,256]{1,0:T(8,128)(2,1)S(1)}, bf16[208,256]{1,0:T(8,128)(2,1)S(1)}, u32[]{:S(2)}, u32[]{:S(2)}) %collective-permute-start.13) | collective-permute-done | bytes 106528 | tf_op jit(solution)/shard_map/ppermute | solution.py:380
  128.9 0.0 copy-done.4
  128.9 0.7 finish.1
  (11 shorter events, 0.1 us)
Async XLA Ops:
  2.3 19.3 %collective-permute-start = (bf16[208,256]{1,0:T(8,128)(2,1)}, bf16[208,256]{1,0:T(8,128)(2,1)S(1)}, u32[]{:S(2)}, u32[]{:S(2)}) collective-permute-start(bf16[208,256]{1,0:T(8,128)(2,1)} %prep.1), channel_id=1, source_target_pairs={{0,0},{16,64},{32,128},{48,192},{64,16},{80,80},{96,144},{112,208}... | collective-permute-start | bytes 319496 | tf_op jit(solution)/shard_map/ppermute | solution.py:380
  21.5 13.3 %copy-start.2 = (s32[16,1,128]{2,1,0:T(1,128)}, s32[16,1,128]{2,1,0:T(1,128)S(1)}, u32[]{:S(2)}) copy-start(s32[16,1,128]{2,1,0:T(1,128)S(1)} %all_to_all.15) | copy-start | bytes 24580
  21.5 3.6 %collective-permute-start.3 = (bf16[208,256]{1,0:T(8,128)(2,1)S(1)}, bf16[208,256]{1,0:T(8,128)(2,1)S(1)}, u32[]{:S(2)}, u32[]{:S(2)}) collective-permute-start(bf16[208,256]{1,0:T(8,128)(2,1)S(1)} %collective-permute-done.refs_0_), channel_id=1, source_target_pairs={{0,12},{4,0},{8,4},{12,8},{1,13},{5,1},{9,5},{13,9},{2,14},{6,2},{... | collective-permute-start | bytes 319496 | tf_op jit(solution)/shard_map/ppermute | solution.py:375
  22.3 8.2 %collective-permute-start.2 = (bf16[208,256]{1,0:T(8,128)(2,1)S(1)}, bf16[208,256]{1,0:T(8,128)(2,1)S(1)}, u32[]{:S(2)}, u32[]{:S(2)}) collective-permute-start(bf16[208,256]{1,0:T(8,128)(2,1)S(1)} %collective-permute-done.refs_0_), channel_id=1, source_target_pairs={{0,8},{4,12},{8,0},{12,4},{1,9},{5,13},{9,1},{13,5},{2,10},{6,14},... | collective-permute-start | bytes 319496 | tf_op jit(solution)/shard_map/ppermute | solution.py:375
  23.5 9.4 %collective-permute-start.1 = (bf16[208,256]{1,0:T(8,128)(2,1)S(1)}, bf16[208,256]{1,0:T(8,128)(2,1)S(1)}, u32[]{:S(2)}, u32[]{:S(2)}) collective-permute-start(bf16[208,256]{1,0:T(8,128)(2,1)S(1)} %collective-permute-done.refs_0_), channel_id=1, source_target_pairs={{0,4},{4,8},{8,12},{12,0},{1,5},{5,9},{9,13},{13,1},{2,6},{6,10},{... | collective-permute-start | bytes 319496 | tf_op jit(solution)/shard_map/ppermute | solution.py:375
  34.8 6.4 %copy-start = (bf16[1,128,3072]{2,1,0:T(8,128)(2,1)S(1)}, bf16[1,128,3072]{2,1,0:T(8,128)(2,1)}, u32[]{:S(2)}) copy-start(bf16[1,128,3072]{2,1,0:T(8,128)(2,1)} %param.7) | copy-start | bytes 2359300
  34.8 30.8 %all-to-all-start.1 = ((bf16[16,208,256]{2,1,0:T(8,128)(2,1)}), bf16[16,208,256]{2,1,0:T(8,128)(2,1)S(1)}, u32[]{:S(2)}, u32[]{:S(2)}) async-start(bf16[16,208,256]{2,1,0:T(8,128)(2,1)} %pick.1), calls=%async_computation.1 | async-start | bytes 3407872 | tf_op jit(solution)/shard_map/all_to_all | solution.py:371
  41.2 24.3 %copy-start.1 = (bf16[128,3072]{1,0:T(8,128)(2,1)S(1)}, bf16[128,3072]{1,0:T(8,128)(2,1)}, u32[]{:S(2)}) copy-start(bf16[128,3072]{1,0:T(8,128)(2,1)} %cotangent.1) | copy-start | bytes 2359300
  41.3 6.7 %collective-permute-start.4 = (bf16[128,768]{1,0:T(8,128)(2,1)S(1)}, bf16[128,768]{1,0:T(8,128)(2,1)S(1)}, u32[]{:S(2)}, u32[]{:S(2)}) collective-permute-start(bf16[128,768]{1,0:T(8,128)(2,1)S(1)} %get-tuple-element.33), channel_id=1, source_target_pairs={{0,64},{64,0},{128,192},{192,128},{1,65},{65,1},{129,193},{193,129... | collective-permute-start | bytes 589832 | tf_op jit(solution)/shard_map/ppermute | solution.py:385
  42.3 17.2 %collective-permute-start.5 = (bf16[128,768]{1,0:T(8,128)(2,1)S(1)}, bf16[128,768]{1,0:T(8,128)(2,1)S(1)}, u32[]{:S(2)}, u32[]{:S(2)}) collective-permute-start(bf16[128,768]{1,0:T(8,128)(2,1)S(1)} %get-tuple-element.34), channel_id=1, source_target_pairs={{0,128},{64,192},{128,0},{192,64},{1,129},{65,193},{129,1},{193,65... | collective-permute-start | bytes 589832 | tf_op jit(solution)/shard_map/ppermute | solution.py:385
  43.4 22.1 %collective-permute-start.6 = (bf16[128,768]{1,0:T(8,128)(2,1)S(1)}, bf16[128,768]{1,0:T(8,128)(2,1)S(1)}, u32[]{:S(2)}, u32[]{:S(2)}) collective-permute-start(bf16[128,768]{1,0:T(8,128)(2,1)S(1)} %get-tuple-element.35), channel_id=1, source_target_pairs={{0,192},{64,128},{128,64},{192,0},{1,193},{65,129},{129,65},{193,1... | collective-permute-start | bytes 589832 | tf_op jit(solution)/shard_map/ppermute | solution.py:385
  69.6 6.8 %copy-start.6 = (bf16[4,128,768]{2,1,0:T(8,128)(2,1)S(1)}, bf16[4,128,768]{2,1,0:T(8,128)(2,1)}, u32[]{:S(2)}) copy-start(bf16[4,128,768]{2,1,0:T(8,128)(2,1)} %get-tuple-element.40.out) | copy-start | bytes 2359300
  69.6 32.4 %all-to-all-start.2 = ((bf16[16,208,256]{2,1,0:T(8,128)(2,1)}), bf16[16,208,256]{2,1,0:T(8,128)(2,1)S(1)}, u32[]{:S(2)}, u32[]{:S(2)}) async-start(bf16[16,208,256]{2,1,0:T(8,128)(2,1)} %get-tuple-element.45), calls=%async_computation.2 | async-start | bytes 3407872 | tf_op jit(solution)/shard_map/all_to_all | solution.py:371
  76.4 25.6 %copy-start.3 = (s32[16,1,128]{2,1,0:T(1,128)S(1)}, s32[16,1,128]{2,1,0:T(1,128)}, u32[]{:S(2)}) copy-start(s32[16,1,128]{2,1,0:T(1,128)} %copy-done.2) | copy-start | bytes 24580
  76.5 6.5 %collective-permute-start.7 = (bf16[128,768]{1,0:T(8,128)(2,1)S(1)}, bf16[128,768]{1,0:T(8,128)(2,1)S(1)}, u32[]{:S(2)}, u32[]{:S(2)}) collective-permute-start(bf16[128,768]{1,0:T(8,128)(2,1)S(1)} %get-tuple-element.42), channel_id=1, source_target_pairs={{0,64},{64,0},{128,192},{192,128},{1,65},{65,1},{129,193},{193,129... | collective-permute-start | bytes 589832 | tf_op jit(solution)/shard_map/ppermute | solution.py:385
  77.4 19.0 %collective-permute-start.8 = (bf16[128,768]{1,0:T(8,128)(2,1)S(1)}, bf16[128,768]{1,0:T(8,128)(2,1)S(1)}, u32[]{:S(2)}, u32[]{:S(2)}) collective-permute-start(bf16[128,768]{1,0:T(8,128)(2,1)S(1)} %get-tuple-element.43), channel_id=1, source_target_pairs={{0,128},{64,192},{128,0},{192,64},{1,129},{65,193},{129,1},{193,65... | collective-permute-start | bytes 589832 | tf_op jit(solution)/shard_map/ppermute | solution.py:385
  78.6 22.0 %collective-permute-start.9 = (bf16[128,768]{1,0:T(8,128)(2,1)S(1)}, bf16[128,768]{1,0:T(8,128)(2,1)S(1)}, u32[]{:S(2)}, u32[]{:S(2)}) collective-permute-start(bf16[128,768]{1,0:T(8,128)(2,1)S(1)} %get-tuple-element.44), channel_id=1, source_target_pairs={{0,192},{64,128},{128,64},{192,0},{1,193},{65,129},{129,65},{193,1... | collective-permute-start | bytes 589832 | tf_op jit(solution)/shard_map/ppermute | solution.py:385
  103.2 4.2 %collective-permute-start.10 = (bf16[208,256]{1,0:T(8,128)(2,1)S(1)}, bf16[208,256]{1,0:T(8,128)(2,1)S(1)}, u32[]{:S(2)}, u32[]{:S(2)}) collective-permute-start(bf16[208,256]{1,0:T(8,128)(2,1)S(1)} %get-tuple-element.48), channel_id=1, source_target_pairs={{0,4},{4,8},{8,12},{12,0},{1,5},{5,9},{9,13},{13,1},{2,6},{6,10},{... | collective-permute-start | bytes 319496 | tf_op jit(solution)/shard_map/ppermute | solution.py:375
  103.8 8.7 %collective-permute-start.11 = (bf16[208,256]{1,0:T(8,128)(2,1)S(1)}, bf16[208,256]{1,0:T(8,128)(2,1)S(1)}, u32[]{:S(2)}, u32[]{:S(2)}) collective-permute-start(bf16[208,256]{1,0:T(8,128)(2,1)S(1)} %get-tuple-element.49), channel_id=1, source_target_pairs={{0,8},{4,12},{8,0},{12,4},{1,9},{5,13},{9,1},{13,5},{2,10},{6,14},... | collective-permute-start | bytes 319496 | tf_op jit(solution)/shard_map/ppermute | solution.py:375
  103.8 9.9 %collective-permute-start.12 = (bf16[208,256]{1,0:T(8,128)(2,1)S(1)}, bf16[208,256]{1,0:T(8,128)(2,1)S(1)}, u32[]{:S(2)}, u32[]{:S(2)}) collective-permute-start(bf16[208,256]{1,0:T(8,128)(2,1)S(1)} %get-tuple-element.50), channel_id=1, source_target_pairs={{0,12},{4,0},{8,4},{12,8},{1,13},{5,1},{9,5},{13,9},{2,14},{6,2},{... | collective-permute-start | bytes 319496 | tf_op jit(solution)/shard_map/ppermute | solution.py:375
  113.7 15.2 %copy-start.4 = (bf16[1,4,48,256]{3,2,1,0:T(8,128)(2,1)S(1)}, bf16[1,4,48,256]{3,2,1,0:T(8,128)(2,1)}, u32[]{:S(2)}) copy-start(bf16[1,4,48,256]{3,2,1,0:T(8,128)(2,1)} %param.11) | copy-start | bytes 294916
  113.7 15.2 %copy-start.5 = (bf16[1,48,256]{2,1,0:T(8,128)(2,1)S(1)}, bf16[1,48,256]{2,1,0:T(8,128)(2,1)}, u32[]{:S(2)}) copy-start(bf16[1,48,256]{2,1,0:T(8,128)(2,1)} %param.10) | copy-start | bytes 73732
  113.8 15.1 %collective-permute-start.13 = (bf16[208,256]{1,0:T(8,128)(2,1)S(1)}, bf16[208,256]{1,0:T(8,128)(2,1)S(1)}, u32[]{:S(2)}, u32[]{:S(2)}) collective-permute-start(bf16[208,256]{1,0:T(8,128)(2,1)S(1)} %total.1), channel_id=1, source_target_pairs={{0,0},{16,64},{32,128},{48,192},{64,16},{80,80},{96,144},{112,208}... | collective-permute-start | bytes 319496 | tf_op jit(solution)/shard_map/ppermute | solution.py:380

commit v9 on v7

--- a/solution.py
+++ b/solution.py
@@ -36,7 +36,8 @@
     )
 
 
-def prep_kernel(at, sw, dw, sb, db, out, wide, tile):
+def prep_kernel(at, own, sw, dw, sb, db, out, ids, wide, tile):
+    ids[...] = jnp.full(ids.shape, own[0], jnp.int32)
     shared = sw[...].astype(F32)
     for k in range(DOMAINS):
         out[k * SHARD : (k + 1) * SHARD, :] = (shared * dw[k].astype(F32)).astype(BF)
@@ -52,16 +53,19 @@
     out[PIECE:, :] = tile[...].astype(BF)
 
 
-def prep(at, sw, dw, sb, db):
+def prep(at, own, sw, dw, sb, db):
     return call(
         prep_kernel,
         "prep",
         limit=58,
-        out_shape=jax.ShapeDtypeStruct((BLOCK, GS), BF),
-        in_specs=[SMEM, VMEM, VMEM, VMEM, VMEM],
-        out_specs=VMEM,
+        out_shape=(
+            jax.ShapeDtypeStruct((BLOCK, GS), BF),
+            jax.ShapeDtypeStruct((NY * NX, 1, 128), jnp.int32),
+        ),
+        in_specs=[SMEM, SMEM, VMEM, VMEM, VMEM, VMEM],
+        out_specs=(VMEM, VMEM),
         scratch_shapes=[pltpu.VMEM((8, SLAB), F32), pltpu.VMEM((TILE, GS), F32)],
-    )(at, sw, dw, sb, db)
+    )(at, own, sw, dw, sb, db)
 
 
 def pick_kernel(ids, z, *refs):
@@ -95,7 +99,7 @@
 
 
 def slab_of(k):
-    return pl.BlockSpec((ROWS, SLAB), lambda i, s: (0, s[0] ^ k))
+    return pl.BlockSpec((ROWS, SLAB), lambda i, s: (0, s[1] ^ k))
 
 
 def cut_kernel(s, *refs):
@@ -142,58 +146,38 @@
     )(section, stash, *others, cotangent)
 
 
-def slope_kernel(own, got, x, slope, kernel, offsets):
+def layers_kernel(s, own, top, got, x, out, send, above, kernel, offsets, tile):
+    @pl.when(pl.program_id(0) == 0)
+    def _():
+        above[...] = top[...]
+
     domain = own[0]
-    tile = got[0, PIECE:, :].astype(F32)
+    biases = got[0, PIECE:, :].astype(F32)
     for i in range(1, NX):
-        tile = tile + got[i, PIECE:, :].astype(F32)
-    offsets[...] = tile
+        biases = biases + got[i, PIECE:, :].astype(F32)
+    offsets[...] = biases
     for z in range(NZ):
         for i in range(NX):
             at = (z * NX + i) * SHARD
-            kernel[0, at : at + SHARD, :] = got[i, z * SHARD : (z + 1) * SHARD, :]
-    for q in range(SG):
-        lanes = slice(q * GS, (q + 1) * GS)
-        offset = offsets[q : q + 1, :] + offsets[pl.ds((1 + domain) * SG + q, 1), :]
-        pre = jnp.dot(x[0, :, lanes], kernel[0, lanes, :], preferred_element_type=F32) + offset
-        sigma = jax.nn.sigmoid(pre)
-        slope[0, :, lanes] = sigma * (1.0 + pre * (1.0 - sigma))
-
-
-def slopes(own, got, x):
-    tokens = pl.BlockSpec((1, ROWS, SLAB), lambda i: (i, 0, 0))
-    return call(
-        slope_kernel,
-        "slopes",
-        grid=(SECTIONS,),
-        out_shape=(
-            jax.ShapeDtypeStruct((SECTIONS, ROWS, SLAB), F32),
-            jax.ShapeDtypeStruct((SECTIONS, SLAB, GS), BF),
-        ),
-        in_specs=[SMEM, pl.BlockSpec((NX, BLOCK, GS), lambda i: (i, 0, 0)), tokens],
-        out_specs=(tokens, pl.BlockSpec((1, SLAB, GS), lambda i: (i, 0, 0))),
-        scratch_shapes=[pltpu.VMEM((TILE, GS), F32)],
-    )(own, got, x)
-
-
-def grads_kernel(s, top, slope, kernel, x, out, send, above, tile):
-    @pl.when(pl.program_id(0) == 0)
-    def _():
-        above[...] = top[...]
-
+            kernel[at : at + SHARD, :] = got[i, z * SHARD : (z + 1) * SHARD, :]
     tile[...] = jnp.zeros_like(tile)
     for q in range(SG):
         lanes = slice(q * GS, (q + 1) * GS)
+        inputs, weights = x[0, :, lanes], kernel[lanes, :]
+        offset = offsets[q : q + 1, :] + offsets[pl.ds((1 + domain) * SG + q, 1), :]
+        pre = jnp.dot(inputs, weights, preferred_element_type=F32) + offset
+        sigma = jax.nn.sigmoid(pre)
+        slope = sigma * (1.0 + pre * (1.0 - sigma))
         incoming = above[:, lanes].astype(F32)
-        signal = (incoming * slope[0, :, lanes]).astype(BF)
+        signal = (incoming * slope).astype(BF)
         back = lax.dot_general(
-            signal, kernel[0, lanes, :], (((1,), (1,)), ((), ())), preferred_element_type=F32
+            signal, weights, (((1,), (1,)), ((), ())), preferred_element_type=F32
         )
         outgoing = (incoming + back).astype(BF)
         out[0, :, lanes] = outgoing
         above[:, lanes] = outgoing
         grad = lax.dot_general(
-            x[0, :, lanes], signal, (((0,), (0,)), ((), ())), preferred_element_type=F32
+            inputs, signal, (((0,), (0,)), ((), ())), preferred_element_type=F32
         ).astype(BF)
         for row in range(q * GS, (q + 1) * GS, TILE):
             shard, inner = row // SHARD, row % SHARD
@@ -207,32 +191,51 @@
         send[i, PIECE:, :] = tile[...].astype(BF)
 
 
-def grads(section, top, slope, kernel, x):
+def layers(section, own, top, got, x):
     last = SECTIONS - 1
-    tokens = pl.BlockSpec((1, ROWS, SLAB), lambda i, s: (last - i, 0, 0))
-    return call(
-        grads_kernel,
-        "grads",
+    block = pl.BlockSpec((NX, BLOCK, GS), lambda i, s, d: (last - i, 0, 0))
+    return call(
+        layers_kernel,
+        "layers",
         out_shape=(
-            jax.ShapeDtypeStruct((SECTIONS, ROWS, SLAB), BF),
+            pltpu.HBM((SECTIONS, ROWS, SLAB), BF),
             jax.ShapeDtypeStruct((SECTIONS * NX, BLOCK, GS), BF),
         ),
         grid_spec=pltpu.PrefetchScalarGridSpec(
-            num_scalar_prefetch=1,
+            num_scalar_prefetch=2,
             grid=(SECTIONS,),
             in_specs=[
-                fixed((ROWS, SLAB)),
-                tokens,
-                pl.BlockSpec((1, SLAB, GS), lambda i, s: (last - i, 0, 0)),
-                tokens,
+                pl.BlockSpec((ROWS, SLAB), lambda i, s, d: (0, 0)),
+                block,
+                pl.BlockSpec((1, ROWS, SLAB), lambda i, s, d: (last - i, 0, 0)),
             ],
             out_specs=[
-                pl.BlockSpec((1, ROWS, SLAB), lambda i, s: ((last - i) ^ s[0], 0, 0)),
-                pl.BlockSpec((NX, BLOCK, GS), lambda i, s: (last - i, 0, 0)),
+                pl.BlockSpec((1, ROWS, SLAB), lambda i, s, d: ((last - i) ^ s[0], 0, 0)),
+                block,
             ],
-            scratch_shapes=[pltpu.VMEM((ROWS, SLAB), BF), pltpu.VMEM((TILE, GS), F32)],
-        ),
-    )(section, top, slope, kernel, x)
+            scratch_shapes=[
+                pltpu.VMEM((ROWS, SLAB), BF),
+                pltpu.VMEM((SLAB, GS), BF),
+                pltpu.VMEM((TILE, GS), F32),
+                pltpu.VMEM((TILE, GS), F32),
+            ],
+        ),
+    )(section, own, top, got, x)
+
+
+def split_kernel(out, *parts):
+    for k in range(SECTIONS):
+        parts[k][...] = out[k]
+
+
+def split(out):
+    return call(
+        split_kernel,
+        "split",
+        out_shape=(jax.ShapeDtypeStruct((ROWS, SLAB), BF),) * SECTIONS,
+        in_specs=[VMEM],
+        out_specs=(VMEM,) * SECTIONS,
+    )(out)
 
 
 def join_kernel(s, own, other1, other2, other3, out):
@@ -247,12 +250,13 @@
     return call(
         join_kernel,
         "join",
+        weight=0,
         out_shape=jax.ShapeDtypeStruct((ROWS, D), BF),
         grid_spec=pltpu.PrefetchScalarGridSpec(
             num_scalar_prefetch=1,
             grid=(SECTIONS,),
             in_specs=[fixed((ROWS, SLAB))] * SECTIONS,
-            out_specs=pl.BlockSpec((ROWS, SLAB), lambda i, s: (0, i ^ s[0])),
+            out_specs=pl.BlockSpec((ROWS, SLAB), lambda i, s: (0, i ^ s[1])),
         ),
     )(section, own, *others)
 
@@ -265,11 +269,11 @@
     def _():
         total[...] = jnp.zeros_like(total)
 
-    for i in range(NX):
-        domain = ids[step * NX + i, 0]
+    for i in range(got.shape[0]):
+        domain = ids[step * got.shape[0] + i, 0]
         total[domain] += got[i].astype(F32)
 
-    @pl.when(step == NY - 1)
+    @pl.when(step == 1)
     def _():
         tile[...] = jnp.zeros_like(tile)
         for k in range(DOMAINS):
@@ -289,9 +293,9 @@
     return call(
         merge_kernel,
         "merge",
-        grid=(NY,),
+        grid=(2,),
         out_shape=(jax.ShapeDtypeStruct((BLOCK, GS), BF),) * NZ,
-        in_specs=[SMEM, SMEM, pl.BlockSpec((NX, BLOCK, GS), lambda i: (i, 0, 0))],
+        in_specs=[SMEM, SMEM, pl.BlockSpec((NY * NX // 2, BLOCK, GS), lambda i: (i, 0, 0))],
         out_specs=(pl.BlockSpec((BLOCK, GS), lambda i: (0, 0)),) * NZ,
         scratch_shapes=[
             pltpu.VMEM((DOMAINS, BLOCK, GS), F32),
@@ -346,13 +350,18 @@
     return lax.all_to_all(block, axes, 0, 0, tiled=True)
 
 
-def turned(block, k):
+def flip(z):
+    return z % 2 * 2
+
+
+def turned(block, k, home):
     pairs = []
-    for section in range(SECTIONS):
-        for y in range(NY):
+    for a in range(SECTIONS):
+        for b in range(NY):
             for z in range(NZ):
-                to = (y * NY + section) * NZ + (z + k) % NZ
-                pairs.append(((section * NY + y) * NZ + z, to))
+                later = (z + k) % NZ
+                to = (b, a ^ flip(z)) if home else (b ^ flip(later), a)
+                pairs.append(((a * NY + b) * NZ + z, (to[0] * NY + to[1]) * NZ + later))
     return lax.ppermute(block, ("zhi", "core", "y", "zlo"), pairs)
 
 
@@ -368,16 +377,14 @@
 def body(stash, cotangent, domain_ids, shared_weight, domain_weight, shared_bias, domain_bias):
     stash = stash[0]
     sw, dw = shared_weight[0], domain_weight[0]
-    section = jnp.reshape(2 * lax.axis_index("zhi") + lax.axis_index("core"), (1,))
+    section = 2 * lax.axis_index("zhi") + lax.axis_index("core")
+    section = jnp.stack([section, section ^ flip(lax.axis_index("zlo"))])
     z = jnp.reshape(lax.axis_index("zlo"), (1,))
     at = PIECE * z + SHARD * lax.axis_index("x")
 
-    plane_ids = exchange(
-        jnp.broadcast_to(domain_ids[0], (NY * NX, 1, 128)), ("y", "x")
-    ).reshape(NY * NX, 128)
-    mine = prep(at, sw, dw, shared_bias, domain_bias[0])
-    (mine,) = after(plane_ids, mine)
-    held = [turned(mine, k) for k in range(NZ)]
+    mine, ids = prep(at, domain_ids, sw, dw, shared_bias, domain_bias[0])
+    plane_ids = exchange(ids, ("y", "x")).reshape(NY * NX, 128)
+    held = [turned(mine, k, False) for k in range(NZ)]
     picked = pick(plane_ids, z, held)
     got = exchange(picked, ("y", "x"))
     (late,) = after(picked, stash)
@@ -385,12 +392,13 @@
     others = [swapped(parts[k - 1], k) for k in range(1, SECTIONS)]
     x, top = gather(section, late, others, cotangent)
 
-    slope, kernel = slopes(domain_ids, got, x)
-    out, send = grads(section, top, slope, kernel, x)
+    out, send = layers(section, domain_ids, top, got, x)
     got = exchange(send, ("y", "x"))
-    d_inputs = join(section, out[0], [swapped(out[k], k) for k in range(1, SECTIONS)])
+    parts = split(out)
+    d_inputs = join(section, parts[0], [swapped(parts[k], k) for k in range(1, SECTIONS)])
+    (got,) = after(d_inputs, got)
     merged = merge(plane_ids, z, got)
-    final = [turned(merged[k], k) for k in range(NZ)]
+    final = [turned(merged[k], k, True) for k in range(NZ)]
     d_shared, d_domain, b_shared, b_domain = finish(at, final, sw, dw)
     return (d_inputs[None], d_shared[None], d_domain[None], b_shared, b_domain[None])
 

time: 140 us -> 128 us (0.914)
  the two profiles are of different devices: /device:TPU:80 before, /device:TPU:64 now
where the time goes in v9:
time: 128 us
  waiting for transfers between devices  60.1 us (47%)
  starting transfers between devices  52.7 us (41%)
  Pallas kernels  13.2 us (10%)
  between operations  1.46 us (1%)
    ppermute x6, waiting for transfers between devices, swapped(): return lax.ppermute(block, ('zhi', 'core'), pairs)  31.9 us
    all_to_all x3, starting transfers between devices, exchange(): return lax.all_to_all(block, axes, 0, 0, tiled=True)  21.6 us
    ppermute x8, starting transfers between devices, turned(): return lax.ppermute(block, ('zhi', 'core', 'y', 'zlo'), pairs)  19.3 us
    ppermute x8, waiting for transfers between devices, turned(): return lax.ppermute(block, ('zhi', 'core', 'y', 'zlo'), pairs)  15.6 us
    all_to_all x3, waiting for transfers between devices, exchange(): return lax.all_to_all(block, axes, 0, 0, tiled=True)  12.6 us
    ppermute x6, starting transfers between devices, swapped(): return lax.ppermute(block, ('zhi', 'core'), pairs)  11.7 us
    pallas_call x1, Pallas kernels, layers(): call(layers_kernel, 'layers', out_shape=(pltpu.HBM((SECTIONS, ROWS, SLAB)...  4.39 us
  transfers between devices with their start and end apart: 17, of which 8 were waited for; matrix products, arithmetic and copies ran while one was open for 0% of the time, Pallas kernels for 3%

profile of v9, /device:TPU:64, one launch (start us, length us, event | category | flops | bytes accessed | tf_op | source)
XLA Modules:
  0.0 127.6 jit_solution(3180010554459352925)
XLA Ops:
  1.3 1.6 %prep.1 = (bf16[208,256]{1,0:T(8,128)(2,1)}, s32[16,1,128]{2,1,0:T(1,128)}) custom-call(s32[1]{0:T(128)S(6)} %add.16.at, s32[1]{0:T(128)S(6)} %copy.13.own, bf16[48,256]{1,0:T(8,128)(2,1)} %bitcast.21, bf16[4,48,256]{2,1,0:T(8,128)(2,1)} %bitcast.19, bf16[1,48]{1,0:T(2,128)(2,1)} %sb.1, bf16[4,48]{1,0:T(4,128)(2,1)} %bitcast.24), custom_call_target="tpu_custom_call" | custom-call | flops 99999997952 | bytes 1000000000 | tf_op jit(solution)/shard_map/prep/pallas_call | solution.py:57
  2.9 4.9 %collective-permute-start.3 = (bf16[208,256]{1,0:T(8,128)(2,1)}, bf16[208,256]{1,0:T(8,128)(2,1)S(1)}, u32[]{:S(2)}, u32[]{:S(2)}) collective-permute-start(bf16[208,256]{1,0:T(8,128)(2,1)} %get-tuple-element.29), channel_id=1, source_target_pairs={{0,140},{4,0},{8,132},{12,8},{16,204},{20,64},{24,196},{28,72},{32... | collective-permute-start | bytes 319496 | tf_op jit(solution)/shard_map/ppermute | solution.py:365
  7.9 0.6 collective-permute-start.2
  8.4 4.5 %collective-permute-start.1 = (bf16[208,256]{1,0:T(8,128)(2,1)}, bf16[208,256]{1,0:T(8,128)(2,1)S(1)}, u32[]{:S(2)}, u32[]{:S(2)}) collective-permute-start(bf16[208,256]{1,0:T(8,128)(2,1)} %get-tuple-element.29), channel_id=1, source_target_pairs={{0,132},{4,8},{8,140},{12,0},{16,196},{20,72},{24,204},{28,64},{32... | collective-permute-start | bytes 319496 | tf_op jit(solution)/shard_map/ppermute | solution.py:365
  13.0 1.5 %collective-permute-start = (bf16[208,256]{1,0:T(8,128)(2,1)}, bf16[208,256]{1,0:T(8,128)(2,1)S(1)}, u32[]{:S(2)}, u32[]{:S(2)}) collective-permute-start(bf16[208,256]{1,0:T(8,128)(2,1)} %get-tuple-element.29), channel_id=1, source_target_pairs={{0,0},{4,132},{8,8},{12,140},{16,64},{20,196},{24,72},{28,204},{32... | collective-permute-start | bytes 319496 | tf_op jit(solution)/shard_map/ppermute | solution.py:365
  14.5 10.5 %all-to-all-start = ((s32[16,1,128]{2,1,0:T(1,128)}), s32[16,1,128]{2,1,0:T(1,128)S(1)}, u32[]{:S(2)}, u32[]{:S(2)}) async-start(s32[16,1,128]{2,1,0:T(1,128)} %get-tuple-element.28), calls=%async_computation | async-start | bytes 16384 | tf_op jit(solution)/shard_map/all_to_all | solution.py:350
  25.1 0.1 pad_add_fusion.s
  25.1 7.4 %all-to-all-done = s32[16,1,128]{2,1,0:T(1,128)S(1)} async-done(((s32[16,1,128]{2,1,0:T(1,128)}), s32[16,1,128]{2,1,0:T(1,128)S(1)}, u32[]{:S(2)}, u32[]{:S(2)}) %all-to-all-start) | async-done | bytes 8224 | tf_op jit(solution)/shard_map/all_to_all | solution.py:350
  32.5 0.0 collective-permute-done.3.refs_3_
  32.5 0.0 collective-permute-done.2.refs_2_
  32.5 0.0 collective-permute-done.1.refs_1_
  32.5 0.0 collective-permute-done.refs_0_
  32.6 2.0 %pick.1 = bf16[16,208,256]{2,1,0:T(8,128)(2,1)} custom-call(s32[16,128]{1,0:T(8,128)S(1)} %bitcast.17, s32[1]{0:T(128)} %bitcast.2.z, bf16[208,256]{1,0:T(8,128)(2,1)S(1)} %collective-permute-done.refs_0_, bf16[208,256]{1,0:T(8,128)(2,1)S(1)} %collective-permute-done.1.refs_1_, bf16[208,256]{1,0:T(8,128)(2,1)S(1)} %collective-permute-done.2.refs_2_, ...), custom_call_target="tpu_custom_call" | custom-call | flops 99999997952 | bytes 1000000000 | tf_op jit(solution)/shard_map/pick/pallas_call | solution.py:87
  34.6 0.0 copy-done.2
  34.6 3.8 %all-to-all-start.1 = ((bf16[16,208,256]{2,1,0:T(8,128)(2,1)}), bf16[16,208,256]{2,1,0:T(8,128)(2,1)S(1)}, u32[]{:S(2)}, u32[]{:S(2)}) async-start(bf16[16,208,256]{2,1,0:T(8,128)(2,1)} %pick.1), calls=%async_computation.1 | async-start | bytes 3407872 | tf_op jit(solution)/shard_map/all_to_all | solution.py:350
  38.4 0.0 copy-done
  38.4 0.0 copy-start.1
  38.4 0.6 cut.1
  39.0 0.1 collective-permute-start.4
  39.1 1.7 %collective-permute-start.5 = (bf16[128,768]{1,0:T(8,128)(2,1)S(1)}, bf16[128,768]{1,0:T(8,128)(2,1)S(1)}, u32[]{:S(2)}, u32[]{:S(2)}) collective-permute-start(bf16[128,768]{1,0:T(8,128)(2,1)S(1)} %get-tuple-element.32), channel_id=1, source_target_pairs={{0,128},{64,192},{128,0},{192,64},{1,129},{65,193},{129,1},{193,65... | collective-permute-start | bytes 589832 | tf_op jit(solution)/shard_map/ppermute | solution.py:370
  40.8 4.1 %collective-permute-start.6 = (bf16[128,768]{1,0:T(8,128)(2,1)S(1)}, bf16[128,768]{1,0:T(8,128)(2,1)S(1)}, u32[]{:S(2)}, u32[]{:S(2)}) collective-permute-start(bf16[128,768]{1,0:T(8,128)(2,1)S(1)} %get-tuple-element.33), channel_id=1, source_target_pairs={{0,192},{64,128},{128,64},{192,0},{1,193},{65,129},{129,65},{193,1... | collective-permute-start | bytes 589832 | tf_op jit(solution)/shard_map/ppermute | solution.py:370
  44.9 0.0 collective-permute-done.4.other1
  44.9 14.4 %collective-permute-done.5.other2 = bf16[128,768]{1,0:T(8,128)(2,1)S(1)} collective-permute-done((bf16[128,768]{1,0:T(8,128)(2,1)S(1)}, bf16[128,768]{1,0:T(8,128)(2,1)S(1)}, u32[]{:S(2)}, u32[]{:S(2)}) %collective-permute-start.5) | collective-permute-done | bytes 196640 | tf_op jit(solution)/shard_map/ppermute | solution.py:370
  59.3 3.3 %collective-permute-done.6.other3 = bf16[128,768]{1,0:T(8,128)(2,1)S(1)} collective-permute-done((bf16[128,768]{1,0:T(8,128)(2,1)S(1)}, bf16[128,768]{1,0:T(8,128)(2,1)S(1)}, u32[]{:S(2)}, u32[]{:S(2)}) %collective-permute-start.6) | collective-permute-done | bytes 196640 | tf_op jit(solution)/shard_map/ppermute | solution.py:370
  62.5 0.6 gather.1
  63.2 0.0 all-to-all-done.1.got
  63.2 4.4 %layers.1 = (bf16[4,128,768]{2,1,0:T(8,128)(2,1)}, bf16[16,208,256]{2,1,0:T(8,128)(2,1)}) custom-call(s32[2]{0:T(128)S(1)} %pad_add_fusion.s, s32[1]{0:T(128)S(6)} %copy.13.own, bf16[128,768]{1,0:T(8,128)(2,1)S(1)} %get-tuple-element.34.top, bf16[16,208,256]{2,1,0:T(8,128)(2,1)S(1)} %all-to-all-done.1.got, bf16[4,128,768]{2,1,0:T(8,128)(2,1)S(1)} %get-tuple-element.35.x), custom_call_target="tpu_custom_call" | custom-call | flops 99999997952 | bytes 1000000000 | tf_op jit(solution)/shard_map/layers/pallas_call | solution.py:197
  67.6 7.3 %all-to-all-start.2 = ((bf16[16,208,256]{2,1,0:T(8,128)(2,1)}), bf16[16,208,256]{2,1,0:T(8,128)(2,1)S(1)}, u32[]{:S(2)}, u32[]{:S(2)}) async-start(bf16[16,208,256]{2,1,0:T(8,128)(2,1)} %get-tuple-element.41), calls=%async_computation.2 | async-start | bytes 3407872 | tf_op jit(solution)/shard_map/all_to_all | solution.py:350
  74.9 0.0 copy-start.3
  74.9 0.1 split.1
  74.9 0.1 collective-permute-start.7
  75.0 2.0 %collective-permute-start.8 = (bf16[128,768]{1,0:T(8,128)(2,1)S(1)}, bf16[128,768]{1,0:T(8,128)(2,1)S(1)}, u32[]{:S(2)}, u32[]{:S(2)}) collective-permute-start(bf16[128,768]{1,0:T(8,128)(2,1)S(1)} %get-tuple-element.39), channel_id=1, source_target_pairs={{0,128},{64,192},{128,0},{192,64},{1,129},{65,193},{129,1},{193,65... | collective-permute-start | bytes 589832 | tf_op jit(solution)/shard_map/ppermute | solution.py:370
  77.0 3.8 %collective-permute-start.9 = (bf16[128,768]{1,0:T(8,128)(2,1)S(1)}, bf16[128,768]{1,0:T(8,128)(2,1)S(1)}, u32[]{:S(2)}, u32[]{:S(2)}) collective-permute-start(bf16[128,768]{1,0:T(8,128)(2,1)S(1)} %get-tuple-element.40), channel_id=1, source_target_pairs={{0,192},{64,128},{128,64},{192,0},{1,193},{65,129},{129,65},{193,1... | collective-permute-start | bytes 589832 | tf_op jit(solution)/shard_map/ppermute | solution.py:370
  80.8 0.0 collective-permute-done.7.other1
  80.8 10.1 %collective-permute-done.8.other2 = bf16[128,768]{1,0:T(8,128)(2,1)S(1)} collective-permute-done((bf16[128,768]{1,0:T(8,128)(2,1)S(1)}, bf16[128,768]{1,0:T(8,128)(2,1)S(1)}, u32[]{:S(2)}, u32[]{:S(2)}) %collective-permute-start.8) | collective-permute-done | bytes 196640 | tf_op jit(solution)/shard_map/ppermute | solution.py:370
  90.9 4.1 %collective-permute-done.9.other3 = bf16[128,768]{1,0:T(8,128)(2,1)S(1)} collective-permute-done((bf16[128,768]{1,0:T(8,128)(2,1)S(1)}, bf16[128,768]{1,0:T(8,128)(2,1)S(1)}, u32[]{:S(2)}, u32[]{:S(2)}) %collective-permute-start.9) | collective-permute-done | bytes 196640 | tf_op jit(solution)/shard_map/ppermute | solution.py:370
  95.1 2.0 %join.1 = bf16[128,3072]{1,0:T(8,128)(2,1)} custom-call(s32[2]{0:T(128)S(1)} %pad_add_fusion.s, bf16[128,768]{1,0:T(8,128)(2,1)S(1)} %get-tuple-element.37.own, bf16[128,768]{1,0:T(8,128)(2,1)S(1)} %collective-permute-done.7.other1, bf16[128,768]{1,0:T(8,128)(2,1)S(1)} %collective-permute-done.8.other2, bf16[128,768]{1,0:T(8,128)(2,1)S(1)} %collective-permute-done.9.other3), custom_call_target="tpu_custom_call" | custom-call | tf_op jit(solution)/shard_map/join/pallas_call | solution.py:250
  97.1 5.2 %all-to-all-done.2.got = bf16[16,208,256]{2,1,0:T(8,128)(2,1)S(1)} async-done(((bf16[16,208,256]{2,1,0:T(8,128)(2,1)}), bf16[16,208,256]{2,1,0:T(8,128)(2,1)S(1)}, u32[]{:S(2)}, u32[]{:S(2)}) %all-to-all-start.2) | async-done | bytes 1703968 | tf_op jit(solution)/shard_map/all_to_all | solution.py:350
  102.3 1.2 merge.1
  103.5 0.7 collective-permute-start.10
  104.1 0.1 collective-permute-start.11
  104.2 4.6 %collective-permute-start.12 = (bf16[208,256]{1,0:T(8,128)(2,1)S(1)}, bf16[208,256]{1,0:T(8,128)(2,1)S(1)}, u32[]{:S(2)}, u32[]{:S(2)}) collective-permute-start(bf16[208,256]{1,0:T(8,128)(2,1)S(1)} %get-tuple-element.45), channel_id=1, source_target_pairs={{0,8},{4,44},{8,0},{12,36},{16,72},{20,108},{24,64},{28,100},{32,1... | collective-permute-start | bytes 319496 | tf_op jit(solution)/shard_map/ppermute | solution.py:365
  108.9 2.4 %collective-permute-start.13 = (bf16[208,256]{1,0:T(8,128)(2,1)S(1)}, bf16[208,256]{1,0:T(8,128)(2,1)S(1)}, u32[]{:S(2)}, u32[]{:S(2)}) collective-permute-start(bf16[208,256]{1,0:T(8,128)(2,1)S(1)} %get-tuple-element.46), channel_id=1, source_target_pairs={{0,12},{4,32},{8,4},{12,40},{16,76},{20,96},{24,68},{28,104},{32,1... | collective-permute-start | bytes 319496 | tf_op jit(solution)/shard_map/ppermute | solution.py:365
  111.2 0.0 collective-permute-done.10.refs_0_
  111.2 8.1 %collective-permute-done.11.refs_1_ = bf16[208,256]{1,0:T(8,128)(2,1)S(1)} collective-permute-done((bf16[208,256]{1,0:T(8,128)(2,1)S(1)}, bf16[208,256]{1,0:T(8,128)(2,1)S(1)}, u32[]{:S(2)}, u32[]{:S(2)}) %collective-permute-start.11) | collective-permute-done | bytes 106528 | tf_op jit(solution)/shard_map/ppermute | solution.py:365
  119.4 0.0 collective-permute-done.12.refs_2_
  119.4 7.5 %collective-permute-done.13.refs_3_ = bf16[208,256]{1,0:T(8,128)(2,1)S(1)} collective-permute-done((bf16[208,256]{1,0:T(8,128)(2,1)S(1)}, bf16[208,256]{1,0:T(8,128)(2,1)S(1)}, u32[]{:S(2)}, u32[]{:S(2)}) %collective-permute-start.13) | collective-permute-done | bytes 106528 | tf_op jit(solution)/shard_map/ppermute | solution.py:365
  126.8 0.8 finish.1
  (10 shorter events, 0.0 us)
Async XLA Ops:
  2.9 29.6 %collective-permute-start.3 = (bf16[208,256]{1,0:T(8,128)(2,1)}, bf16[208,256]{1,0:T(8,128)(2,1)S(1)}, u32[]{:S(2)}, u32[]{:S(2)}) collective-permute-start(bf16[208,256]{1,0:T(8,128)(2,1)} %get-tuple-element.29), channel_id=1, source_target_pairs={{0,140},{4,0},{8,132},{12,8},{16,204},{20,64},{24,196},{28,72},{32... | collective-permute-start | bytes 319496 | tf_op jit(solution)/shard_map/ppermute | solution.py:365
  7.9 24.7 %collective-permute-start.2 = (bf16[208,256]{1,0:T(8,128)(2,1)}, bf16[208,256]{1,0:T(8,128)(2,1)S(1)}, u32[]{:S(2)}, u32[]{:S(2)}) collective-permute-start(bf16[208,256]{1,0:T(8,128)(2,1)} %get-tuple-element.29), channel_id=1, source_target_pairs={{0,8},{4,140},{8,0},{12,132},{16,72},{20,204},{24,64},{28,196},{32... | collective-permute-start | bytes 319496 | tf_op jit(solution)/shard_map/ppermute | solution.py:365
  8.4 24.1 %collective-permute-start.1 = (bf16[208,256]{1,0:T(8,128)(2,1)}, bf16[208,256]{1,0:T(8,128)(2,1)S(1)}, u32[]{:S(2)}, u32[]{:S(2)}) collective-permute-start(bf16[208,256]{1,0:T(8,128)(2,1)} %get-tuple-element.29), channel_id=1, source_target_pairs={{0,132},{4,8},{8,140},{12,0},{16,196},{20,72},{24,204},{28,64},{32... | collective-permute-start | bytes 319496 | tf_op jit(solution)/shard_map/ppermute | solution.py:365
  13.0 19.6 %collective-permute-start = (bf16[208,256]{1,0:T(8,128)(2,1)}, bf16[208,256]{1,0:T(8,128)(2,1)S(1)}, u32[]{:S(2)}, u32[]{:S(2)}) collective-permute-start(bf16[208,256]{1,0:T(8,128)(2,1)} %get-tuple-element.29), channel_id=1, source_target_pairs={{0,0},{4,132},{8,8},{12,140},{16,64},{20,196},{24,72},{28,204},{32... | collective-permute-start | bytes 319496 | tf_op jit(solution)/shard_map/ppermute | solution.py:365
  14.5 18.0 %all-to-all-start = ((s32[16,1,128]{2,1,0:T(1,128)}), s32[16,1,128]{2,1,0:T(1,128)S(1)}, u32[]{:S(2)}, u32[]{:S(2)}) async-start(s32[16,1,128]{2,1,0:T(1,128)} %get-tuple-element.28), calls=%async_computation | async-start | bytes 16384 | tf_op jit(solution)/shard_map/all_to_all | solution.py:350
  32.5 2.1 %copy-start.2 = (s32[16,1,128]{2,1,0:T(1,128)}, s32[16,1,128]{2,1,0:T(1,128)S(1)}, u32[]{:S(2)}) copy-start(s32[16,1,128]{2,1,0:T(1,128)S(1)} %all-to-all-done) | copy-start | bytes 24580
  34.6 3.9 %copy-start = (bf16[1,128,3072]{2,1,0:T(8,128)(2,1)S(1)}, bf16[1,128,3072]{2,1,0:T(8,128)(2,1)}, u32[]{:S(2)}) copy-start(bf16[1,128,3072]{2,1,0:T(8,128)(2,1)} %param.7) | copy-start | bytes 2359300
  34.6 28.6 %all-to-all-start.1 = ((bf16[16,208,256]{2,1,0:T(8,128)(2,1)}), bf16[16,208,256]{2,1,0:T(8,128)(2,1)S(1)}, u32[]{:S(2)}, u32[]{:S(2)}) async-start(bf16[16,208,256]{2,1,0:T(8,128)(2,1)} %pick.1), calls=%async_computation.1 | async-start | bytes 3407872 | tf_op jit(solution)/shard_map/all_to_all | solution.py:350
  38.4 24.1 %copy-start.1 = (bf16[128,3072]{1,0:T(8,128)(2,1)S(1)}, bf16[128,3072]{1,0:T(8,128)(2,1)}, u32[]{:S(2)}) copy-start(bf16[128,3072]{1,0:T(8,128)(2,1)} %cotangent.1) | copy-start | bytes 2359300
  39.0 5.9 %collective-permute-start.4 = (bf16[128,768]{1,0:T(8,128)(2,1)S(1)}, bf16[128,768]{1,0:T(8,128)(2,1)S(1)}, u32[]{:S(2)}, u32[]{:S(2)}) collective-permute-start(bf16[128,768]{1,0:T(8,128)(2,1)S(1)} %get-tuple-element.31), channel_id=1, source_target_pairs={{0,64},{64,0},{128,192},{192,128},{1,65},{65,1},{129,193},{193,129... | collective-permute-start | bytes 589832 | tf_op jit(solution)/shard_map/ppermute | solution.py:370
  39.1 20.1 %collective-permute-start.5 = (bf16[128,768]{1,0:T(8,128)(2,1)S(1)}, bf16[128,768]{1,0:T(8,128)(2,1)S(1)}, u32[]{:S(2)}, u32[]{:S(2)}) collective-permute-start(bf16[128,768]{1,0:T(8,128)(2,1)S(1)} %get-tuple-element.32), channel_id=1, source_target_pairs={{0,128},{64,192},{128,0},{192,64},{1,129},{65,193},{129,1},{193,65... | collective-permute-start | bytes 589832 | tf_op jit(solution)/shard_map/ppermute | solution.py:370
  40.8 21.7 %collective-permute-start.6 = (bf16[128,768]{1,0:T(8,128)(2,1)S(1)}, bf16[128,768]{1,0:T(8,128)(2,1)S(1)}, u32[]{:S(2)}, u32[]{:S(2)}) collective-permute-start(bf16[128,768]{1,0:T(8,128)(2,1)S(1)} %get-tuple-element.33), channel_id=1, source_target_pairs={{0,192},{64,128},{128,64},{192,0},{1,193},{65,129},{129,65},{193,1... | collective-permute-start | bytes 589832 | tf_op jit(solution)/shard_map/ppermute | solution.py:370
  67.6 7.3 %copy-start.6 = (bf16[4,128,768]{2,1,0:T(8,128)(2,1)S(1)}, bf16[4,128,768]{2,1,0:T(8,128)(2,1)}, u32[]{:S(2)}) copy-start(bf16[4,128,768]{2,1,0:T(8,128)(2,1)} %get-tuple-element.36.out) | copy-start | bytes 2359300
  67.6 34.7 %all-to-all-start.2 = ((bf16[16,208,256]{2,1,0:T(8,128)(2,1)}), bf16[16,208,256]{2,1,0:T(8,128)(2,1)S(1)}, u32[]{:S(2)}, u32[]{:S(2)}) async-start(bf16[16,208,256]{2,1,0:T(8,128)(2,1)} %get-tuple-element.41), calls=%async_computation.2 | async-start | bytes 3407872 | tf_op jit(solution)/shard_map/all_to_all | solution.py:350
  74.9 27.4 %copy-start.3 = (s32[16,1,128]{2,1,0:T(1,128)S(1)}, s32[16,1,128]{2,1,0:T(1,128)}, u32[]{:S(2)}) copy-start(s32[16,1,128]{2,1,0:T(1,128)} %copy-done.2) | copy-start | bytes 24580
  74.9 5.9 %collective-permute-start.7 = (bf16[128,768]{1,0:T(8,128)(2,1)S(1)}, bf16[128,768]{1,0:T(8,128)(2,1)S(1)}, u32[]{:S(2)}, u32[]{:S(2)}) collective-permute-start(bf16[128,768]{1,0:T(8,128)(2,1)S(1)} %get-tuple-element.38), channel_id=1, source_target_pairs={{0,64},{64,0},{128,192},{192,128},{1,65},{65,1},{129,193},{193,129... | collective-permute-start | bytes 589832 | tf_op jit(solution)/shard_map/ppermute | solution.py:370
  75.0 15.9 %collective-permute-start.8 = (bf16[128,768]{1,0:T(8,128)(2,1)S(1)}, bf16[128,768]{1,0:T(8,128)(2,1)S(1)}, u32[]{:S(2)}, u32[]{:S(2)}) collective-permute-start(bf16[128,768]{1,0:T(8,128)(2,1)S(1)} %get-tuple-element.39), channel_id=1, source_target_pairs={{0,128},{64,192},{128,0},{192,64},{1,129},{65,193},{129,1},{193,65... | collective-permute-start | bytes 589832 | tf_op jit(solution)/shard_map/ppermute | solution.py:370
  77.0 18.1 %collective-permute-start.9 = (bf16[128,768]{1,0:T(8,128)(2,1)S(1)}, bf16[128,768]{1,0:T(8,128)(2,1)S(1)}, u32[]{:S(2)}, u32[]{:S(2)}) collective-permute-start(bf16[128,768]{1,0:T(8,128)(2,1)S(1)} %get-tuple-element.40), channel_id=1, source_target_pairs={{0,192},{64,128},{128,64},{192,0},{1,193},{65,129},{129,65},{193,1... | collective-permute-start | bytes 589832 | tf_op jit(solution)/shard_map/ppermute | solution.py:370
  97.1 29.7 %copy-start.4 = (bf16[1,4,48,256]{3,2,1,0:T(8,128)(2,1)S(1)}, bf16[1,4,48,256]{3,2,1,0:T(8,128)(2,1)}, u32[]{:S(2)}) copy-start(bf16[1,4,48,256]{3,2,1,0:T(8,128)(2,1)} %param.11) | copy-start | bytes 294916
  97.1 29.7 %copy-start.5 = (bf16[1,48,256]{2,1,0:T(8,128)(2,1)S(1)}, bf16[1,48,256]{2,1,0:T(8,128)(2,1)}, u32[]{:S(2)}) copy-start(bf16[1,48,256]{2,1,0:T(8,128)(2,1)} %param.10) | copy-start | bytes 73732
  103.5 7.8 %collective-permute-start.10 = (bf16[208,256]{1,0:T(8,128)(2,1)S(1)}, bf16[208,256]{1,0:T(8,128)(2,1)S(1)}, u32[]{:S(2)}, u32[]{:S(2)}) collective-permute-start(bf16[208,256]{1,0:T(8,128)(2,1)S(1)} %get-tuple-element.43), channel_id=1, source_target_pairs={{0,0},{4,36},{8,8},{12,44},{16,64},{20,100},{24,72},{28,108},{32,1... | collective-permute-start | bytes 319496 | tf_op jit(solution)/shard_map/ppermute | solution.py:365
  104.1 15.2 %collective-permute-start.11 = (bf16[208,256]{1,0:T(8,128)(2,1)S(1)}, bf16[208,256]{1,0:T(8,128)(2,1)S(1)}, u32[]{:S(2)}, u32[]{:S(2)}) collective-permute-start(bf16[208,256]{1,0:T(8,128)(2,1)S(1)} %get-tuple-element.44), channel_id=1, source_target_pairs={{0,4},{4,40},{8,12},{12,32},{16,68},{20,104},{24,76},{28,96},{32,1... | collective-permute-start | bytes 319496 | tf_op jit(solution)/shard_map/ppermute | solution.py:365
  104.2 15.1 %collective-permute-start.12 = (bf16[208,256]{1,0:T(8,128)(2,1)S(1)}, bf16[208,256]{1,0:T(8,128)(2,1)S(1)}, u32[]{:S(2)}, u32[]{:S(2)}) collective-permute-start(bf16[208,256]{1,0:T(8,128)(2,1)S(1)} %get-tuple-element.45), channel_id=1, source_target_pairs={{0,8},{4,44},{8,0},{12,36},{16,72},{20,108},{24,64},{28,100},{32,1... | collective-permute-start | bytes 319496 | tf_op jit(solution)/shard_map/ppermute | solution.py:365
  108.9 18.0 %collective-permute-start.13 = (bf16[208,256]{1,0:T(8,128)(2,1)S(1)}, bf16[208,256]{1,0:T(8,128)(2,1)S(1)}, u32[]{:S(2)}, u32[]{:S(2)}) collective-permute-start(bf16[208,256]{1,0:T(8,128)(2,1)S(1)} %get-tuple-element.46), channel_id=1, source_target_pairs={{0,12},{4,32},{8,4},{12,40},{16,76},{20,96},{24,68},{28,104},{32,1... | collective-permute-start | bytes 319496 | tf_op jit(solution)/shard_map/ppermute | solution.py:365

commit v10 on v9

--- a/solution.py
+++ b/solution.py
@@ -69,7 +69,7 @@
 
 
 def pick_kernel(ids, z, *refs):
-    held, out = refs[:NZ], refs[NZ]
+    held, out = [refs[0], refs[1], refs[3], refs[2]], refs[NZ]
     step = pl.program_id(0)
     tile = held[0][PIECE:, :].astype(F32)
     for k in range(1, NZ):
@@ -91,7 +91,7 @@
         out_shape=jax.ShapeDtypeStruct((NY * NX, BLOCK, GS), BF),
         in_specs=[SMEM, SMEM] + [pl.BlockSpec((BLOCK, GS), lambda i: (0, 0))] * NZ,
         out_specs=pl.BlockSpec((NY * NX // 2, BLOCK, GS), lambda i: (i, 0, 0)),
-    )(ids, z, *held)
+    )(ids, z, held[0], held[1], held[3], held[2])
 
 
 def fixed(shape):
@@ -122,7 +122,7 @@
     )(section, stash, stash, stash)
 
 
-def gather_kernel(s, own, other1, other2, other3, cotangent, x, top):
+def gather_kernel(s, other3, other2, other1, own, cotangent, x, top):
     for k, part in enumerate((own, other1, other2, other3)):
         x[s[0] ^ k] = part[...]
     top[...] = cotangent[...]
@@ -140,10 +140,10 @@
         grid_spec=pltpu.PrefetchScalarGridSpec(
             num_scalar_prefetch=1,
             grid=(1,),
-            in_specs=[slab_of(0)] + [fixed((ROWS, SLAB))] * (SECTIONS - 1) + [slab_of(0)],
+            in_specs=[fixed((ROWS, SLAB))] * (SECTIONS - 1) + [slab_of(0)] * 2,
             out_specs=[fixed((SECTIONS, ROWS, SLAB)), fixed((ROWS, SLAB))],
         ),
-    )(section, stash, *others, cotangent)
+    )(section, *others[::-1], stash, cotangent)
 
 
 def layers_kernel(s, own, top, got, x, out, send, above, kernel, offsets, tile):
@@ -238,7 +238,7 @@
     )(out)
 
 
-def join_kernel(s, own, other1, other2, other3, out):
+def join_kernel(s, other3, other2, other1, own, out):
     for k, part in enumerate((own, other1, other2, other3)):
 
         @pl.when(pl.program_id(0) == k)
@@ -258,7 +258,7 @@
             in_specs=[fixed((ROWS, SLAB))] * SECTIONS,
             out_specs=pl.BlockSpec((ROWS, SLAB), lambda i, s: (0, i ^ s[1])),
         ),
-    )(section, own, *others)
+    )(section, *others[::-1], own)
 
 
 def merge_kernel(ids, z, got, *refs):
@@ -343,7 +343,7 @@
         in_specs=[SMEM] + [VMEM] * (NZ + 2),
         out_specs=(VMEM,) * 4,
         scratch_shapes=[pltpu.VMEM((8, SLAB), F32)],
-    )(at, *got, sw, dw)
+    )(at, got[2], got[1], got[3], got[0], sw, dw)
 
 
 def exchange(block, axes):

time: 128 us -> 123 us (0.961)
  the two profiles are of different devices: /device:TPU:64 before, /device:TPU:1 now
where the time goes in v10:
time: 123 us; the launch traced here: 122 us
  starting transfers between devices  71.1 us (58%)
  waiting for transfers between devices  35.9 us (29%)
  Pallas kernels  13.2 us (11%)
  between operations  1.47 us (1%)
    ppermute x8, starting transfers between devices, turned(): return lax.ppermute(block, ('zhi', 'core', 'y', 'zlo'), pairs)  39.5 us
    ppermute x6, starting transfers between devices, swapped(): return lax.ppermute(block, ('zhi', 'core'), pairs)  16.9 us
    ppermute x6, waiting for transfers between devices, swapped(): return lax.ppermute(block, ('zhi', 'core'), pairs)  16 us
    all_to_all x3, starting transfers between devices, exchange(): return lax.all_to_all(block, axes, 0, 0, tiled=True)  14.7 us
    all_to_all x3, waiting for transfers between devices, exchange(): return lax.all_to_all(block, axes, 0, 0, tiled=True)  11.9 us
    ppermute x8, waiting for transfers between devices, turned(): return lax.ppermute(block, ('zhi', 'core', 'y', 'zlo'), pairs)  7.94 us
    pallas_call x1, Pallas kernels, layers(): call(layers_kernel, 'layers', out_shape=(pltpu.HBM((SECTIONS, ROWS, SLAB)...  4.38 us
  transfers between devices with their start and end apart: 17, of which 8 were waited for; matrix products, arithmetic and copies ran while one was open for 0% of the time, Pallas kernels for 3%

profile of v10, /device:TPU:1, one launch (start us, length us, event | category | flops | bytes accessed | tf_op | source)
XLA Modules:
  0.0 121.7 jit_solution(2513923734817623304)
XLA Ops:
  1.3 1.6 %prep.1 = (bf16[208,256]{1,0:T(8,128)(2,1)}, s32[16,1,128]{2,1,0:T(1,128)}) custom-call(s32[1]{0:T(128)S(6)} %add.16.at, s32[1]{0:T(128)S(6)} %copy.13.own, bf16[48,256]{1,0:T(8,128)(2,1)} %bitcast.21, bf16[4,48,256]{2,1,0:T(8,128)(2,1)} %bitcast.19, bf16[1,48]{1,0:T(2,128)(2,1)} %sb.1, bf16[4,48]{1,0:T(4,128)(2,1)} %bitcast.24), custom_call_target="tpu_custom_call" | custom-call | flops 99999997952 | bytes 1000000000 | tf_op jit(solution)/shard_map/prep/pallas_call | solution.py:57
  2.9 5.4 %collective-permute-start.3 = (bf16[208,256]{1,0:T(8,128)(2,1)}, bf16[208,256]{1,0:T(8,128)(2,1)S(1)}, u32[]{:S(2)}, u32[]{:S(2)}) collective-permute-start(bf16[208,256]{1,0:T(8,128)(2,1)} %get-tuple-element.29), channel_id=1, source_target_pairs={{0,8},{4,140},{8,0},{12,132},{16,72},{20,204},{24,64},{28,196},{32... | collective-permute-start | bytes 319496 | tf_op jit(solution)/shard_map/ppermute | solution.py:365
  8.3 4.5 %collective-permute-start.2 = (bf16[208,256]{1,0:T(8,128)(2,1)}, bf16[208,256]{1,0:T(8,128)(2,1)S(1)}, u32[]{:S(2)}, u32[]{:S(2)}) collective-permute-start(bf16[208,256]{1,0:T(8,128)(2,1)} %get-tuple-element.29), channel_id=1, source_target_pairs={{0,140},{4,0},{8,132},{12,8},{16,204},{20,64},{24,196},{28,72},{32... | collective-permute-start | bytes 319496 | tf_op jit(solution)/shard_map/ppermute | solution.py:365
  12.8 4.2 %collective-permute-start.1 = (bf16[208,256]{1,0:T(8,128)(2,1)}, bf16[208,256]{1,0:T(8,128)(2,1)S(1)}, u32[]{:S(2)}, u32[]{:S(2)}) collective-permute-start(bf16[208,256]{1,0:T(8,128)(2,1)} %get-tuple-element.29), channel_id=1, source_target_pairs={{0,132},{4,8},{8,140},{12,0},{16,196},{20,72},{24,204},{28,64},{32... | collective-permute-start | bytes 319496 | tf_op jit(solution)/shard_map/ppermute | solution.py:365
  17.0 3.0 %collective-permute-start = (bf16[208,256]{1,0:T(8,128)(2,1)}, bf16[208,256]{1,0:T(8,128)(2,1)S(1)}, u32[]{:S(2)}, u32[]{:S(2)}) collective-permute-start(bf16[208,256]{1,0:T(8,128)(2,1)} %get-tuple-element.29), channel_id=1, source_target_pairs={{0,0},{4,132},{8,8},{12,140},{16,64},{20,196},{24,72},{28,204},{32... | collective-permute-start | bytes 319496 | tf_op jit(solution)/shard_map/ppermute | solution.py:365
  20.0 4.3 %all-to-all-start = ((s32[16,1,128]{2,1,0:T(1,128)}), s32[16,1,128]{2,1,0:T(1,128)S(1)}, u32[]{:S(2)}, u32[]{:S(2)}) async-start(s32[16,1,128]{2,1,0:T(1,128)} %get-tuple-element.28), calls=%async_computation | async-start | bytes 16384 | tf_op jit(solution)/shard_map/all_to_all | solution.py:350
  24.4 0.1 pad_add_fusion.s
  24.5 6.2 %all-to-all-done = s32[16,1,128]{2,1,0:T(1,128)S(1)} async-done(((s32[16,1,128]{2,1,0:T(1,128)}), s32[16,1,128]{2,1,0:T(1,128)S(1)}, u32[]{:S(2)}, u32[]{:S(2)}) %all-to-all-start) | async-done | bytes 8224 | tf_op jit(solution)/shard_map/all_to_all | solution.py:350
  30.7 0.0 collective-permute-done.3.refs_3_
  30.7 0.0 collective-permute-done.2.refs_2_
  30.7 0.0 collective-permute-done.1.refs_1_
  30.7 0.0 collective-permute-done.refs_0_
  30.7 2.0 %pick.1 = bf16[16,208,256]{2,1,0:T(8,128)(2,1)} custom-call(s32[16,128]{1,0:T(8,128)S(1)} %bitcast.17, s32[1]{0:T(128)} %bitcast.2.z, bf16[208,256]{1,0:T(8,128)(2,1)S(1)} %collective-permute-done.refs_0_, bf16[208,256]{1,0:T(8,128)(2,1)S(1)} %collective-permute-done.1.refs_1_, bf16[208,256]{1,0:T(8,128)(2,1)S(1)} %collective-permute-done.2.refs_2_, ...), custom_call_target="tpu_custom_call" | custom-call | flops 99999997952 | bytes 1000000000 | tf_op jit(solution)/shard_map/pick/pallas_call | solution.py:87
  32.7 0.0 copy-done.2
  32.7 3.8 %all-to-all-start.1 = ((bf16[16,208,256]{2,1,0:T(8,128)(2,1)}), bf16[16,208,256]{2,1,0:T(8,128)(2,1)S(1)}, u32[]{:S(2)}, u32[]{:S(2)}) async-start(bf16[16,208,256]{2,1,0:T(8,128)(2,1)} %pick.1), calls=%async_computation.1 | async-start | bytes 3407872 | tf_op jit(solution)/shard_map/all_to_all | solution.py:350
  36.6 0.0 copy-start.1
  36.6 0.6 cut.1
  37.2 4.6 %collective-permute-start.4 = (bf16[128,768]{1,0:T(8,128)(2,1)S(1)}, bf16[128,768]{1,0:T(8,128)(2,1)S(1)}, u32[]{:S(2)}, u32[]{:S(2)}) collective-permute-start(bf16[128,768]{1,0:T(8,128)(2,1)S(1)} %get-tuple-element.31), channel_id=1, source_target_pairs={{0,192},{64,128},{128,64},{192,0},{1,193},{65,129},{129,65},{193,1... | collective-permute-start | bytes 589832 | tf_op jit(solution)/shard_map/ppermute | solution.py:370
  41.8 4.0 %collective-permute-start.5 = (bf16[128,768]{1,0:T(8,128)(2,1)S(1)}, bf16[128,768]{1,0:T(8,128)(2,1)S(1)}, u32[]{:S(2)}, u32[]{:S(2)}) collective-permute-start(bf16[128,768]{1,0:T(8,128)(2,1)S(1)} %get-tuple-element.32), channel_id=1, source_target_pairs={{0,128},{64,192},{128,0},{192,64},{1,129},{65,193},{129,1},{193,65... | collective-permute-start | bytes 589832 | tf_op jit(solution)/shard_map/ppermute | solution.py:370
  45.8 0.0 collective-permute-start.6
  45.8 1.3 %collective-permute-done.4.other3 = bf16[128,768]{1,0:T(8,128)(2,1)S(1)} collective-permute-done((bf16[128,768]{1,0:T(8,128)(2,1)S(1)}, bf16[128,768]{1,0:T(8,128)(2,1)S(1)}, u32[]{:S(2)}, u32[]{:S(2)}) %collective-permute-start.4) | collective-permute-done | bytes 196640 | tf_op jit(solution)/shard_map/ppermute | solution.py:370
  47.1 7.0 %collective-permute-done.5.other2 = bf16[128,768]{1,0:T(8,128)(2,1)S(1)} collective-permute-done((bf16[128,768]{1,0:T(8,128)(2,1)S(1)}, bf16[128,768]{1,0:T(8,128)(2,1)S(1)}, u32[]{:S(2)}, u32[]{:S(2)}) %collective-permute-start.5) | collective-permute-done | bytes 196640 | tf_op jit(solution)/shard_map/ppermute | solution.py:370
  54.2 0.0 collective-permute-done.6.other1
  54.2 0.0 copy-done.1
  54.2 0.6 gather.1
  54.8 2.6 %all-to-all-done.1.got = bf16[16,208,256]{2,1,0:T(8,128)(2,1)S(1)} async-done(((bf16[16,208,256]{2,1,0:T(8,128)(2,1)}), bf16[16,208,256]{2,1,0:T(8,128)(2,1)S(1)}, u32[]{:S(2)}, u32[]{:S(2)}) %all-to-all-start.1) | async-done | bytes 1703968 | tf_op jit(solution)/shard_map/all_to_all | solution.py:350
  57.4 4.4 %layers.1 = (bf16[4,128,768]{2,1,0:T(8,128)(2,1)}, bf16[16,208,256]{2,1,0:T(8,128)(2,1)}) custom-call(s32[2]{0:T(128)S(1)} %pad_add_fusion.s, s32[1]{0:T(128)S(6)} %copy.13.own, bf16[128,768]{1,0:T(8,128)(2,1)S(1)} %get-tuple-element.34.top, bf16[16,208,256]{2,1,0:T(8,128)(2,1)S(1)} %all-to-all-done.1.got, bf16[4,128,768]{2,1,0:T(8,128)(2,1)S(1)} %get-tuple-element.35.x), custom_call_target="tpu_custom_call" | custom-call | flops 99999997952 | bytes 1000000000 | tf_op jit(solution)/shard_map/layers/pallas_call | solution.py:197
  61.8 6.5 %all-to-all-start.2 = ((bf16[16,208,256]{2,1,0:T(8,128)(2,1)}), bf16[16,208,256]{2,1,0:T(8,128)(2,1)S(1)}, u32[]{:S(2)}, u32[]{:S(2)}) async-start(bf16[16,208,256]{2,1,0:T(8,128)(2,1)} %get-tuple-element.41), calls=%async_computation.2 | async-start | bytes 3407872 | tf_op jit(solution)/shard_map/all_to_all | solution.py:350
  68.3 0.0 copy-start.3
  68.3 0.1 split.1
  68.4 5.0 %collective-permute-start.7 = (bf16[128,768]{1,0:T(8,128)(2,1)S(1)}, bf16[128,768]{1,0:T(8,128)(2,1)S(1)}, u32[]{:S(2)}, u32[]{:S(2)}) collective-permute-start(bf16[128,768]{1,0:T(8,128)(2,1)S(1)} %get-tuple-element.37), channel_id=1, source_target_pairs={{0,192},{64,128},{128,64},{192,0},{1,193},{65,129},{129,65},{193,1... | collective-permute-start | bytes 589832 | tf_op jit(solution)/shard_map/ppermute | solution.py:370
  73.4 3.2 %collective-permute-start.8 = (bf16[128,768]{1,0:T(8,128)(2,1)S(1)}, bf16[128,768]{1,0:T(8,128)(2,1)S(1)}, u32[]{:S(2)}, u32[]{:S(2)}) collective-permute-start(bf16[128,768]{1,0:T(8,128)(2,1)S(1)} %get-tuple-element.38), channel_id=1, source_target_pairs={{0,128},{64,192},{128,0},{192,64},{1,129},{65,193},{129,1},{193,65... | collective-permute-start | bytes 589832 | tf_op jit(solution)/shard_map/ppermute | solution.py:370
  76.7 0.0 collective-permute-start.9
  76.7 1.5 %collective-permute-done.7.other3 = bf16[128,768]{1,0:T(8,128)(2,1)S(1)} collective-permute-done((bf16[128,768]{1,0:T(8,128)(2,1)S(1)}, bf16[128,768]{1,0:T(8,128)(2,1)S(1)}, u32[]{:S(2)}, u32[]{:S(2)}) %collective-permute-start.7) | collective-permute-done | bytes 196640 | tf_op jit(solution)/shard_map/ppermute | solution.py:370
  78.1 6.2 %collective-permute-done.8.other2 = bf16[128,768]{1,0:T(8,128)(2,1)S(1)} collective-permute-done((bf16[128,768]{1,0:T(8,128)(2,1)S(1)}, bf16[128,768]{1,0:T(8,128)(2,1)S(1)}, u32[]{:S(2)}, u32[]{:S(2)}) %collective-permute-start.8) | collective-permute-done | bytes 196640 | tf_op jit(solution)/shard_map/ppermute | solution.py:370
  84.3 0.0 collective-permute-done.9.other1
  84.3 2.0 %join.1 = bf16[128,3072]{1,0:T(8,128)(2,1)} custom-call(s32[2]{0:T(128)S(1)} %pad_add_fusion.s, bf16[128,768]{1,0:T(8,128)(2,1)S(1)} %collective-permute-done.7.other3, bf16[128,768]{1,0:T(8,128)(2,1)S(1)} %collective-permute-done.8.other2, bf16[128,768]{1,0:T(8,128)(2,1)S(1)} %collective-permute-done.9.other1, bf16[128,768]{1,0:T(8,128)(2,1)S(1)} %get-tuple-element.40.own), custom_call_target="tpu_custom_call" | custom-call | tf_op jit(solution)/shard_map/join/pallas_call | solution.py:250
  86.4 3.1 %all-to-all-done.2.got = bf16[16,208,256]{2,1,0:T(8,128)(2,1)S(1)} async-done(((bf16[16,208,256]{2,1,0:T(8,128)(2,1)}), bf16[16,208,256]{2,1,0:T(8,128)(2,1)S(1)}, u32[]{:S(2)}, u32[]{:S(2)}) %all-to-all-start.2) | async-done | bytes 1703968 | tf_op jit(solution)/shard_map/all_to_all | solution.py:350
  89.5 1.2 merge.1
  90.6 13.1 %collective-permute-start.10 = (bf16[208,256]{1,0:T(8,128)(2,1)S(1)}, bf16[208,256]{1,0:T(8,128)(2,1)S(1)}, u32[]{:S(2)}, u32[]{:S(2)}) collective-permute-start(bf16[208,256]{1,0:T(8,128)(2,1)S(1)} %get-tuple-element.43), channel_id=1, source_target_pairs={{0,8},{4,44},{8,0},{12,36},{16,72},{20,108},{24,64},{28,100},{32,1... | collective-permute-start | bytes 319496 | tf_op jit(solution)/shard_map/ppermute | solution.py:365
  103.7 0.1 collective-permute-start.11
  103.8 5.4 %collective-permute-start.12 = (bf16[208,256]{1,0:T(8,128)(2,1)S(1)}, bf16[208,256]{1,0:T(8,128)(2,1)S(1)}, u32[]{:S(2)}, u32[]{:S(2)}) collective-permute-start(bf16[208,256]{1,0:T(8,128)(2,1)S(1)} %get-tuple-element.45), channel_id=1, source_target_pairs={{0,12},{4,32},{8,4},{12,40},{16,76},{20,96},{24,68},{28,104},{32,1... | collective-permute-start | bytes 319496 | tf_op jit(solution)/shard_map/ppermute | solution.py:365
  109.2 3.8 %collective-permute-start.13 = (bf16[208,256]{1,0:T(8,128)(2,1)S(1)}, bf16[208,256]{1,0:T(8,128)(2,1)S(1)}, u32[]{:S(2)}, u32[]{:S(2)}) collective-permute-start(bf16[208,256]{1,0:T(8,128)(2,1)S(1)} %get-tuple-element.46), channel_id=1, source_target_pairs={{0,0},{4,36},{8,8},{12,44},{16,64},{20,100},{24,72},{28,108},{32,1... | collective-permute-start | bytes 319496 | tf_op jit(solution)/shard_map/ppermute | solution.py:365
  113.0 0.0 collective-permute-done.10.refs_0_
  113.0 7.9 %collective-permute-done.11.refs_1_ = bf16[208,256]{1,0:T(8,128)(2,1)S(1)} collective-permute-done((bf16[208,256]{1,0:T(8,128)(2,1)S(1)}, bf16[208,256]{1,0:T(8,128)(2,1)S(1)}, u32[]{:S(2)}, u32[]{:S(2)}) %collective-permute-start.11) | collective-permute-done | bytes 106528 | tf_op jit(solution)/shard_map/ppermute | solution.py:365
  120.9 0.0 collective-permute-done.12.refs_2_
  121.0 0.0 collective-permute-done.13.refs_3_
  121.0 0.8 finish.1
  (10 shorter events, 0.0 us)
Async XLA Ops:
  2.9 27.8 %collective-permute-start.3 = (bf16[208,256]{1,0:T(8,128)(2,1)}, bf16[208,256]{1,0:T(8,128)(2,1)S(1)}, u32[]{:S(2)}, u32[]{:S(2)}) collective-permute-start(bf16[208,256]{1,0:T(8,128)(2,1)} %get-tuple-element.29), channel_id=1, source_target_pairs={{0,8},{4,140},{8,0},{12,132},{16,72},{20,204},{24,64},{28,196},{32... | collective-permute-start | bytes 319496 | tf_op jit(solution)/shard_map/ppermute | solution.py:365
  8.3 22.4 %collective-permute-start.2 = (bf16[208,256]{1,0:T(8,128)(2,1)}, bf16[208,256]{1,0:T(8,128)(2,1)S(1)}, u32[]{:S(2)}, u32[]{:S(2)}) collective-permute-start(bf16[208,256]{1,0:T(8,128)(2,1)} %get-tuple-element.29), channel_id=1, source_target_pairs={{0,140},{4,0},{8,132},{12,8},{16,204},{20,64},{24,196},{28,72},{32... | collective-permute-start | bytes 319496 | tf_op jit(solution)/shard_map/ppermute | solution.py:365
  12.8 17.9 %collective-permute-start.1 = (bf16[208,256]{1,0:T(8,128)(2,1)}, bf16[208,256]{1,0:T(8,128)(2,1)S(1)}, u32[]{:S(2)}, u32[]{:S(2)}) collective-permute-start(bf16[208,256]{1,0:T(8,128)(2,1)} %get-tuple-element.29), channel_id=1, source_target_pairs={{0,132},{4,8},{8,140},{12,0},{16,196},{20,72},{24,204},{28,64},{32... | collective-permute-start | bytes 319496 | tf_op jit(solution)/shard_map/ppermute | solution.py:365
  17.0 13.7 %collective-permute-start = (bf16[208,256]{1,0:T(8,128)(2,1)}, bf16[208,256]{1,0:T(8,128)(2,1)S(1)}, u32[]{:S(2)}, u32[]{:S(2)}) collective-permute-start(bf16[208,256]{1,0:T(8,128)(2,1)} %get-tuple-element.29), channel_id=1, source_target_pairs={{0,0},{4,132},{8,8},{12,140},{16,64},{20,196},{24,72},{28,204},{32... | collective-permute-start | bytes 319496 | tf_op jit(solution)/shard_map/ppermute | solution.py:365
  20.0 10.7 %all-to-all-start = ((s32[16,1,128]{2,1,0:T(1,128)}), s32[16,1,128]{2,1,0:T(1,128)S(1)}, u32[]{:S(2)}, u32[]{:S(2)}) async-start(s32[16,1,128]{2,1,0:T(1,128)} %get-tuple-element.28), calls=%async_computation | async-start | bytes 16384 | tf_op jit(solution)/shard_map/all_to_all | solution.py:350
  30.7 2.1 %copy-start.2 = (s32[16,1,128]{2,1,0:T(1,128)}, s32[16,1,128]{2,1,0:T(1,128)S(1)}, u32[]{:S(2)}) copy-start(s32[16,1,128]{2,1,0:T(1,128)S(1)} %all-to-all-done) | copy-start | bytes 24580
  32.7 3.9 %copy-start = (bf16[1,128,3072]{2,1,0:T(8,128)(2,1)S(1)}, bf16[1,128,3072]{2,1,0:T(8,128)(2,1)}, u32[]{:S(2)}) copy-start(bf16[1,128,3072]{2,1,0:T(8,128)(2,1)} %param.7) | copy-start | bytes 2359300
  32.7 24.6 %all-to-all-start.1 = ((bf16[16,208,256]{2,1,0:T(8,128)(2,1)}), bf16[16,208,256]{2,1,0:T(8,128)(2,1)S(1)}, u32[]{:S(2)}, u32[]{:S(2)}) async-start(bf16[16,208,256]{2,1,0:T(8,128)(2,1)} %pick.1), calls=%async_computation.1 | async-start | bytes 3407872 | tf_op jit(solution)/shard_map/all_to_all | solution.py:350
  36.6 17.6 %copy-start.1 = (bf16[128,3072]{1,0:T(8,128)(2,1)S(1)}, bf16[128,3072]{1,0:T(8,128)(2,1)}, u32[]{:S(2)}) copy-start(bf16[128,3072]{1,0:T(8,128)(2,1)} %cotangent.1) | copy-start | bytes 2359300
  37.2 9.9 %collective-permute-start.4 = (bf16[128,768]{1,0:T(8,128)(2,1)S(1)}, bf16[128,768]{1,0:T(8,128)(2,1)S(1)}, u32[]{:S(2)}, u32[]{:S(2)}) collective-permute-start(bf16[128,768]{1,0:T(8,128)(2,1)S(1)} %get-tuple-element.31), channel_id=1, source_target_pairs={{0,192},{64,128},{128,64},{192,0},{1,193},{65,129},{129,65},{193,1... | collective-permute-start | bytes 589832 | tf_op jit(solution)/shard_map/ppermute | solution.py:370
  41.8 12.4 %collective-permute-start.5 = (bf16[128,768]{1,0:T(8,128)(2,1)S(1)}, bf16[128,768]{1,0:T(8,128)(2,1)S(1)}, u32[]{:S(2)}, u32[]{:S(2)}) collective-permute-start(bf16[128,768]{1,0:T(8,128)(2,1)S(1)} %get-tuple-element.32), channel_id=1, source_target_pairs={{0,128},{64,192},{128,0},{192,64},{1,129},{65,193},{129,1},{193,65... | collective-permute-start | bytes 589832 | tf_op jit(solution)/shard_map/ppermute | solution.py:370
  45.8 8.3 %collective-permute-start.6 = (bf16[128,768]{1,0:T(8,128)(2,1)S(1)}, bf16[128,768]{1,0:T(8,128)(2,1)S(1)}, u32[]{:S(2)}, u32[]{:S(2)}) collective-permute-start(bf16[128,768]{1,0:T(8,128)(2,1)S(1)} %get-tuple-element.33), channel_id=1, source_target_pairs={{0,64},{64,0},{128,192},{192,128},{1,65},{65,1},{129,193},{193,129... | collective-permute-start | bytes 589832 | tf_op jit(solution)/shard_map/ppermute | solution.py:370
  61.8 6.5 %copy-start.6 = (bf16[4,128,768]{2,1,0:T(8,128)(2,1)S(1)}, bf16[4,128,768]{2,1,0:T(8,128)(2,1)}, u32[]{:S(2)}) copy-start(bf16[4,128,768]{2,1,0:T(8,128)(2,1)} %get-tuple-element.36.out) | copy-start | bytes 2359300
  61.8 27.7 %all-to-all-start.2 = ((bf16[16,208,256]{2,1,0:T(8,128)(2,1)}), bf16[16,208,256]{2,1,0:T(8,128)(2,1)S(1)}, u32[]{:S(2)}, u32[]{:S(2)}) async-start(bf16[16,208,256]{2,1,0:T(8,128)(2,1)} %get-tuple-element.41), calls=%async_computation.2 | async-start | bytes 3407872 | tf_op jit(solution)/shard_map/all_to_all | solution.py:350
  68.3 21.1 %copy-start.3 = (s32[16,1,128]{2,1,0:T(1,128)S(1)}, s32[16,1,128]{2,1,0:T(1,128)}, u32[]{:S(2)}) copy-start(s32[16,1,128]{2,1,0:T(1,128)} %copy-done.2) | copy-start | bytes 24580
  68.4 9.7 %collective-permute-start.7 = (bf16[128,768]{1,0:T(8,128)(2,1)S(1)}, bf16[128,768]{1,0:T(8,128)(2,1)S(1)}, u32[]{:S(2)}, u32[]{:S(2)}) collective-permute-start(bf16[128,768]{1,0:T(8,128)(2,1)S(1)} %get-tuple-element.37), channel_id=1, source_target_pairs={{0,192},{64,128},{128,64},{192,0},{1,193},{65,129},{129,65},{193,1... | collective-permute-start | bytes 589832 | tf_op jit(solution)/shard_map/ppermute | solution.py:370
  73.4 10.9 %collective-permute-start.8 = (bf16[128,768]{1,0:T(8,128)(2,1)S(1)}, bf16[128,768]{1,0:T(8,128)(2,1)S(1)}, u32[]{:S(2)}, u32[]{:S(2)}) collective-permute-start(bf16[128,768]{1,0:T(8,128)(2,1)S(1)} %get-tuple-element.38), channel_id=1, source_target_pairs={{0,128},{64,192},{128,0},{192,64},{1,129},{65,193},{129,1},{193,65... | collective-permute-start | bytes 589832 | tf_op jit(solution)/shard_map/ppermute | solution.py:370
  76.7 7.7 %collective-permute-start.9 = (bf16[128,768]{1,0:T(8,128)(2,1)S(1)}, bf16[128,768]{1,0:T(8,128)(2,1)S(1)}, u32[]{:S(2)}, u32[]{:S(2)}) collective-permute-start(bf16[128,768]{1,0:T(8,128)(2,1)S(1)} %get-tuple-element.39), channel_id=1, source_target_pairs={{0,64},{64,0},{128,192},{192,128},{1,65},{65,1},{129,193},{193,129... | collective-permute-start | bytes 589832 | tf_op jit(solution)/shard_map/ppermute | solution.py:370
  86.4 34.6 %copy-start.4 = (bf16[1,4,48,256]{3,2,1,0:T(8,128)(2,1)S(1)}, bf16[1,4,48,256]{3,2,1,0:T(8,128)(2,1)}, u32[]{:S(2)}) copy-start(bf16[1,4,48,256]{3,2,1,0:T(8,128)(2,1)} %param.11) | copy-start | bytes 294916
  86.4 34.6 %copy-start.5 = (bf16[1,48,256]{2,1,0:T(8,128)(2,1)S(1)}, bf16[1,48,256]{2,1,0:T(8,128)(2,1)}, u32[]{:S(2)}) copy-start(bf16[1,48,256]{2,1,0:T(8,128)(2,1)} %param.10) | copy-start | bytes 73732
  90.6 22.4 %collective-permute-start.10 = (bf16[208,256]{1,0:T(8,128)(2,1)S(1)}, bf16[208,256]{1,0:T(8,128)(2,1)S(1)}, u32[]{:S(2)}, u32[]{:S(2)}) collective-permute-start(bf16[208,256]{1,0:T(8,128)(2,1)S(1)} %get-tuple-element.43), channel_id=1, source_target_pairs={{0,8},{4,44},{8,0},{12,36},{16,72},{20,108},{24,64},{28,100},{32,1... | collective-permute-start | bytes 319496 | tf_op jit(solution)/shard_map/ppermute | solution.py:365
  103.7 17.3 %collective-permute-start.11 = (bf16[208,256]{1,0:T(8,128)(2,1)S(1)}, bf16[208,256]{1,0:T(8,128)(2,1)S(1)}, u32[]{:S(2)}, u32[]{:S(2)}) collective-permute-start(bf16[208,256]{1,0:T(8,128)(2,1)S(1)} %get-tuple-element.44), channel_id=1, source_target_pairs={{0,4},{4,40},{8,12},{12,32},{16,68},{20,104},{24,76},{28,96},{32,1... | collective-permute-start | bytes 319496 | tf_op jit(solution)/shard_map/ppermute | solution.py:365
  103.8 17.1 %collective-permute-start.12 = (bf16[208,256]{1,0:T(8,128)(2,1)S(1)}, bf16[208,256]{1,0:T(8,128)(2,1)S(1)}, u32[]{:S(2)}, u32[]{:S(2)}) collective-permute-start(bf16[208,256]{1,0:T(8,128)(2,1)S(1)} %get-tuple-element.45), channel_id=1, source_target_pairs={{0,12},{4,32},{8,4},{12,40},{16,76},{20,96},{24,68},{28,104},{32,1... | collective-permute-start | bytes 319496 | tf_op jit(solution)/shard_map/ppermute | solution.py:365
  109.2 11.8 %collective-permute-start.13 = (bf16[208,256]{1,0:T(8,128)(2,1)S(1)}, bf16[208,256]{1,0:T(8,128)(2,1)S(1)}, u32[]{:S(2)}, u32[]{:S(2)}) collective-permute-start(bf16[208,256]{1,0:T(8,128)(2,1)S(1)} %get-tuple-element.46), channel_id=1, source_target_pairs={{0,0},{4,36},{8,8},{12,44},{16,64},{20,100},{24,72},{28,108},{32,1... | collective-permute-start | bytes 319496 | tf_op jit(solution)/shard_map/ppermute | solution.py:365

commit v11 on v10

--- a/solution.py
+++ b/solution.py
@@ -87,10 +87,10 @@
     return call(
         pick_kernel,
         "pick",
-        grid=(2,),
+        grid=(1,),
         out_shape=jax.ShapeDtypeStruct((NY * NX, BLOCK, GS), BF),
         in_specs=[SMEM, SMEM] + [pl.BlockSpec((BLOCK, GS), lambda i: (0, 0))] * NZ,
-        out_specs=pl.BlockSpec((NY * NX // 2, BLOCK, GS), lambda i: (i, 0, 0)),
+        out_specs=pl.BlockSpec((NY * NX, BLOCK, GS), lambda i: (i, 0, 0)),
     )(ids, z, held[0], held[1], held[3], held[2])
 
 
@@ -273,7 +273,7 @@
         domain = ids[step * got.shape[0] + i, 0]
         total[domain] += got[i].astype(F32)
 
-    @pl.when(step == 1)
+    @pl.when(step == 0)
     def _():
         tile[...] = jnp.zeros_like(tile)
         for k in range(DOMAINS):
@@ -293,9 +293,9 @@
     return call(
         merge_kernel,
         "merge",
-        grid=(2,),
+        grid=(1,),
         out_shape=(jax.ShapeDtypeStruct((BLOCK, GS), BF),) * NZ,
-        in_specs=[SMEM, SMEM, pl.BlockSpec((NY * NX // 2, BLOCK, GS), lambda i: (i, 0, 0))],
+        in_specs=[SMEM, SMEM, pl.BlockSpec((NY * NX, BLOCK, GS), lambda i: (i, 0, 0))],
         out_specs=(pl.BlockSpec((BLOCK, GS), lambda i: (0, 0)),) * NZ,
         scratch_shapes=[
             pltpu.VMEM((DOMAINS, BLOCK, GS), F32),

time: 123 us -> 123 us (level)
  no operation moved by 1% of the time
where the time goes in v11:
time: 123 us; the launch traced here: 122 us
  starting transfers between devices  71.1 us (58%)
  waiting for transfers between devices  35.9 us (29%)
  Pallas kernels  13.2 us (11%)
  between operations  1.46 us (1%)
    ppermute x8, starting transfers between devices, turned(): return lax.ppermute(block, ('zhi', 'core', 'y', 'zlo'), pairs)  39.5 us
    ppermute x6, starting transfers between devices, swapped(): return lax.ppermute(block, ('zhi', 'core'), pairs)  16.9 us
    ppermute x6, waiting for transfers between devices, swapped(): return lax.ppermute(block, ('zhi', 'core'), pairs)  16 us
    all_to_all x3, starting transfers between devices, exchange(): return lax.all_to_all(block, axes, 0, 0, tiled=True)  14.7 us
    all_to_all x3, waiting for transfers between devices, exchange(): return lax.all_to_all(block, axes, 0, 0, tiled=True)  11.9 us
    ppermute x8, waiting for transfers between devices, turned(): return lax.ppermute(block, ('zhi', 'core', 'y', 'zlo'), pairs)  7.94 us
    pallas_call x1, Pallas kernels, layers(): call(layers_kernel, 'layers', out_shape=(pltpu.HBM((SECTIONS, ROWS, SLAB)...  4.38 us
  transfers between devices with their start and end apart: 17, of which 8 were waited for; matrix products, arithmetic and copies ran while one was open for 0% of the time, Pallas kernels for 3%

profile of v11, /device:TPU:1, one launch (start us, length us, event | category | flops | bytes accessed | tf_op | source)
XLA Modules:
  0.0 121.7 jit_solution(6278344763065353199)
XLA Ops:
  1.3 1.6 %prep.1 = (bf16[208,256]{1,0:T(8,128)(2,1)}, s32[16,1,128]{2,1,0:T(1,128)}) custom-call(s32[1]{0:T(128)S(6)} %add.16.at, s32[1]{0:T(128)S(6)} %copy.13.own, bf16[48,256]{1,0:T(8,128)(2,1)} %bitcast.21, bf16[4,48,256]{2,1,0:T(8,128)(2,1)} %bitcast.19, bf16[1,48]{1,0:T(2,128)(2,1)} %sb.1, bf16[4,48]{1,0:T(4,128)(2,1)} %bitcast.24), custom_call_target="tpu_custom_call" | custom-call | flops 99999997952 | bytes 1000000000 | tf_op jit(solution)/shard_map/prep/pallas_call | solution.py:57
  2.9 5.4 %collective-permute-start.3 = (bf16[208,256]{1,0:T(8,128)(2,1)}, bf16[208,256]{1,0:T(8,128)(2,1)S(1)}, u32[]{:S(2)}, u32[]{:S(2)}) collective-permute-start(bf16[208,256]{1,0:T(8,128)(2,1)} %get-tuple-element.29), channel_id=1, source_target_pairs={{0,8},{4,140},{8,0},{12,132},{16,72},{20,204},{24,64},{28,196},{32... | collective-permute-start | bytes 319496 | tf_op jit(solution)/shard_map/ppermute | solution.py:365
  8.3 4.5 %collective-permute-start.2 = (bf16[208,256]{1,0:T(8,128)(2,1)}, bf16[208,256]{1,0:T(8,128)(2,1)S(1)}, u32[]{:S(2)}, u32[]{:S(2)}) collective-permute-start(bf16[208,256]{1,0:T(8,128)(2,1)} %get-tuple-element.29), channel_id=1, source_target_pairs={{0,140},{4,0},{8,132},{12,8},{16,204},{20,64},{24,196},{28,72},{32... | collective-permute-start | bytes 319496 | tf_op jit(solution)/shard_map/ppermute | solution.py:365
  12.8 4.2 %collective-permute-start.1 = (bf16[208,256]{1,0:T(8,128)(2,1)}, bf16[208,256]{1,0:T(8,128)(2,1)S(1)}, u32[]{:S(2)}, u32[]{:S(2)}) collective-permute-start(bf16[208,256]{1,0:T(8,128)(2,1)} %get-tuple-element.29), channel_id=1, source_target_pairs={{0,132},{4,8},{8,140},{12,0},{16,196},{20,72},{24,204},{28,64},{32... | collective-permute-start | bytes 319496 | tf_op jit(solution)/shard_map/ppermute | solution.py:365
  17.0 3.0 %collective-permute-start = (bf16[208,256]{1,0:T(8,128)(2,1)}, bf16[208,256]{1,0:T(8,128)(2,1)S(1)}, u32[]{:S(2)}, u32[]{:S(2)}) collective-permute-start(bf16[208,256]{1,0:T(8,128)(2,1)} %get-tuple-element.29), channel_id=1, source_target_pairs={{0,0},{4,132},{8,8},{12,140},{16,64},{20,196},{24,72},{28,204},{32... | collective-permute-start | bytes 319496 | tf_op jit(solution)/shard_map/ppermute | solution.py:365
  20.0 4.3 %all-to-all-start = ((s32[16,1,128]{2,1,0:T(1,128)}), s32[16,1,128]{2,1,0:T(1,128)S(1)}, u32[]{:S(2)}, u32[]{:S(2)}) async-start(s32[16,1,128]{2,1,0:T(1,128)} %get-tuple-element.28), calls=%async_computation | async-start | bytes 16384 | tf_op jit(solution)/shard_map/all_to_all | solution.py:350
  24.4 0.1 pad_add_fusion.s
  24.5 6.2 %all-to-all-done = s32[16,1,128]{2,1,0:T(1,128)S(1)} async-done(((s32[16,1,128]{2,1,0:T(1,128)}), s32[16,1,128]{2,1,0:T(1,128)S(1)}, u32[]{:S(2)}, u32[]{:S(2)}) %all-to-all-start) | async-done | bytes 8224 | tf_op jit(solution)/shard_map/all_to_all | solution.py:350
  30.7 0.0 collective-permute-done.3.refs_3_
  30.7 0.0 collective-permute-done.2.refs_2_
  30.7 0.0 collective-permute-done.1.refs_1_
  30.7 0.0 collective-permute-done.refs_0_
  30.7 2.0 %pick.1 = bf16[16,208,256]{2,1,0:T(8,128)(2,1)} custom-call(s32[16,128]{1,0:T(8,128)S(1)} %bitcast.17, s32[1]{0:T(128)} %bitcast.2.z, bf16[208,256]{1,0:T(8,128)(2,1)S(1)} %collective-permute-done.refs_0_, bf16[208,256]{1,0:T(8,128)(2,1)S(1)} %collective-permute-done.1.refs_1_, bf16[208,256]{1,0:T(8,128)(2,1)S(1)} %collective-permute-done.2.refs_2_, ...), custom_call_target="tpu_custom_call" | custom-call | flops 99999997952 | bytes 1000000000 | tf_op jit(solution)/shard_map/pick/pallas_call | solution.py:87
  32.7 0.0 copy-done.2
  32.7 3.8 %all-to-all-start.1 = ((bf16[16,208,256]{2,1,0:T(8,128)(2,1)}), bf16[16,208,256]{2,1,0:T(8,128)(2,1)S(1)}, u32[]{:S(2)}, u32[]{:S(2)}) async-start(bf16[16,208,256]{2,1,0:T(8,128)(2,1)} %pick.1), calls=%async_computation.1 | async-start | bytes 3407872 | tf_op jit(solution)/shard_map/all_to_all | solution.py:350
  36.6 0.0 copy-start.1
  36.6 0.6 cut.1
  37.2 4.6 %collective-permute-start.4 = (bf16[128,768]{1,0:T(8,128)(2,1)S(1)}, bf16[128,768]{1,0:T(8,128)(2,1)S(1)}, u32[]{:S(2)}, u32[]{:S(2)}) collective-permute-start(bf16[128,768]{1,0:T(8,128)(2,1)S(1)} %get-tuple-element.31), channel_id=1, source_target_pairs={{0,192},{64,128},{128,64},{192,0},{1,193},{65,129},{129,65},{193,1... | collective-permute-start | bytes 589832 | tf_op jit(solution)/shard_map/ppermute | solution.py:370
  41.8 4.0 %collective-permute-start.5 = (bf16[128,768]{1,0:T(8,128)(2,1)S(1)}, bf16[128,768]{1,0:T(8,128)(2,1)S(1)}, u32[]{:S(2)}, u32[]{:S(2)}) collective-permute-start(bf16[128,768]{1,0:T(8,128)(2,1)S(1)} %get-tuple-element.32), channel_id=1, source_target_pairs={{0,128},{64,192},{128,0},{192,64},{1,129},{65,193},{129,1},{193,65... | collective-permute-start | bytes 589832 | tf_op jit(solution)/shard_map/ppermute | solution.py:370
  45.8 0.0 collective-permute-start.6
  45.8 1.3 %collective-permute-done.4.other3 = bf16[128,768]{1,0:T(8,128)(2,1)S(1)} collective-permute-done((bf16[128,768]{1,0:T(8,128)(2,1)S(1)}, bf16[128,768]{1,0:T(8,128)(2,1)S(1)}, u32[]{:S(2)}, u32[]{:S(2)}) %collective-permute-start.4) | collective-permute-done | bytes 196640 | tf_op jit(solution)/shard_map/ppermute | solution.py:370
  47.1 7.0 %collective-permute-done.5.other2 = bf16[128,768]{1,0:T(8,128)(2,1)S(1)} collective-permute-done((bf16[128,768]{1,0:T(8,128)(2,1)S(1)}, bf16[128,768]{1,0:T(8,128)(2,1)S(1)}, u32[]{:S(2)}, u32[]{:S(2)}) %collective-permute-start.5) | collective-permute-done | bytes 196640 | tf_op jit(solution)/shard_map/ppermute | solution.py:370
  54.1 0.0 collective-permute-done.6.other1
  54.2 0.6 gather.1
  54.8 2.6 %all-to-all-done.1.got = bf16[16,208,256]{2,1,0:T(8,128)(2,1)S(1)} async-done(((bf16[16,208,256]{2,1,0:T(8,128)(2,1)}), bf16[16,208,256]{2,1,0:T(8,128)(2,1)S(1)}, u32[]{:S(2)}, u32[]{:S(2)}) %all-to-all-start.1) | async-done | bytes 1703968 | tf_op jit(solution)/shard_map/all_to_all | solution.py:350
  57.4 4.4 %layers.1 = (bf16[4,128,768]{2,1,0:T(8,128)(2,1)}, bf16[16,208,256]{2,1,0:T(8,128)(2,1)}) custom-call(s32[2]{0:T(128)S(1)} %pad_add_fusion.s, s32[1]{0:T(128)S(6)} %copy.13.own, bf16[128,768]{1,0:T(8,128)(2,1)S(1)} %get-tuple-element.34.top, bf16[16,208,256]{2,1,0:T(8,128)(2,1)S(1)} %all-to-all-done.1.got, bf16[4,128,768]{2,1,0:T(8,128)(2,1)S(1)} %get-tuple-element.35.x), custom_call_target="tpu_custom_call" | custom-call | flops 99999997952 | bytes 1000000000 | tf_op jit(solution)/shard_map/layers/pallas_call | solution.py:197
  61.8 6.5 %all-to-all-start.2 = ((bf16[16,208,256]{2,1,0:T(8,128)(2,1)}), bf16[16,208,256]{2,1,0:T(8,128)(2,1)S(1)}, u32[]{:S(2)}, u32[]{:S(2)}) async-start(bf16[16,208,256]{2,1,0:T(8,128)(2,1)} %get-tuple-element.41), calls=%async_computation.2 | async-start | bytes 3407872 | tf_op jit(solution)/shard_map/all_to_all | solution.py:350
  68.3 0.0 copy-start.3
  68.3 0.1 split.1
  68.4 5.0 %collective-permute-start.7 = (bf16[128,768]{1,0:T(8,128)(2,1)S(1)}, bf16[128,768]{1,0:T(8,128)(2,1)S(1)}, u32[]{:S(2)}, u32[]{:S(2)}) collective-permute-start(bf16[128,768]{1,0:T(8,128)(2,1)S(1)} %get-tuple-element.37), channel_id=1, source_target_pairs={{0,192},{64,128},{128,64},{192,0},{1,193},{65,129},{129,65},{193,1... | collective-permute-start | bytes 589832 | tf_op jit(solution)/shard_map/ppermute | solution.py:370
  73.4 3.2 %collective-permute-start.8 = (bf16[128,768]{1,0:T(8,128)(2,1)S(1)}, bf16[128,768]{1,0:T(8,128)(2,1)S(1)}, u32[]{:S(2)}, u32[]{:S(2)}) collective-permute-start(bf16[128,768]{1,0:T(8,128)(2,1)S(1)} %get-tuple-element.38), channel_id=1, source_target_pairs={{0,128},{64,192},{128,0},{192,64},{1,129},{65,193},{129,1},{193,65... | collective-permute-start | bytes 589832 | tf_op jit(solution)/shard_map/ppermute | solution.py:370
  76.7 0.0 collective-permute-start.9
  76.7 1.5 %collective-permute-done.7.other3 = bf16[128,768]{1,0:T(8,128)(2,1)S(1)} collective-permute-done((bf16[128,768]{1,0:T(8,128)(2,1)S(1)}, bf16[128,768]{1,0:T(8,128)(2,1)S(1)}, u32[]{:S(2)}, u32[]{:S(2)}) %collective-permute-start.7) | collective-permute-done | bytes 196640 | tf_op jit(solution)/shard_map/ppermute | solution.py:370
  78.1 6.2 %collective-permute-done.8.other2 = bf16[128,768]{1,0:T(8,128)(2,1)S(1)} collective-permute-done((bf16[128,768]{1,0:T(8,128)(2,1)S(1)}, bf16[128,768]{1,0:T(8,128)(2,1)S(1)}, u32[]{:S(2)}, u32[]{:S(2)}) %collective-permute-start.8) | collective-permute-done | bytes 196640 | tf_op jit(solution)/shard_map/ppermute | solution.py:370
  84.3 0.0 collective-permute-done.9.other1
  84.3 2.0 %join.1 = bf16[128,3072]{1,0:T(8,128)(2,1)} custom-call(s32[2]{0:T(128)S(1)} %pad_add_fusion.s, bf16[128,768]{1,0:T(8,128)(2,1)S(1)} %collective-permute-done.7.other3, bf16[128,768]{1,0:T(8,128)(2,1)S(1)} %collective-permute-done.8.other2, bf16[128,768]{1,0:T(8,128)(2,1)S(1)} %collective-permute-done.9.other1, bf16[128,768]{1,0:T(8,128)(2,1)S(1)} %get-tuple-element.40.own), custom_call_target="tpu_custom_call" | custom-call | tf_op jit(solution)/shard_map/join/pallas_call | solution.py:250
  86.4 3.1 %all-to-all-done.2.got = bf16[16,208,256]{2,1,0:T(8,128)(2,1)S(1)} async-done(((bf16[16,208,256]{2,1,0:T(8,128)(2,1)}), bf16[16,208,256]{2,1,0:T(8,128)(2,1)S(1)}, u32[]{:S(2)}, u32[]{:S(2)}) %all-to-all-start.2) | async-done | bytes 1703968 | tf_op jit(solution)/shard_map/all_to_all | solution.py:350
  89.5 1.1 merge.1
  90.6 13.0 %collective-permute-start.10 = (bf16[208,256]{1,0:T(8,128)(2,1)S(1)}, bf16[208,256]{1,0:T(8,128)(2,1)S(1)}, u32[]{:S(2)}, u32[]{:S(2)}) collective-permute-start(bf16[208,256]{1,0:T(8,128)(2,1)S(1)} %get-tuple-element.43), channel_id=1, source_target_pairs={{0,8},{4,44},{8,0},{12,36},{16,72},{20,108},{24,64},{28,100},{32,1... | collective-permute-start | bytes 319496 | tf_op jit(solution)/shard_map/ppermute | solution.py:365
  103.6 0.2 collective-permute-start.11
  103.8 5.4 %collective-permute-start.12 = (bf16[208,256]{1,0:T(8,128)(2,1)S(1)}, bf16[208,256]{1,0:T(8,128)(2,1)S(1)}, u32[]{:S(2)}, u32[]{:S(2)}) collective-permute-start(bf16[208,256]{1,0:T(8,128)(2,1)S(1)} %get-tuple-element.45), channel_id=1, source_target_pairs={{0,12},{4,32},{8,4},{12,40},{16,76},{20,96},{24,68},{28,104},{32,1... | collective-permute-start | bytes 319496 | tf_op jit(solution)/shard_map/ppermute | solution.py:365
  109.2 3.8 %collective-permute-start.13 = (bf16[208,256]{1,0:T(8,128)(2,1)S(1)}, bf16[208,256]{1,0:T(8,128)(2,1)S(1)}, u32[]{:S(2)}, u32[]{:S(2)}) collective-permute-start(bf16[208,256]{1,0:T(8,128)(2,1)S(1)} %get-tuple-element.46), channel_id=1, source_target_pairs={{0,0},{4,36},{8,8},{12,44},{16,64},{20,100},{24,72},{28,108},{32,1... | collective-permute-start | bytes 319496 | tf_op jit(solution)/shard_map/ppermute | solution.py:365
  113.0 0.0 collective-permute-done.10.refs_0_
  113.0 7.9 %collective-permute-done.11.refs_1_ = bf16[208,256]{1,0:T(8,128)(2,1)S(1)} collective-permute-done((bf16[208,256]{1,0:T(8,128)(2,1)S(1)}, bf16[208,256]{1,0:T(8,128)(2,1)S(1)}, u32[]{:S(2)}, u32[]{:S(2)}) %collective-permute-start.11) | collective-permute-done | bytes 106528 | tf_op jit(solution)/shard_map/ppermute | solution.py:365
  120.9 0.0 collective-permute-done.12.refs_2_
  120.9 0.0 collective-permute-done.13.refs_3_
  120.9 0.0 copy-done.5
  120.9 0.8 finish.1
  (10 shorter events, 0.0 us)
Async XLA Ops:
  2.9 27.8 %collective-permute-start.3 = (bf16[208,256]{1,0:T(8,128)(2,1)}, bf16[208,256]{1,0:T(8,128)(2,1)S(1)}, u32[]{:S(2)}, u32[]{:S(2)}) collective-permute-start(bf16[208,256]{1,0:T(8,128)(2,1)} %get-tuple-element.29), channel_id=1, source_target_pairs={{0,8},{4,140},{8,0},{12,132},{16,72},{20,204},{24,64},{28,196},{32... | collective-permute-start | bytes 319496 | tf_op jit(solution)/shard_map/ppermute | solution.py:365
  8.3 22.4 %collective-permute-start.2 = (bf16[208,256]{1,0:T(8,128)(2,1)}, bf16[208,256]{1,0:T(8,128)(2,1)S(1)}, u32[]{:S(2)}, u32[]{:S(2)}) collective-permute-start(bf16[208,256]{1,0:T(8,128)(2,1)} %get-tuple-element.29), channel_id=1, source_target_pairs={{0,140},{4,0},{8,132},{12,8},{16,204},{20,64},{24,196},{28,72},{32... | collective-permute-start | bytes 319496 | tf_op jit(solution)/shard_map/ppermute | solution.py:365
  12.8 17.9 %collective-permute-start.1 = (bf16[208,256]{1,0:T(8,128)(2,1)}, bf16[208,256]{1,0:T(8,128)(2,1)S(1)}, u32[]{:S(2)}, u32[]{:S(2)}) collective-permute-start(bf16[208,256]{1,0:T(8,128)(2,1)} %get-tuple-element.29), channel_id=1, source_target_pairs={{0,132},{4,8},{8,140},{12,0},{16,196},{20,72},{24,204},{28,64},{32... | collective-permute-start | bytes 319496 | tf_op jit(solution)/shard_map/ppermute | solution.py:365
  17.0 13.7 %collective-permute-start = (bf16[208,256]{1,0:T(8,128)(2,1)}, bf16[208,256]{1,0:T(8,128)(2,1)S(1)}, u32[]{:S(2)}, u32[]{:S(2)}) collective-permute-start(bf16[208,256]{1,0:T(8,128)(2,1)} %get-tuple-element.29), channel_id=1, source_target_pairs={{0,0},{4,132},{8,8},{12,140},{16,64},{20,196},{24,72},{28,204},{32... | collective-permute-start | bytes 319496 | tf_op jit(solution)/shard_map/ppermute | solution.py:365
  20.0 10.7 %all-to-all-start = ((s32[16,1,128]{2,1,0:T(1,128)}), s32[16,1,128]{2,1,0:T(1,128)S(1)}, u32[]{:S(2)}, u32[]{:S(2)}) async-start(s32[16,1,128]{2,1,0:T(1,128)} %get-tuple-element.28), calls=%async_computation | async-start | bytes 16384 | tf_op jit(solution)/shard_map/all_to_all | solution.py:350
  30.7 2.1 %copy-start.2 = (s32[16,1,128]{2,1,0:T(1,128)}, s32[16,1,128]{2,1,0:T(1,128)S(1)}, u32[]{:S(2)}) copy-start(s32[16,1,128]{2,1,0:T(1,128)S(1)} %all-to-all-done) | copy-start | bytes 24580
  32.7 3.9 %copy-start = (bf16[1,128,3072]{2,1,0:T(8,128)(2,1)S(1)}, bf16[1,128,3072]{2,1,0:T(8,128)(2,1)}, u32[]{:S(2)}) copy-start(bf16[1,128,3072]{2,1,0:T(8,128)(2,1)} %param.7) | copy-start | bytes 2359300
  32.7 24.6 %all-to-all-start.1 = ((bf16[16,208,256]{2,1,0:T(8,128)(2,1)}), bf16[16,208,256]{2,1,0:T(8,128)(2,1)S(1)}, u32[]{:S(2)}, u32[]{:S(2)}) async-start(bf16[16,208,256]{2,1,0:T(8,128)(2,1)} %pick.1), calls=%async_computation.1 | async-start | bytes 3407872 | tf_op jit(solution)/shard_map/all_to_all | solution.py:350
  36.6 17.5 %copy-start.1 = (bf16[128,3072]{1,0:T(8,128)(2,1)S(1)}, bf16[128,3072]{1,0:T(8,128)(2,1)}, u32[]{:S(2)}) copy-start(bf16[128,3072]{1,0:T(8,128)(2,1)} %cotangent.1) | copy-start | bytes 2359300
  37.2 9.9 %collective-permute-start.4 = (bf16[128,768]{1,0:T(8,128)(2,1)S(1)}, bf16[128,768]{1,0:T(8,128)(2,1)S(1)}, u32[]{:S(2)}, u32[]{:S(2)}) collective-permute-start(bf16[128,768]{1,0:T(8,128)(2,1)S(1)} %get-tuple-element.31), channel_id=1, source_target_pairs={{0,192},{64,128},{128,64},{192,0},{1,193},{65,129},{129,65},{193,1... | collective-permute-start | bytes 589832 | tf_op jit(solution)/shard_map/ppermute | solution.py:370
  41.8 12.4 %collective-permute-start.5 = (bf16[128,768]{1,0:T(8,128)(2,1)S(1)}, bf16[128,768]{1,0:T(8,128)(2,1)S(1)}, u32[]{:S(2)}, u32[]{:S(2)}) collective-permute-start(bf16[128,768]{1,0:T(8,128)(2,1)S(1)} %get-tuple-element.32), channel_id=1, source_target_pairs={{0,128},{64,192},{128,0},{192,64},{1,129},{65,193},{129,1},{193,65... | collective-permute-start | bytes 589832 | tf_op jit(solution)/shard_map/ppermute | solution.py:370
  45.8 8.3 %collective-permute-start.6 = (bf16[128,768]{1,0:T(8,128)(2,1)S(1)}, bf16[128,768]{1,0:T(8,128)(2,1)S(1)}, u32[]{:S(2)}, u32[]{:S(2)}) collective-permute-start(bf16[128,768]{1,0:T(8,128)(2,1)S(1)} %get-tuple-element.33), channel_id=1, source_target_pairs={{0,64},{64,0},{128,192},{192,128},{1,65},{65,1},{129,193},{193,129... | collective-permute-start | bytes 589832 | tf_op jit(solution)/shard_map/ppermute | solution.py:370
  61.8 6.5 %copy-start.6 = (bf16[4,128,768]{2,1,0:T(8,128)(2,1)S(1)}, bf16[4,128,768]{2,1,0:T(8,128)(2,1)}, u32[]{:S(2)}) copy-start(bf16[4,128,768]{2,1,0:T(8,128)(2,1)} %get-tuple-element.36.out) | copy-start | bytes 2359300
  61.8 27.7 %all-to-all-start.2 = ((bf16[16,208,256]{2,1,0:T(8,128)(2,1)}), bf16[16,208,256]{2,1,0:T(8,128)(2,1)S(1)}, u32[]{:S(2)}, u32[]{:S(2)}) async-start(bf16[16,208,256]{2,1,0:T(8,128)(2,1)} %get-tuple-element.41), calls=%async_computation.2 | async-start | bytes 3407872 | tf_op jit(solution)/shard_map/all_to_all | solution.py:350
  68.3 21.1 %copy-start.3 = (s32[16,1,128]{2,1,0:T(1,128)S(1)}, s32[16,1,128]{2,1,0:T(1,128)}, u32[]{:S(2)}) copy-start(s32[16,1,128]{2,1,0:T(1,128)} %copy-done.2) | copy-start | bytes 24580
  68.4 9.8 %collective-permute-start.7 = (bf16[128,768]{1,0:T(8,128)(2,1)S(1)}, bf16[128,768]{1,0:T(8,128)(2,1)S(1)}, u32[]{:S(2)}, u32[]{:S(2)}) collective-permute-start(bf16[128,768]{1,0:T(8,128)(2,1)S(1)} %get-tuple-element.37), channel_id=1, source_target_pairs={{0,192},{64,128},{128,64},{192,0},{1,193},{65,129},{129,65},{193,1... | collective-permute-start | bytes 589832 | tf_op jit(solution)/shard_map/ppermute | solution.py:370
  73.4 10.9 %collective-permute-start.8 = (bf16[128,768]{1,0:T(8,128)(2,1)S(1)}, bf16[128,768]{1,0:T(8,128)(2,1)S(1)}, u32[]{:S(2)}, u32[]{:S(2)}) collective-permute-start(bf16[128,768]{1,0:T(8,128)(2,1)S(1)} %get-tuple-element.38), channel_id=1, source_target_pairs={{0,128},{64,192},{128,0},{192,64},{1,129},{65,193},{129,1},{193,65... | collective-permute-start | bytes 589832 | tf_op jit(solution)/shard_map/ppermute | solution.py:370
  76.7 7.7 %collective-permute-start.9 = (bf16[128,768]{1,0:T(8,128)(2,1)S(1)}, bf16[128,768]{1,0:T(8,128)(2,1)S(1)}, u32[]{:S(2)}, u32[]{:S(2)}) collective-permute-start(bf16[128,768]{1,0:T(8,128)(2,1)S(1)} %get-tuple-element.39), channel_id=1, source_target_pairs={{0,64},{64,0},{128,192},{192,128},{1,65},{65,1},{129,193},{193,129... | collective-permute-start | bytes 589832 | tf_op jit(solution)/shard_map/ppermute | solution.py:370
  86.4 34.6 %copy-start.4 = (bf16[1,4,48,256]{3,2,1,0:T(8,128)(2,1)S(1)}, bf16[1,4,48,256]{3,2,1,0:T(8,128)(2,1)}, u32[]{:S(2)}) copy-start(bf16[1,4,48,256]{3,2,1,0:T(8,128)(2,1)} %param.11) | copy-start | bytes 294916
  86.4 34.6 %copy-start.5 = (bf16[1,48,256]{2,1,0:T(8,128)(2,1)S(1)}, bf16[1,48,256]{2,1,0:T(8,128)(2,1)}, u32[]{:S(2)}) copy-start(bf16[1,48,256]{2,1,0:T(8,128)(2,1)} %param.10) | copy-start | bytes 73732
  90.6 22.4 %collective-permute-start.10 = (bf16[208,256]{1,0:T(8,128)(2,1)S(1)}, bf16[208,256]{1,0:T(8,128)(2,1)S(1)}, u32[]{:S(2)}, u32[]{:S(2)}) collective-permute-start(bf16[208,256]{1,0:T(8,128)(2,1)S(1)} %get-tuple-element.43), channel_id=1, source_target_pairs={{0,8},{4,44},{8,0},{12,36},{16,72},{20,108},{24,64},{28,100},{32,1... | collective-permute-start | bytes 319496 | tf_op jit(solution)/shard_map/ppermute | solution.py:365
  103.6 17.3 %collective-permute-start.11 = (bf16[208,256]{1,0:T(8,128)(2,1)S(1)}, bf16[208,256]{1,0:T(8,128)(2,1)S(1)}, u32[]{:S(2)}, u32[]{:S(2)}) collective-permute-start(bf16[208,256]{1,0:T(8,128)(2,1)S(1)} %get-tuple-element.44), channel_id=1, source_target_pairs={{0,4},{4,40},{8,12},{12,32},{16,68},{20,104},{24,76},{28,96},{32,1... | collective-permute-start | bytes 319496 | tf_op jit(solution)/shard_map/ppermute | solution.py:365
  103.8 17.1 %collective-permute-start.12 = (bf16[208,256]{1,0:T(8,128)(2,1)S(1)}, bf16[208,256]{1,0:T(8,128)(2,1)S(1)}, u32[]{:S(2)}, u32[]{:S(2)}) collective-permute-start(bf16[208,256]{1,0:T(8,128)(2,1)S(1)} %get-tuple-element.45), channel_id=1, source_target_pairs={{0,12},{4,32},{8,4},{12,40},{16,76},{20,96},{24,68},{28,104},{32,1... | collective-permute-start | bytes 319496 | tf_op jit(solution)/shard_map/ppermute | solution.py:365
  109.2 11.7 %collective-permute-start.13 = (bf16[208,256]{1,0:T(8,128)(2,1)S(1)}, bf16[208,256]{1,0:T(8,128)(2,1)S(1)}, u32[]{:S(2)}, u32[]{:S(2)}) collective-permute-start(bf16[208,256]{1,0:T(8,128)(2,1)S(1)} %get-tuple-element.46), channel_id=1, source_target_pairs={{0,0},{4,36},{8,8},{12,44},{16,64},{20,100},{24,72},{28,108},{32,1... | collective-permute-start | bytes 319496 | tf_op jit(solution)/shard_map/ppermute | solution.py:365

commit v12 on v11

--- a/solution.py
+++ b/solution.py
@@ -69,18 +69,20 @@
 
 
 def pick_kernel(ids, z, *refs):
-    held, out = [refs[0], refs[1], refs[3], refs[2]], refs[NZ]
+    held, out, ready = [refs[0], refs[1], refs[3], refs[2]], refs[NZ], refs[NZ + 1]
     step = pl.program_id(0)
     tile = held[0][PIECE:, :].astype(F32)
     for k in range(1, NZ):
         tile = tile + held[k][PIECE:, :].astype(F32)
     tile = tile.astype(BF)
+    for k in range(NZ):
+        to = pl.multiple_of(((z[0] + NZ - k) % NZ) * SHARD, TILE)
+        for d in range(DOMAINS):
+            ready[d, pl.ds(to, SHARD), :] = held[k][d * SHARD : (d + 1) * SHARD, :]
+    for d in range(DOMAINS):
+        ready[d, PIECE:, :] = tile
     for i in range(out.shape[0]):
-        start = pl.multiple_of(ids[step * out.shape[0] + i, 0] * SHARD, TILE)
-        for k in range(NZ):
-            to = pl.multiple_of(((z[0] + NZ - k) % NZ) * SHARD, TILE)
-            out[i, pl.ds(to, SHARD), :] = held[k][pl.ds(start, SHARD), :]
-        out[i, PIECE:, :] = tile
+        out[i] = ready[ids[step * out.shape[0] + i, 0]]
 
 
 def pick(ids, z, held):
@@ -91,6 +93,7 @@
         out_shape=jax.ShapeDtypeStruct((NY * NX, BLOCK, GS), BF),
         in_specs=[SMEM, SMEM] + [pl.BlockSpec((BLOCK, GS), lambda i: (0, 0))] * NZ,
         out_specs=pl.BlockSpec((NY * NX, BLOCK, GS), lambda i: (i, 0, 0)),
+        scratch_shapes=[pltpu.VMEM((DOMAINS, BLOCK, GS), BF)],
     )(ids, z, held[0], held[1], held[3], held[2])
 
 

time: 123 us -> 123 us (level)
  no operation moved by 1% of the time
where the time goes in v12:
time: 123 us; the launch traced here: 122 us
  starting transfers between devices  71.1 us (58%)
  waiting for transfers between devices  35.8 us (29%)
  Pallas kernels  13.2 us (11%)
  between operations  1.46 us (1%)
    ppermute x8, starting transfers between devices, turned(): return lax.ppermute(block, ('zhi', 'core', 'y', 'zlo'), pairs)  39.5 us
    ppermute x6, starting transfers between devices, swapped(): return lax.ppermute(block, ('zhi', 'core'), pairs)  16.9 us
    ppermute x6, waiting for transfers between devices, swapped(): return lax.ppermute(block, ('zhi', 'core'), pairs)  16 us
    all_to_all x3, starting transfers between devices, exchange(): return lax.all_to_all(block, axes, 0, 0, tiled=True)  14.7 us
    all_to_all x3, waiting for transfers between devices, exchange(): return lax.all_to_all(block, axes, 0, 0, tiled=True)  11.9 us
    ppermute x8, waiting for transfers between devices, turned(): return lax.ppermute(block, ('zhi', 'core', 'y', 'zlo'), pairs)  7.93 us
    pallas_call x1, Pallas kernels, layers(): call(layers_kernel, 'layers', out_shape=(pltpu.HBM((SECTIONS, ROWS, SLAB)...  4.38 us
  transfers between devices with their start and end apart: 17, of which 8 were waited for; matrix products, arithmetic and copies ran while one was open for 0% of the time, Pallas kernels for 3%

profile of v12, /device:TPU:1, one launch (start us, length us, event | category | flops | bytes accessed | tf_op | source)
XLA Modules:
  0.0 121.7 jit_solution(12541417281743567504)
XLA Ops:
  1.3 1.6 %prep.1 = (bf16[208,256]{1,0:T(8,128)(2,1)}, s32[16,1,128]{2,1,0:T(1,128)}) custom-call(s32[1]{0:T(128)S(6)} %add.16.at, s32[1]{0:T(128)S(6)} %copy.13.own, bf16[48,256]{1,0:T(8,128)(2,1)} %bitcast.21, bf16[4,48,256]{2,1,0:T(8,128)(2,1)} %bitcast.19, bf16[1,48]{1,0:T(2,128)(2,1)} %sb.1, bf16[4,48]{1,0:T(4,128)(2,1)} %bitcast.24), custom_call_target="tpu_custom_call" | custom-call | flops 99999997952 | bytes 1000000000 | tf_op jit(solution)/shard_map/prep/pallas_call | solution.py:57
  2.9 5.4 %collective-permute-start.3 = (bf16[208,256]{1,0:T(8,128)(2,1)}, bf16[208,256]{1,0:T(8,128)(2,1)S(1)}, u32[]{:S(2)}, u32[]{:S(2)}) collective-permute-start(bf16[208,256]{1,0:T(8,128)(2,1)} %get-tuple-element.29), channel_id=1, source_target_pairs={{0,8},{4,140},{8,0},{12,132},{16,72},{20,204},{24,64},{28,196},{32... | collective-permute-start | bytes 319496 | tf_op jit(solution)/shard_map/ppermute | solution.py:368
  8.3 4.5 %collective-permute-start.2 = (bf16[208,256]{1,0:T(8,128)(2,1)}, bf16[208,256]{1,0:T(8,128)(2,1)S(1)}, u32[]{:S(2)}, u32[]{:S(2)}) collective-permute-start(bf16[208,256]{1,0:T(8,128)(2,1)} %get-tuple-element.29), channel_id=1, source_target_pairs={{0,140},{4,0},{8,132},{12,8},{16,204},{20,64},{24,196},{28,72},{32... | collective-permute-start | bytes 319496 | tf_op jit(solution)/shard_map/ppermute | solution.py:368
  12.8 4.2 %collective-permute-start.1 = (bf16[208,256]{1,0:T(8,128)(2,1)}, bf16[208,256]{1,0:T(8,128)(2,1)S(1)}, u32[]{:S(2)}, u32[]{:S(2)}) collective-permute-start(bf16[208,256]{1,0:T(8,128)(2,1)} %get-tuple-element.29), channel_id=1, source_target_pairs={{0,132},{4,8},{8,140},{12,0},{16,196},{20,72},{24,204},{28,64},{32... | collective-permute-start | bytes 319496 | tf_op jit(solution)/shard_map/ppermute | solution.py:368
  17.0 3.0 %collective-permute-start = (bf16[208,256]{1,0:T(8,128)(2,1)}, bf16[208,256]{1,0:T(8,128)(2,1)S(1)}, u32[]{:S(2)}, u32[]{:S(2)}) collective-permute-start(bf16[208,256]{1,0:T(8,128)(2,1)} %get-tuple-element.29), channel_id=1, source_target_pairs={{0,0},{4,132},{8,8},{12,140},{16,64},{20,196},{24,72},{28,204},{32... | collective-permute-start | bytes 319496 | tf_op jit(solution)/shard_map/ppermute | solution.py:368
  20.0 4.3 %all-to-all-start = ((s32[16,1,128]{2,1,0:T(1,128)}), s32[16,1,128]{2,1,0:T(1,128)S(1)}, u32[]{:S(2)}, u32[]{:S(2)}) async-start(s32[16,1,128]{2,1,0:T(1,128)} %get-tuple-element.28), calls=%async_computation | async-start | bytes 16384 | tf_op jit(solution)/shard_map/all_to_all | solution.py:353
  24.4 0.1 pad_add_fusion.s
  24.5 6.2 %all-to-all-done = s32[16,1,128]{2,1,0:T(1,128)S(1)} async-done(((s32[16,1,128]{2,1,0:T(1,128)}), s32[16,1,128]{2,1,0:T(1,128)S(1)}, u32[]{:S(2)}, u32[]{:S(2)}) %all-to-all-start) | async-done | bytes 8224 | tf_op jit(solution)/shard_map/all_to_all | solution.py:353
  30.7 0.0 collective-permute-done.3.refs_3_
  30.7 0.0 collective-permute-done.2.refs_2_
  30.7 0.0 collective-permute-done.1.refs_1_
  30.7 0.0 collective-permute-done.refs_0_
  30.7 2.0 %pick.1 = bf16[16,208,256]{2,1,0:T(8,128)(2,1)} custom-call(s32[16,128]{1,0:T(8,128)S(1)} %bitcast.17, s32[1]{0:T(128)} %bitcast.2.z, bf16[208,256]{1,0:T(8,128)(2,1)S(1)} %collective-permute-done.refs_0_, bf16[208,256]{1,0:T(8,128)(2,1)S(1)} %collective-permute-done.1.refs_1_, bf16[208,256]{1,0:T(8,128)(2,1)S(1)} %collective-permute-done.2.refs_2_, ...), custom_call_target="tpu_custom_call" | custom-call | flops 99999997952 | bytes 1000000000 | tf_op jit(solution)/shard_map/pick/pallas_call | solution.py:89
  32.8 0.0 copy-done.2
  32.8 3.8 %all-to-all-start.1 = ((bf16[16,208,256]{2,1,0:T(8,128)(2,1)}), bf16[16,208,256]{2,1,0:T(8,128)(2,1)S(1)}, u32[]{:S(2)}, u32[]{:S(2)}) async-start(bf16[16,208,256]{2,1,0:T(8,128)(2,1)} %pick.1), calls=%async_computation.1 | async-start | bytes 3407872 | tf_op jit(solution)/shard_map/all_to_all | solution.py:353
  36.6 0.0 copy-done
  36.6 0.0 copy-start.1
  36.6 0.6 cut.1
  37.2 4.6 %collective-permute-start.4 = (bf16[128,768]{1,0:T(8,128)(2,1)S(1)}, bf16[128,768]{1,0:T(8,128)(2,1)S(1)}, u32[]{:S(2)}, u32[]{:S(2)}) collective-permute-start(bf16[128,768]{1,0:T(8,128)(2,1)S(1)} %get-tuple-element.31), channel_id=1, source_target_pairs={{0,192},{64,128},{128,64},{192,0},{1,193},{65,129},{129,65},{193,1... | collective-permute-start | bytes 589832 | tf_op jit(solution)/shard_map/ppermute | solution.py:373
  41.8 4.0 %collective-permute-start.5 = (bf16[128,768]{1,0:T(8,128)(2,1)S(1)}, bf16[128,768]{1,0:T(8,128)(2,1)S(1)}, u32[]{:S(2)}, u32[]{:S(2)}) collective-permute-start(bf16[128,768]{1,0:T(8,128)(2,1)S(1)} %get-tuple-element.32), channel_id=1, source_target_pairs={{0,128},{64,192},{128,0},{192,64},{1,129},{65,193},{129,1},{193,65... | collective-permute-start | bytes 589832 | tf_op jit(solution)/shard_map/ppermute | solution.py:373
  45.9 0.0 collective-permute-start.6
  45.9 1.3 %collective-permute-done.4.other3 = bf16[128,768]{1,0:T(8,128)(2,1)S(1)} collective-permute-done((bf16[128,768]{1,0:T(8,128)(2,1)S(1)}, bf16[128,768]{1,0:T(8,128)(2,1)S(1)}, u32[]{:S(2)}, u32[]{:S(2)}) %collective-permute-start.4) | collective-permute-done | bytes 196640 | tf_op jit(solution)/shard_map/ppermute | solution.py:373
  47.1 7.0 %collective-permute-done.5.other2 = bf16[128,768]{1,0:T(8,128)(2,1)S(1)} collective-permute-done((bf16[128,768]{1,0:T(8,128)(2,1)S(1)}, bf16[128,768]{1,0:T(8,128)(2,1)S(1)}, u32[]{:S(2)}, u32[]{:S(2)}) %collective-permute-start.5) | collective-permute-done | bytes 196640 | tf_op jit(solution)/shard_map/ppermute | solution.py:373
  54.2 0.0 collective-permute-done.6.other1
  54.2 0.6 gather.1
  54.8 2.6 %all-to-all-done.1.got = bf16[16,208,256]{2,1,0:T(8,128)(2,1)S(1)} async-done(((bf16[16,208,256]{2,1,0:T(8,128)(2,1)}), bf16[16,208,256]{2,1,0:T(8,128)(2,1)S(1)}, u32[]{:S(2)}, u32[]{:S(2)}) %all-to-all-start.1) | async-done | bytes 1703968 | tf_op jit(solution)/shard_map/all_to_all | solution.py:353
  57.4 4.4 %layers.1 = (bf16[4,128,768]{2,1,0:T(8,128)(2,1)}, bf16[16,208,256]{2,1,0:T(8,128)(2,1)}) custom-call(s32[2]{0:T(128)S(1)} %pad_add_fusion.s, s32[1]{0:T(128)S(6)} %copy.13.own, bf16[128,768]{1,0:T(8,128)(2,1)S(1)} %get-tuple-element.34.top, bf16[16,208,256]{2,1,0:T(8,128)(2,1)S(1)} %all-to-all-done.1.got, bf16[4,128,768]{2,1,0:T(8,128)(2,1)S(1)} %get-tuple-element.35.x), custom_call_target="tpu_custom_call" | custom-call | flops 99999997952 | bytes 1000000000 | tf_op jit(solution)/shard_map/layers/pallas_call | solution.py:200
  61.8 6.5 %all-to-all-start.2 = ((bf16[16,208,256]{2,1,0:T(8,128)(2,1)}), bf16[16,208,256]{2,1,0:T(8,128)(2,1)S(1)}, u32[]{:S(2)}, u32[]{:S(2)}) async-start(bf16[16,208,256]{2,1,0:T(8,128)(2,1)} %get-tuple-element.41), calls=%async_computation.2 | async-start | bytes 3407872 | tf_op jit(solution)/shard_map/all_to_all | solution.py:353
  68.3 0.0 copy-start.3
  68.4 0.1 split.1
  68.4 5.0 %collective-permute-start.7 = (bf16[128,768]{1,0:T(8,128)(2,1)S(1)}, bf16[128,768]{1,0:T(8,128)(2,1)S(1)}, u32[]{:S(2)}, u32[]{:S(2)}) collective-permute-start(bf16[128,768]{1,0:T(8,128)(2,1)S(1)} %get-tuple-element.37), channel_id=1, source_target_pairs={{0,192},{64,128},{128,64},{192,0},{1,193},{65,129},{129,65},{193,1... | collective-permute-start | bytes 589832 | tf_op jit(solution)/shard_map/ppermute | solution.py:373
  73.4 3.2 %collective-permute-start.8 = (bf16[128,768]{1,0:T(8,128)(2,1)S(1)}, bf16[128,768]{1,0:T(8,128)(2,1)S(1)}, u32[]{:S(2)}, u32[]{:S(2)}) collective-permute-start(bf16[128,768]{1,0:T(8,128)(2,1)S(1)} %get-tuple-element.38), channel_id=1, source_target_pairs={{0,128},{64,192},{128,0},{192,64},{1,129},{65,193},{129,1},{193,65... | collective-permute-start | bytes 589832 | tf_op jit(solution)/shard_map/ppermute | solution.py:373
  76.7 0.0 collective-permute-start.9
  76.7 1.5 %collective-permute-done.7.other3 = bf16[128,768]{1,0:T(8,128)(2,1)S(1)} collective-permute-done((bf16[128,768]{1,0:T(8,128)(2,1)S(1)}, bf16[128,768]{1,0:T(8,128)(2,1)S(1)}, u32[]{:S(2)}, u32[]{:S(2)}) %collective-permute-start.7) | collective-permute-done | bytes 196640 | tf_op jit(solution)/shard_map/ppermute | solution.py:373
  78.2 6.2 %collective-permute-done.8.other2 = bf16[128,768]{1,0:T(8,128)(2,1)S(1)} collective-permute-done((bf16[128,768]{1,0:T(8,128)(2,1)S(1)}, bf16[128,768]{1,0:T(8,128)(2,1)S(1)}, u32[]{:S(2)}, u32[]{:S(2)}) %collective-permute-start.8) | collective-permute-done | bytes 196640 | tf_op jit(solution)/shard_map/ppermute | solution.py:373
  84.3 0.0 collective-permute-done.9.other1
  84.3 2.0 %join.1 = bf16[128,3072]{1,0:T(8,128)(2,1)} custom-call(s32[2]{0:T(128)S(1)} %pad_add_fusion.s, bf16[128,768]{1,0:T(8,128)(2,1)S(1)} %collective-permute-done.7.other3, bf16[128,768]{1,0:T(8,128)(2,1)S(1)} %collective-permute-done.8.other2, bf16[128,768]{1,0:T(8,128)(2,1)S(1)} %collective-permute-done.9.other1, bf16[128,768]{1,0:T(8,128)(2,1)S(1)} %get-tuple-element.40.own), custom_call_target="tpu_custom_call" | custom-call | tf_op jit(solution)/shard_map/join/pallas_call | solution.py:253
  86.4 3.1 %all-to-all-done.2.got = bf16[16,208,256]{2,1,0:T(8,128)(2,1)S(1)} async-done(((bf16[16,208,256]{2,1,0:T(8,128)(2,1)}), bf16[16,208,256]{2,1,0:T(8,128)(2,1)S(1)}, u32[]{:S(2)}, u32[]{:S(2)}) %all-to-all-start.2) | async-done | bytes 1703968 | tf_op jit(solution)/shard_map/all_to_all | solution.py:353
  89.5 1.1 merge.1
  90.6 13.1 %collective-permute-start.10 = (bf16[208,256]{1,0:T(8,128)(2,1)S(1)}, bf16[208,256]{1,0:T(8,128)(2,1)S(1)}, u32[]{:S(2)}, u32[]{:S(2)}) collective-permute-start(bf16[208,256]{1,0:T(8,128)(2,1)S(1)} %get-tuple-element.43), channel_id=1, source_target_pairs={{0,8},{4,44},{8,0},{12,36},{16,72},{20,108},{24,64},{28,100},{32,1... | collective-permute-start | bytes 319496 | tf_op jit(solution)/shard_map/ppermute | solution.py:368
  103.6 0.2 collective-permute-start.11
  103.8 5.4 %collective-permute-start.12 = (bf16[208,256]{1,0:T(8,128)(2,1)S(1)}, bf16[208,256]{1,0:T(8,128)(2,1)S(1)}, u32[]{:S(2)}, u32[]{:S(2)}) collective-permute-start(bf16[208,256]{1,0:T(8,128)(2,1)S(1)} %get-tuple-element.45), channel_id=1, source_target_pairs={{0,12},{4,32},{8,4},{12,40},{16,76},{20,96},{24,68},{28,104},{32,1... | collective-permute-start | bytes 319496 | tf_op jit(solution)/shard_map/ppermute | solution.py:368
  109.2 3.8 %collective-permute-start.13 = (bf16[208,256]{1,0:T(8,128)(2,1)S(1)}, bf16[208,256]{1,0:T(8,128)(2,1)S(1)}, u32[]{:S(2)}, u32[]{:S(2)}) collective-permute-start(bf16[208,256]{1,0:T(8,128)(2,1)S(1)} %get-tuple-element.46), channel_id=1, source_target_pairs={{0,0},{4,36},{8,8},{12,44},{16,64},{20,100},{24,72},{28,108},{32,1... | collective-permute-start | bytes 319496 | tf_op jit(solution)/shard_map/ppermute | solution.py:368
  113.0 0.0 collective-permute-done.10.refs_0_
  113.0 7.9 %collective-permute-done.11.refs_1_ = bf16[208,256]{1,0:T(8,128)(2,1)S(1)} collective-permute-done((bf16[208,256]{1,0:T(8,128)(2,1)S(1)}, bf16[208,256]{1,0:T(8,128)(2,1)S(1)}, u32[]{:S(2)}, u32[]{:S(2)}) %collective-permute-start.11) | collective-permute-done | bytes 106528 | tf_op jit(solution)/shard_map/ppermute | solution.py:368
  120.9 0.0 collective-permute-done.12.refs_2_
  120.9 0.0 collective-permute-done.13.refs_3_
  121.0 0.8 finish.1
  (10 shorter events, 0.0 us)
Async XLA Ops:
  2.9 27.8 %collective-permute-start.3 = (bf16[208,256]{1,0:T(8,128)(2,1)}, bf16[208,256]{1,0:T(8,128)(2,1)S(1)}, u32[]{:S(2)}, u32[]{:S(2)}) collective-permute-start(bf16[208,256]{1,0:T(8,128)(2,1)} %get-tuple-element.29), channel_id=1, source_target_pairs={{0,8},{4,140},{8,0},{12,132},{16,72},{20,204},{24,64},{28,196},{32... | collective-permute-start | bytes 319496 | tf_op jit(solution)/shard_map/ppermute | solution.py:368
  8.3 22.4 %collective-permute-start.2 = (bf16[208,256]{1,0:T(8,128)(2,1)}, bf16[208,256]{1,0:T(8,128)(2,1)S(1)}, u32[]{:S(2)}, u32[]{:S(2)}) collective-permute-start(bf16[208,256]{1,0:T(8,128)(2,1)} %get-tuple-element.29), channel_id=1, source_target_pairs={{0,140},{4,0},{8,132},{12,8},{16,204},{20,64},{24,196},{28,72},{32... | collective-permute-start | bytes 319496 | tf_op jit(solution)/shard_map/ppermute | solution.py:368
  12.8 17.9 %collective-permute-start.1 = (bf16[208,256]{1,0:T(8,128)(2,1)}, bf16[208,256]{1,0:T(8,128)(2,1)S(1)}, u32[]{:S(2)}, u32[]{:S(2)}) collective-permute-start(bf16[208,256]{1,0:T(8,128)(2,1)} %get-tuple-element.29), channel_id=1, source_target_pairs={{0,132},{4,8},{8,140},{12,0},{16,196},{20,72},{24,204},{28,64},{32... | collective-permute-start | bytes 319496 | tf_op jit(solution)/shard_map/ppermute | solution.py:368
  17.0 13.7 %collective-permute-start = (bf16[208,256]{1,0:T(8,128)(2,1)}, bf16[208,256]{1,0:T(8,128)(2,1)S(1)}, u32[]{:S(2)}, u32[]{:S(2)}) collective-permute-start(bf16[208,256]{1,0:T(8,128)(2,1)} %get-tuple-element.29), channel_id=1, source_target_pairs={{0,0},{4,132},{8,8},{12,140},{16,64},{20,196},{24,72},{28,204},{32... | collective-permute-start | bytes 319496 | tf_op jit(solution)/shard_map/ppermute | solution.py:368
  20.0 10.7 %all-to-all-start = ((s32[16,1,128]{2,1,0:T(1,128)}), s32[16,1,128]{2,1,0:T(1,128)S(1)}, u32[]{:S(2)}, u32[]{:S(2)}) async-start(s32[16,1,128]{2,1,0:T(1,128)} %get-tuple-element.28), calls=%async_computation | async-start | bytes 16384 | tf_op jit(solution)/shard_map/all_to_all | solution.py:353
  30.7 2.1 %copy-start.2 = (s32[16,1,128]{2,1,0:T(1,128)}, s32[16,1,128]{2,1,0:T(1,128)S(1)}, u32[]{:S(2)}) copy-start(s32[16,1,128]{2,1,0:T(1,128)S(1)} %all-to-all-done) | copy-start | bytes 24580
  32.8 3.9 %copy-start = (bf16[1,128,3072]{2,1,0:T(8,128)(2,1)S(1)}, bf16[1,128,3072]{2,1,0:T(8,128)(2,1)}, u32[]{:S(2)}) copy-start(bf16[1,128,3072]{2,1,0:T(8,128)(2,1)} %param.7) | copy-start | bytes 2359300
  32.8 24.6 %all-to-all-start.1 = ((bf16[16,208,256]{2,1,0:T(8,128)(2,1)}), bf16[16,208,256]{2,1,0:T(8,128)(2,1)S(1)}, u32[]{:S(2)}, u32[]{:S(2)}) async-start(bf16[16,208,256]{2,1,0:T(8,128)(2,1)} %pick.1), calls=%async_computation.1 | async-start | bytes 3407872 | tf_op jit(solution)/shard_map/all_to_all | solution.py:353
  36.6 17.5 %copy-start.1 = (bf16[128,3072]{1,0:T(8,128)(2,1)S(1)}, bf16[128,3072]{1,0:T(8,128)(2,1)}, u32[]{:S(2)}) copy-start(bf16[128,3072]{1,0:T(8,128)(2,1)} %cotangent.1) | copy-start | bytes 2359300
  37.2 9.9 %collective-permute-start.4 = (bf16[128,768]{1,0:T(8,128)(2,1)S(1)}, bf16[128,768]{1,0:T(8,128)(2,1)S(1)}, u32[]{:S(2)}, u32[]{:S(2)}) collective-permute-start(bf16[128,768]{1,0:T(8,128)(2,1)S(1)} %get-tuple-element.31), channel_id=1, source_target_pairs={{0,192},{64,128},{128,64},{192,0},{1,193},{65,129},{129,65},{193,1... | collective-permute-start | bytes 589832 | tf_op jit(solution)/shard_map/ppermute | solution.py:373
  41.8 12.4 %collective-permute-start.5 = (bf16[128,768]{1,0:T(8,128)(2,1)S(1)}, bf16[128,768]{1,0:T(8,128)(2,1)S(1)}, u32[]{:S(2)}, u32[]{:S(2)}) collective-permute-start(bf16[128,768]{1,0:T(8,128)(2,1)S(1)} %get-tuple-element.32), channel_id=1, source_target_pairs={{0,128},{64,192},{128,0},{192,64},{1,129},{65,193},{129,1},{193,65... | collective-permute-start | bytes 589832 | tf_op jit(solution)/shard_map/ppermute | solution.py:373
  45.9 8.3 %collective-permute-start.6 = (bf16[128,768]{1,0:T(8,128)(2,1)S(1)}, bf16[128,768]{1,0:T(8,128)(2,1)S(1)}, u32[]{:S(2)}, u32[]{:S(2)}) collective-permute-start(bf16[128,768]{1,0:T(8,128)(2,1)S(1)} %get-tuple-element.33), channel_id=1, source_target_pairs={{0,64},{64,0},{128,192},{192,128},{1,65},{65,1},{129,193},{193,129... | collective-permute-start | bytes 589832 | tf_op jit(solution)/shard_map/ppermute | solution.py:373
  61.8 6.5 %copy-start.6 = (bf16[4,128,768]{2,1,0:T(8,128)(2,1)S(1)}, bf16[4,128,768]{2,1,0:T(8,128)(2,1)}, u32[]{:S(2)}) copy-start(bf16[4,128,768]{2,1,0:T(8,128)(2,1)} %get-tuple-element.36.out) | copy-start | bytes 2359300
  61.8 27.7 %all-to-all-start.2 = ((bf16[16,208,256]{2,1,0:T(8,128)(2,1)}), bf16[16,208,256]{2,1,0:T(8,128)(2,1)S(1)}, u32[]{:S(2)}, u32[]{:S(2)}) async-start(bf16[16,208,256]{2,1,0:T(8,128)(2,1)} %get-tuple-element.41), calls=%async_computation.2 | async-start | bytes 3407872 | tf_op jit(solution)/shard_map/all_to_all | solution.py:353
  68.3 21.1 %copy-start.3 = (s32[16,1,128]{2,1,0:T(1,128)S(1)}, s32[16,1,128]{2,1,0:T(1,128)}, u32[]{:S(2)}) copy-start(s32[16,1,128]{2,1,0:T(1,128)} %copy-done.2) | copy-start | bytes 24580
  68.4 9.7 %collective-permute-start.7 = (bf16[128,768]{1,0:T(8,128)(2,1)S(1)}, bf16[128,768]{1,0:T(8,128)(2,1)S(1)}, u32[]{:S(2)}, u32[]{:S(2)}) collective-permute-start(bf16[128,768]{1,0:T(8,128)(2,1)S(1)} %get-tuple-element.37), channel_id=1, source_target_pairs={{0,192},{64,128},{128,64},{192,0},{1,193},{65,129},{129,65},{193,1... | collective-permute-start | bytes 589832 | tf_op jit(solution)/shard_map/ppermute | solution.py:373
  73.4 10.9 %collective-permute-start.8 = (bf16[128,768]{1,0:T(8,128)(2,1)S(1)}, bf16[128,768]{1,0:T(8,128)(2,1)S(1)}, u32[]{:S(2)}, u32[]{:S(2)}) collective-permute-start(bf16[128,768]{1,0:T(8,128)(2,1)S(1)} %get-tuple-element.38), channel_id=1, source_target_pairs={{0,128},{64,192},{128,0},{192,64},{1,129},{65,193},{129,1},{193,65... | collective-permute-start | bytes 589832 | tf_op jit(solution)/shard_map/ppermute | solution.py:373
  76.7 7.7 %collective-permute-start.9 = (bf16[128,768]{1,0:T(8,128)(2,1)S(1)}, bf16[128,768]{1,0:T(8,128)(2,1)S(1)}, u32[]{:S(2)}, u32[]{:S(2)}) collective-permute-start(bf16[128,768]{1,0:T(8,128)(2,1)S(1)} %get-tuple-element.39), channel_id=1, source_target_pairs={{0,64},{64,0},{128,192},{192,128},{1,65},{65,1},{129,193},{193,129... | collective-permute-start | bytes 589832 | tf_op jit(solution)/shard_map/ppermute | solution.py:373
  86.4 34.6 %copy-start.4 = (bf16[1,4,48,256]{3,2,1,0:T(8,128)(2,1)S(1)}, bf16[1,4,48,256]{3,2,1,0:T(8,128)(2,1)}, u32[]{:S(2)}) copy-start(bf16[1,4,48,256]{3,2,1,0:T(8,128)(2,1)} %param.11) | copy-start | bytes 294916
  86.4 34.6 %copy-start.5 = (bf16[1,48,256]{2,1,0:T(8,128)(2,1)S(1)}, bf16[1,48,256]{2,1,0:T(8,128)(2,1)}, u32[]{:S(2)}) copy-start(bf16[1,48,256]{2,1,0:T(8,128)(2,1)} %param.10) | copy-start | bytes 73732
  90.6 22.4 %collective-permute-start.10 = (bf16[208,256]{1,0:T(8,128)(2,1)S(1)}, bf16[208,256]{1,0:T(8,128)(2,1)S(1)}, u32[]{:S(2)}, u32[]{:S(2)}) collective-permute-start(bf16[208,256]{1,0:T(8,128)(2,1)S(1)} %get-tuple-element.43), channel_id=1, source_target_pairs={{0,8},{4,44},{8,0},{12,36},{16,72},{20,108},{24,64},{28,100},{32,1... | collective-permute-start | bytes 319496 | tf_op jit(solution)/shard_map/ppermute | solution.py:368
  103.6 17.3 %collective-permute-start.11 = (bf16[208,256]{1,0:T(8,128)(2,1)S(1)}, bf16[208,256]{1,0:T(8,128)(2,1)S(1)}, u32[]{:S(2)}, u32[]{:S(2)}) collective-permute-start(bf16[208,256]{1,0:T(8,128)(2,1)S(1)} %get-tuple-element.44), channel_id=1, source_target_pairs={{0,4},{4,40},{8,12},{12,32},{16,68},{20,104},{24,76},{28,96},{32,1... | collective-permute-start | bytes 319496 | tf_op jit(solution)/shard_map/ppermute | solution.py:368
  103.8 17.1 %collective-permute-start.12 = (bf16[208,256]{1,0:T(8,128)(2,1)S(1)}, bf16[208,256]{1,0:T(8,128)(2,1)S(1)}, u32[]{:S(2)}, u32[]{:S(2)}) collective-permute-start(bf16[208,256]{1,0:T(8,128)(2,1)S(1)} %get-tuple-element.45), channel_id=1, source_target_pairs={{0,12},{4,32},{8,4},{12,40},{16,76},{20,96},{24,68},{28,104},{32,1... | collective-permute-start | bytes 319496 | tf_op jit(solution)/shard_map/ppermute | solution.py:368
  109.2 11.7 %collective-permute-start.13 = (bf16[208,256]{1,0:T(8,128)(2,1)S(1)}, bf16[208,256]{1,0:T(8,128)(2,1)S(1)}, u32[]{:S(2)}, u32[]{:S(2)}) collective-permute-start(bf16[208,256]{1,0:T(8,128)(2,1)S(1)} %get-tuple-element.46), channel_id=1, source_target_pairs={{0,0},{4,36},{8,8},{12,44},{16,64},{20,100},{24,72},{28,108},{32,1... | collective-permute-start | bytes 319496 | tf_op jit(solution)/shard_map/ppermute | solution.py:368
